TPU v7x, 512 devices: a whole 4x4x16 slice. The times are simulated.
512 devices in a mesh: rows: 128 (over z, x_lo, y), cols: 4 (over x_hi, core).
Axes of the slice: x: 4 (x_hi: 2, x_lo: 2; x = x_hi * 2 + x_lo), y: 4, z: 16, core: 2. Of those that a mesh axis runs over, the one named last changes fastest.
Arguments:
- feature_one: bfloat16 [1024, 20480], P('rows', 'cols'), may hold values from -6 to 6
- feature_two: bfloat16 [512, 20480], P('rows', 'cols'), may hold values from -6 to 6
- feature_three: bfloat16 [256, 20480], P('rows', 'cols'), may hold values from -6 to 6
- feature_four: bfloat16 [128, 20480], P('rows', 'cols'), may hold values from -6 to 6
- kernel_one: bfloat16 [3, 3, 64, 64], replicated, may hold values from -0.25 to 0.25
- kernel_two: bfloat16 [3, 3, 128, 128], replicated, may hold values from -0.1875 to 0.1875
- kernel_three: bfloat16 [3, 3, 256, 256], replicated, may hold values from -0.125 to 0.125
- project_two: bfloat16 [128, 64], replicated, may hold values from -0.5 to 0.5
- project_three: bfloat16 [256, 64], replicated, may hold values from -0.375 to 0.375
- project_four: bfloat16 [512, 64], replicated, may hold values from -0.25 to 0.25
- cotangent: bfloat16 [1024, 20480], P('rows', 'cols'), may hold values from -6 to 6
Outputs:
- grad_feature_one: bfloat16 [1024, 20480], P('rows', 'cols')
- grad_feature_two: bfloat16 [512, 20480], P('rows', 'cols')
- grad_feature_three: bfloat16 [256, 20480], P('rows', 'cols')
- grad_feature_four: bfloat16 [128, 20480], P('rows', 'cols')
- grad_kernel_one: bfloat16 [3, 3, 64, 64], replicated
- grad_kernel_two: bfloat16 [3, 3, 128, 128], replicated
- grad_kernel_three: bfloat16 [3, 3, 256, 256], replicated
- grad_project_two: bfloat16 [128, 64], replicated
- grad_project_three: bfloat16 [256, 64], replicated
- grad_project_four: bfloat16 [512, 64], replicated
All inputs are finite; a program needn't handle non-finite values.
Results may differ from a plain program's by a relative error of at most 0.017.
Values may be sent and summed in bfloat16 or wider, within the bound.
No kernel may reach another device: no remote copies, remote signals or barrier semaphores. Data moves between devices by JAX's collectives and lax.ppermute only.
A program may use at most 64 MiB of HBM per device.

v0:
```python
import jax
import jax.numpy as jnp
import numpy as np
from jax import lax
from jax.sharding import PartitionSpec as P

FEAT_ONE = 64
FEAT_TWO = 128
FEAT_THREE = 256
FEAT_FOUR = 512


def passed_along(block, axis, distance):
    devices = range(lax.axis_size(axis))
    route = [(i - distance, i) for i in devices if i - distance in devices]
    return lax.ppermute(block, axis, route)


def padded_2(cells, sides, width):
    for axis, dim in sides:
        count = lax.axis_size(axis)
        ends = count - 1
        head = lax.slice_in_dim(cells, 0, width, axis=dim)
        tail = lax.slice_in_dim(cells, cells.shape[dim] - width, cells.shape[dim], axis=dim)
        cells = jnp.concatenate(
            [
                lax.ppermute(tail, axis, [(i, (i + 1) % count) for i in range(ends)]),
                cells,
                lax.ppermute(head, axis, [((i + 1) % count, i) for i in range(ends)]),
            ],
            axis=dim,
        )
    return cells


def up_table(scale):
    places = (np.arange(scale) + 0.5) / scale - 0.5
    table = np.stack([np.maximum(-places, 0.0), 1.0 - np.abs(places), np.maximum(places, 0.0)], 1)
    return jnp.asarray(table, jnp.float32)


def upsample(padded, scale):
    table = up_table(scale)
    row_count = padded.shape[0] - 2
    col_count = padded.shape[1] - 2
    stacked = jnp.stack([padded[offset : offset + row_count] for offset in range(3)])
    finer = jnp.einsum("ij,jkmc->kimc", table, stacked, precision=lax.Precision.HIGHEST)
    finer = finer.reshape(row_count * scale, col_count + 2, -1)
    stacked = jnp.stack([finer[:, offset : offset + col_count] for offset in range(3)])
    finer = jnp.einsum("ij,jakc->akic", table, stacked, precision=lax.Precision.HIGHEST)
    return finer.reshape(row_count * scale, col_count * scale, -1)


def upsample_back(grad_fine, scale):
    table = up_table(scale)
    big_rows, big_cols, chans = grad_fine.shape
    row_count = big_rows // scale
    col_count = big_cols // scale
    split = grad_fine.reshape(big_rows, col_count, scale, chans)
    pieces = jnp.einsum("ij,akic->jakc", table, split, precision=lax.Precision.HIGHEST)
    middle = jnp.zeros((big_rows, col_count + 2, chans), jnp.float32)
    for offset in range(3):
        middle = middle.at[:, offset : offset + col_count].add(pieces[offset])
    split = middle.reshape(row_count, scale, col_count + 2, chans)
    pieces = jnp.einsum("ij,kimc->jkmc", table, split, precision=lax.Precision.HIGHEST)
    result = jnp.zeros((row_count + 2, col_count + 2, chans), jnp.float32)
    for offset in range(3):
        result = result.at[offset : offset + row_count].add(pieces[offset])
    return result


def conv_taps(padded, kernel):
    row_count = padded.shape[0] - 2
    col_count = padded.shape[1] - 2
    total = jnp.zeros((row_count * col_count, kernel.shape[3]), jnp.float32)
    for tap_row in range(3):
        for tap_col in range(3):
            window = padded[tap_row : tap_row + row_count, tap_col : tap_col + col_count].reshape(
                row_count * col_count, -1
            )
            total = total + jnp.dot(
                window, kernel[tap_row, tap_col], preferred_element_type=jnp.float32
            )
    return total.reshape(row_count, col_count, -1)


def kernel_grad(padded, grad_pre):
    row_count, col_count, chans = grad_pre.shape
    flat_grad = grad_pre.reshape(row_count * col_count, chans)
    taps = []
    for tap_row in range(3):
        for tap_col in range(3):
            window = padded[tap_row : tap_row + row_count, tap_col : tap_col + col_count].reshape(
                row_count * col_count, -1
            )
            taps.append(
                lax.dot_general(
                    window, flat_grad, (((0,), (0,)), ((), ())), preferred_element_type=jnp.float32
                )
            )
    return jnp.stack(taps).reshape(3, 3, taps[0].shape[0], chans)


def edge_fix(padded):
    at_top = lax.axis_index("rows") == 0
    at_bottom = lax.axis_index("rows") == lax.axis_size("rows") - 1
    at_left = lax.axis_index("cols") == 0
    at_right = lax.axis_index("cols") == lax.axis_size("cols") - 1
    padded = padded.at[0].set(jnp.where(at_top, padded[1], padded[0]))
    padded = padded.at[-1].set(jnp.where(at_bottom, padded[-2], padded[-1]))
    padded = padded.at[:, 0].set(jnp.where(at_left, padded[:, 1], padded[:, 0]))
    padded = padded.at[:, -1].set(jnp.where(at_right, padded[:, -2], padded[:, -1]))
    return padded


def fold_rims(padded):
    from_above = passed_along(padded[-1], "rows", 1)
    from_below = passed_along(padded[0], "rows", -1)
    from_above = jnp.where(lax.axis_index("rows") == 0, padded[0], from_above)
    from_below = jnp.where(
        lax.axis_index("rows") == lax.axis_size("rows") - 1, padded[-1], from_below
    )
    inner = padded[1:-1].at[0].add(from_above).at[-1].add(from_below)
    from_left = passed_along(inner[:, -1], "cols", 1)
    from_right = passed_along(inner[:, 0], "cols", -1)
    from_left = jnp.where(lax.axis_index("cols") == 0, inner[:, 0], from_left)
    from_right = jnp.where(
        lax.axis_index("cols") == lax.axis_size("cols") - 1, inner[:, -1], from_right
    )
    inner = inner[:, 1:-1]
    return inner.at[:, 0].add(from_left).at[:, -1].add(from_right)


def gelu_back(values, grad_out):
    return jax.vjp(jax.nn.gelu, values)[1](grad_out)[0]


def on_device(
    feature_one,
    feature_two,
    feature_three,
    feature_four,
    kernel_one,
    kernel_two,
    kernel_three,
    project_two,
    project_three,
    project_four,
    cotangent,
):
    widths = (FEAT_ONE, FEAT_TWO, FEAT_THREE, FEAT_FOUR)
    inputs = (feature_one, feature_two, feature_three, feature_four)
    maps = [
        arr.reshape(arr.shape[0], arr.shape[1] // chans, chans)
        for arr, chans in zip(inputs, widths)
    ]
    kernels = (kernel_one, kernel_two, kernel_three)
    projects = (project_two, project_three, project_four)
    scales = (2, 4, 8)
    padded_in = []
    pres = []
    acts = []
    for branch in range(3):
        padded = padded_2(maps[branch], (("rows", 0), ("cols", 1)), 1)
        pre_act = maps[branch].astype(jnp.float32) + conv_taps(padded, kernels[branch])
        padded_in.append(padded)
        pres.append(pre_act)
        acts.append(jax.nn.gelu(pre_act).astype(jnp.bfloat16))
    coarse_in = (acts[1], acts[2], maps[3])
    merged = acts[0].astype(jnp.float32)
    for branch in range(3):
        source = coarse_in[branch]
        shape_now = source.shape
        edged = edge_fix(padded_2(source, (("rows", 0), ("cols", 1)), 1))
        small = jnp.dot(
            edged.reshape(-1, shape_now[2]), projects[branch], preferred_element_type=jnp.float32
        )
        small = small.astype(jnp.bfloat16).reshape(shape_now[0] + 2, shape_now[1] + 2, FEAT_ONE)
        merged = merged + upsample(small.astype(jnp.float32), scales[branch])
    upstream_grad = cotangent.reshape(merged.shape).astype(jnp.float32)
    gate_grad = gelu_back(merged, upstream_grad).astype(jnp.bfloat16)
    gate_float = gate_grad.astype(jnp.float32)
    proj_sums = []
    backs = []
    for branch in range(3):
        source = coarse_in[branch]
        shape_now = source.shape
        small_grad = fold_rims(upsample_back(gate_float, scales[branch])).astype(jnp.bfloat16)
        flat = small_grad.reshape(-1, FEAT_ONE)
        proj_sums.append(
            lax.dot_general(
                source.reshape(-1, shape_now[2]),
                flat,
                (((0,), (0,)), ((), ())),
                preferred_element_type=jnp.float32,
            )
        )
        back = lax.dot_general(
            flat, projects[branch], (((1,), (1,)), ((), ())), preferred_element_type=jnp.float32
        )
        backs.append(back.reshape(shape_now))
    grad_four = backs[2].astype(jnp.bfloat16)
    upstream = (gate_float, backs[0], backs[1])
    feat_grads = []
    kern_sums = []
    for branch in range(3):
        grad_pre = gelu_back(pres[branch], upstream[branch]).astype(jnp.bfloat16)
        grad_padded = padded_2(grad_pre, (("rows", 0), ("cols", 1)), 1)
        flipped = jnp.transpose(kernels[branch][::-1, ::-1], (0, 1, 3, 2))
        back = conv_taps(grad_padded, flipped)
        feat_grads.append((grad_pre.astype(jnp.float32) + back).astype(jnp.bfloat16))
        kern_sums.append(kernel_grad(padded_in[branch], grad_pre))
    total_cells = (
        maps[0].shape[0] * lax.axis_size("rows") * maps[0].shape[1] * lax.axis_size("cols")
    )
    factors = [(total_cells // 4**branch) ** (-0.5) for branch in range(3)]
    factors = factors + [(total_cells // 4 ** (branch + 1)) ** (-0.5) for branch in range(3)]
    totals = lax.psum(
        (kern_sums[0], kern_sums[1], kern_sums[2], proj_sums[0], proj_sums[1], proj_sums[2]),
        ("rows", "cols"),
    )
    finals = [(totals[index] * factors[index]).astype(jnp.bfloat16) for index in range(6)]
    outputs = [grad.reshape(arr.shape) for grad, arr in zip(feat_grads, inputs[:3])]
    return (
        outputs[0],
        outputs[1],
        outputs[2],
        grad_four.reshape(feature_four.shape),
        finals[0],
        finals[1],
        finals[2],
        finals[3],
        finals[4],
        finals[5],
    )


def solution(mesh):
    in_specs = (
        P("rows", "cols"),
        P("rows", "cols"),
        P("rows", "cols"),
        P("rows", "cols"),
        P(),
        P(),
        P(),
        P(),
        P(),
        P(),
        P("rows", "cols"),
    )
    out_specs = (
        P("rows", "cols"),
        P("rows", "cols"),
        P("rows", "cols"),
        P("rows", "cols"),
        P(),
        P(),
        P(),
        P(),
        P(),
        P(),
    )
    return jax.shard_map(
        on_device, mesh=mesh, in_specs=in_specs, out_specs=out_specs, check_vma=False
    )
```

profile of v0, /device:TPU:1, one launch (start us, length us, event | category | flops | bytes accessed | tf_op | source)
XLA Modules:
  0.0 943.9 jit_solution(16950409552419549524)
XLA Ops:
  8.1 4.6 collective-permute-start.20
  17.3 4.6 collective-permute-start
  23.5 3.3 collective-permute-start.12
  44.3 4.0 collective-permute-start.4
  50.4 7.7 collective-permute-start.3
  62.4 2.5 collective-permute-start.14
  68.6 2.4 collective-permute-start.15
  71.7 4.6 collective-permute-start.6
  114.3 5.3 collective-permute-start.22
  129.4 5.9 collective-permute-start.8
  150.9 4.0 collective-permute-start.16
  160.5 5.1 collective-permute-start.10
  167.6 5.1 collective-permute-start.18
  182.9 2.2 fusion.54
  204.3 5.5 collective-permute-start.36
  215.3 6.2 collective-permute-start.44
  224.8 4.9 collective-permute-start.24
  231.3 2.8 collective-permute-start.46
  235.0 5.8 collective-permute-start.28
  242.8 4.4 collective-permute-done.47
  250.9 2.0 collective-permute-start.26
  252.9 2.3 collective-permute-start.27
  258.8 4.7 collective-permute-start.38
  281.1 8.4 collective-permute-start.40
  290.4 5.6 collective-permute-start.30
  297.9 5.1 collective-permute-start.42
  307.3 4.3 collective-permute-start.32
  313.2 132.0 %psum.45 = f32[128,64]{0,1:T(8,128)S(1)} all-reduce(f32[128,64]{0,1:T(8,128)S(1)} %convolution_bitcast_fusion.25), channel_id=1, replica_groups=mesh['rows'=128,'cols'=4] {'rows','cols'}, use_global_device_ids=true, to_apply=%region_3.4 | all-reduce | flops 8192 | bytes 65536 | tf_op jit(solution)/shard_map/psum | solution.py:218
  448.2 3.3 collective-permute-start.34
  453.6 4.3 collective-permute-done.35
  460.0 469.4 %all-reduce.8.cloned.1.call-done = (f32[3,3,64,64]{3,2,1,0:T(8,128)}, f32[3,3,128,128]{3,2,1,0:T(8,128)}, f32[3,3,256,256]{3,2,1,0:T(8,128)}, f32[256,64]{0,1:T(8,128)}, f32[512,64]{0,1:T(8,128)}) async-done(((f32[3,3,64,64]{3,2,1,0:T(8,128)}, f32[3,3,128,128]{3,2,1,0:T(8,128)}, f32[3,3,256,256]{3,2,1,0:T(8,128)}, f32[256,64]{0,1:T(8,128)}, f32[512,64]{0,1:T(8,128)}), (f32[3,3,64,64]{3,2,1,0:T(8,128)}, ...) | async-done | bytes 3293200 | tf_op jit(solution)/shard_map/psum | solution.py:218
  932.9 3.0 multiply_convert_fusion
  (655 shorter events, 191.4 us)
Async XLA Ops:
  7.2 922.2 %all-reduce.8.cloned.1.call-start = ((), (), s32[]{:S(2)}) async-start(), calls=%async_computation | async-start | bytes 6881280 | tf_op jit(solution)/shard_map/psum | solution.py:218
  8.1 60.6 %collective-permute-start.20 = (bf16[1,10,512]{2,1,0:T(8,128)(2,1)S(1)}, bf16[1,10,512]{2,1,0:T(8,128)(2,1)}, u32[]{:S(2)}, u32[]{:S(2)}) collective-permute-start(bf16[1,10,512]{2,1,0:T(8,128)(2,1)S(1)} %reshape.1665), channel_id=1, source_target_pairs={{0,4},{4,8},{8,12},{12,16},{16,20},{20,24},{24,28},{28,32},{32,36}... | collective-permute-start | bytes 30728 | tf_op jit(solution)/shard_map/ppermute | solution.py:27
  12.7 59.1 %collective-permute-start.21 = (bf16[1,10,512]{2,1,0:T(8,128)(2,1)S(1)}, bf16[1,10,512]{2,1,0:T(8,128)(2,1)}, u32[]{:S(2)}, u32[]{:S(2)}) collective-permute-start(bf16[1,10,512]{2,1,0:T(8,128)(2,1)S(1)} %reshape.1665), channel_id=1, source_target_pairs={{4,0},{8,4},{12,8},{16,12},{20,16},{24,20},{28,24},{32,28},{36,32}... | collective-permute-start | bytes 30728 | tf_op jit(solution)/shard_map/ppermute | solution.py:29
  15.2 27.7 %collective-permute-start.1 = (bf16[1,80,64]{1,2,0:T(8,128)(2,1)S(1)}, bf16[1,80,64]{1,2,0:T(8,128)(2,1)S(1)}, u32[]{:S(2)}, u32[]{:S(2)}) collective-permute-start(bf16[1,80,64]{1,2,0:T(8,128)(2,1)S(1)} %copy.484), channel_id=1, source_target_pairs={{4,0},{8,4},{12,8},{16,12},{20,16},{24,20},{28,24},{32,28},{36,32}... | collective-permute-start | bytes 30728 | tf_op jit(solution)/shard_map/ppermute | solution.py:29
  17.3 26.9 %collective-permute-start = (bf16[1,80,64]{1,2,0:T(8,128)(2,1)}, bf16[1,80,64]{1,2,0:T(8,128)(2,1)S(1)}, u32[]{:S(2)}, u32[]{:S(2)}) collective-permute-start(bf16[1,80,64]{1,2,0:T(8,128)(2,1)} %copy.483), channel_id=1, source_target_pairs={{0,4},{4,8},{8,12},{12,16},{16,20},{20,24},{24,28},{28,32},{32,36}... | collective-permute-start | bytes 30728 | tf_op jit(solution)/shard_map/ppermute | solution.py:27
  23.5 25.6 %collective-permute-start.12 = (bf16[1,20,256]{2,1,0:T(8,128)(2,1)}, bf16[1,20,256]{2,1,0:T(8,128)(2,1)S(1)}, u32[]{:S(2)}, u32[]{:S(2)}) collective-permute-start(bf16[1,20,256]{2,1,0:T(8,128)(2,1)} %slice.1735), channel_id=1, source_target_pairs={{0,4},{4,8},{8,12},{12,16},{16,20},{20,24},{24,28},{28,32},{32,36}... | collective-permute-start | bytes 30728 | tf_op jit(solution)/shard_map/ppermute | solution.py:27
  44.3 15.5 %collective-permute-start.4 = (bf16[1,40,128]{2,1,0:T(8,128)(2,1)}, bf16[1,40,128]{2,1,0:T(8,128)(2,1)S(1)}, u32[]{:S(2)}, u32[]{:S(2)}) collective-permute-start(bf16[1,40,128]{2,1,0:T(8,128)(2,1)} %bitcast.808), channel_id=1, source_target_pairs={{0,4},{4,8},{8,12},{12,16},{16,20},{20,24},{24,28},{28,32},{32,36}... | collective-permute-start | bytes 30728 | tf_op jit(solution)/shard_map/ppermute | solution.py:27
  50.4 29.8 %collective-permute-start.3 = (bf16[10,1,64]{1,2,0:T(8,128)(2,1)}, bf16[10,1,64]{1,2,0:T(8,128)(2,1)}, u32[]{:S(2)}, u32[]{:S(2)}) collective-permute-start(bf16[10,1,64]{1,2,0:T(8,128)(2,1)} %get-tuple-element.564), channel_id=1, source_target_pairs={{1,0},{2,1},{3,2},{5,4},{6,5},{7,6},{9,8},{10,9},{11,10},{13,12},{... | collective-permute-start | bytes 3848 | tf_op jit(solution)/shard_map/ppermute | solution.py:29
  59.8 22.3 %collective-permute-start.2 = (bf16[10,1,64]{1,2,0:T(8,128)(2,1)S(1)}, bf16[10,1,64]{1,2,0:T(8,128)(2,1)}, u32[]{:S(2)}, u32[]{:S(2)}) collective-permute-start(bf16[10,1,64]{1,2,0:T(8,128)(2,1)S(1)} %get-tuple-element.565), channel_id=1, source_target_pairs={{0,1},{1,2},{2,3},{4,5},{5,6},{6,7},{8,9},{9,10},{10,11},{12,13},{... | collective-permute-start | bytes 3848 | tf_op jit(solution)/shard_map/ppermute | solution.py:27
  62.4 67.0 %collective-permute-start.14 = (bf16[4,1,256]{2,1,0:T(2,128)(2,1)}, bf16[4,1,256]{2,1,0:T(2,128)(2,1)}, u32[]{:S(2)}, u32[]{:S(2)}) collective-permute-start(bf16[4,1,256]{2,1,0:T(2,128)(2,1)} %get-tuple-element.624), channel_id=1, source_target_pairs={{0,1},{1,2},{2,3},{4,5},{5,6},{6,7},{8,9},{9,10},{10,11},{12,13},{... | collective-permute-start | bytes 6152 | tf_op jit(solution)/shard_map/ppermute | solution.py:27
  68.6 66.7 %collective-permute-start.15 = (bf16[4,1,256]{2,1,0:T(2,128)(2,1)}, bf16[4,1,256]{2,1,0:T(2,128)(2,1)}, u32[]{:S(2)}, u32[]{:S(2)}) collective-permute-start(bf16[4,1,256]{2,1,0:T(2,128)(2,1)} %get-tuple-element.625), channel_id=1, source_target_pairs={{1,0},{2,1},{3,2},{5,4},{6,5},{7,6},{9,8},{10,9},{11,10},{13,12},{... | collective-permute-start | bytes 6152 | tf_op jit(solution)/shard_map/ppermute | solution.py:29
  71.7 42.6 %collective-permute-start.6 = (bf16[6,1,128]{2,1,0:T(2,128)(2,1)}, bf16[6,1,128]{2,1,0:T(2,128)(2,1)}, u32[]{:S(2)}, u32[]{:S(2)}) collective-permute-start(bf16[6,1,128]{2,1,0:T(2,128)(2,1)} %get-tuple-element.601), channel_id=1, source_target_pairs={{0,1},{1,2},{2,3},{4,5},{5,6},{6,7},{8,9},{9,10},{10,11},{12,13},{... | collective-permute-start | bytes 4616 | tf_op jit(solution)/shard_map/ppermute | solution.py:27
  80.1 39.5 %collective-permute-start.7 = (bf16[6,1,128]{2,1,0:T(2,128)(2,1)}, bf16[6,1,128]{2,1,0:T(2,128)(2,1)}, u32[]{:S(2)}, u32[]{:S(2)}) collective-permute-start(bf16[6,1,128]{2,1,0:T(2,128)(2,1)} %get-tuple-element.602), channel_id=1, source_target_pairs={{1,0},{2,1},{3,2},{5,4},{6,5},{7,6},{9,8},{10,9},{11,10},{13,12},{... | collective-permute-start | bytes 4616 | tf_op jit(solution)/shard_map/ppermute | solution.py:29
  82.1 68.8 %collective-permute-start.23 = (bf16[3,1,512]{2,1,0:T(2,128)(2,1)}, bf16[3,1,512]{2,1,0:T(2,128)(2,1)}, u32[]{:S(2)}, u32[]{:S(2)}) collective-permute-start(bf16[3,1,512]{2,1,0:T(2,128)(2,1)} %get-tuple-element.630), channel_id=1, source_target_pairs={{1,0},{2,1},{3,2},{5,4},{6,5},{7,6},{9,8},{10,9},{11,10},{13,12},{... | collective-permute-start | bytes 9224 | tf_op jit(solution)/shard_map/ppermute | solution.py:29
  114.3 40.6 %collective-permute-start.22 = (bf16[3,1,512]{2,1,0:T(2,128)(2,1)}, bf16[3,1,512]{2,1,0:T(2,128)(2,1)}, u32[]{:S(2)}, u32[]{:S(2)}) collective-permute-start(bf16[3,1,512]{2,1,0:T(2,128)(2,1)} %get-tuple-element.629), channel_id=1, source_target_pairs={{0,1},{1,2},{2,3},{4,5},{5,6},{6,7},{8,9},{9,10},{10,11},{12,13},{... | collective-permute-start | bytes 9224 | tf_op jit(solution)/shard_map/ppermute | solution.py:27
  128.1 29.8 %collective-permute-start.9 = (bf16[1,40,128]{2,1,0:T(8,128)(2,1)}, bf16[1,40,128]{2,1,0:T(8,128)(2,1)}, u32[]{:S(2)}, u32[]{:S(2)}) collective-permute-start(bf16[1,40,128]{2,1,0:T(8,128)(2,1)} %get-tuple-element.638), channel_id=1, source_target_pairs={{4,0},{8,4},{12,8},{16,12},{20,16},{24,20},{28,24},{32,28},{36,32}... | collective-permute-start | bytes 30728 | tf_op jit(solution)/shard_map/ppermute | solution.py:29
  129.4 28.4 %collective-permute-start.8 = (bf16[1,40,128]{2,1,0:T(8,128)(2,1)}, bf16[1,40,128]{2,1,0:T(8,128)(2,1)}, u32[]{:S(2)}, u32[]{:S(2)}) collective-permute-start(bf16[1,40,128]{2,1,0:T(8,128)(2,1)} %get-tuple-element.637), channel_id=1, source_target_pairs={{0,4},{4,8},{8,12},{12,16},{16,20},{20,24},{24,28},{28,32},{32,36}... | collective-permute-start | bytes 30728 | tf_op jit(solution)/shard_map/ppermute | solution.py:27
  149.6 16.1 %collective-permute-start.17 = (bf16[1,20,256]{2,1,0:T(8,128)(2,1)S(1)}, bf16[1,20,256]{2,1,0:T(8,128)(2,1)S(1)}, u32[]{:S(2)}, u32[]{:S(2)}) collective-permute-start(bf16[1,20,256]{2,1,0:T(8,128)(2,1)S(1)} %get-tuple-element.656), channel_id=1, source_target_pairs={{4,0},{8,4},{12,8},{16,12},{20,16},{24,20},{28,24},{32,28},{36,32}... | collective-permute-start | bytes 30728 | tf_op jit(solution)/shard_map/ppermute | solution.py:29
  190.8 59.4 %collective-permute-start.25 = (bf16[1,80,64]{2,1,0:T(8,128)(2,1)}, bf16[1,80,64]{2,1,0:T(8,128)(2,1)}, u32[]{:S(2)}, u32[]{:S(2)}) collective-permute-start(bf16[1,80,64]{2,1,0:T(8,128)(2,1)} %get-tuple-element.555), channel_id=1, source_target_pairs={{4,0},{8,4},{12,8},{16,12},{20,16},{24,20},{28,24},{32,28},{36,32}... | collective-permute-start | bytes 30728 | tf_op jit(solution)/shard_map/ppermute | solution.py:29
  204.3 44.5 %collective-permute-start.36 = (f32[22,64]{1,0:T(8,128)}, f32[22,64]{1,0:T(8,128)}, u32[]{:S(2)}, u32[]{:S(2)}) collective-permute-start(f32[22,64]{1,0:T(8,128)} %slice_bitcast_fusion.61), channel_id=1, source_target_pairs={{0,4},{4,8},{8,12},{12,16},{16,20},{20,24},{24,28},{28,32},{32,36}... | collective-permute-start | bytes 16904 | tf_op jit(solution)/shard_map/ppermute | solution.py:16
  213.3 17.2 %collective-permute-start.45 = (f32[12,64]{1,0:T(8,128)}, f32[12,64]{1,0:T(8,128)}, u32[]{:S(2)}, u32[]{:S(2)}) collective-permute-start(f32[12,64]{1,0:T(8,128)} %get-tuple-element.646), channel_id=1, source_target_pairs={{4,0},{8,4},{12,8},{16,12},{20,16},{24,20},{28,24},{32,28},{36,32}... | collective-permute-start | bytes 9224 | tf_op jit(solution)/shard_map/ppermute | solution.py:16
  215.3 15.3 %collective-permute-start.44 = (f32[12,64]{1,0:T(8,128)}, f32[12,64]{1,0:T(8,128)}, u32[]{:S(2)}, u32[]{:S(2)}) collective-permute-start(f32[12,64]{1,0:T(8,128)} %bitcast.729), channel_id=1, source_target_pairs={{0,4},{4,8},{8,12},{12,16},{16,20},{20,24},{24,28},{28,32},{32,36}... | collective-permute-start | bytes 9224 | tf_op jit(solution)/shard_map/ppermute | solution.py:16
  224.8 25.4 %collective-permute-start.24 = (bf16[1,80,64]{2,1,0:T(8,128)(2,1)}, bf16[1,80,64]{2,1,0:T(8,128)(2,1)S(1)}, u32[]{:S(2)}, u32[]{:S(2)}) collective-permute-start(bf16[1,80,64]{2,1,0:T(8,128)(2,1)} %get-tuple-element.554), channel_id=1, source_target_pairs={{0,4},{4,8},{8,12},{12,16},{16,20},{20,24},{24,28},{28,32},{32,36}... | collective-permute-start | bytes 30728 | tf_op jit(solution)/shard_map/ppermute | solution.py:27
  235.0 21.2 %collective-permute-start.28 = (f32[42,64]{1,0:T(8,128)S(1)}, f32[42,64]{1,0:T(8,128)S(1)}, u32[]{:S(2)}, u32[]{:S(2)}) collective-permute-start(f32[42,64]{1,0:T(8,128)S(1)} %slice_bitcast_fusion.42), channel_id=1, source_target_pairs={{0,4},{4,8},{8,12},{12,16},{16,20},{20,24},{24,28},{28,32},{32,36}... | collective-permute-start | bytes 32264 | tf_op jit(solution)/shard_map/ppermute | solution.py:16
  256.8 32.7 %collective-permute-start.29 = (f32[42,64]{1,0:T(8,128)}, f32[42,64]{1,0:T(8,128)}, u32[]{:S(2)}, u32[]{:S(2)}) collective-permute-start(f32[42,64]{1,0:T(8,128)} %get-tuple-element.660), channel_id=1, source_target_pairs={{4,0},{8,4},{12,8},{16,12},{20,16},{24,20},{28,24},{32,28},{36,32}... | collective-permute-start | bytes 32264 | tf_op jit(solution)/shard_map/ppermute | solution.py:16
  271.6 26.3 %collective-permute-start.41 = (bf16[1,20,256]{2,1,0:T(8,128)(2,1)S(1)}, bf16[1,20,256]{2,1,0:T(8,128)(2,1)S(1)}, u32[]{:S(2)}, u32[]{:S(2)}) collective-permute-start(bf16[1,20,256]{2,1,0:T(8,128)(2,1)S(1)} %get-tuple-element.652), channel_id=1, source_target_pairs={{4,0},{8,4},{12,8},{16,12},{20,16},{24,20},{28,24},{32,28},{36,32}... | collective-permute-start | bytes 30728 | tf_op jit(solution)/shard_map/ppermute | solution.py:29
  281.1 16.8 %collective-permute-start.40 = (bf16[1,20,256]{2,1,0:T(8,128)(2,1)S(1)}, bf16[1,20,256]{2,1,0:T(8,128)(2,1)S(1)}, u32[]{:S(2)}, u32[]{:S(2)}) collective-permute-start(bf16[1,20,256]{2,1,0:T(8,128)(2,1)S(1)} %get-tuple-element.651), channel_id=1, source_target_pairs={{0,4},{4,8},{8,12},{12,16},{16,20},{20,24},{24,28},{28,32},{32,36}... | collective-permute-start | bytes 30728 | tf_op jit(solution)/shard_map/ppermute | solution.py:27
  290.4 14.9 %collective-permute-start.30 = (f32[4,64]{1,0:T(4,128)S(1)}, f32[4,64]{1,0:T(4,128)S(1)}, u32[]{:S(2)}, u32[]{:S(2)}) collective-permute-start(f32[4,64]{1,0:T(4,128)S(1)} %bitcast.809), channel_id=1, source_target_pairs={{0,1},{1,2},{2,3},{4,5},{5,6},{6,7},{8,9},{9,10},{10,11},{12,13},{... | collective-permute-start | bytes 3080 | tf_op jit(solution)/shard_map/ppermute | solution.py:16
  297.9 147.9 %collective-permute-start.42 = (bf16[4,1,256]{2,1,0:T(2,128)(2,1)S(1)}, bf16[4,1,256]{2,1,0:T(2,128)(2,1)S(1)}, u32[]{:S(2)}, u32[]{:S(2)}) collective-permute-start(bf16[4,1,256]{2,1,0:T(2,128)(2,1)S(1)} %get-tuple-element.617), channel_id=1, source_target_pairs={{0,1},{1,2},{2,3},{4,5},{5,6},{6,7},{8,9},{9,10},{10,11},{12,13},{... | collective-permute-start | bytes 6152 | tf_op jit(solution)/shard_map/ppermute | solution.py:27
  303.1 142.8 %collective-permute-start.43 = (bf16[4,1,256]{2,1,0:T(2,128)(2,1)S(1)}, bf16[4,1,256]{2,1,0:T(2,128)(2,1)S(1)}, u32[]{:S(2)}, u32[]{:S(2)}) collective-permute-start(bf16[4,1,256]{2,1,0:T(2,128)(2,1)S(1)} %get-tuple-element.618), channel_id=1, source_target_pairs={{1,0},{2,1},{3,2},{5,4},{6,5},{7,6},{9,8},{10,9},{11,10},{13,12},{... | collective-permute-start | bytes 6152 | tf_op jit(solution)/shard_map/ppermute | solution.py:29
  306.0 142.3 %collective-permute-start.33 = (bf16[1,40,128]{2,1,0:T(8,128)(2,1)S(1)}, bf16[1,40,128]{2,1,0:T(8,128)(2,1)S(1)}, u32[]{:S(2)}, u32[]{:S(2)}) collective-permute-start(bf16[1,40,128]{2,1,0:T(8,128)(2,1)S(1)} %get-tuple-element.636), channel_id=1, source_target_pairs={{4,0},{8,4},{12,8},{16,12},{20,16},{24,20},{28,24},{32,28},{36,32}... | collective-permute-start | bytes 30728 | tf_op jit(solution)/shard_map/ppermute | solution.py:29
  307.3 141.0 %collective-permute-start.32 = (bf16[1,40,128]{2,1,0:T(8,128)(2,1)S(1)}, bf16[1,40,128]{2,1,0:T(8,128)(2,1)S(1)}, u32[]{:S(2)}, u32[]{:S(2)}) collective-permute-start(bf16[1,40,128]{2,1,0:T(8,128)(2,1)S(1)} %get-tuple-element.635), channel_id=1, source_target_pairs={{0,4},{4,8},{8,12},{12,16},{16,20},{20,24},{24,28},{28,32},{32,36}... | collective-permute-start | bytes 30728 | tf_op jit(solution)/shard_map/ppermute | solution.py:27
  (126 other events, 1734.3 us)
Sparse Core Ops, SparseCore 0:
  446.0 483.3 all-reduce.7
where the time goes:
time: 950 us; the launch traced here: 944 us
  waiting for transfers between devices  478 us (50%)
  starting transfers between devices  155 us (16%)
  blocking collectives  132 us (14%)
  local copies, waits for them, and re-layouts  73.4 us (8%)
  matrix products  61.4 us (6%)
  other arithmetic  26.8 us (3%)
  between operations  17.2 us (2%)
    psum x1, waiting for transfers between devices, on_device(): lax.psum((kern_sums[0], kern_sums[1], kern_sums[2], proj_sums[0], proj_su...  469 us
    psum x1, blocking collectives, on_device(): lax.psum((kern_sums[0], kern_sums[1], kern_sums[2], proj_sums[0], proj_su...  132 us
    ppermute x18, starting transfers between devices, padded_2(): lax.ppermute(tail, axis, [(i, (i + 1) % count) for i in range(ends)])  79.1 us
    ppermute x12, starting transfers between devices, passed_along(): return lax.ppermute(block, axis, route)  40.1 us
    ppermute x18, starting transfers between devices, padded_2(): lax.ppermute(head, axis, [((i + 1) % count, i) for i in range(ends)])  35.8 us
    dot_general x54, matrix products, conv_taps(): jnp.dot(window, kernel[tap_row, tap_col], preferred_element_type=jnp.floa...  33.6 us
  transfers between devices with their start and end apart: 49, of which 3 were waited for; matrix products, arithmetic and copies ran while one was open for 15% of the time, Pallas kernels for 0%

commit v1 on v0

--- a/solution.py
+++ b/solution.py
@@ -2,12 +2,18 @@
 import jax.numpy as jnp
 import numpy as np
 from jax import lax
+from jax.sharding import Mesh
 from jax.sharding import PartitionSpec as P
 
 FEAT_ONE = 64
 FEAT_TWO = 128
 FEAT_THREE = 256
 FEAT_FOUR = 512
+
+ROWS = ("z", "x_lo", "y")
+COLS = ("x_hi", "core")
+PLANE = ("x_lo", "y", "x_hi")
+PACK_ROWS = 3328
 
 
 def passed_along(block, axis, distance):
@@ -102,10 +108,10 @@
 
 
 def edge_fix(padded):
-    at_top = lax.axis_index("rows") == 0
-    at_bottom = lax.axis_index("rows") == lax.axis_size("rows") - 1
-    at_left = lax.axis_index("cols") == 0
-    at_right = lax.axis_index("cols") == lax.axis_size("cols") - 1
+    at_top = lax.axis_index(ROWS) == 0
+    at_bottom = lax.axis_index(ROWS) == lax.axis_size(ROWS) - 1
+    at_left = lax.axis_index(COLS) == 0
+    at_right = lax.axis_index(COLS) == lax.axis_size(COLS) - 1
     padded = padded.at[0].set(jnp.where(at_top, padded[1], padded[0]))
     padded = padded.at[-1].set(jnp.where(at_bottom, padded[-2], padded[-1]))
     padded = padded.at[:, 0].set(jnp.where(at_left, padded[:, 1], padded[:, 0]))
@@ -114,18 +120,18 @@
 
 
 def fold_rims(padded):
-    from_above = passed_along(padded[-1], "rows", 1)
-    from_below = passed_along(padded[0], "rows", -1)
-    from_above = jnp.where(lax.axis_index("rows") == 0, padded[0], from_above)
+    from_above = passed_along(padded[-1], ROWS, 1)
+    from_below = passed_along(padded[0], ROWS, -1)
+    from_above = jnp.where(lax.axis_index(ROWS) == 0, padded[0], from_above)
     from_below = jnp.where(
-        lax.axis_index("rows") == lax.axis_size("rows") - 1, padded[-1], from_below
+        lax.axis_index(ROWS) == lax.axis_size(ROWS) - 1, padded[-1], from_below
     )
     inner = padded[1:-1].at[0].add(from_above).at[-1].add(from_below)
-    from_left = passed_along(inner[:, -1], "cols", 1)
-    from_right = passed_along(inner[:, 0], "cols", -1)
-    from_left = jnp.where(lax.axis_index("cols") == 0, inner[:, 0], from_left)
+    from_left = passed_along(inner[:, -1], COLS, 1)
+    from_right = passed_along(inner[:, 0], COLS, -1)
+    from_left = jnp.where(lax.axis_index(COLS) == 0, inner[:, 0], from_left)
     from_right = jnp.where(
-        lax.axis_index("cols") == lax.axis_size("cols") - 1, inner[:, -1], from_right
+        lax.axis_index(COLS) == lax.axis_size(COLS) - 1, inner[:, -1], from_right
     )
     inner = inner[:, 1:-1]
     return inner.at[:, 0].add(from_left).at[:, -1].add(from_right)
@@ -133,6 +139,66 @@
 
 def gelu_back(values, grad_out):
     return jax.vjp(jax.nn.gelu, values)[1](grad_out)[0]
+
+
+def packed_sums(sums):
+    first = sums[0].reshape(576, 64)
+    rest = jnp.concatenate([first, sums[3], sums[4], sums[5]], axis=0)
+    rest = jnp.concatenate(jnp.split(rest, 4, axis=0), axis=1)
+    second = jnp.concatenate(jnp.split(sums[1].reshape(1152, 128), 2, axis=0), axis=1)
+    third = sums[2].reshape(2304, 256)
+    packed = jnp.concatenate([third, second, rest], axis=0)
+    return jnp.pad(packed, ((0, PACK_ROWS - packed.shape[0]), (0, 0)))
+
+
+def unpacked_sums(packed):
+    third = packed[:2304].reshape(3, 3, 256, 256)
+    second = packed[2304:2880]
+    second = jnp.concatenate(jnp.split(second, 2, axis=1), axis=0).reshape(3, 3, 128, 128)
+    rest = packed[2880:3248]
+    rest = jnp.concatenate(jnp.split(rest, 4, axis=1), axis=0)
+    first = rest[:576].reshape(3, 3, 64, 64)
+    return first, second, third, rest[576:704], rest[704:960], rest[960:1472]
+
+
+def swapped(block, axis, flip):
+    return lax.ppermute(block, axis, [(i, i ^ flip) for i in range(lax.axis_size(axis))])
+
+
+def kept_half(values, axis, flip, dim):
+    bit = (lax.axis_index(axis) // flip) % 2
+    half = values.shape[dim] // 2
+    keep = lax.dynamic_slice_in_dim(values, bit * half, half, axis=dim)
+    send = lax.dynamic_slice_in_dim(values, (1 - bit) * half, half, axis=dim)
+    got = swapped(send.astype(jnp.bfloat16), axis, flip)
+    return keep + got.astype(jnp.float32)
+
+
+def both_halves(values, axis, flip, dim):
+    bit = (lax.axis_index(axis) // flip) % 2
+    got = swapped(values, axis, flip)
+    low = jnp.where(bit == 0, values, got)
+    high = jnp.where(bit == 0, got, values)
+    return jnp.concatenate([low, high], axis=dim)
+
+
+def summed_over_devices(packed):
+    width = packed.shape[1]
+    part = kept_half(packed, "core", 1, 0)
+    pieces = part.astype(jnp.bfloat16).reshape(16, -1, width)
+    pieces = lax.all_to_all(pieces, PLANE, 0, 0)
+    part = jnp.sum(pieces.astype(jnp.float32), axis=0)
+    part = kept_half(part, "z", 1, 1)
+    part = kept_half(part, "z", 2, 0)
+    for flip in (4, 8):
+        part = part.astype(jnp.bfloat16)
+        part = part.astype(jnp.float32) + swapped(part, "z", flip).astype(jnp.float32)
+    part = part.astype(jnp.bfloat16)
+    part = both_halves(part, "z", 2, 0)
+    part = both_halves(part, "z", 1, 1)
+    pieces = jnp.broadcast_to(part[None], (16,) + part.shape)
+    part = lax.all_to_all(pieces, PLANE, 0, 0).reshape(-1, width)
+    return both_halves(part, "core", 1, 0)
 
 
 def on_device(
@@ -161,7 +227,7 @@
     pres = []
     acts = []
     for branch in range(3):
-        padded = padded_2(maps[branch], (("rows", 0), ("cols", 1)), 1)
+        padded = padded_2(maps[branch], ((ROWS, 0), (COLS, 1)), 1)
         pre_act = maps[branch].astype(jnp.float32) + conv_taps(padded, kernels[branch])
         padded_in.append(padded)
         pres.append(pre_act)
@@ -171,7 +237,7 @@
     for branch in range(3):
         source = coarse_in[branch]
         shape_now = source.shape
-        edged = edge_fix(padded_2(source, (("rows", 0), ("cols", 1)), 1))
+        edged = edge_fix(padded_2(source, ((ROWS, 0), (COLS, 1)), 1))
         small = jnp.dot(
             edged.reshape(-1, shape_now[2]), projects[branch], preferred_element_type=jnp.float32
         )
@@ -205,21 +271,19 @@
     kern_sums = []
     for branch in range(3):
         grad_pre = gelu_back(pres[branch], upstream[branch]).astype(jnp.bfloat16)
-        grad_padded = padded_2(grad_pre, (("rows", 0), ("cols", 1)), 1)
+        grad_padded = padded_2(grad_pre, ((ROWS, 0), (COLS, 1)), 1)
         flipped = jnp.transpose(kernels[branch][::-1, ::-1], (0, 1, 3, 2))
         back = conv_taps(grad_padded, flipped)
         feat_grads.append((grad_pre.astype(jnp.float32) + back).astype(jnp.bfloat16))
         kern_sums.append(kernel_grad(padded_in[branch], grad_pre))
     total_cells = (
-        maps[0].shape[0] * lax.axis_size("rows") * maps[0].shape[1] * lax.axis_size("cols")
+        maps[0].shape[0] * lax.axis_size(ROWS) * maps[0].shape[1] * lax.axis_size(COLS)
     )
     factors = [(total_cells // 4**branch) ** (-0.5) for branch in range(3)]
     factors = factors + [(total_cells // 4 ** (branch + 1)) ** (-0.5) for branch in range(3)]
-    totals = lax.psum(
-        (kern_sums[0], kern_sums[1], kern_sums[2], proj_sums[0], proj_sums[1], proj_sums[2]),
-        ("rows", "cols"),
-    )
-    finals = [(totals[index] * factors[index]).astype(jnp.bfloat16) for index in range(6)]
+    sums = (kern_sums[0], kern_sums[1], kern_sums[2], proj_sums[0], proj_sums[1], proj_sums[2])
+    packed = packed_sums([sums[index] * factors[index] for index in range(6)])
+    finals = unpacked_sums(summed_over_devices(packed))
     outputs = [grad.reshape(arr.shape) for grad, arr in zip(feat_grads, inputs[:3])]
     return (
         outputs[0],
@@ -236,24 +300,25 @@
 
 
 def solution(mesh):
+    mesh = Mesh(mesh.devices.reshape(16, 2, 4, 2, 2), ("z", "x_lo", "y", "x_hi", "core"))
     in_specs = (
-        P("rows", "cols"),
-        P("rows", "cols"),
-        P("rows", "cols"),
-        P("rows", "cols"),
-        P(),
-        P(),
-        P(),
-        P(),
-        P(),
-        P(),
-        P("rows", "cols"),
+        P(ROWS, COLS),
+        P(ROWS, COLS),
+        P(ROWS, COLS),
+        P(ROWS, COLS),
+        P(),
+        P(),
+        P(),
+        P(),
+        P(),
+        P(),
+        P(ROWS, COLS),
     )
     out_specs = (
-        P("rows", "cols"),
-        P("rows", "cols"),
-        P("rows", "cols"),
-        P("rows", "cols"),
+        P(ROWS, COLS),
+        P(ROWS, COLS),
+        P(ROWS, COLS),
+        P(ROWS, COLS),
         P(),
         P(),
         P(),

time: 950 us -> 483 us (0.51)
  waiting for transfers between devices: 478 us -> 25.2 us
  blocking collectives: 132 us -> 0 us
  starting transfers between devices: 155 us -> 236 us
  local copies, waits for them, and re-layouts: 73.4 us -> 99.2 us
  matrix products: 61.4 us -> 75.3 us
  between operations: 17.2 us -> 3.98 us
    psum x1 -> x0, waiting for transfers between devices: 469 us -> none  [on_device(): lax.psum((kern_sums[0], kern_sums[1], kern_sums[2], proj_sums[0], proj_su...]
    psum x1 -> x0, blocking collectives: 132 us -> none  [on_device(): lax.psum((kern_sums[0], kern_sums[1], kern_sums[2], proj_sums[0], proj_su...]
    ppermute x0 -> x8, starting transfers between devices: none -> 55.3 us  [swapped(): lax.ppermute(block, axis, [(i, i ^ flip) for i in range(lax.axis_size(axi...]
    all_to_all x0 -> x2, starting transfers between devices: none -> 26.4 us  [the longest x1 20.8 us: summed_over_devices(): pieces = lax.all_to_all(pieces, PLANE, 0, 0)]
    reshape x25, local copies, waits for them, and re-layouts: 15.4 us -> 28.6 us  [conv_taps(): padded[tap_row:tap_row + row_count, tap_col:tap_col + col_count]]
    dot_general x54, matrix products: 33.6 us -> 46.3 us  [conv_taps(): jnp.dot(window, kernel[tap_row, tap_col], preferred_element_type=jnp.floa...]
    all_to_all x0 -> x2, waiting for transfers between devices: none -> 11.9 us  [the longest x1 9.2 us: summed_over_devices(): part = lax.all_to_all(pieces, PLANE, 0, 0).reshape(-1, width)]
  transfers between devices with their start and end apart: 49 -> 58, of which waited for: 3 -> 10; matrix products, arithmetic and copies ran while one was open for 15% -> 38% of each run, Pallas kernels for 0% -> 0%
where the time goes in v1:
time: 483 us; the launch traced here: 476 us
  starting transfers between devices  236 us (49%)
  local copies, waits for them, and re-layouts  99.2 us (21%)
  matrix products  75.3 us (16%)
  other arithmetic  35.7 us (7%)
  waiting for transfers between devices  25.2 us (5%)
    ppermute x18, starting transfers between devices, padded_2(): lax.ppermute(tail, axis, [(i, (i + 1) % count) for i in range(ends)])  78.7 us
    ppermute x8, starting transfers between devices, swapped(): lax.ppermute(block, axis, [(i, i ^ flip) for i in range(lax.axis_size(axi...  55.3 us
    dot_general x54, matrix products, conv_taps(): jnp.dot(window, kernel[tap_row, tap_col], preferred_element_type=jnp.floa...  46.3 us
    ppermute x12, starting transfers between devices, passed_along(): return lax.ppermute(block, axis, route)  40 us
    ppermute x18, starting transfers between devices, padded_2(): lax.ppermute(head, axis, [((i + 1) % count, i) for i in range(ends)])  35.8 us
    reshape x25, local copies, waits for them, and re-layouts, conv_taps(): padded[tap_row:tap_row + row_count, tap_col:tap_col + col_count]  28.6 us
    all_to_all x1, starting transfers between devices, summed_over_devices(): pieces = lax.all_to_all(pieces, PLANE, 0, 0)  20.8 us
    concatenate x13, other arithmetic, padded_2(): jnp.concatenate([lax.ppermute(tail, axis, [(i, (i + 1) % count) for i in...  11 us
  transfers between devices with their start and end apart: 58, of which 10 were waited for; matrix products, arithmetic and copies ran while one was open for 38% of the time, Pallas kernels for 0%

profile of v1, /device:TPU:1, one launch (start us, length us, event | category | flops | bytes accessed | tf_op | source)
XLA Modules:
  0.0 475.6 jit_solution(5996295551036107494)
XLA Ops:
  2.2 4.6 collective-permute-start.20
  10.9 4.6 collective-permute-start
  17.0 3.9 collective-permute-start.12
  38.3 4.0 collective-permute-start.4
  45.2 7.7 %collective-permute-start.3 = (bf16[10,1,64]{1,2,0:T(8,128)(2,1)}, bf16[10,1,64]{1,2,0:T(8,128)(2,1)}, u32[]{:S(2)}, u32[]{:S(2)}) collective-permute-start(bf16[10,1,64]{1,2,0:T(8,128)(2,1)} %get-tuple-element.619), channel_id=1, source_target_pairs={{1,0},{2,1},{3,2},{5,4},{6,5},{7,6},{9,8},{10,9},{11,10},{13,12},{... | collective-permute-start | bytes 3848 | tf_op jit(solution)/shard_map/ppermute | solution.py:35
  67.2 4.6 collective-permute-start.6
  112.9 5.1 %collective-permute-start.22 = (bf16[3,1,512]{2,1,0:T(2,128)(2,1)}, bf16[3,1,512]{2,1,0:T(2,128)(2,1)}, u32[]{:S(2)}, u32[]{:S(2)}) collective-permute-start(bf16[3,1,512]{2,1,0:T(2,128)(2,1)} %get-tuple-element.686), channel_id=1, source_target_pairs={{0,1},{1,2},{2,3},{4,5},{5,6},{6,7},{8,9},{9,10},{10,11},{12,13},{... | collective-permute-start | bytes 9224 | tf_op jit(solution)/shard_map/ppermute | solution.py:33
  129.4 5.5 %collective-permute-start.8 = (bf16[1,40,128]{2,1,0:T(8,128)(2,1)}, bf16[1,40,128]{2,1,0:T(8,128)(2,1)}, u32[]{:S(2)}, u32[]{:S(2)}) collective-permute-start(bf16[1,40,128]{2,1,0:T(8,128)(2,1)} %get-tuple-element.694), channel_id=1, source_target_pairs={{0,4},{4,8},{8,12},{12,16},{16,20},{20,24},{24,28},{28,32},{32,36}... | collective-permute-start | bytes 30728 | tf_op jit(solution)/shard_map/ppermute | solution.py:33
  155.2 4.0 collective-permute-start.16
  164.8 5.1 %collective-permute-start.10 = (bf16[6,1,128]{2,1,0:T(2,128)(2,1)S(1)}, bf16[6,1,128]{2,1,0:T(2,128)(2,1)S(1)}, u32[]{:S(2)}, u32[]{:S(2)}) collective-permute-start(bf16[6,1,128]{2,1,0:T(2,128)(2,1)S(1)} %get-tuple-element.651), channel_id=1, source_target_pairs={{0,1},{1,2},{2,3},{4,5},{5,6},{6,7},{8,9},{9,10},{10,11},{12,13},{... | collective-permute-start | bytes 4616 | tf_op jit(solution)/shard_map/ppermute | solution.py:33
  172.5 5.1 %collective-permute-start.18 = (bf16[4,1,256]{2,1,0:T(2,128)(2,1)S(1)}, bf16[4,1,256]{2,1,0:T(2,128)(2,1)}, u32[]{:S(2)}, u32[]{:S(2)}) collective-permute-start(bf16[4,1,256]{2,1,0:T(2,128)(2,1)S(1)} %get-tuple-element.676), channel_id=1, source_target_pairs={{0,1},{1,2},{2,3},{4,5},{5,6},{6,7},{8,9},{9,10},{10,11},{12,13},{... | collective-permute-start | bytes 6152 | tf_op jit(solution)/shard_map/ppermute | solution.py:33
  222.7 5.9 %collective-permute-start.44 = (f32[12,64]{1,0:T(8,128)}, f32[12,64]{1,0:T(8,128)}, u32[]{:S(2)}, u32[]{:S(2)}) collective-permute-start(f32[12,64]{1,0:T(8,128)} %bitcast.740), channel_id=1, source_target_pairs={{0,4},{4,8},{8,12},{12,16},{16,20},{20,24},{24,28},{28,32},{32,36}... | collective-permute-start | bytes 9224 | tf_op jit(solution)/shard_map/ppermute | solution.py:22
  232.7 4.9 %collective-permute-start.24 = (bf16[1,80,64]{2,1,0:T(8,128)(2,1)}, bf16[1,80,64]{2,1,0:T(8,128)(2,1)S(1)}, u32[]{:S(2)}, u32[]{:S(2)}) collective-permute-start(bf16[1,80,64]{2,1,0:T(8,128)(2,1)} %get-tuple-element.609), channel_id=1, source_target_pairs={{0,4},{4,8},{8,12},{12,16},{16,20},{20,24},{24,28},{28,32},{32,36}... | collective-permute-start | bytes 30728 | tf_op jit(solution)/shard_map/ppermute | solution.py:33
  238.1 5.5 %collective-permute-start.28 = (f32[42,64]{1,0:T(8,128)}, f32[42,64]{1,0:T(8,128)S(1)}, u32[]{:S(2)}, u32[]{:S(2)}) collective-permute-start(f32[42,64]{1,0:T(8,128)} %slice_bitcast_fusion.42), channel_id=1, source_target_pairs={{0,4},{4,8},{8,12},{12,16},{16,20},{20,24},{24,28},{28,32},{32,36}... | collective-permute-start | bytes 32264 | tf_op jit(solution)/shard_map/ppermute | solution.py:22
  243.6 5.5 %collective-permute-start.36 = (f32[22,64]{1,0:T(8,128)S(1)}, f32[22,64]{1,0:T(8,128)S(1)}, u32[]{:S(2)}, u32[]{:S(2)}) collective-permute-start(f32[22,64]{1,0:T(8,128)S(1)} %slice_bitcast_fusion.61), channel_id=1, source_target_pairs={{0,4},{4,8},{8,12},{12,16},{16,20},{20,24},{24,28},{28,32},{32,36}... | collective-permute-start | bytes 16904 | tf_op jit(solution)/shard_map/ppermute | solution.py:22
  256.3 4.4 collective-permute-done.47
  273.9 4.7 collective-permute-start.38
  291.5 5.5 %collective-permute-start.40 = (bf16[1,20,256]{2,1,0:T(8,128)(2,1)S(1)}, bf16[1,20,256]{2,1,0:T(8,128)(2,1)S(1)}, u32[]{:S(2)}, u32[]{:S(2)}) collective-permute-start(bf16[1,20,256]{2,1,0:T(8,128)(2,1)S(1)} %get-tuple-element.710), channel_id=1, source_target_pairs={{0,4},{4,8},{8,12},{12,16},{16,20},{20,24},{24,28},{28,32},{32,36}... | collective-permute-start | bytes 30728 | tf_op jit(solution)/shard_map/ppermute | solution.py:33
  303.2 5.4 %collective-permute-start.30 = (f32[4,64]{1,0:T(4,128)S(1)}, f32[4,64]{1,0:T(4,128)S(1)}, u32[]{:S(2)}, u32[]{:S(2)}) collective-permute-start(f32[4,64]{1,0:T(4,128)S(1)} %bitcast.826), channel_id=1, source_target_pairs={{0,1},{1,2},{2,3},{4,5},{5,6},{6,7},{8,9},{9,10},{10,11},{12,13},{... | collective-permute-start | bytes 3080 | tf_op jit(solution)/shard_map/ppermute | solution.py:22
  311.2 5.1 %collective-permute-start.42 = (bf16[4,1,256]{2,1,0:T(2,128)(2,1)}, bf16[4,1,256]{2,1,0:T(2,128)(2,1)}, u32[]{:S(2)}, u32[]{:S(2)}) collective-permute-start(bf16[4,1,256]{2,1,0:T(2,128)(2,1)} %get-tuple-element.674), channel_id=1, source_target_pairs={{0,1},{1,2},{2,3},{4,5},{5,6},{6,7},{8,9},{9,10},{10,11},{12,13},{... | collective-permute-start | bytes 6152 | tf_op jit(solution)/shard_map/ppermute | solution.py:33
  322.3 4.9 %collective-permute-start.32 = (bf16[1,40,128]{2,1,0:T(8,128)(2,1)}, bf16[1,40,128]{2,1,0:T(8,128)(2,1)}, u32[]{:S(2)}, u32[]{:S(2)}) collective-permute-start(bf16[1,40,128]{2,1,0:T(8,128)(2,1)} %get-tuple-element.692), channel_id=1, source_target_pairs={{0,4},{4,8},{8,12},{12,16},{16,20},{20,24},{24,28},{28,32},{32,36}... | collective-permute-start | bytes 30728 | tf_op jit(solution)/shard_map/ppermute | solution.py:33
  354.3 20.8 %all-to-all-start = ((bf16[16,104,256]{2,1,0:T(8,128)(2,1)}), bf16[16,104,256]{2,1,0:T(8,128)(2,1)S(1)}, u32[]{:S(2)}, u32[]{:S(2)}) async-start(bf16[16,104,256]{2,1,0:T(8,128)(2,1)} %bitcast.745), calls=%async_computation | async-start | bytes 1703936 | tf_op jit(solution)/shard_map/all_to_all | solution.py:189
  378.6 5.2 %collective-permute-start.34 = (bf16[6,1,128]{2,1,0:T(2,128)(2,1)S(1)}, bf16[6,1,128]{2,1,0:T(2,128)(2,1)S(1)}, u32[]{:S(2)}, u32[]{:S(2)}) collective-permute-start(bf16[6,1,128]{2,1,0:T(2,128)(2,1)S(1)} %get-tuple-element.649), channel_id=1, source_target_pairs={{0,1},{1,2},{2,3},{4,5},{5,6},{6,7},{8,9},{9,10},{10,11},{12,13},{... | collective-permute-start | bytes 4616 | tf_op jit(solution)/shard_map/ppermute | solution.py:33
  388.6 3.6 collective-permute-start.49
  393.4 14.6 %collective-permute-start.50 = (bf16[52,128]{1,0:T(8,128)(2,1)S(1)}, bf16[52,128]{1,0:T(8,128)(2,1)S(1)}, u32[]{:S(2)}, u32[]{:S(2)}) collective-permute-start(bf16[52,128]{1,0:T(8,128)(2,1)S(1)} %dynamic-slice_convert_fusion.2), channel_id=1, source_target_pairs={{0,64},{32,96},{64,0},{96,32},{128,192},{160,224},{192,128},{224,1... | collective-permute-start | bytes 39944 | tf_op jit(solution)/shard_map/ppermute | solution.py:165
  409.1 8.8 %collective-permute-start.51 = (bf16[52,128]{1,0:T(8,128)(2,1)S(1)}, bf16[52,128]{1,0:T(8,128)(2,1)S(1)}, u32[]{:S(2)}, u32[]{:S(2)}) collective-permute-start(bf16[52,128]{1,0:T(8,128)(2,1)S(1)} %add_convert_fusion.6), channel_id=1, source_target_pairs={{0,128},{32,160},{64,192},{96,224},{128,0},{160,32},{192,64},{224,... | collective-permute-start | bytes 39944 | tf_op jit(solution)/shard_map/ppermute | solution.py:165
  419.0 9.1 %collective-permute-start.52 = (bf16[52,128]{1,0:T(8,128)(2,1)S(1)}, bf16[52,128]{1,0:T(8,128)(2,1)S(1)}, u32[]{:S(2)}, u32[]{:S(2)}) collective-permute-start(bf16[52,128]{1,0:T(8,128)(2,1)S(1)} %add_convert_fusion.5), channel_id=1, source_target_pairs={{0,256},{32,288},{64,320},{96,352},{128,384},{160,416},{192,448},{... | collective-permute-start | bytes 39944 | tf_op jit(solution)/shard_map/ppermute | solution.py:165
  428.2 4.0 collective-permute-done.52
  432.2 4.3 collective-permute-start.53
  443.2 5.6 %all-to-all-start.1 = ((bf16[16,104,256]{2,1,0:T(8,128)(2,1)}), bf16[16,104,256]{2,1,0:T(8,128)(2,1)S(1)}, u32[]{:S(2)}, u32[]{:S(2)}) async-start(bf16[16,104,256]{2,1,0:T(8,128)(2,1)} %broadcast_in_dim.2), calls=%async_computation.1 | async-start | bytes 1703936 | tf_op jit(solution)/shard_map/all_to_all | solution.py:200
  449.5 9.2 %all-to-all-done.1 = bf16[16,104,256]{2,1,0:T(8,128)(2,1)S(1)} async-done(((bf16[16,104,256]{2,1,0:T(8,128)(2,1)}), bf16[16,104,256]{2,1,0:T(8,128)(2,1)S(1)}, u32[]{:S(2)}, u32[]{:S(2)}) %all-to-all-start.1) | async-done | bytes 852000 | tf_op jit(solution)/shard_map/all_to_all | solution.py:200
  458.7 9.8 %collective-permute-start.55 = (bf16[1664,256]{1,0:T(8,128)(2,1)S(1)}, bf16[1664,256]{1,0:T(8,128)(2,1)S(1)}, u32[]{:S(2)}, u32[]{:S(2)}) collective-permute-start(bf16[1664,256]{1,0:T(8,128)(2,1)S(1)} %bitcast.744), channel_id=1, source_target_pairs={{0,1},{1,0},{2,3},{3,2},{4,5},{5,4},{6,7},{7,6},{8,9},{9,8},{10,11... | collective-permute-start | bytes 2555912 | tf_op jit(solution)/shard_map/ppermute | solution.py:165
  (676 shorter events, 270.4 us)
Async XLA Ops:
  2.2 61.1 %collective-permute-start.20 = (bf16[1,10,512]{2,1,0:T(8,128)(2,1)}, bf16[1,10,512]{2,1,0:T(8,128)(2,1)}, u32[]{:S(2)}, u32[]{:S(2)}) collective-permute-start(bf16[1,10,512]{2,1,0:T(8,128)(2,1)} %reshape.1687), channel_id=1, source_target_pairs={{0,4},{4,8},{8,12},{12,16},{16,20},{20,24},{24,28},{28,32},{32,36}... | collective-permute-start | bytes 30728 | tf_op jit(solution)/shard_map/ppermute | solution.py:33
  6.8 60.4 %collective-permute-start.21 = (bf16[1,10,512]{2,1,0:T(8,128)(2,1)}, bf16[1,10,512]{2,1,0:T(8,128)(2,1)}, u32[]{:S(2)}, u32[]{:S(2)}) collective-permute-start(bf16[1,10,512]{2,1,0:T(8,128)(2,1)} %reshape.1687), channel_id=1, source_target_pairs={{4,0},{8,4},{12,8},{16,12},{20,16},{24,20},{28,24},{32,28},{36,32}... | collective-permute-start | bytes 30728 | tf_op jit(solution)/shard_map/ppermute | solution.py:35
  9.4 27.6 %collective-permute-start.1 = (bf16[1,80,64]{1,2,0:T(8,128)(2,1)S(1)}, bf16[1,80,64]{1,2,0:T(8,128)(2,1)S(1)}, u32[]{:S(2)}, u32[]{:S(2)}) collective-permute-start(bf16[1,80,64]{1,2,0:T(8,128)(2,1)S(1)} %copy.501), channel_id=1, source_target_pairs={{4,0},{8,4},{12,8},{16,12},{20,16},{24,20},{28,24},{32,28},{36,32}... | collective-permute-start | bytes 30728 | tf_op jit(solution)/shard_map/ppermute | solution.py:35
  10.9 27.4 %collective-permute-start = (bf16[1,80,64]{1,2,0:T(8,128)(2,1)S(1)}, bf16[1,80,64]{1,2,0:T(8,128)(2,1)S(1)}, u32[]{:S(2)}, u32[]{:S(2)}) collective-permute-start(bf16[1,80,64]{1,2,0:T(8,128)(2,1)S(1)} %copy.500), channel_id=1, source_target_pairs={{0,4},{4,8},{8,12},{12,16},{16,20},{20,24},{24,28},{28,32},{32,36}... | collective-permute-start | bytes 30728 | tf_op jit(solution)/shard_map/ppermute | solution.py:33
  17.0 26.1 %collective-permute-start.12 = (bf16[1,20,256]{2,1,0:T(8,128)(2,1)}, bf16[1,20,256]{2,1,0:T(8,128)(2,1)}, u32[]{:S(2)}, u32[]{:S(2)}) collective-permute-start(bf16[1,20,256]{2,1,0:T(8,128)(2,1)} %slice.1764), channel_id=1, source_target_pairs={{0,4},{4,8},{8,12},{12,16},{16,20},{20,24},{24,28},{28,32},{32,36}... | collective-permute-start | bytes 30728 | tf_op jit(solution)/shard_map/ppermute | solution.py:33
  45.2 30.6 %collective-permute-start.3 = (bf16[10,1,64]{1,2,0:T(8,128)(2,1)}, bf16[10,1,64]{1,2,0:T(8,128)(2,1)}, u32[]{:S(2)}, u32[]{:S(2)}) collective-permute-start(bf16[10,1,64]{1,2,0:T(8,128)(2,1)} %get-tuple-element.619), channel_id=1, source_target_pairs={{1,0},{2,1},{3,2},{5,4},{6,5},{7,6},{9,8},{10,9},{11,10},{13,12},{... | collective-permute-start | bytes 3848 | tf_op jit(solution)/shard_map/ppermute | solution.py:35
  54.5 23.1 %collective-permute-start.2 = (bf16[10,1,64]{1,2,0:T(8,128)(2,1)}, bf16[10,1,64]{1,2,0:T(8,128)(2,1)}, u32[]{:S(2)}, u32[]{:S(2)}) collective-permute-start(bf16[10,1,64]{1,2,0:T(8,128)(2,1)} %get-tuple-element.620), channel_id=1, source_target_pairs={{0,1},{1,2},{2,3},{4,5},{5,6},{6,7},{8,9},{9,10},{10,11},{12,13},{... | collective-permute-start | bytes 3848 | tf_op jit(solution)/shard_map/ppermute | solution.py:33
  57.1 72.3 %collective-permute-start.14 = (bf16[4,1,256]{2,1,0:T(2,128)(2,1)}, bf16[4,1,256]{2,1,0:T(2,128)(2,1)}, u32[]{:S(2)}, u32[]{:S(2)}) collective-permute-start(bf16[4,1,256]{2,1,0:T(2,128)(2,1)} %get-tuple-element.681), channel_id=1, source_target_pairs={{0,1},{1,2},{2,3},{4,5},{5,6},{6,7},{8,9},{9,10},{10,11},{12,13},{... | collective-permute-start | bytes 6152 | tf_op jit(solution)/shard_map/ppermute | solution.py:33
  63.4 71.6 %collective-permute-start.15 = (bf16[4,1,256]{2,1,0:T(2,128)(2,1)}, bf16[4,1,256]{2,1,0:T(2,128)(2,1)}, u32[]{:S(2)}, u32[]{:S(2)}) collective-permute-start(bf16[4,1,256]{2,1,0:T(2,128)(2,1)} %get-tuple-element.682), channel_id=1, source_target_pairs={{1,0},{2,1},{3,2},{5,4},{6,5},{7,6},{9,8},{10,9},{11,10},{13,12},{... | collective-permute-start | bytes 6152 | tf_op jit(solution)/shard_map/ppermute | solution.py:35
  67.2 45.7 %collective-permute-start.6 = (bf16[6,1,128]{2,1,0:T(2,128)(2,1)}, bf16[6,1,128]{2,1,0:T(2,128)(2,1)}, u32[]{:S(2)}, u32[]{:S(2)}) collective-permute-start(bf16[6,1,128]{2,1,0:T(2,128)(2,1)} %get-tuple-element.656), channel_id=1, source_target_pairs={{0,1},{1,2},{2,3},{4,5},{5,6},{6,7},{8,9},{9,10},{10,11},{12,13},{... | collective-permute-start | bytes 4616 | tf_op jit(solution)/shard_map/ppermute | solution.py:33
  75.7 42.4 %collective-permute-start.7 = (bf16[6,1,128]{2,1,0:T(2,128)(2,1)}, bf16[6,1,128]{2,1,0:T(2,128)(2,1)}, u32[]{:S(2)}, u32[]{:S(2)}) collective-permute-start(bf16[6,1,128]{2,1,0:T(2,128)(2,1)} %get-tuple-element.657), channel_id=1, source_target_pairs={{1,0},{2,1},{3,2},{5,4},{6,5},{7,6},{9,8},{10,9},{11,10},{13,12},{... | collective-permute-start | bytes 4616 | tf_op jit(solution)/shard_map/ppermute | solution.py:35
  77.6 77.5 %collective-permute-start.23 = (bf16[3,1,512]{2,1,0:T(2,128)(2,1)}, bf16[3,1,512]{2,1,0:T(2,128)(2,1)}, u32[]{:S(2)}, u32[]{:S(2)}) collective-permute-start(bf16[3,1,512]{2,1,0:T(2,128)(2,1)} %get-tuple-element.687), channel_id=1, source_target_pairs={{1,0},{2,1},{3,2},{5,4},{6,5},{7,6},{9,8},{10,9},{11,10},{13,12},{... | collective-permute-start | bytes 9224 | tf_op jit(solution)/shard_map/ppermute | solution.py:35
  112.9 46.2 %collective-permute-start.22 = (bf16[3,1,512]{2,1,0:T(2,128)(2,1)}, bf16[3,1,512]{2,1,0:T(2,128)(2,1)}, u32[]{:S(2)}, u32[]{:S(2)}) collective-permute-start(bf16[3,1,512]{2,1,0:T(2,128)(2,1)} %get-tuple-element.686), channel_id=1, source_target_pairs={{0,1},{1,2},{2,3},{4,5},{5,6},{6,7},{8,9},{9,10},{10,11},{12,13},{... | collective-permute-start | bytes 9224 | tf_op jit(solution)/shard_map/ppermute | solution.py:33
  128.1 34.0 %collective-permute-start.9 = (bf16[1,40,128]{2,1,0:T(8,128)(2,1)}, bf16[1,40,128]{2,1,0:T(8,128)(2,1)}, u32[]{:S(2)}, u32[]{:S(2)}) collective-permute-start(bf16[1,40,128]{2,1,0:T(8,128)(2,1)} %get-tuple-element.695), channel_id=1, source_target_pairs={{4,0},{8,4},{12,8},{16,12},{20,16},{24,20},{28,24},{32,28},{36,32}... | collective-permute-start | bytes 30728 | tf_op jit(solution)/shard_map/ppermute | solution.py:35
  129.4 32.7 %collective-permute-start.8 = (bf16[1,40,128]{2,1,0:T(8,128)(2,1)}, bf16[1,40,128]{2,1,0:T(8,128)(2,1)}, u32[]{:S(2)}, u32[]{:S(2)}) collective-permute-start(bf16[1,40,128]{2,1,0:T(8,128)(2,1)} %get-tuple-element.694), channel_id=1, source_target_pairs={{0,4},{4,8},{8,12},{12,16},{16,20},{20,24},{24,28},{28,32},{32,36}... | collective-permute-start | bytes 30728 | tf_op jit(solution)/shard_map/ppermute | solution.py:33
  207.1 57.5 %collective-permute-start.25 = (bf16[1,80,64]{2,1,0:T(8,128)(2,1)}, bf16[1,80,64]{2,1,0:T(8,128)(2,1)}, u32[]{:S(2)}, u32[]{:S(2)}) collective-permute-start(bf16[1,80,64]{2,1,0:T(8,128)(2,1)} %get-tuple-element.610), channel_id=1, source_target_pairs={{4,0},{8,4},{12,8},{16,12},{20,16},{24,20},{28,24},{32,28},{36,32}... | collective-permute-start | bytes 30728 | tf_op jit(solution)/shard_map/ppermute | solution.py:35
  220.8 22.8 %collective-permute-start.45 = (f32[12,64]{1,0:T(8,128)}, f32[12,64]{1,0:T(8,128)}, u32[]{:S(2)}, u32[]{:S(2)}) collective-permute-start(f32[12,64]{1,0:T(8,128)} %get-tuple-element.705), channel_id=1, source_target_pairs={{4,0},{8,4},{12,8},{16,12},{20,16},{24,20},{28,24},{32,28},{36,32}... | collective-permute-start | bytes 9224 | tf_op jit(solution)/shard_map/ppermute | solution.py:22
  222.7 26.4 %collective-permute-start.44 = (f32[12,64]{1,0:T(8,128)}, f32[12,64]{1,0:T(8,128)}, u32[]{:S(2)}, u32[]{:S(2)}) collective-permute-start(f32[12,64]{1,0:T(8,128)} %bitcast.740), channel_id=1, source_target_pairs={{0,4},{4,8},{8,12},{12,16},{16,20},{20,24},{24,28},{28,32},{32,36}... | collective-permute-start | bytes 9224 | tf_op jit(solution)/shard_map/ppermute | solution.py:22
  232.7 31.8 %collective-permute-start.24 = (bf16[1,80,64]{2,1,0:T(8,128)(2,1)}, bf16[1,80,64]{2,1,0:T(8,128)(2,1)S(1)}, u32[]{:S(2)}, u32[]{:S(2)}) collective-permute-start(bf16[1,80,64]{2,1,0:T(8,128)(2,1)} %get-tuple-element.609), channel_id=1, source_target_pairs={{0,4},{4,8},{8,12},{12,16},{16,20},{20,24},{24,28},{28,32},{32,36}... | collective-permute-start | bytes 30728 | tf_op jit(solution)/shard_map/ppermute | solution.py:33
  238.1 33.2 %collective-permute-start.28 = (f32[42,64]{1,0:T(8,128)}, f32[42,64]{1,0:T(8,128)S(1)}, u32[]{:S(2)}, u32[]{:S(2)}) collective-permute-start(f32[42,64]{1,0:T(8,128)} %slice_bitcast_fusion.42), channel_id=1, source_target_pairs={{0,4},{4,8},{8,12},{12,16},{16,20},{20,24},{24,28},{28,32},{32,36}... | collective-permute-start | bytes 32264 | tf_op jit(solution)/shard_map/ppermute | solution.py:22
  243.6 19.6 %collective-permute-start.36 = (f32[22,64]{1,0:T(8,128)S(1)}, f32[22,64]{1,0:T(8,128)S(1)}, u32[]{:S(2)}, u32[]{:S(2)}) collective-permute-start(f32[22,64]{1,0:T(8,128)S(1)} %slice_bitcast_fusion.61), channel_id=1, source_target_pairs={{0,4},{4,8},{8,12},{12,16},{16,20},{20,24},{24,28},{28,32},{32,36}... | collective-permute-start | bytes 16904 | tf_op jit(solution)/shard_map/ppermute | solution.py:22
  271.9 30.5 %collective-permute-start.29 = (f32[42,64]{1,0:T(8,128)}, f32[42,64]{1,0:T(8,128)}, u32[]{:S(2)}, u32[]{:S(2)}) collective-permute-start(f32[42,64]{1,0:T(8,128)} %get-tuple-element.719), channel_id=1, source_target_pairs={{4,0},{8,4},{12,8},{16,12},{20,16},{24,20},{28,24},{32,28},{36,32}... | collective-permute-start | bytes 32264 | tf_op jit(solution)/shard_map/ppermute | solution.py:22
  290.2 20.4 %collective-permute-start.41 = (bf16[1,20,256]{2,1,0:T(8,128)(2,1)S(1)}, bf16[1,20,256]{2,1,0:T(8,128)(2,1)S(1)}, u32[]{:S(2)}, u32[]{:S(2)}) collective-permute-start(bf16[1,20,256]{2,1,0:T(8,128)(2,1)S(1)} %get-tuple-element.711), channel_id=1, source_target_pairs={{4,0},{8,4},{12,8},{16,12},{20,16},{24,20},{28,24},{32,28},{36,32}... | collective-permute-start | bytes 30728 | tf_op jit(solution)/shard_map/ppermute | solution.py:35
  291.5 19.1 %collective-permute-start.40 = (bf16[1,20,256]{2,1,0:T(8,128)(2,1)S(1)}, bf16[1,20,256]{2,1,0:T(8,128)(2,1)S(1)}, u32[]{:S(2)}, u32[]{:S(2)}) collective-permute-start(bf16[1,20,256]{2,1,0:T(8,128)(2,1)S(1)} %get-tuple-element.710), channel_id=1, source_target_pairs={{0,4},{4,8},{8,12},{12,16},{16,20},{20,24},{24,28},{28,32},{32,36}... | collective-permute-start | bytes 30728 | tf_op jit(solution)/shard_map/ppermute | solution.py:33
  311.2 22.0 %collective-permute-start.42 = (bf16[4,1,256]{2,1,0:T(2,128)(2,1)}, bf16[4,1,256]{2,1,0:T(2,128)(2,1)}, u32[]{:S(2)}, u32[]{:S(2)}) collective-permute-start(bf16[4,1,256]{2,1,0:T(2,128)(2,1)} %get-tuple-element.674), channel_id=1, source_target_pairs={{0,1},{1,2},{2,3},{4,5},{5,6},{6,7},{8,9},{9,10},{10,11},{12,13},{... | collective-permute-start | bytes 6152 | tf_op jit(solution)/shard_map/ppermute | solution.py:33
  316.4 16.9 %collective-permute-start.43 = (bf16[4,1,256]{2,1,0:T(2,128)(2,1)S(1)}, bf16[4,1,256]{2,1,0:T(2,128)(2,1)}, u32[]{:S(2)}, u32[]{:S(2)}) collective-permute-start(bf16[4,1,256]{2,1,0:T(2,128)(2,1)S(1)} %get-tuple-element.675), channel_id=1, source_target_pairs={{1,0},{2,1},{3,2},{5,4},{6,5},{7,6},{9,8},{10,9},{11,10},{13,12},{... | collective-permute-start | bytes 6152 | tf_op jit(solution)/shard_map/ppermute | solution.py:35
  321.0 56.9 %collective-permute-start.33 = (bf16[1,40,128]{2,1,0:T(8,128)(2,1)}, bf16[1,40,128]{2,1,0:T(8,128)(2,1)}, u32[]{:S(2)}, u32[]{:S(2)}) collective-permute-start(bf16[1,40,128]{2,1,0:T(8,128)(2,1)} %get-tuple-element.693), channel_id=1, source_target_pairs={{4,0},{8,4},{12,8},{16,12},{20,16},{24,20},{28,24},{32,28},{36,32}... | collective-permute-start | bytes 30728 | tf_op jit(solution)/shard_map/ppermute | solution.py:35
  322.3 55.6 %collective-permute-start.32 = (bf16[1,40,128]{2,1,0:T(8,128)(2,1)}, bf16[1,40,128]{2,1,0:T(8,128)(2,1)}, u32[]{:S(2)}, u32[]{:S(2)}) collective-permute-start(bf16[1,40,128]{2,1,0:T(8,128)(2,1)} %get-tuple-element.692), channel_id=1, source_target_pairs={{0,4},{4,8},{8,12},{12,16},{16,20},{20,24},{24,28},{28,32},{32,36}... | collective-permute-start | bytes 30728 | tf_op jit(solution)/shard_map/ppermute | solution.py:33
  331.3 20.7 %collective-permute-start.48 = (bf16[1664,256]{1,0:T(8,128)(2,1)}, bf16[1664,256]{1,0:T(8,128)(2,1)}, u32[]{:S(2)}, u32[]{:S(2)}) collective-permute-start(bf16[1664,256]{1,0:T(8,128)(2,1)} %dynamic-slice_convert_fusion), channel_id=1, source_target_pairs={{0,1},{1,0},{2,3},{3,2},{4,5},{5,4},{6,7},{7,6},{8,9},{9,8},{10,11... | collective-permute-start | bytes 2555912 | tf_op jit(solution)/shard_map/ppermute | solution.py:165
  354.3 34.2 %all-to-all-start = ((bf16[16,104,256]{2,1,0:T(8,128)(2,1)}), bf16[16,104,256]{2,1,0:T(8,128)(2,1)S(1)}, u32[]{:S(2)}, u32[]{:S(2)}) async-start(bf16[16,104,256]{2,1,0:T(8,128)(2,1)} %bitcast.745), calls=%async_computation | async-start | bytes 1703936 | tf_op jit(solution)/shard_map/all_to_all | solution.py:189
  378.6 39.3 %collective-permute-start.34 = (bf16[6,1,128]{2,1,0:T(2,128)(2,1)S(1)}, bf16[6,1,128]{2,1,0:T(2,128)(2,1)S(1)}, u32[]{:S(2)}, u32[]{:S(2)}) collective-permute-start(bf16[6,1,128]{2,1,0:T(2,128)(2,1)S(1)} %get-tuple-element.649), channel_id=1, source_target_pairs={{0,1},{1,2},{2,3},{4,5},{5,6},{6,7},{8,9},{9,10},{10,11},{12,13},{... | collective-permute-start | bytes 4616 | tf_op jit(solution)/shard_map/ppermute | solution.py:33
  383.8 34.1 %collective-permute-start.35 = (bf16[6,1,128]{2,1,0:T(2,128)(2,1)S(1)}, bf16[6,1,128]{2,1,0:T(2,128)(2,1)S(1)}, u32[]{:S(2)}, u32[]{:S(2)}) collective-permute-start(bf16[6,1,128]{2,1,0:T(2,128)(2,1)S(1)} %get-tuple-element.650), channel_id=1, source_target_pairs={{1,0},{2,1},{3,2},{5,4},{6,5},{7,6},{9,8},{10,9},{11,10},{13,12},{... | collective-permute-start | bytes 4616 | tf_op jit(solution)/shard_map/ppermute | solution.py:35
  (123 other events, 2283.5 us)

commit v2 on v1

v2 whole, which is shorter than its diff:
```python
import functools

import jax
import jax.numpy as jnp
from jax import lax
from jax.experimental import pallas as pl
from jax.experimental.pallas import tpu as pltpu
from jax.sharding import Mesh
from jax.sharding import PartitionSpec as P

FEAT_ONE = 64
FEAT_TWO = 128
FEAT_THREE = 256
FEAT_FOUR = 512

ROWS = ("z", "x_lo", "y")
COLS = ("x_hi", "core")
PLANE = ("x_lo", "y", "x_hi")
PACK_ROWS = 3328
HALF = PACK_ROWS // 2
WIDE = 5120
RIM = 1024
BF = jnp.bfloat16
F32 = jnp.float32
NT = (((1,), (1,)), ((), ()))
TN = (((0,), (0,)), ((), ()))


def moved(block, axis, distance):
    count = lax.axis_size(axis)
    route = [(i, i + distance) for i in range(count) if 0 <= i + distance < count]
    return lax.ppermute(block, axis, route)


def halos(x1, x2, x3, x4, cot):
    own = jnp.concatenate([x1, cot, x2, x3, x4, jnp.zeros_like(x4)], axis=0)
    last = jnp.concatenate([x2[-1:], x3[-1:], x4], axis=0)
    first = jnp.concatenate([x2[:1], x3[:1], x4], axis=0)
    above = moved(own, ROWS, 1)
    below = moved(own, ROWS, -1)
    above2 = moved(last, ROWS, 2)
    below2 = moved(first, ROWS, -2)
    parts = (own, above, below, above2, below2)
    left = moved(jnp.concatenate([p[:, -RIM:] for p in parts], axis=0), COLS, 1)
    right = moved(jnp.concatenate([p[:, :RIM] for p in parts], axis=0), COLS, -1)
    return own, above, below, above2, below2, left, right


def gelu_both(v):
    c = 0.7978845608028654
    sq = v * v
    t = jnp.tanh(c * v * (1.0 + 0.044715 * sq))
    half = 0.5 * (1.0 + t)
    slope = half + 0.5 * v * (1.0 - t * t) * (c * (1.0 + 3.0 * 0.044715 * sq))
    return v * half, slope


def tile(wide, at):
    return wide[:, 128 * at : 128 * (at + 1)]


def row_weights(shape, coarse_dim, row_block):
    k = lax.broadcasted_iota(jnp.int32, shape, coarse_dim)
    r = lax.broadcasted_iota(jnp.int32, shape, 1 - coarse_dim)
    two, three = k < 16, k < 24
    scale = jnp.where(two, 2, jnp.where(three, 4, 8))
    count = jnp.where(two, 4, jnp.where(three, 2, 1))
    shift = jnp.where(two, 6, jnp.where(three, 16 + 3, 24 + 2))
    total = (jnp.where(two, 512, jnp.where(three, 256, 128)) - 1).astype(F32)
    coarse = (row_block * count + k - shift).astype(F32)
    fine = (row_block * 8 + r - 8).astype(F32)
    inverse = jnp.where(two, 0.5, jnp.where(three, 0.25, 0.125)).astype(F32)
    place = jnp.clip((fine + 0.5) * inverse - 0.5, 0.0, total)
    return jnp.maximum(0.0, 1.0 - jnp.abs(place - coarse))


def forward_kernel(
    place_ref, own, above, below, above2, below2, left, right,
    t1, k2, k3, p2, p3, p4,
    keep_ref, send_ref, g1_ref, g2_ref, g3_ref, gf4_ref,
    wx1, wc, wx2, wx3, wx4, xw1, xw2, xw3, d1, d2, d3, gm1, gm2, gm3, sums,
):
    row_block = place_ref[0]
    at_left = place_ref[1] == 0
    at_right = place_ref[2] == 1
    core = place_ref[3]
    lane = lax.broadcasted_iota(jnp.int32, (1, 128), 1)
    low = lane < 64

    def lanes(a, b):
        return jnp.where(low, a, b).astype(F32)

    wx2[...] = jnp.zeros_like(wx2)
    wx4[...] = jnp.zeros_like(wx4)
    sources = (
        (own, above, below, above2, below2, 0, WIDE, RIM),
        (left, left, left, left, left, None, RIM, 0),
        (right, right, right, right, right, None, RIM, RIM + WIDE),
    )
    for mid, up, down, up2, down2, flat, width, to in sources:
        cols = slice(to, to + width)
        if flat is None:
            whole = mid[...].astype(F32)
            v_mid, v_up, v_down = whole[0:24], whole[24:48], whole[48:72]
            v_up2, v_down2 = whole[72:75], whole[75:78]
        else:
            v_mid, v_up, v_down = (ref[...].astype(F32) for ref in (mid, up, down))
            v_up2, v_down2 = up2[...].astype(F32), down2[...].astype(F32)
        for n, v in enumerate((v_up, v_mid, v_down)):
            wx1[8 * n : 8 * n + 8, cols] = v[0:8]
            wc[8 * n : 8 * n + 8, cols] = v[8:16]
            wx2[2 + 4 * n : 6 + 4 * n, cols] = v[16:20]
            wx3[1 + 2 * n : 3 + 2 * n, cols] = v[20:22]
            wx4[1 + n : 2 + n, cols] = v[22:23]
        wx2[1:2, cols] = v_up2[0:1]
        wx2[14:15, cols] = v_down2[0:1]
        wx3[0:1, cols] = v_up2[1:2]
        wx3[7:8, cols] = v_down2[1:2]
        wx4[0:1, cols] = v_up2[2:3]
        wx4[4:5, cols] = v_down2[2:3]

    for f in range(-3, 43):
        at = 8 + 24 * (f + 3)
        xw1[at : at + 24, 0:128] = tile(wx1, 8 + f)
        xw1[at : at + 24, 128:256] = jnp.where(low, tile(wx1, 9 + f), tile(wx1, 7 + f))
    xw1[0:8, :] = jnp.zeros((8, 256), F32)
    xw1[1112:1120, :] = jnp.zeros((8, 256), F32)
    pre1 = xw1[8:1112, 0:128]
    for i in range(3):
        pre1 = pre1 + jnp.dot(xw1[7 + i : 1111 + i, :].astype(BF), t1[i], preferred_element_type=F32)
    y1, slope = gelu_both(pre1)
    y1 = y1.astype(BF).astype(F32)
    d1[...] = slope

    for j in range(3):
        for c in range(-4, 44):
            at = 8 + 16 * (c + 4)
            xw2[at : at + 16, 128 * j : 128 * j + 128] = tile(wx2, 7 + c + j)
    xw2[0:8, :] = jnp.zeros((8, 384), F32)
    xw2[776:784, :] = jnp.zeros((8, 384), F32)
    pre2 = xw2[8:776, 128:256]
    for i in range(3):
        pre2 = pre2 + jnp.dot(xw2[7 + i : 775 + i, :].astype(BF), k2[i], preferred_element_type=F32)
    y2, slope = gelu_both(pre2)
    y2 = y2.astype(BF)
    d2[...] = slope

    for j in range(3):
        for c in range(-2, 22):
            at = 8 + 8 * (c + 2)
            first = RIM + 256 * (c + j - 1)
            xw3[at : at + 8, 256 * j : 256 * j + 256] = wx3[:, first : first + 256]
    xw3[0:8, :] = jnp.zeros((8, 768), F32)
    xw3[200:208, :] = jnp.zeros((8, 768), F32)
    pre3 = xw3[8:200, 256:512]
    for i in range(3):
        pre3 = pre3 + jnp.dot(xw3[7 + i : 199 + i, :].astype(BF), k3[i], preferred_element_type=F32)
    y3, slope = gelu_both(pre3)
    y3 = y3.astype(BF)
    d3[...] = slope

    x4 = jnp.concatenate([wx4[:, 512 * c : 512 * c + 512] for c in range(14)], axis=0).astype(BF)

    weights = row_weights((24, 32), 1, row_block).astype(BF)
    rows_up = []
    for y, p, rim, rows, wlo in ((y2, p2, 4, 16, 0), (y3, p3, 2, 8, 16), (x4, p4, 2, 8, 24)):
        twice = jnp.concatenate([p[...], p[...]], axis=1)
        coarse = jnp.dot(y, twice, preferred_element_type=F32).astype(BF).astype(F32)
        cols = [coarse[rows * n : rows * (n + 1)] for n in range(coarse.shape[0] // rows)]
        end = len(cols) - rim
        cols[rim - 1] = jnp.where(at_left, cols[rim], cols[rim - 1])
        cols[end] = jnp.where(at_right, cols[end - 1], cols[end])
        flat = jnp.concatenate(cols, axis=1).astype(BF)
        rows_up.append(jnp.dot(weights[:, wlo : wlo + rows], flat, preferred_element_type=F32))
    up2, up3, up4 = rows_up

    gates = []
    for f in range(-3, 43):
        k = f + 4
        merged = y1[24 * (f + 3) : 24 * (f + 4)]
        merged = merged + 0.75 * tile(up2, k) + 0.25 * jnp.where(low, tile(up2, k - 1), tile(up2, k + 1))
        k, h = f // 2 + 2, f % 2
        if h == 0:
            merged = merged + lanes(0.375, 0.125) * tile(up3, k - 1) + lanes(0.625, 0.875) * tile(up3, k)
        else:
            merged = merged + lanes(0.875, 0.625) * tile(up3, k) + lanes(0.125, 0.375) * tile(up3, k + 1)
        k, h = f // 4 + 2, f % 4
        p_low, p_high = (2 * h + 0.5) / 8 - 0.5, (2 * h + 1.5) / 8 - 0.5
        other = k - 1 if h < 2 else k + 1
        merged = merged + lanes(1 - abs(p_low), 1 - abs(p_high)) * tile(up4, k)
        merged = merged + lanes(abs(p_low), abs(p_high)) * tile(up4, other)
        slope = gelu_both(merged)[1]
        gate = (slope * tile(wc, 8 + f)).astype(BF).astype(F32)
        gates.append(gate)
        if -1 <= f <= 40:
            g = (d1[24 * (f + 3) : 24 * (f + 4)] * gate).astype(BF).astype(F32)
            g1_ref[24 * (f + 1) : 24 * (f + 2), :] = g
            if 0 <= f < 40:
                row = lax.broadcasted_iota(jnp.int32, (24, 1), 0)
                gm1[8 + 24 * f : 32 + 24 * f, :] = jnp.where((row >= 8) & (row < 16), g, 0.0)
    gm1[0:8, :] = jnp.zeros((8, 128), F32)
    gm1[968:976, :] = jnp.zeros((8, 128), F32)

    flat = jnp.concatenate(gates, axis=1).astype(BF)
    weights_back = row_weights((32, 24), 0, row_block).astype(BF)
    down = jnp.dot(weights_back, flat, preferred_element_type=F32)
    down2, down3, down4 = down[0:16], down[16:24], down[24:32]

    def folded(v):
        return v + pltpu.roll(v, 64, 1)

    cg2 = []
    for c in range(-1, 41):
        v = 0.75 * tile(down2, c + 3) + 0.25 * jnp.where(low, tile(down2, c + 4), tile(down2, c + 2))
        cg2.append(folded(v))
    cg3 = []
    for c in range(-1, 21):
        at = 2 * c + 2
        v = lanes(0.125, 0.375) * tile(down3, at) + lanes(0.625, 0.875) * tile(down3, at + 1)
        v = v + lanes(0.875, 0.625) * tile(down3, at + 2) + lanes(0.375, 0.125) * tile(down3, at + 3)
        cg3.append(folded(v))
    cg4 = []
    for c in range(10):
        v = jnp.zeros((8, 128), F32)
        for n in range(8):
            a, b = (2 * n + 0.5) / 8, (2 * n + 1.5) / 8
            a, b = (a, b) if n < 4 else (2 - a, 2 - b)
            v = v + lanes(a, b) * tile(down4, 4 * c + 1 + n)
        if c == 0:
            rim = lanes(0.4375, 0.3125) * tile(down4, 3) + lanes(0.1875, 0.0625) * tile(down4, 4)
            v = v + jnp.where(at_left, rim, 0.0)
        if c == 9:
            rim = lanes(0.0625, 0.1875) * tile(down4, 41) + lanes(0.3125, 0.4375) * tile(down4, 42)
            v = v + jnp.where(at_right, rim, 0.0)
        cg4.append(folded(v))
    for cg in (cg2, cg3):
        cg[1] = cg[1] + jnp.where(at_left, cg[0], 0.0)
        cg[-2] = cg[-2] + jnp.where(at_right, cg[-1], 0.0)
        cg[0] = jnp.where(at_left, 0.0, cg[0])
        cg[-1] = jnp.where(at_right, 0.0, cg[-1])

    flat2 = jnp.concatenate(cg2, axis=0).astype(BF).astype(F32)
    flat3 = jnp.concatenate(cg3, axis=0).astype(BF).astype(F32)
    flat4 = jnp.concatenate(cg4, axis=0).astype(BF).astype(F32)
    back2 = lax.dot_general(flat2[:, 0:64].astype(BF), p2[...], NT, preferred_element_type=F32)
    back3 = lax.dot_general(flat3[:, 0:64].astype(BF), p3[...], NT, preferred_element_type=F32)
    back4 = lax.dot_general(flat4[:, 0:64].astype(BF), p4[...], NT, preferred_element_type=F32)
    for c in range(10):
        gf4_ref[0:1, 512 * c : 512 * c + 512] = back4[8 * c + 2 : 8 * c + 3].astype(BF)
    g2 = (d2[48:720, :] * back2).astype(BF).astype(F32)
    g3 = (d3[8:184, :] * back3).astype(BF).astype(F32)
    g2_ref[...] = g2
    g3_ref[...] = g3

    row2 = lax.broadcasted_iota(jnp.int32, (640, 1), 0) % 16
    own2 = (row2 >= 6) & (row2 < 10)
    row3 = lax.broadcasted_iota(jnp.int32, (160, 1), 0) % 8
    own3 = (row3 >= 3) & (row3 < 5)
    row4 = lax.broadcasted_iota(jnp.int32, (80, 1), 0) % 8
    gm2[0:8, :] = jnp.zeros((8, 128), F32)
    gm2[8:648, :] = jnp.where(own2, g2[16:656], 0.0)
    gm2[648:656, :] = jnp.zeros((8, 128), F32)
    gm3[0:8, :] = jnp.zeros((8, 256), F32)
    gm3[8:168, :] = jnp.where(own3, g3[8:168], 0.0)
    gm3[168:176, :] = jnp.zeros((8, 256), F32)

    cells = 327680
    x = xw3[24:184, :].astype(BF)
    shifted = jnp.concatenate([gm3[9 - i : 169 - i, :] for i in range(3)], axis=1).astype(BF)
    z = lax.dot_general(x, shifted, TN, preferred_element_type=F32) * (cells // 16) ** -0.5
    for i in range(3):
        sums[768 * i : 768 * (i + 1), :] = z[:, 256 * i : 256 * (i + 1)]
    x = xw2[72:712, :].astype(BF)
    shifted = jnp.concatenate([gm2[9 - i : 649 - i, :] for i in range(3)], axis=1).astype(BF)
    z = lax.dot_general(x, shifted, TN, preferred_element_type=F32) * (cells // 4) ** -0.5
    base = 2304
    sums[base : base + 384, 0:128] = z[:, 0:128]
    sums[base + 384 : base + 576, 0:128] = z[0:192, 128:256]
    sums[base : base + 192, 128:256] = z[192:384, 128:256]
    sums[base + 192 : base + 576, 128:256] = z[:, 256:384]
    x = xw1[80:1040, :].astype(BF)
    shifted = jnp.concatenate([gm1[9 - i : 969 - i, :] for i in range(3)], axis=1).astype(BF)
    z = lax.dot_general(x, shifted, TN, preferred_element_type=F32) * cells**-0.5
    window = (192, 0, 64, 128)
    blocks = []
    for i in range(3):
        zi = z[:, 128 * i : 128 * (i + 1)]
        for j in range(3):
            a, b = window[j], window[j + 1]
            blocks.append(zi[a : a + 64] + pltpu.roll(zi[b : b + 64], 64, 1))
    y2_own, y3_own, x4_own = y2[64:704], y3[16:176], x4[16:96]
    for y, flat, mask, branch in (
        (y2_own, flat2[16:656], own2, 1),
        (y3_own, flat3[8:168], own3, 2),
        (x4_own, flat4, row4 == 2, 3),
    ):
        masked = jnp.where(mask, flat, 0.0).astype(BF)
        z = lax.dot_general(y, masked, TN, preferred_element_type=F32) * (cells // 4**branch) ** -0.5
        blocks += [z[64 * n : 64 * (n + 1)] for n in range(z.shape[0] // 64)]
    blocks.append(jnp.zeros((64, 128), F32))
    base = 2880
    for n in range(6):
        for side in range(2):
            a, b = blocks[4 * n + 2 * side], blocks[4 * n + 2 * side + 1]
            if 4 * n + 2 * side + 1 < 9:
                b = pltpu.roll(b, 64, 1)
            at = base + 64 * n
            sums[at : at + 64, 128 * side : 128 * side + 128] = jnp.where(low, a, b)
    sums[3264:3328, :] = jnp.zeros((64, 256), F32)
    keep_ref[...] = sums[pl.ds(pl.multiple_of(core * HALF, 64), HALF), :]
    send_ref[...] = sums[pl.ds(pl.multiple_of((1 - core) * HALF, 64), HALF), :].astype(BF)


def backward_kernel(g1, g2, g3, t1b, k2, k3, gf1_ref, gf2_ref, gf3_ref, xw1, xw2, xw3, out2, out3):
    low = lax.broadcasted_iota(jnp.int32, (1, 128), 1) < 64
    for ref, n in ((xw1, 960), (xw2, 640), (xw3, 160)):
        ref[0:8, :] = jnp.zeros((8, ref.shape[1]), F32)
        ref[8 + n : 16 + n, :] = jnp.zeros((8, ref.shape[1]), F32)

    xw1[8:968, 0:128] = g1[24:984, :]
    xw1[8:968, 128:256] = jnp.where(low, g1[48:1008, :], g1[0:960, :])
    total = xw1[8:968, 0:128]
    for i in range(3):
        total = total + lax.dot_general(
            xw1[9 - i : 969 - i, :].astype(BF), t1b[i], NT, preferred_element_type=F32
        )
    for f in range(40):
        gf1_ref[:, 128 * f : 128 * (f + 1)] = total[24 * f + 8 : 24 * f + 16].astype(BF)

    for j in range(3):
        xw2[8:648, 128 * j : 128 * j + 128] = g2[32 - 16 * j : 672 - 16 * j, :]
    total = xw2[8:648, 128:256]
    for i in range(3):
        kernel = jnp.concatenate([k2[i, 128 * j : 128 * j + 128, :] for j in range(3)], axis=1)
        total = total + lax.dot_general(
            xw2[9 - i : 649 - i, :].astype(BF), kernel, NT, preferred_element_type=F32
        )
    out2[...] = total
    for c in range(40):
        gf2_ref[:, 128 * c : 128 * (c + 1)] = out2[16 * c + 6 : 16 * c + 10, :].astype(BF)

    for j in range(3):
        xw3[8:168, 256 * j : 256 * j + 256] = g3[16 - 8 * j : 176 - 8 * j, :]
    total = xw3[8:168, 256:512]
    for i in range(3):
        kernel = jnp.concatenate([k3[i, 256 * j : 256 * j + 256, :] for j in range(3)], axis=1)
        total = total + lax.dot_general(
            xw3[9 - i : 169 - i, :].astype(BF), kernel, NT, preferred_element_type=F32
        )
    out3[...] = total
    for c in range(20):
        gf3_ref[:, 256 * c : 256 * (c + 1)] = out3[8 * c + 3 : 8 * c + 5, :].astype(BF)


def swapped(block, axis, flip):
    return lax.ppermute(block, axis, [(i, i ^ flip) for i in range(lax.axis_size(axis))])


def kept_half(values, axis, flip, dim):
    bit = (lax.axis_index(axis) // flip) % 2
    half = values.shape[dim] // 2
    keep = lax.dynamic_slice_in_dim(values, bit * half, half, axis=dim)
    send = lax.dynamic_slice_in_dim(values, (1 - bit) * half, half, axis=dim)
    got = swapped(send.astype(BF), axis, flip)
    return keep + got.astype(F32)


def both_halves(values, axis, flip, dim):
    bit = (lax.axis_index(axis) // flip) % 2
    got = swapped(values, axis, flip)
    first = jnp.where(bit == 0, values, got)
    second = jnp.where(bit == 0, got, values)
    return jnp.concatenate([first, second], axis=dim)


def summed_over_devices(keep, send):
    width = keep.shape[1]
    part = keep + swapped(send, "core", 1).astype(F32)
    pieces = part.astype(BF).reshape(16, -1, width)
    pieces = lax.all_to_all(pieces, PLANE, 0, 0)
    part = jnp.sum(pieces.astype(F32), axis=0)
    part = kept_half(part, "z", 1, 1)
    part = kept_half(part, "z", 2, 0)
    for flip in (4, 8):
        part = part.astype(BF)
        part = part.astype(F32) + swapped(part, "z", flip).astype(F32)
    part = part.astype(BF)
    part = both_halves(part, "z", 2, 0)
    part = both_halves(part, "z", 1, 1)
    pieces = jnp.broadcast_to(part[None], (16,) + part.shape)
    part = lax.all_to_all(pieces, PLANE, 0, 0).reshape(-1, width)
    return part, swapped(part, "core", 1)


def unpack_kernel(place_ref, mine, got, k1_ref, k2_ref, k3_ref, p2_ref, p3_ref, p4_ref, whole):
    core = place_ref[3]
    whole[pl.ds(pl.multiple_of(core * HALF, 64), HALF), :] = mine[...]
    whole[pl.ds(pl.multiple_of((1 - core) * HALF, 64), HALF), :] = got[...]
    k3_ref[...] = whole[0:2304, :]
    k2_ref[0:576, :] = whole[2304:2880, 0:128]
    k2_ref[576:1152, :] = whole[2304:2880, 128:256]
    block = 0
    for ref, count in ((k1_ref, 9), (p2_ref, 2), (p3_ref, 4), (p4_ref, 8)):
        for n in range(count):
            at, side = 2880 + 64 * (block // 4), 64 * (block % 4)
            ref[64 * n : 64 * (n + 1), :] = whole[at : at + 64, side : side + 64]
            block += 1


def call(kernel, out_shapes, scratch, count, scalars=0):
    vmem = pl.BlockSpec(memory_space=pltpu.VMEM)
    smem = pl.BlockSpec(memory_space=pltpu.SMEM)
    return pl.pallas_call(
        kernel,
        out_shape=[jax.ShapeDtypeStruct(shape, dtype) for shape, dtype in out_shapes],
        in_specs=[smem] * scalars + [vmem] * count,
        out_specs=[vmem] * len(out_shapes),
        scratch_shapes=[pltpu.VMEM(shape, dtype) for shape, dtype in scratch],
        compiler_params=pltpu.CompilerParams(vmem_limit_bytes=48 * 1024 * 1024),
    )


def pair_weights(kernel_one):
    none = jnp.zeros((3, FEAT_ONE, FEAT_ONE), BF)
    tap = lambda j: kernel_one[:, j] if 0 <= j < 3 else none
    windows = (1, 2, 3, 0)
    ahead = jnp.concatenate(
        [jnp.concatenate([tap(w - e) for w in windows], axis=1) for e in range(2)], axis=2
    )
    back = jnp.concatenate(
        [jnp.concatenate([tap(e - w + 2) for e in range(2)], axis=1) for w in windows], axis=2
    )
    return ahead, back


def local_part(x1, x2, x3, x4, kernel_one, kernel_two, kernel_three, p2, p3, p4, cot):
    place = jnp.stack(
        [
            lax.axis_index(ROWS),
            lax.axis_index(COLS),
            (lax.axis_index(COLS) == lax.axis_size(COLS) - 1).astype(jnp.int32),
            lax.axis_index("core"),
        ]
    ).astype(jnp.int32)
    ahead, back = pair_weights(kernel_one)
    k2 = kernel_two.reshape(3, 384, 128)
    k3 = kernel_three.reshape(3, 768, 256)
    packs = halos(x1, x2, x3, x4, cot)
    total = RIM + WIDE + RIM
    keep, send, g1, g2, g3, gf4 = call(
        forward_kernel,
        [
            ((HALF, 256), F32), ((HALF, 256), BF),
            ((1008, 128), F32), ((672, 128), F32), ((176, 256), F32), ((1, WIDE), BF),
        ],
        [
            ((24, total), F32), ((24, total), F32), ((16, total), F32), ((8, total), F32), ((8, total), F32),
            ((1120, 256), F32), ((784, 384), F32), ((208, 768), F32),
            ((1104, 128), F32), ((768, 128), F32), ((192, 256), F32),
            ((976, 128), F32), ((656, 128), F32), ((176, 256), F32),
            ((PACK_ROWS, 256), F32),
        ],
        13,
        1,
    )(place, *packs, ahead, k2, k3, p2, p3, p4)
    gf1, gf2, gf3 = call(
        backward_kernel,
        [((8, WIDE), BF), ((4, WIDE), BF), ((2, WIDE), BF)],
        [
            ((976, 256), F32), ((656, 384), F32), ((176, 768), F32),
            ((640, 128), F32), ((160, 256), F32),
        ],
        6,
    )(g1, g2, g3, back, k2, k3)
    return place, keep, send, gf1, gf2, gf3, gf4


def unpacked(place, mine, got):
    outs = call(
        unpack_kernel,
        [((576, 64), BF), ((1152, 128), BF), ((2304, 256), BF), ((128, 64), BF), ((256, 64), BF), ((512, 64), BF)],
        [((PACK_ROWS, 256), BF)],
        2,
        1,
    )(place, mine, got)
    return (
        outs[0].reshape(3, 3, 64, 64), outs[1].reshape(3, 3, 128, 128), outs[2].reshape(3, 3, 256, 256),
        outs[3], outs[4], outs[5],
    )


def on_device(*args):
    place, keep, send, gf1, gf2, gf3, gf4 = local_part(*args)
    mine, got = summed_over_devices(keep, send)
    return (gf1, gf2, gf3, gf4) + unpacked(place, mine, got)


def solution(mesh):
    mesh = Mesh(mesh.devices.reshape(16, 2, 4, 2, 2), ("z", "x_lo", "y", "x_hi", "core"))
    split = P(ROWS, COLS)
    in_specs = (split,) * 4 + (P(),) * 6 + (split,)
    out_specs = (split,) * 4 + (P(),) * 6
    return jax.shard_map(on_device, mesh=mesh, in_specs=in_specs, out_specs=out_specs, check_vma=False)
```

time: 483 us -> 158 us (0.33); the launches traced: 476 us -> 156 us
  starting transfers between devices: 236 us -> 85.1 us
  local copies, waits for them, and re-layouts: 99.2 us -> 11.9 us
  matrix products: 75.3 us -> 0 us
  other arithmetic: 35.7 us -> 5.11 us
  blocking collectives: 0 us -> 14.9 us
  Pallas kernels: 0 us -> 10.6 us
    ppermute x48 -> x6, starting transfers between devices: 154 us -> 24.2 us  [moved(): return lax.ppermute(block, axis, route)]
    dot_general x102 -> x0, matrix products: 75.3 us -> none  [the longest x54 46.3 us: conv_taps(): jnp.dot(window, kernel[tap_row, tap_col], preferred_element_type=jnp.floa...]
    reshape x42 -> x0, local copies, waits for them, and re-layouts: 35.2 us -> none  [the longest x25 28.6 us: conv_taps(): padded[tap_row:tap_row + row_count, tap_col:tap_col + col_count]]
    slice x70 -> x6, local copies, waits for them, and re-layouts: 25.1 us -> 0.98 us  [the longest x1 0.94 us: halos(): first = jnp.concatenate([x2[:1], x3[:1], x4], axis=0)]
    all_to_all x0 -> x1, blocking collectives: none -> 14.9 us  [summed_over_devices(): part = lax.all_to_all(pieces, PLANE, 0, 0).reshape(-1, width)]
    concatenate x22 -> x5, other arithmetic: 14 us -> 1.15 us  [the longest x1 0.86 us: halos(): first = jnp.concatenate([x2[:1], x3[:1], x4], axis=0)]
    all_to_all x1, starting transfers between devices: 20.8 us -> 9.39 us  [summed_over_devices(): pieces = lax.all_to_all(pieces, PLANE, 0, 0)]
    pallas_call x0 -> x3, Pallas kernels: none -> 10.6 us  [the longest x1 6.68 us: local_part(): call(forward_kernel, [((HALF, 256), F32), ((HALF, 256), BF), ((1008, 128)...]
  transfers between devices with their start and end apart: 58 -> 15, of which waited for: 10 -> 10; matrix products, arithmetic and copies ran while one was open for 38% -> 2% of each run, Pallas kernels for 0% -> 1%
where the time goes in v2:
time: 158 us; the launch traced here: 156 us
  starting transfers between devices  85.1 us (54%)
  waiting for transfers between devices  27.6 us (17%)
  blocking collectives  14.9 us (9%)
  local copies, waits for them, and re-layouts  11.9 us (8%)
  Pallas kernels  10.6 us (7%)
  other arithmetic  5.11 us (3%)
    ppermute x8, starting transfers between devices, swapped(): lax.ppermute(block, axis, [(i, i ^ flip) for i in range(lax.axis_size(axi...  51.5 us
    ppermute x6, starting transfers between devices, moved(): return lax.ppermute(block, axis, route)  24.2 us
    all_to_all x1, blocking collectives, summed_over_devices(): part = lax.all_to_all(pieces, PLANE, 0, 0).reshape(-1, width)  14.9 us
    ppermute x8, waiting for transfers between devices, swapped(): lax.ppermute(block, axis, [(i, i ^ flip) for i in range(lax.axis_size(axi...  13.2 us
    all_to_all x1, waiting for transfers between devices, summed_over_devices(): pieces = lax.all_to_all(pieces, PLANE, 0, 0)  13.1 us
    all_to_all x1, starting transfers between devices, summed_over_devices(): pieces = lax.all_to_all(pieces, PLANE, 0, 0)  9.39 us
    unnamed x40, local copies, waits for them, and re-layouts  7.02 us
    pallas_call x1, Pallas kernels, local_part(): call(forward_kernel, [((HALF, 256), F32), ((HALF, 256), BF), ((1008, 128)...  6.68 us
  transfers between devices with their start and end apart: 15, of which 10 were waited for; matrix products, arithmetic and copies ran while one was open for 2% of the time, Pallas kernels for 1%

profile of v2, /device:TPU:1, one launch (start us, length us, event | category | flops | bytes accessed | tf_op | source)
XLA Modules:
  0.0 156.5 jit_solution(16388892091070582185)
XLA Ops:
  0.7 2.8 %concatenate.45.own = bf16[24,5120]{1,0:T(8,128)(2,1)S(1)} concatenate(bf16[8,5120]{1,0:T(8,128)(2,1)} %param.11, bf16[8,5120]{1,0:T(8,128)(2,1)} %param.21, bf16[4,5120]{1,0:T(4,128)(2,1)} %param.12, bf16[2,5120]{1,0:T(2,128)(2,1)} %param.13, bf16[1,5120]{1,0:T(2,128)(2,1)} %param.14, bf16[1,5120]{1,0:T(2,128)(2,1)S(1)} %broadcast_in_dim.12), dimensions={0} | concatenate | bytes 491520 | tf_op jit(solution)/shard_map/concatenate | solution.py:36
  3.5 1.3 collective-permute-start.1
  4.8 4.7 %collective-permute-start = (bf16[24,5120]{1,0:T(8,128)(2,1)S(1)}, bf16[24,5120]{1,0:T(8,128)(2,1)S(1)}, u32[]{:S(2)}, u32[]{:S(2)}) collective-permute-start(bf16[24,5120]{1,0:T(8,128)(2,1)S(1)} %concatenate.45.own), channel_id=1, source_target_pairs={{0,4},{4,8},{8,12},{12,16},{16,20},{20,24},{24,28},{28,32},{32,36}... | collective-permute-start | bytes 737288 | tf_op jit(solution)/shard_map/ppermute | solution.py:32
  9.5 0.9 fusion.10
  11.3 1.3 collective-permute-start.3
  12.6 5.6 %collective-permute-start.2 = (bf16[3,5120]{1,0:T(4,128)(2,1)S(1)}, bf16[3,5120]{1,0:T(4,128)(2,1)S(1)}, u32[]{:S(2)}, u32[]{:S(2)}) collective-permute-start(bf16[3,5120]{1,0:T(4,128)(2,1)S(1)} %get-tuple-element.70), channel_id=1, source_target_pairs={{0,8},{4,12},{8,16},{12,20},{16,24},{20,28},{24,32},{28,36},{32,40... | collective-permute-start | bytes 92168 | tf_op jit(solution)/shard_map/ppermute | solution.py:32
  20.2 9.4 %collective-permute-start.5 = (bf16[78,1024]{1,0:T(8,128)(2,1)S(1)}, bf16[78,1024]{1,0:T(8,128)(2,1)S(1)}, u32[]{:S(2)}, u32[]{:S(2)}) collective-permute-start(bf16[78,1024]{1,0:T(8,128)(2,1)S(1)} %concatenate.49), channel_id=1, source_target_pairs={{1,0},{2,1},{3,2},{5,4},{6,5},{7,6},{9,8},{10,9},{11,10},{13,12},{... | collective-permute-start | bytes 479240 | tf_op jit(solution)/shard_map/ppermute | solution.py:32
  29.7 1.9 %collective-permute-start.4 = (bf16[78,1024]{1,0:T(8,128)(2,1)S(1)}, bf16[78,1024]{1,0:T(8,128)(2,1)S(1)}, u32[]{:S(2)}, u32[]{:S(2)}) collective-permute-start(bf16[78,1024]{1,0:T(8,128)(2,1)S(1)} %concatenate.48), channel_id=1, source_target_pairs={{0,1},{1,2},{2,3},{4,5},{5,6},{6,7},{8,9},{9,10},{10,11},{12,13},{... | collective-permute-start | bytes 479240 | tf_op jit(solution)/shard_map/ppermute | solution.py:32
  32.9 0.9 collective-permute-done.4.left
  37.2 6.7 %shard_map.186 = (f32[1664,256]{1,0:T(8,128)}, bf16[1664,256]{1,0:T(8,128)(2,1)S(1)}, f32[1008,128]{1,0:T(8,128)S(1)}, f32[672,128]{1,0:T(8,128)S(1)}, f32[176,256]{1,0:T(8,128)S(1)}, /*index=5*/bf16[1,5120]{1,0:T(2,128)(2,1)}) custom-call(s32[4]{0:T(128)S(1)} %pad_add_fusion.place_ref, bf16[24,5120]{1,0:T(8,128)(2,1)S(1)} %concatenate.45.own, ...), custom_call_target="tpu_custom_call" | custom-call | tf_op jit(solution)/shard_map/pallas_call | solution.py:450
  43.9 1.9 %collective-permute-start.6 = (bf16[1664,256]{1,0:T(8,128)(2,1)S(1)}, bf16[1664,256]{1,0:T(8,128)(2,1)S(1)}, u32[]{:S(2)}, u32[]{:S(2)}) collective-permute-start(bf16[1664,256]{1,0:T(8,128)(2,1)S(1)} %get-tuple-element.33), channel_id=1, source_target_pairs={{0,1},{1,0},{2,3},{3,2},{4,5},{5,4},{6,7},{7,6},{8,9},{9,8},{10,11... | collective-permute-start | bytes 2555912 | tf_op jit(solution)/shard_map/ppermute | solution.py:356
  45.8 2.3 %collective-permute-done.6 = bf16[1664,256]{1,0:T(8,128)(2,1)S(1)} collective-permute-done((bf16[1664,256]{1,0:T(8,128)(2,1)S(1)}, bf16[1664,256]{1,0:T(8,128)(2,1)S(1)}, u32[]{:S(2)}, u32[]{:S(2)}) %collective-permute-start.6) | collective-permute-done | bytes 852000 | tf_op jit(solution)/shard_map/ppermute | solution.py:356
  48.1 2.5 %add_convert_fusion = bf16[1664,256]{1,0:T(8,128)(2,1)} fusion(f32[1664,256]{1,0:T(8,128)} %get-tuple-element.32, bf16[1664,256]{1,0:T(8,128)(2,1)S(1)} %collective-permute-done.6), kind=kLoop, calls=%fused_computation.1 | loop fusion | flops 1277952 | bytes 3407872 | tf_op jit(solution)/shard_map/convert_element_type | solution.py:379
  50.7 9.4 %all-to-all-start = ((bf16[16,104,256]{2,1,0:T(8,128)(2,1)}), bf16[16,104,256]{2,1,0:T(8,128)(2,1)}, u32[]{:S(2)}, u32[]{:S(2)}) async-start(bf16[16,104,256]{2,1,0:T(8,128)(2,1)} %bitcast.9), calls=%async_computation | async-start | bytes 1703936 | tf_op jit(solution)/shard_map/all_to_all | solution.py:380
  60.1 13.1 %all-to-all-done = bf16[16,104,256]{2,1,0:T(8,128)(2,1)} async-done(((bf16[16,104,256]{2,1,0:T(8,128)(2,1)}), bf16[16,104,256]{2,1,0:T(8,128)(2,1)}, u32[]{:S(2)}, u32[]{:S(2)}) %all-to-all-start) | async-done | bytes 852000 | tf_op jit(solution)/shard_map/all_to_all | solution.py:380
  73.2 1.3 convert_reduce_fusion
  74.5 5.3 %collective-permute-start.7 = (bf16[104,128]{1,0:T(8,128)(2,1)S(1)}, bf16[104,128]{1,0:T(8,128)(2,1)S(1)}, u32[]{:S(2)}, u32[]{:S(2)}) collective-permute-start(bf16[104,128]{1,0:T(8,128)(2,1)S(1)} %dynamic-slice_convert_fusion), channel_id=1, source_target_pairs={{0,32},{32,0},{64,96},{96,64},{128,160},{160,128},{192,224},{224,1... | collective-permute-start | bytes 79880 | tf_op jit(solution)/shard_map/ppermute | solution.py:356
  79.8 1.2 collective-permute-done.7
  81.1 5.7 %collective-permute-start.8 = (bf16[52,128]{1,0:T(8,128)(2,1)S(1)}, bf16[52,128]{1,0:T(8,128)(2,1)S(1)}, u32[]{:S(2)}, u32[]{:S(2)}) collective-permute-start(bf16[52,128]{1,0:T(8,128)(2,1)S(1)} %dynamic-slice_convert_fusion.1), channel_id=1, source_target_pairs={{0,64},{32,96},{64,0},{96,32},{128,192},{160,224},{192,128},{224,1... | collective-permute-start | bytes 39944 | tf_op jit(solution)/shard_map/ppermute | solution.py:356
  86.8 1.1 collective-permute-done.8
  87.9 9.6 %collective-permute-start.9 = (bf16[52,128]{1,0:T(8,128)(2,1)S(1)}, bf16[52,128]{1,0:T(8,128)(2,1)S(1)}, u32[]{:S(2)}, u32[]{:S(2)}) collective-permute-start(bf16[52,128]{1,0:T(8,128)(2,1)S(1)} %add_convert_fusion.3), channel_id=1, source_target_pairs={{0,128},{32,160},{64,192},{96,224},{128,0},{160,32},{192,64},{224,... | collective-permute-start | bytes 39944 | tf_op jit(solution)/shard_map/ppermute | solution.py:356
  97.5 1.1 collective-permute-done.9
  98.6 14.1 %collective-permute-start.10 = (bf16[52,128]{1,0:T(8,128)(2,1)S(1)}, bf16[52,128]{1,0:T(8,128)(2,1)S(1)}, u32[]{:S(2)}, u32[]{:S(2)}) collective-permute-start(bf16[52,128]{1,0:T(8,128)(2,1)S(1)} %add_convert_fusion.2), channel_id=1, source_target_pairs={{0,256},{32,288},{64,320},{96,352},{128,384},{160,416},{192,448},{... | collective-permute-start | bytes 39944 | tf_op jit(solution)/shard_map/ppermute | solution.py:356
  112.7 1.1 collective-permute-done.10
  113.8 1.9 %collective-permute-start.11 = (bf16[52,128]{1,0:T(8,128)(2,1)S(1)}, bf16[52,128]{1,0:T(8,128)(2,1)S(1)}, u32[]{:S(2)}, u32[]{:S(2)}) collective-permute-start(bf16[52,128]{1,0:T(8,128)(2,1)S(1)} %add_convert_fusion.1), channel_id=1, source_target_pairs={{0,64},{32,96},{64,0},{96,32},{128,192},{160,224},{192,128},{224,1... | collective-permute-start | bytes 39944 | tf_op jit(solution)/shard_map/ppermute | solution.py:356
  115.7 3.7 %collective-permute-done.11 = bf16[52,128]{1,0:T(8,128)(2,1)S(1)} collective-permute-done((bf16[52,128]{1,0:T(8,128)(2,1)S(1)}, bf16[52,128]{1,0:T(8,128)(2,1)S(1)}, u32[]{:S(2)}, u32[]{:S(2)}) %collective-permute-start.11) | collective-permute-done | bytes 13344 | tf_op jit(solution)/shard_map/ppermute | solution.py:356
  119.5 1.9 %collective-permute-start.12 = (bf16[104,128]{1,0:T(8,128)(2,1)S(1)}, bf16[104,128]{1,0:T(8,128)(2,1)S(1)}, u32[]{:S(2)}, u32[]{:S(2)}) collective-permute-start(bf16[104,128]{1,0:T(8,128)(2,1)S(1)} %pad_maximum_fusion.3), channel_id=1, source_target_pairs={{0,32},{32,0},{64,96},{96,64},{128,160},{160,128},{192,224},{224,1... | collective-permute-start | bytes 79880 | tf_op jit(solution)/shard_map/ppermute | solution.py:356
  121.4 2.7 %collective-permute-done.12 = bf16[104,128]{1,0:T(8,128)(2,1)S(1)} collective-permute-done((bf16[104,128]{1,0:T(8,128)(2,1)S(1)}, bf16[104,128]{1,0:T(8,128)(2,1)S(1)}, u32[]{:S(2)}, u32[]{:S(2)}) %collective-permute-start.12) | collective-permute-done | bytes 26656 | tf_op jit(solution)/shard_map/ppermute | solution.py:356
  124.2 14.9 %all_to_all.10 = bf16[16,104,256]{2,1,0:T(8,128)(2,1)S(1)} all-to-all(bf16[16,104,256]{2,1,0:T(8,128)(2,1)S(1)} %broadcast_in_dim.14), channel_id=1, replica_groups=mesh['z'=16,'x_lo'=2,'y'=4,'x_hi'=2,'core'=2] {'x_lo','y','x_hi'}, dimensions={0} | all-to-all | bytes 1703936 | tf_op jit(solution)/shard_map/all_to_all | solution.py:391
  139.2 11.1 %collective-permute-start.13 = (bf16[1664,256]{1,0:T(8,128)(2,1)S(1)}, bf16[1664,256]{1,0:T(8,128)(2,1)S(1)}, u32[]{:S(2)}, u32[]{:S(2)}) collective-permute-start(bf16[1664,256]{1,0:T(8,128)(2,1)S(1)} %bitcast.25), channel_id=1, source_target_pairs={{0,1},{1,0},{2,3},{3,2},{4,5},{5,4},{6,7},{7,6},{8,9},{9,8},{10,11... | collective-permute-start | bytes 2555912 | tf_op jit(solution)/shard_map/ppermute | solution.py:356
  150.4 2.0 %shard_map.187 = (bf16[8,5120]{1,0:T(8,128)(2,1)}, bf16[4,5120]{1,0:T(4,128)(2,1)}, bf16[2,5120]{1,0:T(2,128)(2,1)}) custom-call(f32[1008,128]{1,0:T(8,128)S(1)} %get-tuple-element.25.g1, f32[672,128]{1,0:T(8,128)S(1)} %get-tuple-element.26.g2, f32[176,256]{1,0:T(8,128)S(1)} %get-tuple-element.27.g3, bf16[3,128,256]{2,1,0:T(8,128)(2,1)S(1)} %fusion.4.t1b, ...), custom_call_target="tpu_custom_call" | custom-call | tf_op jit(solution)/shard_map/pallas_call | solution.py:466
  152.4 1.9 %shard_map.188 = (bf16[576,64]{1,0:T(8,128)(2,1)}, bf16[1152,128]{1,0:T(8,128)(2,1)}, bf16[2304,256]{1,0:T(8,128)(2,1)}, bf16[128,64]{1,0:T(8,128)(2,1)S(1)}, bf...) custom-call(s32[4]{0:T(128)S(1)} %pad_add_fusion.place_ref, bf16[1664,256]{1,0:T(8,128)(2,1)S(1)} %bitcast.26, ...), custom_call_target="tpu_custom_call" | custom-call | tf_op jit(solution)/shard_map/pallas_call | solution.py:479
  (71 shorter events, 9.8 us)
Async XLA Ops:
  0.6 31.1 %copy-start.14 = (bf16[512,64]{0,1:T(8,128)(2,1)S(1)}, bf16[512,64]{0,1:T(8,128)(2,1)}, u32[]{:S(2)}) copy-start(bf16[512,64]{0,1:T(8,128)(2,1)} %param.20) | copy-start | bytes 196612
  0.7 31.2 %copy-start.15 = (bf16[256,64]{0,1:T(8,128)(2,1)S(1)}, bf16[256,64]{0,1:T(8,128)(2,1)}, u32[]{:S(2)}) copy-start(bf16[256,64]{0,1:T(8,128)(2,1)} %param.19) | copy-start | bytes 98308
  0.7 31.3 %copy-start.16 = (bf16[128,64]{0,1:T(8,128)(2,1)S(1)}, bf16[128,64]{0,1:T(8,128)(2,1)}, u32[]{:S(2)}) copy-start(bf16[128,64]{0,1:T(8,128)(2,1)} %param.18) | copy-start | bytes 49156
  0.7 33.9 %copy-start.1 = (bf16[3,3,128,128]{3,2,1,0:T(8,128)(2,1)S(1)}, bf16[3,3,128,128]{3,2,1,0:T(8,128)(2,1)}, u32[]{:S(2)}) copy-start(bf16[3,3,128,128]{3,2,1,0:T(8,128)(2,1)} %param.16) | copy-start | bytes 884740
  0.7 33.9 %copy-start = (bf16[3,3,256,256]{3,2,1,0:T(8,128)(2,1)S(1)}, bf16[3,3,256,256]{3,2,1,0:T(8,128)(2,1)}, u32[]{:S(2)}) copy-start(bf16[3,3,256,256]{3,2,1,0:T(8,128)(2,1)} %param.17) | copy-start | bytes 3538948
  3.5 16.1 %collective-permute-start.1 = (bf16[24,5120]{1,0:T(8,128)(2,1)S(1)}, bf16[24,5120]{1,0:T(8,128)(2,1)S(1)}, u32[]{:S(2)}, u32[]{:S(2)}) collective-permute-start(bf16[24,5120]{1,0:T(8,128)(2,1)S(1)} %concatenate.45.own), channel_id=1, source_target_pairs={{4,0},{8,4},{12,8},{16,12},{20,16},{24,20},{28,24},{32,28},{36,32}... | collective-permute-start | bytes 737288 | tf_op jit(solution)/shard_map/ppermute | solution.py:32
  4.8 14.8 %collective-permute-start = (bf16[24,5120]{1,0:T(8,128)(2,1)S(1)}, bf16[24,5120]{1,0:T(8,128)(2,1)S(1)}, u32[]{:S(2)}, u32[]{:S(2)}) collective-permute-start(bf16[24,5120]{1,0:T(8,128)(2,1)S(1)} %concatenate.45.own), channel_id=1, source_target_pairs={{0,4},{4,8},{8,12},{12,16},{16,20},{20,24},{24,28},{28,32},{32,36}... | collective-permute-start | bytes 737288 | tf_op jit(solution)/shard_map/ppermute | solution.py:32
  11.3 7.8 %collective-permute-start.3 = (bf16[3,5120]{1,0:T(4,128)(2,1)S(1)}, bf16[3,5120]{1,0:T(4,128)(2,1)S(1)}, u32[]{:S(2)}, u32[]{:S(2)}) collective-permute-start(bf16[3,5120]{1,0:T(4,128)(2,1)S(1)} %get-tuple-element.69), channel_id=1, source_target_pairs={{8,0},{12,4},{16,8},{20,12},{24,16},{28,20},{32,24},{36,28},{40,32... | collective-permute-start | bytes 92168 | tf_op jit(solution)/shard_map/ppermute | solution.py:32
  12.6 7.0 %collective-permute-start.2 = (bf16[3,5120]{1,0:T(4,128)(2,1)S(1)}, bf16[3,5120]{1,0:T(4,128)(2,1)S(1)}, u32[]{:S(2)}, u32[]{:S(2)}) collective-permute-start(bf16[3,5120]{1,0:T(4,128)(2,1)S(1)} %get-tuple-element.70), channel_id=1, source_target_pairs={{0,8},{4,12},{8,16},{12,20},{16,24},{20,28},{24,32},{28,36},{32,40... | collective-permute-start | bytes 92168 | tf_op jit(solution)/shard_map/ppermute | solution.py:32
  19.1 15.5 %copy-start.8 = (bf16[3,64,64]{2,1,0:T(8,128)(2,1)}, bf16[3,64,64]{2,1,0:T(8,128)(2,1)S(1)}, u32[]{:S(2)}) copy-start(bf16[3,64,64]{2,1,0:T(8,128)(2,1)S(1)} %get-tuple-element.56) | copy-start | bytes 73732
  19.1 15.4 %copy-start.10 = (bf16[3,64,64]{2,1,0:T(8,128)(2,1)}, bf16[3,64,64]{2,1,0:T(8,128)(2,1)S(1)}, u32[]{:S(2)}) copy-start(bf16[3,64,64]{2,1,0:T(8,128)(2,1)S(1)} %get-tuple-element.57) | copy-start | bytes 73732
  19.1 15.4 %copy-start.12 = (bf16[3,64,64]{2,1,0:T(8,128)(2,1)}, bf16[3,64,64]{2,1,0:T(8,128)(2,1)S(1)}, u32[]{:S(2)}) copy-start(bf16[3,64,64]{2,1,0:T(8,128)(2,1)S(1)} %get-tuple-element.58) | copy-start | bytes 73732
  19.6 0.6 copy-start.6
  20.2 12.0 %collective-permute-start.5 = (bf16[78,1024]{1,0:T(8,128)(2,1)S(1)}, bf16[78,1024]{1,0:T(8,128)(2,1)S(1)}, u32[]{:S(2)}, u32[]{:S(2)}) collective-permute-start(bf16[78,1024]{1,0:T(8,128)(2,1)S(1)} %concatenate.49), channel_id=1, source_target_pairs={{1,0},{2,1},{3,2},{5,4},{6,5},{7,6},{9,8},{10,9},{11,10},{13,12},{... | collective-permute-start | bytes 479240 | tf_op jit(solution)/shard_map/ppermute | solution.py:32
  29.7 4.2 %collective-permute-start.4 = (bf16[78,1024]{1,0:T(8,128)(2,1)S(1)}, bf16[78,1024]{1,0:T(8,128)(2,1)S(1)}, u32[]{:S(2)}, u32[]{:S(2)}) collective-permute-start(bf16[78,1024]{1,0:T(8,128)(2,1)S(1)} %concatenate.48), channel_id=1, source_target_pairs={{0,1},{1,2},{2,3},{4,5},{5,6},{6,7},{8,9},{9,10},{10,11},{12,13},{... | collective-permute-start | bytes 479240 | tf_op jit(solution)/shard_map/ppermute | solution.py:32
  32.3 0.7 copy-start.2
  33.9 0.7 copy-start.4
  34.6 0.9 copy-start.3
  35.5 0.9 copy-start.5
  36.4 0.8 copy-start.7
  43.9 4.3 %collective-permute-start.6 = (bf16[1664,256]{1,0:T(8,128)(2,1)S(1)}, bf16[1664,256]{1,0:T(8,128)(2,1)S(1)}, u32[]{:S(2)}, u32[]{:S(2)}) collective-permute-start(bf16[1664,256]{1,0:T(8,128)(2,1)S(1)} %get-tuple-element.33), channel_id=1, source_target_pairs={{0,1},{1,0},{2,3},{3,2},{4,5},{5,4},{6,7},{7,6},{8,9},{9,8},{10,11... | collective-permute-start | bytes 2555912 | tf_op jit(solution)/shard_map/ppermute | solution.py:356
  50.7 22.5 %all-to-all-start = ((bf16[16,104,256]{2,1,0:T(8,128)(2,1)}), bf16[16,104,256]{2,1,0:T(8,128)(2,1)}, u32[]{:S(2)}, u32[]{:S(2)}) async-start(bf16[16,104,256]{2,1,0:T(8,128)(2,1)} %bitcast.9), calls=%async_computation | async-start | bytes 1703936 | tf_op jit(solution)/shard_map/all_to_all | solution.py:380
  74.5 75.8 %copy-start.9 = (bf16[3,64,64]{2,1,0:T(8,128)(2,1)S(1)}, bf16[3,64,64]{2,1,0:T(8,128)(2,1)}, u32[]{:S(2)}) copy-start(bf16[3,64,64]{2,1,0:T(8,128)(2,1)} %copy-done.8) | copy-start | bytes 73732
  74.5 75.8 %copy-start.11 = (bf16[3,64,64]{2,1,0:T(8,128)(2,1)S(1)}, bf16[3,64,64]{2,1,0:T(8,128)(2,1)}, u32[]{:S(2)}) copy-start(bf16[3,64,64]{2,1,0:T(8,128)(2,1)} %copy-done.10) | copy-start | bytes 73732
  74.5 75.8 %copy-start.13 = (bf16[3,64,64]{2,1,0:T(8,128)(2,1)S(1)}, bf16[3,64,64]{2,1,0:T(8,128)(2,1)}, u32[]{:S(2)}) copy-start(bf16[3,64,64]{2,1,0:T(8,128)(2,1)} %copy-done.12) | copy-start | bytes 73732
  74.5 6.5 %collective-permute-start.7 = (bf16[104,128]{1,0:T(8,128)(2,1)S(1)}, bf16[104,128]{1,0:T(8,128)(2,1)S(1)}, u32[]{:S(2)}, u32[]{:S(2)}) collective-permute-start(bf16[104,128]{1,0:T(8,128)(2,1)S(1)} %dynamic-slice_convert_fusion), channel_id=1, source_target_pairs={{0,32},{32,0},{64,96},{96,64},{128,160},{160,128},{192,224},{224,1... | collective-permute-start | bytes 79880 | tf_op jit(solution)/shard_map/ppermute | solution.py:356
  81.1 6.8 %collective-permute-start.8 = (bf16[52,128]{1,0:T(8,128)(2,1)S(1)}, bf16[52,128]{1,0:T(8,128)(2,1)S(1)}, u32[]{:S(2)}, u32[]{:S(2)}) collective-permute-start(bf16[52,128]{1,0:T(8,128)(2,1)S(1)} %dynamic-slice_convert_fusion.1), channel_id=1, source_target_pairs={{0,64},{32,96},{64,0},{96,32},{128,192},{160,224},{192,128},{224,1... | collective-permute-start | bytes 39944 | tf_op jit(solution)/shard_map/ppermute | solution.py:356
  87.9 10.7 %collective-permute-start.9 = (bf16[52,128]{1,0:T(8,128)(2,1)S(1)}, bf16[52,128]{1,0:T(8,128)(2,1)S(1)}, u32[]{:S(2)}, u32[]{:S(2)}) collective-permute-start(bf16[52,128]{1,0:T(8,128)(2,1)S(1)} %add_convert_fusion.3), channel_id=1, source_target_pairs={{0,128},{32,160},{64,192},{96,224},{128,0},{160,32},{192,64},{224,... | collective-permute-start | bytes 39944 | tf_op jit(solution)/shard_map/ppermute | solution.py:356
  98.6 15.2 %collective-permute-start.10 = (bf16[52,128]{1,0:T(8,128)(2,1)S(1)}, bf16[52,128]{1,0:T(8,128)(2,1)S(1)}, u32[]{:S(2)}, u32[]{:S(2)}) collective-permute-start(bf16[52,128]{1,0:T(8,128)(2,1)S(1)} %add_convert_fusion.2), channel_id=1, source_target_pairs={{0,256},{32,288},{64,320},{96,352},{128,384},{160,416},{192,448},{... | collective-permute-start | bytes 39944 | tf_op jit(solution)/shard_map/ppermute | solution.py:356
  113.8 5.7 %collective-permute-start.11 = (bf16[52,128]{1,0:T(8,128)(2,1)S(1)}, bf16[52,128]{1,0:T(8,128)(2,1)S(1)}, u32[]{:S(2)}, u32[]{:S(2)}) collective-permute-start(bf16[52,128]{1,0:T(8,128)(2,1)S(1)} %add_convert_fusion.1), channel_id=1, source_target_pairs={{0,64},{32,96},{64,0},{96,32},{128,192},{160,224},{192,128},{224,1... | collective-permute-start | bytes 39944 | tf_op jit(solution)/shard_map/ppermute | solution.py:356
  119.5 4.6 %collective-permute-start.12 = (bf16[104,128]{1,0:T(8,128)(2,1)S(1)}, bf16[104,128]{1,0:T(8,128)(2,1)S(1)}, u32[]{:S(2)}, u32[]{:S(2)}) collective-permute-start(bf16[104,128]{1,0:T(8,128)(2,1)S(1)} %pad_maximum_fusion.3), channel_id=1, source_target_pairs={{0,32},{32,0},{64,96},{96,64},{128,160},{160,128},{192,224},{224,1... | collective-permute-start | bytes 79880 | tf_op jit(solution)/shard_map/ppermute | solution.py:356
  139.2 13.3 %collective-permute-start.13 = (bf16[1664,256]{1,0:T(8,128)(2,1)S(1)}, bf16[1664,256]{1,0:T(8,128)(2,1)S(1)}, u32[]{:S(2)}, u32[]{:S(2)}) collective-permute-start(bf16[1664,256]{1,0:T(8,128)(2,1)S(1)} %bitcast.25), channel_id=1, source_target_pairs={{0,1},{1,0},{2,3},{3,2},{4,5},{5,4},{6,7},{7,6},{8,9},{9,8},{10,11... | collective-permute-start | bytes 2555912 | tf_op jit(solution)/shard_map/ppermute | solution.py:356

commit v3 on v2

--- a/solution.py
+++ b/solution.py
@@ -32,8 +32,17 @@
     return lax.ppermute(block, axis, route)
 
 
+def stacked(parts, rows):
+    total, at = None, 0
+    for part in parts:
+        padded = jnp.pad(part, ((at, rows - at - part.shape[0]), (0, 0)))
+        total = padded if total is None else total + padded
+        at += part.shape[0]
+    return total
+
+
 def halos(x1, x2, x3, x4, cot):
-    own = jnp.concatenate([x1, cot, x2, x3, x4, jnp.zeros_like(x4)], axis=0)
+    own = stacked((x1, cot, x2, x3, x4), 24)
     last = jnp.concatenate([x2[-1:], x3[-1:], x4], axis=0)
     first = jnp.concatenate([x2[:1], x3[:1], x4], axis=0)
     above = moved(own, ROWS, 1)
@@ -75,11 +84,16 @@
 
 
 def forward_kernel(
-    place_ref, own, above, below, above2, below2, left, right,
-    t1, k2, k3, p2, p3, p4,
-    keep_ref, send_ref, g1_ref, g2_ref, g3_ref, gf4_ref,
-    wx1, wc, wx2, wx3, wx4, xw1, xw2, xw3, d1, d2, d3, gm1, gm2, gm3, sums,
+    place_ref, p2, p3, p4, *refs
 ):
+    far, refs = refs[:10], refs[10:]
+    keep_ref, send_ref, g1_ref, g2_ref, g3_ref, gf4_ref = refs[:6]
+    wx1, wc, wx2, wx3, wx4, xw1, xw2, xw3, d1, d2, d3, gm1, gm2, gm3, sums = refs[6:21]
+    near, sems = refs[21:31], refs[31]
+    copies = [pltpu.make_async_copy(far[n], near[n], sems.at[n]) for n in range(10)]
+    for copy in copies:
+        copy.start()
+    own, above, below, above2, below2, left, right, t1, k2, k3 = near
     row_block = place_ref[0]
     at_left = place_ref[1] == 0
     at_right = place_ref[2] == 1
@@ -92,6 +106,8 @@
 
     wx2[...] = jnp.zeros_like(wx2)
     wx4[...] = jnp.zeros_like(wx4)
+    for copy in copies[:8]:
+        copy.wait()
     sources = (
         (own, above, below, above2, below2, 0, WIDE, RIM),
         (left, left, left, left, left, None, RIM, 0),
@@ -132,6 +148,7 @@
     y1 = y1.astype(BF).astype(F32)
     d1[...] = slope
 
+    copies[8].wait()
     for j in range(3):
         for c in range(-4, 44):
             at = 8 + 16 * (c + 4)
@@ -145,6 +162,7 @@
     y2 = y2.astype(BF)
     d2[...] = slope
 
+    copies[9].wait()
     for j in range(3):
         for c in range(-2, 22):
             at = 8 + 8 * (c + 2)
@@ -164,8 +182,8 @@
     weights = row_weights((24, 32), 1, row_block).astype(BF)
     rows_up = []
     for y, p, rim, rows, wlo in ((y2, p2, 4, 16, 0), (y3, p3, 2, 8, 16), (x4, p4, 2, 8, 24)):
-        twice = jnp.concatenate([p[...], p[...]], axis=1)
-        coarse = jnp.dot(y, twice, preferred_element_type=F32).astype(BF).astype(F32)
+        twice = jnp.concatenate([p[...], p[...]], axis=0)
+        coarse = lax.dot_general(y, twice, NT, preferred_element_type=F32).astype(BF).astype(F32)
         cols = [coarse[rows * n : rows * (n + 1)] for n in range(coarse.shape[0] // rows)]
         end = len(cols) - rim
         cols[rim - 1] = jnp.where(at_left, cols[rim], cols[rim - 1])
@@ -174,7 +192,7 @@
         rows_up.append(jnp.dot(weights[:, wlo : wlo + rows], flat, preferred_element_type=F32))
     up2, up3, up4 = rows_up
 
-    gates = []
+    gates, g1 = [], []
     for f in range(-3, 43):
         k = f + 4
         merged = y1[24 * (f + 3) : 24 * (f + 4)]
@@ -194,10 +212,11 @@
         gates.append(gate)
         if -1 <= f <= 40:
             g = (d1[24 * (f + 3) : 24 * (f + 4)] * gate).astype(BF).astype(F32)
-            g1_ref[24 * (f + 1) : 24 * (f + 2), :] = g
+            g1.append(g)
             if 0 <= f < 40:
                 row = lax.broadcasted_iota(jnp.int32, (24, 1), 0)
                 gm1[8 + 24 * f : 32 + 24 * f, :] = jnp.where((row >= 8) & (row < 16), g, 0.0)
+    g1_ref[...] = jnp.concatenate(g1, axis=0).astype(BF)
     gm1[0:8, :] = jnp.zeros((8, 128), F32)
     gm1[968:976, :] = jnp.zeros((8, 128), F32)
 
@@ -242,15 +261,15 @@
     flat2 = jnp.concatenate(cg2, axis=0).astype(BF).astype(F32)
     flat3 = jnp.concatenate(cg3, axis=0).astype(BF).astype(F32)
     flat4 = jnp.concatenate(cg4, axis=0).astype(BF).astype(F32)
-    back2 = lax.dot_general(flat2[:, 0:64].astype(BF), p2[...], NT, preferred_element_type=F32)
-    back3 = lax.dot_general(flat3[:, 0:64].astype(BF), p3[...], NT, preferred_element_type=F32)
-    back4 = lax.dot_general(flat4[:, 0:64].astype(BF), p4[...], NT, preferred_element_type=F32)
+    back2 = jnp.dot(flat2[:, 0:64].astype(BF), p2[...], preferred_element_type=F32)
+    back3 = jnp.dot(flat3[:, 0:64].astype(BF), p3[...], preferred_element_type=F32)
+    back4 = jnp.dot(flat4[:, 0:64].astype(BF), p4[...], preferred_element_type=F32)
     for c in range(10):
         gf4_ref[0:1, 512 * c : 512 * c + 512] = back4[8 * c + 2 : 8 * c + 3].astype(BF)
     g2 = (d2[48:720, :] * back2).astype(BF).astype(F32)
     g3 = (d3[8:184, :] * back3).astype(BF).astype(F32)
-    g2_ref[...] = g2
-    g3_ref[...] = g3
+    g2_ref[...] = g2.astype(BF)
+    g3_ref[...] = g3.astype(BF)
 
     row2 = lax.broadcasted_iota(jnp.int32, (640, 1), 0) % 16
     own2 = (row2 >= 6) & (row2 < 10)
@@ -288,6 +307,8 @@
         for j in range(3):
             a, b = window[j], window[j + 1]
             blocks.append(zi[a : a + 64] + pltpu.roll(zi[b : b + 64], 64, 1))
+    blocks.append(jnp.zeros((64, 128), F32))
+    pairs = [jnp.where(low, blocks[n], pltpu.roll(blocks[n + 1], 64, 1)) for n in range(0, 10, 2)]
     y2_own, y3_own, x4_own = y2[64:704], y3[16:176], x4[16:96]
     for y, flat, mask, branch in (
         (y2_own, flat2[16:656], own2, 1),
@@ -295,28 +316,24 @@
         (x4_own, flat4, row4 == 2, 3),
     ):
         masked = jnp.where(mask, flat, 0.0).astype(BF)
-        z = lax.dot_general(y, masked, TN, preferred_element_type=F32) * (cells // 4**branch) ** -0.5
-        blocks += [z[64 * n : 64 * (n + 1)] for n in range(z.shape[0] // 64)]
-    blocks.append(jnp.zeros((64, 128), F32))
+        z = lax.dot_general(masked, y, TN, preferred_element_type=F32) * (cells // 4**branch) ** -0.5
+        pairs += [z[0:64, 128 * n : 128 * (n + 1)] for n in range(z.shape[1] // 128)]
     base = 2880
-    for n in range(6):
-        for side in range(2):
-            a, b = blocks[4 * n + 2 * side], blocks[4 * n + 2 * side + 1]
-            if 4 * n + 2 * side + 1 < 9:
-                b = pltpu.roll(b, 64, 1)
-            at = base + 64 * n
-            sums[at : at + 64, 128 * side : 128 * side + 128] = jnp.where(low, a, b)
+    for n in range(12):
+        at, side = base + 64 * (n // 2), 128 * (n % 2)
+        sums[at : at + 64, side : side + 128] = pairs[n]
     sums[3264:3328, :] = jnp.zeros((64, 256), F32)
-    keep_ref[...] = sums[pl.ds(pl.multiple_of(core * HALF, 64), HALF), :]
+    keep_ref[...] = sums[pl.ds(pl.multiple_of(core * HALF, 64), HALF), :].astype(BF)
     send_ref[...] = sums[pl.ds(pl.multiple_of((1 - core) * HALF, 64), HALF), :].astype(BF)
 
 
-def backward_kernel(g1, g2, g3, t1b, k2, k3, gf1_ref, gf2_ref, gf3_ref, xw1, xw2, xw3, out2, out3):
+def backward_kernel(g1_ref, g2_ref, g3_ref, t1b, k2, k3, gf1_ref, gf2_ref, gf3_ref, xw1, xw2, xw3, out2, out3):
     low = lax.broadcasted_iota(jnp.int32, (1, 128), 1) < 64
     for ref, n in ((xw1, 960), (xw2, 640), (xw3, 160)):
         ref[0:8, :] = jnp.zeros((8, ref.shape[1]), F32)
         ref[8 + n : 16 + n, :] = jnp.zeros((8, ref.shape[1]), F32)
 
+    g1, g2, g3 = (ref[...].astype(F32) for ref in (g1_ref, g2_ref, g3_ref))
     xw1[8:968, 0:128] = g1[24:984, :]
     xw1[8:968, 128:256] = jnp.where(low, g1[48:1008, :], g1[0:960, :])
     total = xw1[8:968, 0:128]
@@ -356,40 +373,18 @@
     return lax.ppermute(block, axis, [(i, i ^ flip) for i in range(lax.axis_size(axis))])
 
 
-def kept_half(values, axis, flip, dim):
-    bit = (lax.axis_index(axis) // flip) % 2
-    half = values.shape[dim] // 2
-    keep = lax.dynamic_slice_in_dim(values, bit * half, half, axis=dim)
-    send = lax.dynamic_slice_in_dim(values, (1 - bit) * half, half, axis=dim)
-    got = swapped(send.astype(BF), axis, flip)
-    return keep + got.astype(F32)
-
-
-def both_halves(values, axis, flip, dim):
-    bit = (lax.axis_index(axis) // flip) % 2
-    got = swapped(values, axis, flip)
-    first = jnp.where(bit == 0, values, got)
-    second = jnp.where(bit == 0, got, values)
-    return jnp.concatenate([first, second], axis=dim)
-
-
-def summed_over_devices(keep, send):
+def summed_over_devices(keep, send, others):
     width = keep.shape[1]
-    part = keep + swapped(send, "core", 1).astype(F32)
+    part = keep.astype(F32) + swapped(send, "core", 1).astype(F32)
     pieces = part.astype(BF).reshape(16, -1, width)
     pieces = lax.all_to_all(pieces, PLANE, 0, 0)
-    part = jnp.sum(pieces.astype(F32), axis=0)
-    part = kept_half(part, "z", 1, 1)
-    part = kept_half(part, "z", 2, 0)
-    for flip in (4, 8):
-        part = part.astype(BF)
-        part = part.astype(F32) + swapped(part, "z", flip).astype(F32)
-    part = part.astype(BF)
-    part = both_halves(part, "z", 2, 0)
-    part = both_halves(part, "z", 1, 1)
+    pieces, others = lax.optimization_barrier((pieces, others))
+    part = jnp.sum(pieces.astype(F32), axis=0).astype(BF)
+    pieces = lax.all_gather(part, "z")
+    part = jnp.sum(pieces.astype(F32), axis=0).astype(BF)
     pieces = jnp.broadcast_to(part[None], (16,) + part.shape)
     part = lax.all_to_all(pieces, PLANE, 0, 0).reshape(-1, width)
-    return part, swapped(part, "core", 1)
+    return part, swapped(part, "core", 1), others
 
 
 def unpack_kernel(place_ref, mine, got, k1_ref, k2_ref, k3_ref, p2_ref, p3_ref, p4_ref, whole):
@@ -399,23 +394,27 @@
     k3_ref[...] = whole[0:2304, :]
     k2_ref[0:576, :] = whole[2304:2880, 0:128]
     k2_ref[576:1152, :] = whole[2304:2880, 128:256]
-    block = 0
-    for ref, count in ((k1_ref, 9), (p2_ref, 2), (p3_ref, 4), (p4_ref, 8)):
-        for n in range(count):
-            at, side = 2880 + 64 * (block // 4), 64 * (block % 4)
-            ref[64 * n : 64 * (n + 1), :] = whole[at : at + 64, side : side + 64]
-            block += 1
-
-
-def call(kernel, out_shapes, scratch, count, scalars=0):
+    for n in range(9):
+        at, side = 2880 + 64 * (n // 4), 64 * (n % 4)
+        k1_ref[64 * n : 64 * (n + 1), :] = whole[at : at + 64, side : side + 64]
+    n = 5
+    for ref, count in ((p2_ref, 1), (p3_ref, 2), (p4_ref, 4)):
+        for m in range(count):
+            at, side = 2880 + 64 * (n // 2), 128 * (n % 2)
+            ref[:, 128 * m : 128 * (m + 1)] = whole[at : at + 64, side : side + 128]
+            n += 1
+
+
+def call(kernel, out_shapes, scratch, count, scalars=0, far=0):
     vmem = pl.BlockSpec(memory_space=pltpu.VMEM)
     smem = pl.BlockSpec(memory_space=pltpu.SMEM)
     return pl.pallas_call(
         kernel,
         out_shape=[jax.ShapeDtypeStruct(shape, dtype) for shape, dtype in out_shapes],
-        in_specs=[smem] * scalars + [vmem] * count,
+        in_specs=[smem] * scalars + [vmem] * count + [pl.BlockSpec(memory_space=pl.ANY)] * far,
         out_specs=[vmem] * len(out_shapes),
-        scratch_shapes=[pltpu.VMEM(shape, dtype) for shape, dtype in scratch],
+        scratch_shapes=[pltpu.VMEM(shape, dtype) for shape, dtype in scratch]
+        + ([pltpu.SemaphoreType.DMA((far,))] if far else []),
         compiler_params=pltpu.CompilerParams(vmem_limit_bytes=48 * 1024 * 1024),
     )
 
@@ -445,13 +444,13 @@
     ahead, back = pair_weights(kernel_one)
     k2 = kernel_two.reshape(3, 384, 128)
     k3 = kernel_three.reshape(3, 768, 256)
-    packs = halos(x1, x2, x3, x4, cot)
+    fars = halos(x1, x2, x3, x4, cot) + (ahead, k2, k3)
     total = RIM + WIDE + RIM
     keep, send, g1, g2, g3, gf4 = call(
         forward_kernel,
         [
-            ((HALF, 256), F32), ((HALF, 256), BF),
-            ((1008, 128), F32), ((672, 128), F32), ((176, 256), F32), ((1, WIDE), BF),
+            ((HALF, 256), BF), ((HALF, 256), BF),
+            ((1008, 128), BF), ((672, 128), BF), ((176, 256), BF), ((1, WIDE), BF),
         ],
         [
             ((24, total), F32), ((24, total), F32), ((16, total), F32), ((8, total), F32), ((8, total), F32),
@@ -459,10 +458,12 @@
             ((1104, 128), F32), ((768, 128), F32), ((192, 256), F32),
             ((976, 128), F32), ((656, 128), F32), ((176, 256), F32),
             ((PACK_ROWS, 256), F32),
-        ],
-        13,
+        ]
+        + [(far.shape, BF) for far in fars],
+        3,
         1,
-    )(place, *packs, ahead, k2, k3, p2, p3, p4)
+        10,
+    )(place, p2.T, p3.T, p4.T, *fars)
     gf1, gf2, gf3 = call(
         backward_kernel,
         [((8, WIDE), BF), ((4, WIDE), BF), ((2, WIDE), BF)],
@@ -478,21 +479,21 @@
 def unpacked(place, mine, got):
     outs = call(
         unpack_kernel,
-        [((576, 64), BF), ((1152, 128), BF), ((2304, 256), BF), ((128, 64), BF), ((256, 64), BF), ((512, 64), BF)],
+        [((576, 64), BF), ((1152, 128), BF), ((2304, 256), BF), ((64, 128), BF), ((64, 256), BF), ((64, 512), BF)],
         [((PACK_ROWS, 256), BF)],
         2,
         1,
     )(place, mine, got)
     return (
         outs[0].reshape(3, 3, 64, 64), outs[1].reshape(3, 3, 128, 128), outs[2].reshape(3, 3, 256, 256),
-        outs[3], outs[4], outs[5],
+        outs[3].T, outs[4].T, outs[5].T,
     )
 
 
 def on_device(*args):
     place, keep, send, gf1, gf2, gf3, gf4 = local_part(*args)
-    mine, got = summed_over_devices(keep, send)
-    return (gf1, gf2, gf3, gf4) + unpacked(place, mine, got)
+    mine, got, others = summed_over_devices(keep, send, (gf1, gf2, gf3, gf4))
+    return others + unpacked(place, mine, got)
 
 
 def solution(mesh):

time: 158 us -> 139 us (0.88)
  starting transfers between devices: 85.1 us -> 46.8 us
  blocking collectives: 14.9 us -> 52.4 us
  local copies, waits for them, and re-layouts: 11.9 us -> 2.02 us
  waiting for transfers between devices: 27.6 us -> 17.8 us
  Pallas kernels: 10.6 us -> 13.1 us
    ppermute x8 -> x2, starting transfers between devices: 51.5 us -> 13.2 us  [swapped(): lax.ppermute(block, axis, [(i, i ^ flip) for i in range(lax.axis_size(axi...]
    all_gather x0 -> x1, blocking collectives: none -> 36.5 us  [summed_over_devices(): pieces = lax.all_gather(part, 'z')]
    ppermute x8 -> x2, waiting for transfers between devices: 13.2 us -> 4.33 us  [swapped(): lax.ppermute(block, axis, [(i, i ^ flip) for i in range(lax.axis_size(axi...]
    unnamed x40 -> x10, local copies, waits for them, and re-layouts: 7.02 us -> 0.03 us
    concatenate x1 -> x0, local copies, waits for them, and re-layouts: 2.81 us -> none  [halos(): own = jnp.concatenate([x1, cot, x2, x3, x4, jnp.zeros_like(x4)], axis=0)]
    pallas_call x1, Pallas kernels: 6.68 us -> 9.26 us  [local_part(): call(forward_kernel, [((HALF, 256), BF), ((HALF, 256), BF), ((1008, 128),...]
    all_to_all x1, waiting for transfers between devices: 13.1 us -> 11 us  [summed_over_devices(): pieces = lax.all_to_all(pieces, PLANE, 0, 0)]
  transfers between devices with their start and end apart: 15 -> 9, of which waited for: 10 -> 5; matrix products, arithmetic and copies ran while one was open for 2% -> 2% of each run, Pallas kernels for 1% -> 1%
where the time goes in v3:
time: 139 us; the launch traced here: 138 us
  blocking collectives  52.4 us (38%)
  starting transfers between devices  46.8 us (34%)
  waiting for transfers between devices  17.8 us (13%)
  Pallas kernels  13.1 us (9%)
  other arithmetic  4.89 us (4%)
  local copies, waits for them, and re-layouts  2.02 us (1%)
    all_gather x1, blocking collectives, summed_over_devices(): pieces = lax.all_gather(part, 'z')  36.5 us
    ppermute x6, starting transfers between devices, moved(): return lax.ppermute(block, axis, route)  24.2 us
    all_to_all x1, blocking collectives, summed_over_devices(): part = lax.all_to_all(pieces, PLANE, 0, 0).reshape(-1, width)  15.9 us
    ppermute x2, starting transfers between devices, swapped(): lax.ppermute(block, axis, [(i, i ^ flip) for i in range(lax.axis_size(axi...  13.2 us
    all_to_all x1, waiting for transfers between devices, summed_over_devices(): pieces = lax.all_to_all(pieces, PLANE, 0, 0)  11 us
    all_to_all x1, starting transfers between devices, summed_over_devices(): pieces = lax.all_to_all(pieces, PLANE, 0, 0)  9.39 us
    pallas_call x1, Pallas kernels, local_part(): call(forward_kernel, [((HALF, 256), BF), ((HALF, 256), BF), ((1008, 128),...  9.26 us
    ppermute x2, waiting for transfers between devices, swapped(): lax.ppermute(block, axis, [(i, i ^ flip) for i in range(lax.axis_size(axi...  4.33 us
  transfers between devices with their start and end apart: 9, of which 5 were waited for; matrix products, arithmetic and copies ran while one was open for 2% of the time, Pallas kernels for 1%

profile of v3, /device:TPU:1, one launch (start us, length us, event | category | flops | bytes accessed | tf_op | source)
XLA Modules:
  0.0 137.9 jit_solution(6015633169199150468)
XLA Ops:
  0.6 1.1 pad_add_fusion.refs_0_
  1.7 1.3 collective-permute-start.1
  3.0 4.7 %collective-permute-start = (bf16[24,5120]{1,0:T(8,128)(2,1)S(1)}, bf16[24,5120]{1,0:T(8,128)(2,1)S(1)}, u32[]{:S(2)}, u32[]{:S(2)}) collective-permute-start(bf16[24,5120]{1,0:T(8,128)(2,1)S(1)} %pad_add_fusion.refs_0_), channel_id=1, source_target_pairs={{0,4},{4,8},{8,12},{12,16},{16,20},{20,24},{24,28},{28,32},{32,36}... | collective-permute-start | bytes 737288 | tf_op jit(solution)/shard_map/ppermute | solution.py:32
  7.7 0.9 fusion.10
  8.6 0.0 copy-start.1
  8.7 0.0 copy-start.2
  8.7 1.0 pad_maximum_fusion
  9.7 1.3 collective-permute-start.3
  11.0 5.6 %collective-permute-start.2 = (bf16[3,5120]{1,0:T(4,128)(2,1)S(1)}, bf16[3,5120]{1,0:T(4,128)(2,1)S(1)}, u32[]{:S(2)}, u32[]{:S(2)}) collective-permute-start(bf16[3,5120]{1,0:T(4,128)(2,1)S(1)} %get-tuple-element.66), channel_id=1, source_target_pairs={{0,8},{4,12},{8,16},{12,20},{16,24},{20,28},{24,32},{28,36},{32,40... | collective-permute-start | bytes 92168 | tf_op jit(solution)/shard_map/ppermute | solution.py:32
  16.6 0.9 slice_bitcast_fusion
  17.5 0.4 collective-permute-done.2.refs_3_
  18.0 9.4 %collective-permute-start.5 = (bf16[78,1024]{1,0:T(8,128)(2,1)S(1)}, bf16[78,1024]{1,0:T(8,128)(2,1)S(1)}, u32[]{:S(2)}, u32[]{:S(2)}) collective-permute-start(bf16[78,1024]{1,0:T(8,128)(2,1)S(1)} %concatenate.39), channel_id=1, source_target_pairs={{1,0},{2,1},{3,2},{5,4},{6,5},{7,6},{9,8},{10,9},{11,10},{13,12},{... | collective-permute-start | bytes 479240 | tf_op jit(solution)/shard_map/ppermute | solution.py:32
  27.5 1.9 %collective-permute-start.4 = (bf16[78,1024]{1,0:T(8,128)(2,1)S(1)}, bf16[78,1024]{1,0:T(8,128)(2,1)S(1)}, u32[]{:S(2)}, u32[]{:S(2)}) collective-permute-start(bf16[78,1024]{1,0:T(8,128)(2,1)S(1)} %concatenate.38), channel_id=1, source_target_pairs={{0,1},{1,2},{2,3},{4,5},{5,6},{6,7},{8,9},{9,10},{10,11},{12,13},{... | collective-permute-start | bytes 479240 | tf_op jit(solution)/shard_map/ppermute | solution.py:32
  29.4 0.1 pad_add_fusion.1.place_ref
  29.5 0.1 maximum_maximum_fusion.refs_7_
  29.7 2.0 %collective-permute-done.4.refs_5_ = bf16[78,1024]{1,0:T(8,128)(2,1)S(1)} collective-permute-done((bf16[78,1024]{1,0:T(8,128)(2,1)S(1)}, bf16[78,1024]{1,0:T(8,128)(2,1)S(1)}, u32[]{:S(2)}, u32[]{:S(2)}) %collective-permute-start.4) | collective-permute-done | bytes 159776 | tf_op jit(solution)/shard_map/ppermute | solution.py:32
  31.7 9.3 %shard_map.186 = (bf16[1664,256]{1,0:T(8,128)(2,1)S(1)}, bf16[1664,256]{1,0:T(8,128)(2,1)S(1)}, bf16[1008,128]{1,0:T(8,128)(2,1)S(1)}, bf16[672,128]{1,0:T(8,128...) custom-call(s32[4]{0:T(128)S(1)} %pad_add_fusion.1.place_ref, bf16[64,128]{1,0:T(8,128)(2,1)S(1)} %bitcast.38, ...), custom_call_target="tpu_custom_call" | custom-call | tf_op jit(solution)/shard_map/pallas_call | solution.py:449
  41.0 1.9 %collective-permute-start.6 = (bf16[1664,256]{1,0:T(8,128)(2,1)S(1)}, bf16[1664,256]{1,0:T(8,128)(2,1)S(1)}, u32[]{:S(2)}, u32[]{:S(2)}) collective-permute-start(bf16[1664,256]{1,0:T(8,128)(2,1)S(1)} %get-tuple-element.31), channel_id=1, source_target_pairs={{0,1},{1,0},{2,3},{3,2},{4,5},{5,4},{6,7},{7,6},{8,9},{9,8},{10,11... | collective-permute-start | bytes 2555912 | tf_op jit(solution)/shard_map/ppermute | solution.py:373
  42.9 2.3 %collective-permute-done.6 = bf16[1664,256]{1,0:T(8,128)(2,1)S(1)} collective-permute-done((bf16[1664,256]{1,0:T(8,128)(2,1)S(1)}, bf16[1664,256]{1,0:T(8,128)(2,1)S(1)}, u32[]{:S(2)}, u32[]{:S(2)}) %collective-permute-start.6) | collective-permute-done | bytes 852000 | tf_op jit(solution)/shard_map/ppermute | solution.py:373
  45.2 1.1 add_convert_fusion
  46.3 9.4 %all-to-all-start = ((bf16[16,104,256]{2,1,0:T(8,128)(2,1)}), bf16[16,104,256]{2,1,0:T(8,128)(2,1)}, u32[]{:S(2)}, u32[]{:S(2)}) async-start(bf16[16,104,256]{2,1,0:T(8,128)(2,1)} %bitcast.12), calls=%async_computation | async-start | bytes 1703936 | tf_op jit(solution)/shard_map/all_to_all | solution.py:380
  55.7 0.1 fusion.4.t1b
  55.9 2.0 %shard_map.187 = (bf16[8,5120]{1,0:T(8,128)(2,1)}, bf16[4,5120]{1,0:T(4,128)(2,1)}, bf16[2,5120]{1,0:T(2,128)(2,1)}) custom-call(bf16[1008,128]{1,0:T(8,128)(2,1)S(1)} %get-tuple-element.32.g1_ref, bf16[672,128]{1,0:T(8,128)(2,1)S(1)} %get-tuple-element.33.g2_ref, bf16[176,256]{1,0:T(8,128)(2,1)S(1)} %get-tuple-element.34.g3_ref, ...), custom_call_target="tpu_custom_call" | custom-call | tf_op jit(solution)/shard_map/pallas_call | solution.py:467
  57.9 11.0 %all-to-all-done = bf16[16,104,256]{2,1,0:T(8,128)(2,1)} async-done(((bf16[16,104,256]{2,1,0:T(8,128)(2,1)}), bf16[16,104,256]{2,1,0:T(8,128)(2,1)}, u32[]{:S(2)}, u32[]{:S(2)}) %all-to-all-start) | async-done | bytes 852000 | tf_op jit(solution)/shard_map/all_to_all | solution.py:380
  68.9 1.3 reduce_sum.24
  70.2 36.5 %all-gather = bf16[1664,256]{1,0:T(8,128)(2,1)S(1)} all-gather(bf16[104,256]{1,0:T(8,128)(2,1)S(1)} %reduce_sum.24), channel_id=2, replica_groups=mesh['z'=16,'x_lo'=2,'y'=4,'x_hi'=2,'core'=2] {'z'}, dimensions={0}, use_global_device_ids=true | all-gather | bytes 905216 | tf_op jit(solution)/shard_map/all_gather | solution.py:383
  106.6 0.1 reduce_sum.25
  106.7 0.1 broadcast_in_dim.10
  106.8 15.9 %all_to_all.10 = bf16[16,104,256]{2,1,0:T(8,128)(2,1)S(1)} all-to-all(bf16[16,104,256]{2,1,0:T(8,128)(2,1)S(1)} %broadcast_in_dim.10), channel_id=1, replica_groups=mesh['z'=16,'x_lo'=2,'y'=4,'x_hi'=2,'core'=2] {'x_lo','y','x_hi'}, dimensions={0} | all-to-all | bytes 1703936 | tf_op jit(solution)/shard_map/all_to_all | solution.py:386
  122.7 11.2 %collective-permute-start.7 = (bf16[1664,256]{1,0:T(8,128)(2,1)S(1)}, bf16[1664,256]{1,0:T(8,128)(2,1)S(1)}, u32[]{:S(2)}, u32[]{:S(2)}) collective-permute-start(bf16[1664,256]{1,0:T(8,128)(2,1)S(1)} %bitcast.32), channel_id=1, source_target_pairs={{0,1},{1,0},{2,3},{3,2},{4,5},{5,4},{6,7},{7,6},{8,9},{9,8},{10,11... | collective-permute-start | bytes 2555912 | tf_op jit(solution)/shard_map/ppermute | solution.py:373
  134.0 2.0 %collective-permute-done.7.got = bf16[1664,256]{1,0:T(8,128)(2,1)S(1)} collective-permute-done((bf16[1664,256]{1,0:T(8,128)(2,1)S(1)}, bf16[1664,256]{1,0:T(8,128)(2,1)S(1)}, u32[]{:S(2)}, u32[]{:S(2)}) %collective-permute-start.7) | collective-permute-done | bytes 852000 | tf_op jit(solution)/shard_map/ppermute | solution.py:373
  136.0 1.9 %shard_map.188 = (bf16[576,64]{1,0:T(8,128)(2,1)}, bf16[1152,128]{1,0:T(8,128)(2,1)}, bf16[2304,256]{1,0:T(8,128)(2,1)}, bf16[64,128]{1,0:T(8,128)(2,1)}, bf16[6...) custom-call(s32[4]{0:T(128)S(1)} %pad_add_fusion.1.place_ref, bf16[1664,256]{1,0:T(8,128)(2,1)S(1)} %bitcast.33, ...), custom_call_target="tpu_custom_call" | custom-call | tf_op jit(solution)/shard_map/pallas_call | solution.py:480
  (20 shorter events, 0.2 us)
Async XLA Ops:
  1.7 16.2 %collective-permute-start.1 = (bf16[24,5120]{1,0:T(8,128)(2,1)S(1)}, bf16[24,5120]{1,0:T(8,128)(2,1)S(1)}, u32[]{:S(2)}, u32[]{:S(2)}) collective-permute-start(bf16[24,5120]{1,0:T(8,128)(2,1)S(1)} %pad_add_fusion.refs_0_), channel_id=1, source_target_pairs={{4,0},{8,4},{12,8},{16,12},{20,16},{24,20},{28,24},{32,28},{36,32}... | collective-permute-start | bytes 737288 | tf_op jit(solution)/shard_map/ppermute | solution.py:32
  3.0 15.0 %collective-permute-start = (bf16[24,5120]{1,0:T(8,128)(2,1)S(1)}, bf16[24,5120]{1,0:T(8,128)(2,1)S(1)}, u32[]{:S(2)}, u32[]{:S(2)}) collective-permute-start(bf16[24,5120]{1,0:T(8,128)(2,1)S(1)} %pad_add_fusion.refs_0_), channel_id=1, source_target_pairs={{0,4},{4,8},{8,12},{12,16},{16,20},{20,24},{24,28},{28,32},{32,36}... | collective-permute-start | bytes 737288 | tf_op jit(solution)/shard_map/ppermute | solution.py:32
  8.6 23.0 %copy-start = (bf16[3,3,256,256]{3,2,1,0:T(8,128)(2,1)S(1)}, bf16[3,3,256,256]{3,2,1,0:T(8,128)(2,1)}, u32[]{:S(2)}) copy-start(bf16[3,3,256,256]{3,2,1,0:T(8,128)(2,1)} %param.17) | copy-start | bytes 3538948
  8.6 23.0 %copy-start.1 = (bf16[3,3,128,128]{3,2,1,0:T(8,128)(2,1)S(1)}, bf16[3,3,128,128]{3,2,1,0:T(8,128)(2,1)}, u32[]{:S(2)}) copy-start(bf16[3,3,128,128]{3,2,1,0:T(8,128)(2,1)} %param.16) | copy-start | bytes 884740
  8.7 23.0 %copy-start.2 = (bf16[512,64]{0,1:T(8,128)(2,1)S(1)}, bf16[512,64]{0,1:T(8,128)(2,1)}, u32[]{:S(2)}) copy-start(bf16[512,64]{0,1:T(8,128)(2,1)} %param.20) | copy-start | bytes 196612
  8.7 23.0 %copy-start.3 = (bf16[256,64]{0,1:T(8,128)(2,1)S(1)}, bf16[256,64]{0,1:T(8,128)(2,1)}, u32[]{:S(2)}) copy-start(bf16[256,64]{0,1:T(8,128)(2,1)} %param.19) | copy-start | bytes 98308
  8.7 23.0 %copy-start.4 = (bf16[128,64]{0,1:T(8,128)(2,1)S(1)}, bf16[128,64]{0,1:T(8,128)(2,1)}, u32[]{:S(2)}) copy-start(bf16[128,64]{0,1:T(8,128)(2,1)} %param.18) | copy-start | bytes 49156
  9.7 7.8 %collective-permute-start.3 = (bf16[3,5120]{1,0:T(4,128)(2,1)S(1)}, bf16[3,5120]{1,0:T(4,128)(2,1)S(1)}, u32[]{:S(2)}, u32[]{:S(2)}) collective-permute-start(bf16[3,5120]{1,0:T(4,128)(2,1)S(1)} %get-tuple-element.65), channel_id=1, source_target_pairs={{8,0},{12,4},{16,8},{20,12},{24,16},{28,20},{32,24},{36,28},{40,32... | collective-permute-start | bytes 92168 | tf_op jit(solution)/shard_map/ppermute | solution.py:32
  11.0 7.0 %collective-permute-start.2 = (bf16[3,5120]{1,0:T(4,128)(2,1)S(1)}, bf16[3,5120]{1,0:T(4,128)(2,1)S(1)}, u32[]{:S(2)}, u32[]{:S(2)}) collective-permute-start(bf16[3,5120]{1,0:T(4,128)(2,1)S(1)} %get-tuple-element.66), channel_id=1, source_target_pairs={{0,8},{4,12},{8,16},{12,20},{16,24},{20,28},{24,32},{28,36},{32,40... | collective-permute-start | bytes 92168 | tf_op jit(solution)/shard_map/ppermute | solution.py:32
  18.0 11.6 %collective-permute-start.5 = (bf16[78,1024]{1,0:T(8,128)(2,1)S(1)}, bf16[78,1024]{1,0:T(8,128)(2,1)S(1)}, u32[]{:S(2)}, u32[]{:S(2)}) collective-permute-start(bf16[78,1024]{1,0:T(8,128)(2,1)S(1)} %concatenate.39), channel_id=1, source_target_pairs={{1,0},{2,1},{3,2},{5,4},{6,5},{7,6},{9,8},{10,9},{11,10},{13,12},{... | collective-permute-start | bytes 479240 | tf_op jit(solution)/shard_map/ppermute | solution.py:32
  27.5 4.2 %collective-permute-start.4 = (bf16[78,1024]{1,0:T(8,128)(2,1)S(1)}, bf16[78,1024]{1,0:T(8,128)(2,1)S(1)}, u32[]{:S(2)}, u32[]{:S(2)}) collective-permute-start(bf16[78,1024]{1,0:T(8,128)(2,1)S(1)} %concatenate.38), channel_id=1, source_target_pairs={{0,1},{1,2},{2,3},{4,5},{5,6},{6,7},{8,9},{9,10},{10,11},{12,13},{... | collective-permute-start | bytes 479240 | tf_op jit(solution)/shard_map/ppermute | solution.py:32
  41.0 4.3 %collective-permute-start.6 = (bf16[1664,256]{1,0:T(8,128)(2,1)S(1)}, bf16[1664,256]{1,0:T(8,128)(2,1)S(1)}, u32[]{:S(2)}, u32[]{:S(2)}) collective-permute-start(bf16[1664,256]{1,0:T(8,128)(2,1)S(1)} %get-tuple-element.31), channel_id=1, source_target_pairs={{0,1},{1,0},{2,3},{3,2},{4,5},{5,4},{6,7},{7,6},{8,9},{9,8},{10,11... | collective-permute-start | bytes 2555912 | tf_op jit(solution)/shard_map/ppermute | solution.py:373
  46.3 22.5 %all-to-all-start = ((bf16[16,104,256]{2,1,0:T(8,128)(2,1)}), bf16[16,104,256]{2,1,0:T(8,128)(2,1)}, u32[]{:S(2)}, u32[]{:S(2)}) async-start(bf16[16,104,256]{2,1,0:T(8,128)(2,1)} %bitcast.12), calls=%async_computation | async-start | bytes 1703936 | tf_op jit(solution)/shard_map/all_to_all | solution.py:380
  122.7 13.2 %collective-permute-start.7 = (bf16[1664,256]{1,0:T(8,128)(2,1)S(1)}, bf16[1664,256]{1,0:T(8,128)(2,1)S(1)}, u32[]{:S(2)}, u32[]{:S(2)}) collective-permute-start(bf16[1664,256]{1,0:T(8,128)(2,1)S(1)} %bitcast.32), channel_id=1, source_target_pairs={{0,1},{1,0},{2,3},{3,2},{4,5},{5,4},{6,7},{7,6},{8,9},{9,8},{10,11... | collective-permute-start | bytes 2555912 | tf_op jit(solution)/shard_map/ppermute | solution.py:373

commit v4 on v3

v4 whole, which is shorter than its diff:
```python
import functools

import jax
import jax.numpy as jnp
from jax import lax
from jax.experimental import pallas as pl
from jax.experimental.pallas import tpu as pltpu
from jax.sharding import Mesh
from jax.sharding import PartitionSpec as P

FEAT_ONE = 64
FEAT_TWO = 128
FEAT_THREE = 256
FEAT_FOUR = 512

ROWS = ("z", "x_lo", "y")
COLS = ("x_hi", "core")
PLANE = ("x_lo", "y", "x_hi")
PACK_ROWS = 3328
HALF = PACK_ROWS // 2
WIDE = 5120
RIM = 512
BF = jnp.bfloat16
F32 = jnp.float32
NT = (((1,), (1,)), ((), ()))
TN = (((0,), (0,)), ((), ()))


def moved(block, axis, distance):
    count = lax.axis_size(axis)
    route = [(i, i + distance) for i in range(count) if 0 <= i + distance < count]
    return lax.ppermute(block, axis, route)


def stacked(parts, rows):
    total, at = None, 0
    for part in parts:
        padded = jnp.pad(part, ((at, rows - at - part.shape[0]), (0, 0)))
        total = padded if total is None else total + padded
        at += part.shape[0]
    return total


def halos(x1, x2, x3, x4, cot):
    last = stacked((x1[5:], cot[6:], x2[1:], x3, x4), 16)
    first = stacked((x1[:3], cot[:2], x2[:3], x3, x4), 16)
    above = moved(last, ROWS, 1)
    below = moved(first, ROWS, -1)
    parts = (x1, cot, x2, x3, x4, above[:11], below[:11])
    left = moved(stacked([p[:, -RIM:] for p in parts], 48), COLS, 1)
    right = moved(stacked([p[:, :RIM] for p in parts], 48), COLS, -1)
    return x1, cot, x2, x3, x4, above, below, left, right


def gelu_both(v):
    c = 0.7978845608028654
    sq = v * v
    t = jnp.tanh(c * v * (1.0 + 0.044715 * sq))
    half = 0.5 * (1.0 + t)
    slope = half + 0.5 * v * (1.0 - t * t) * (c * (1.0 + 3.0 * 0.044715 * sq))
    return v * half, slope


def tile(wide, at):
    return wide[:, 128 * at : 128 * (at + 1)]


def row_weights(shape, coarse_dim, row_block):
    k = lax.broadcasted_iota(jnp.int32, shape, coarse_dim)
    r = lax.broadcasted_iota(jnp.int32, shape, 1 - coarse_dim)
    two, three = k < 16, k < 24
    scale = jnp.where(two, 2, jnp.where(three, 4, 8))
    count = jnp.where(two, 4, jnp.where(three, 2, 1))
    shift = jnp.where(two, 3, jnp.where(three, 16 + 2, 24 + 1))
    total = (jnp.where(two, 512, jnp.where(three, 256, 128)) - 1).astype(F32)
    coarse = (row_block * count + k - shift).astype(F32)
    fine = (row_block * 8 + r - 4).astype(F32)
    inverse = jnp.where(two, 0.5, jnp.where(three, 0.25, 0.125)).astype(F32)
    place = jnp.clip((fine + 0.5) * inverse - 0.5, 0.0, total)
    return jnp.maximum(0.0, 1.0 - jnp.abs(place - coarse))


def forward_kernel(
    place_ref, p2, p3, p4, *refs
):
    far, refs = refs[:12], refs[12:]
    keep_ref, send_ref, g1_ref, g2_ref, g3_ref, rim_ref, up_ref, down_ref = refs[:8]
    wx1, wc, wx2, wx3, wx4, xw1, xw2, xw3, d1, d2, d3, gm1, gm2, gm3, sums, upward, downward = refs[8:25]
    near, sems = refs[25:37], refs[37]
    copies = [pltpu.make_async_copy(far[n], near[n], sems.at[n]) for n in range(12)]
    for copy in copies:
        copy.start()
    x1, cot, x2, x3, x4, above, below, left, right, t1, k2, k3 = near
    row_block = place_ref[0]
    at_left = place_ref[1] == 0
    at_right = place_ref[2] == 1
    core = place_ref[3]
    lane = lax.broadcasted_iota(jnp.int32, (1, 128), 1)
    low = lane < 64

    def lanes(a, b):
        return jnp.where(low, a, b).astype(F32)

    for ref in (wx1, wc, wx2, wx3, wx4, upward, downward):
        ref[...] = jnp.zeros_like(ref)
    for copy in copies[:10]:
        copy.wait()
    for side, to in ((None, RIM), (left, 0), (right, RIM + WIDE)):
        if side is None:
            cols = slice(to, to + WIDE)
            mid = [ref[...].astype(F32) for ref in (x1, cot, x2, x3, x4)]
            up, down = above[...].astype(F32), below[...].astype(F32)
        else:
            cols = slice(to, to + RIM)
            v = side[...].astype(F32)
            mid = [v[0:8], v[8:16], v[16:20], v[20:22], v[22:23]]
            up, down = v[23:34], v[34:45]
        wx1[1:4, cols] = up[0:3]
        wx1[4:12, cols] = mid[0]
        wx1[12:15, cols] = down[0:3]
        wc[2:4, cols] = up[3:5]
        wc[4:12, cols] = mid[1]
        wc[12:14, cols] = down[3:5]
        wx2[0:3, cols] = up[5:8]
        wx2[3:7, cols] = mid[2]
        wx2[7:10, cols] = down[5:8]
        wx3[0:2, cols] = up[8:10]
        wx3[2:4, cols] = mid[3]
        wx3[4:6, cols] = down[8:10]
        wx4[0:1, cols] = up[10:11]
        wx4[1:2, cols] = mid[4]
        wx4[2:3, cols] = down[10:11]

    for f in range(-1, 41):
        at = 8 + 16 * (f + 1)
        xw1[at : at + 16, 0:128] = tile(wx1, 4 + f)
        xw1[at : at + 16, 128:256] = jnp.where(low, tile(wx1, 5 + f), tile(wx1, 3 + f))
    xw1[0:8, :] = jnp.zeros((8, 256), F32)
    xw1[680:688, :] = jnp.zeros((8, 256), F32)
    pre1 = xw1[8:680, 0:128]
    for i in range(3):
        pre1 = pre1 + jnp.dot(xw1[7 + i : 679 + i, :].astype(BF), t1[i], preferred_element_type=F32)
    y1, slope = gelu_both(pre1)
    y1 = y1.astype(BF).astype(F32)
    d1[...] = slope

    copies[10].wait()
    for j in range(3):
        for c in range(-2, 42):
            at = 8 + 16 * (c + 2)
            xw2[at : at + 16, 128 * j : 128 * j + 128] = tile(wx2, 3 + c + j)
    xw2[0:8, :] = jnp.zeros((8, 384), F32)
    xw2[712:720, :] = jnp.zeros((8, 384), F32)
    pre2 = xw2[8:712, 128:256]
    for i in range(3):
        pre2 = pre2 + jnp.dot(xw2[7 + i : 711 + i, :].astype(BF), k2[i], preferred_element_type=F32)
    y2, slope = gelu_both(pre2)
    y2 = y2.astype(BF)
    d2[...] = slope

    copies[11].wait()
    for j in range(3):
        for c in range(-1, 21):
            at = 8 + 8 * (c + 1)
            first = RIM + 256 * (c + j - 1)
            xw3[at : at + 8, 256 * j : 256 * j + 256] = wx3[:, first : first + 256]
    xw3[0:8, :] = jnp.zeros((8, 768), F32)
    xw3[184:192, :] = jnp.zeros((8, 768), F32)
    pre3 = xw3[8:184, 256:512]
    for i in range(3):
        pre3 = pre3 + jnp.dot(xw3[7 + i : 183 + i, :].astype(BF), k3[i], preferred_element_type=F32)
    y3, slope = gelu_both(pre3)
    y3 = y3.astype(BF)
    d3[...] = slope

    y4 = jnp.concatenate([wx4[:, 512 * c : 512 * c + 512] for c in range(12)], axis=0).astype(BF)

    weights = row_weights((16, 32), 1, row_block).astype(BF)
    rows_up = []
    for y, p, rim, rows, wlo in ((y2, p2, 2, 16, 0), (y3, p3, 1, 8, 16), (y4, p4, 1, 8, 24)):
        twice = jnp.concatenate([p[...], p[...]], axis=0)
        coarse = lax.dot_general(y, twice, NT, preferred_element_type=F32).astype(BF).astype(F32)
        cols = [coarse[rows * n : rows * (n + 1)] for n in range(coarse.shape[0] // rows)]
        end = len(cols) - rim
        cols[rim - 1] = jnp.where(at_left, cols[rim], cols[rim - 1])
        cols[end] = jnp.where(at_right, cols[end - 1], cols[end])
        flat = jnp.concatenate(cols, axis=1).astype(BF)
        rows_up.append(jnp.dot(weights[:, wlo : wlo + rows], flat, preferred_element_type=F32))
    up2, up3, up4 = rows_up

    gates = []
    for f in range(-1, 41):
        k = f + 2
        merged = y1[16 * (f + 1) : 16 * (f + 2)]
        merged = merged + 0.75 * tile(up2, k) + 0.25 * jnp.where(low, tile(up2, k - 1), tile(up2, k + 1))
        k, h = f // 2 + 1, f % 2
        if h == 0:
            merged = merged + lanes(0.375, 0.125) * tile(up3, k - 1) + lanes(0.625, 0.875) * tile(up3, k)
        else:
            merged = merged + lanes(0.875, 0.625) * tile(up3, k) + lanes(0.125, 0.375) * tile(up3, k + 1)
        k, h = f // 4 + 1, f % 4
        p_low, p_high = (2 * h + 0.5) / 8 - 0.5, (2 * h + 1.5) / 8 - 0.5
        other = k - 1 if h < 2 else k + 1
        merged = merged + lanes(1 - abs(p_low), 1 - abs(p_high)) * tile(up4, k)
        merged = merged + lanes(abs(p_low), abs(p_high)) * tile(up4, other)
        slope = gelu_both(merged)[1]
        gate = (slope * tile(wc, 4 + f)).astype(BF).astype(F32)
        gates.append(gate)
        if 0 <= f < 40:
            g = (d1[16 * (f + 1) : 16 * (f + 2)] * gate).astype(BF).astype(F32)
            row = lax.broadcasted_iota(jnp.int32, (16, 1), 0)
            gm1[8 + 16 * f : 24 + 16 * f, :] = jnp.where((row >= 4) & (row < 12), g, 0.0)
            cols = slice(128 * f, 128 * (f + 1))
            g1_ref[:, cols] = g[4:12].astype(BF)
            upward[0:1, cols] = g[4:5]
            downward[0:1, cols] = g[11:12]
    gm1[0:8, :] = jnp.zeros((8, 128), F32)
    gm1[648:656, :] = jnp.zeros((8, 128), F32)

    flat = jnp.concatenate(gates, axis=1).astype(BF)
    weights_back = row_weights((32, 16), 0, row_block)
    k = lax.broadcasted_iota(jnp.int32, (32, 16), 0)
    r = lax.broadcasted_iota(jnp.int32, (32, 16), 1)
    weights_back = jnp.where((k < 24) | ((r >= 4) & (r < 12)), weights_back, 0.0).astype(BF)
    down = jnp.dot(weights_back, flat, preferred_element_type=F32)
    down2, down3, down4 = down[0:16], down[16:24], down[24:32]

    def folded(v):
        return v + pltpu.roll(v, 64, 1)

    cg2 = []
    for c in range(40):
        v = 0.75 * tile(down2, c + 1) + 0.25 * jnp.where(low, tile(down2, c + 2), tile(down2, c))
        if c == 0:
            v = v + jnp.where(at_left, lanes(0.25, 0.0) * tile(down2, 1), 0.0)
        if c == 39:
            v = v + jnp.where(at_right, lanes(0.0, 0.25) * tile(down2, 40), 0.0)
        cg2.append(folded(v))
    cg3 = []
    for c in range(20):
        at = 2 * c
        v = lanes(0.125, 0.375) * tile(down3, at) + lanes(0.625, 0.875) * tile(down3, at + 1)
        v = v + lanes(0.875, 0.625) * tile(down3, at + 2) + lanes(0.375, 0.125) * tile(down3, at + 3)
        if c == 0:
            v = v + jnp.where(at_left, lanes(0.375, 0.125) * tile(down3, 1), 0.0)
        if c == 19:
            v = v + jnp.where(at_right, lanes(0.125, 0.375) * tile(down3, 40), 0.0)
        cg3.append(folded(v))
    cg4 = []
    for c in range(-1, 11):
        v = jnp.zeros((8, 128), F32)
        for n in range(8):
            a, b = (2 * n + 0.5) / 8, (2 * n + 1.5) / 8
            a, b = (a, b) if n < 4 else (2 - a, 2 - b)
            pair = 4 * c - 2 + n
            if 0 <= pair < 40:
                v = v + lanes(a, b) * tile(down4, pair + 1)
        cg4.append(folded(v))
    cg4[1] = cg4[1] + jnp.where(at_left, cg4[0], 0.0)
    cg4[-2] = cg4[-2] + jnp.where(at_right, cg4[-1], 0.0)
    cg4[0] = jnp.where(at_left, 0.0, cg4[0])
    cg4[-1] = jnp.where(at_right, 0.0, cg4[-1])
    for n in range(12):
        cols = slice(128 * n, 128 * (n + 1))
        upward[3:4, cols] = cg4[n][0:1]
        rim_ref[0:1, cols] = cg4[n][1:2]
        downward[3:4, cols] = cg4[n][2:3]

    flat2 = jnp.concatenate(cg2, axis=0).astype(BF).astype(F32)
    flat3 = jnp.concatenate(cg3, axis=0).astype(BF).astype(F32)
    flat4 = jnp.concatenate(cg4, axis=0).astype(BF).astype(F32)
    back2 = jnp.dot(flat2[:, 0:64].astype(BF), p2[...], preferred_element_type=F32)
    back3 = jnp.dot(flat3[:, 0:64].astype(BF), p3[...], preferred_element_type=F32)
    g2 = (d2[32:672, :] * back2).astype(BF).astype(F32)
    g3 = (d3[8:168, :] * back3).astype(BF).astype(F32)

    row2 = lax.broadcasted_iota(jnp.int32, (640, 1), 0) % 16
    own2 = (row2 >= 3) & (row2 < 7)
    row3 = lax.broadcasted_iota(jnp.int32, (160, 1), 0) % 8
    own3 = (row3 >= 2) & (row3 < 4)
    gm2[0:8, :] = jnp.zeros((8, 128), F32)
    gm2[8:648, :] = jnp.where(own2, g2, 0.0)
    gm2[648:656, :] = jnp.zeros((8, 128), F32)
    gm3[0:8, :] = jnp.zeros((8, 256), F32)
    gm3[8:168, :] = jnp.where(own3, g3, 0.0)
    gm3[168:176, :] = jnp.zeros((8, 256), F32)
    for c in range(40):
        at, cols = 8 + 16 * c + 3, slice(128 * c, 128 * (c + 1))
        g2_ref[:, cols] = gm2[at : at + 4, :].astype(BF)
        upward[1:2, cols] = gm2[at : at + 1, :]
        downward[1:2, cols] = gm2[at + 3 : at + 4, :]
    for c in range(20):
        at, cols = 8 + 8 * c + 2, slice(256 * c, 256 * (c + 1))
        g3_ref[:, cols] = gm3[at : at + 2, :].astype(BF)
        upward[2:3, cols] = gm3[at : at + 1, :]
        downward[2:3, cols] = gm3[at + 1 : at + 2, :]
    up_ref[...] = upward[...].astype(BF)
    down_ref[...] = downward[...].astype(BF)

    cells = 327680
    x = xw3[16:176, :].astype(BF)
    shifted = jnp.concatenate([gm3[9 - i : 169 - i, :] for i in range(3)], axis=1).astype(BF)
    z = lax.dot_general(x, shifted, TN, preferred_element_type=F32) * (cells // 16) ** -0.5
    for i in range(3):
        sums[768 * i : 768 * (i + 1), :] = z[:, 256 * i : 256 * (i + 1)]
    x = xw2[40:680, :].astype(BF)
    shifted = jnp.concatenate([gm2[9 - i : 649 - i, :] for i in range(3)], axis=1).astype(BF)
    z = lax.dot_general(x, shifted, TN, preferred_element_type=F32) * (cells // 4) ** -0.5
    base = 2304
    sums[base : base + 384, 0:128] = z[:, 0:128]
    sums[base + 384 : base + 576, 0:128] = z[0:192, 128:256]
    sums[base : base + 192, 128:256] = z[192:384, 128:256]
    sums[base + 192 : base + 576, 128:256] = z[:, 256:384]
    x = xw1[24:664, :].astype(BF)
    shifted = jnp.concatenate([gm1[9 - i : 649 - i, :] for i in range(3)], axis=1).astype(BF)
    z = lax.dot_general(x, shifted, TN, preferred_element_type=F32) * cells**-0.5
    window = (192, 0, 64, 128)
    blocks = []
    for i in range(3):
        zi = z[:, 128 * i : 128 * (i + 1)]
        for j in range(3):
            a, b = window[j], window[j + 1]
            blocks.append(zi[a : a + 64] + pltpu.roll(zi[b : b + 64], 64, 1))
    blocks.append(jnp.zeros((64, 128), F32))
    pairs = [jnp.where(low, blocks[n], pltpu.roll(blocks[n + 1], 64, 1)) for n in range(0, 10, 2)]
    y2_own, y3_own = y2[32:672], y3.astype(F32)[8:168].astype(BF)
    for y, flat, mask, branch in (
        (y2_own, flat2, own2, 1),
        (y3_own, flat3, own3, 2),
        (y4, flat4, None, 3),
    ):
        masked = (flat if mask is None else jnp.where(mask, flat, 0.0)).astype(BF)
        z = lax.dot_general(masked, y, TN, preferred_element_type=F32) * (cells // 4**branch) ** -0.5
        pairs += [z[0:64, 128 * n : 128 * (n + 1)] for n in range(z.shape[1] // 128)]
    base = 2880
    for n in range(12):
        at, side = base + 64 * (n // 2), 128 * (n % 2)
        sums[at : at + 64, side : side + 128] = pairs[n]
    sums[3264:3328, :] = jnp.zeros((64, 256), F32)
    keep_ref[...] = sums[pl.ds(pl.multiple_of(core * HALF, 64), HALF), :].astype(BF)
    send_ref[...] = sums[pl.ds(pl.multiple_of((1 - core) * HALF, 64), HALF), :].astype(BF)


def rims_kernel(g1_ref, g2_ref, g3_ref, rim_ref, above_ref, below_ref, left_ref, right_ref, out):
    g1, g2, g3, above, below = (ref[...].astype(F32) for ref in (g1_ref, g2_ref, g3_ref, above_ref, below_ref))
    rim = rim_ref[...] + above[3:4, 0:1536] + below[3:4, 0:1536]
    for ref, one, three, four in ((left_ref, 0, 0, 0), (right_ref, WIDE - 128, WIDE - 256, 1408)):
        ones, threes = slice(one, one + 128), slice(three, three + 256)
        out[...] = jnp.zeros_like(out)
        out[0:1, 0:128] = above[0:1, ones]
        out[1:9, 0:128] = g1[:, ones]
        out[9:10, 0:128] = below[0:1, ones]
        out[10:11, 0:128] = above[1:2, ones]
        out[11:15, 0:128] = g2[:, ones]
        out[15:16, 0:128] = below[1:2, ones]
        out[16:17, :] = above[2:3, threes]
        out[17:19, :] = g3[:, threes]
        out[19:20, :] = below[2:3, threes]
        out[20:21, 0:128] = rim[:, four : four + 128]
        ref[...] = out[...].astype(BF)


def backward_kernel(
    g1_ref, g2_ref, g3_ref, rim_ref, above_ref, below_ref, left_ref, right_ref, t1b, k2, k3, p4,
    gf1_ref, gf2_ref, gf3_ref, gf4_ref, wide1, wide2, wide3, xw1, xw2, xw3, out2, out3,
):
    low = lax.broadcasted_iota(jnp.int32, (1, 128), 1) < 64
    for ref, n in ((xw1, 640), (xw2, 320), (xw3, 160)):
        ref[0:8, :] = jnp.zeros((8, ref.shape[1]), F32)
        ref[8 + n : 16 + n, :] = jnp.zeros((8, ref.shape[1]), F32)
    above, below, left, right = (ref[...].astype(F32) for ref in (above_ref, below_ref, left_ref, right_ref))
    for n, (wide, g_ref, top, rows, start, step) in enumerate(
        ((wide1, g1_ref, 3, 8, 0, 128), (wide2, g2_ref, 0, 4, 10, 128), (wide3, g3_ref, 0, 2, 16, 256))
    ):
        wide[...] = jnp.zeros_like(wide)
        mid, end = slice(step, step + WIDE), step + WIDE
        wide[top : top + 1, mid] = above[n : n + 1]
        wide[top + 1 : top + 1 + rows, mid] = g_ref[...].astype(F32)
        wide[top + 1 + rows : top + 2 + rows, mid] = below[n : n + 1]
        wide[top : top + 2 + rows, 0:step] = left[start : start + 2 + rows, 0:step]
        wide[top : top + 2 + rows, end : end + step] = right[start : start + 2 + rows, 0:step]

    for f in range(40):
        at = 8 + 16 * f
        xw1[at : at + 16, 0:128] = tile(wide1, f + 1)
        xw1[at : at + 16, 128:256] = jnp.where(low, tile(wide1, f + 2), tile(wide1, f))
    total = xw1[8:648, 0:128]
    for i in range(3):
        total = total + lax.dot_general(
            xw1[9 - i : 649 - i, :].astype(BF), t1b[i], NT, preferred_element_type=F32
        )
    for f in range(40):
        gf1_ref[:, 128 * f : 128 * (f + 1)] = total[16 * f + 4 : 16 * f + 12].astype(BF)

    for j in range(3):
        for c in range(40):
            xw2[8 + 8 * c : 16 + 8 * c, 128 * j : 128 * j + 128] = tile(wide2, c + 2 - j)
    total = xw2[8:328, 128:256]
    for i in range(3):
        kernel = jnp.concatenate([k2[i, 128 * j : 128 * j + 128, :] for j in range(3)], axis=1)
        total = total + lax.dot_general(
            xw2[9 - i : 329 - i, :].astype(BF), kernel, NT, preferred_element_type=F32
        )
    out2[...] = total
    for c in range(40):
        gf2_ref[:, 128 * c : 128 * (c + 1)] = out2[8 * c + 1 : 8 * c + 5, :].astype(BF)

    for j in range(3):
        for c in range(20):
            first = 256 * (c + 2 - j)
            xw3[8 + 8 * c : 16 + 8 * c, 256 * j : 256 * j + 256] = wide3[:, first : first + 256]
    total = xw3[8:168, 256:512]
    for i in range(3):
        kernel = jnp.concatenate([k3[i, 256 * j : 256 * j + 256, :] for j in range(3)], axis=1)
        total = total + lax.dot_general(
            xw3[9 - i : 169 - i, :].astype(BF), kernel, NT, preferred_element_type=F32
        )
    out3[...] = total
    for c in range(20):
        gf3_ref[:, 256 * c : 256 * (c + 1)] = out3[8 * c + 1 : 8 * c + 3, :].astype(BF)

    rim = rim_ref[...] + above[3:4, 0:1536] + below[3:4, 0:1536]
    for c in range(10):
        cg = rim[:, 128 * (c + 1) : 128 * (c + 2)]
        if c == 0:
            cg = cg + left[20:21, 0:128]
        if c == 9:
            cg = cg + right[20:21, 0:128]
        cg = jnp.broadcast_to(cg[:, 0:64], (8, 64)).astype(BF)
        back = jnp.dot(cg, p4[...], preferred_element_type=F32)
        gf4_ref[0:1, 512 * c : 512 * c + 512] = back[0:1].astype(BF)


def swapped(block, axis, flip):
    return lax.ppermute(block, axis, [(i, i ^ flip) for i in range(lax.axis_size(axis))])


def unpack_kernel(place_ref, mine, got, k1_ref, k2_ref, k3_ref, p2_ref, p3_ref, p4_ref, whole):
    core = place_ref[3]
    whole[pl.ds(pl.multiple_of(core * HALF, 64), HALF), :] = mine[...]
    whole[pl.ds(pl.multiple_of((1 - core) * HALF, 64), HALF), :] = got[...]
    k3_ref[...] = whole[0:2304, :]
    k2_ref[0:576, :] = whole[2304:2880, 0:128]
    k2_ref[576:1152, :] = whole[2304:2880, 128:256]
    for n in range(9):
        at, side = 2880 + 64 * (n // 4), 64 * (n % 4)
        k1_ref[64 * n : 64 * (n + 1), :] = whole[at : at + 64, side : side + 64]
    n = 5
    for ref, count in ((p2_ref, 1), (p3_ref, 2), (p4_ref, 4)):
        for m in range(count):
            at, side = 2880 + 64 * (n // 2), 128 * (n % 2)
            ref[:, 128 * m : 128 * (m + 1)] = whole[at : at + 64, side : side + 128]
            n += 1


def call(kernel, out_shapes, scratch, count, scalars=0, far=0):
    vmem = pl.BlockSpec(memory_space=pltpu.VMEM)
    smem = pl.BlockSpec(memory_space=pltpu.SMEM)
    return pl.pallas_call(
        kernel,
        out_shape=[jax.ShapeDtypeStruct(shape, dtype) for shape, dtype in out_shapes],
        in_specs=[smem] * scalars + [vmem] * count + [pl.BlockSpec(memory_space=pl.ANY)] * far,
        out_specs=[vmem] * len(out_shapes),
        scratch_shapes=[pltpu.VMEM(shape, dtype) for shape, dtype in scratch]
        + ([pltpu.SemaphoreType.DMA((far,))] if far else []),
        compiler_params=pltpu.CompilerParams(vmem_limit_bytes=48 * 1024 * 1024),
    )


def pair_weights(kernel_one):
    none = jnp.zeros((3, FEAT_ONE, FEAT_ONE), BF)
    tap = lambda j: kernel_one[:, j] if 0 <= j < 3 else none
    windows = (1, 2, 3, 0)
    ahead = jnp.concatenate(
        [jnp.concatenate([tap(w - e) for w in windows], axis=1) for e in range(2)], axis=2
    )
    back = jnp.concatenate(
        [jnp.concatenate([tap(e - w + 2) for e in range(2)], axis=1) for w in windows], axis=2
    )
    return ahead, back


def local_part(x1, x2, x3, x4, kernel_one, kernel_two, kernel_three, p2, p3, p4, cot):
    place = jnp.stack(
        [
            lax.axis_index(ROWS),
            lax.axis_index(COLS),
            (lax.axis_index(COLS) == lax.axis_size(COLS) - 1).astype(jnp.int32),
            lax.axis_index("core"),
        ]
    ).astype(jnp.int32)
    ahead, back = pair_weights(kernel_one)
    k2 = kernel_two.reshape(3, 384, 128)
    k3 = kernel_three.reshape(3, 768, 256)
    fars = halos(x1, x2, x3, x4, cot) + (ahead, k2, k3)
    total = RIM + WIDE + RIM
    keep, send, g1, g2, g3, rim, up, down = call(
        forward_kernel,
        [
            ((HALF, 256), BF), ((HALF, 256), BF),
            ((8, WIDE), BF), ((4, WIDE), BF), ((2, WIDE), BF), ((1, 1536), F32),
            ((8, WIDE), BF), ((8, WIDE), BF),
        ],
        [
            ((16, total), F32), ((16, total), F32), ((16, total), F32), ((8, total), F32), ((8, total), F32),
            ((688, 256), F32), ((720, 384), F32), ((192, 768), F32),
            ((672, 128), F32), ((704, 128), F32), ((176, 256), F32),
            ((656, 128), F32), ((656, 128), F32), ((176, 256), F32),
            ((PACK_ROWS, 256), F32), ((8, WIDE), F32), ((8, WIDE), F32),
        ]
        + [(far.shape, BF) for far in fars],
        3,
        1,
        12,
    )(place, p2.T, p3.T, p4.T, *fars)
    return place, keep, send, (g1, g2, g3, rim), up, down, (back, k2, k3, p4.T)


def from_beside(grads, above, below):
    left, right = call(
        rims_kernel, [((32, 256), BF), ((32, 256), BF)], [((32, 256), F32)], 6
    )(*grads, above, below)
    return moved(right, COLS, 1), moved(left, COLS, -1)


def input_grads(grads, above, below, left, right, weights):
    return call(
        backward_kernel,
        [((8, WIDE), BF), ((4, WIDE), BF), ((2, WIDE), BF), ((1, WIDE), BF)],
        [
            ((16, 42 * 128), F32), ((8, 42 * 128), F32), ((8, 22 * 256), F32),
            ((656, 256), F32), ((336, 384), F32), ((176, 768), F32),
            ((320, 128), F32), ((160, 256), F32),
        ],
        12,
    )(*grads, above, below, left, right, *weights)


def unpacked(place, mine, got):
    outs = call(
        unpack_kernel,
        [((576, 64), BF), ((1152, 128), BF), ((2304, 256), BF), ((64, 128), BF), ((64, 256), BF), ((64, 512), BF)],
        [((PACK_ROWS, 256), BF)],
        2,
        1,
    )(place, mine, got)
    return (
        outs[0].reshape(3, 3, 64, 64), outs[1].reshape(3, 3, 128, 128), outs[2].reshape(3, 3, 256, 256),
        outs[3].T, outs[4].T, outs[5].T,
    )


def on_device(*args):
    place, keep, send, grads, up, down, weights = local_part(*args)
    part = (keep.astype(F32) + swapped(send, "core", 1).astype(F32)).astype(BF)
    part, up, down = lax.optimization_barrier((part, up, down))

    pieces = lax.all_to_all(part.reshape(16, -1, part.shape[1]), PLANE, 0, 0)
    above, below = moved(down, ROWS, 1), moved(up, ROWS, -1)
    pieces, above, below = lax.optimization_barrier((pieces, above, below))
    part = jnp.sum(pieces.astype(F32), axis=0).astype(BF)

    pieces = lax.all_gather(part, "z")
    part = jnp.sum(pieces.astype(F32), axis=0).astype(BF)
    part, above, below = lax.optimization_barrier((part, above, below))

    pieces = jnp.broadcast_to(part[None], (16,) + part.shape)
    mine = lax.all_to_all(pieces, PLANE, 0, 0).reshape(keep.shape)
    left, right = from_beside(grads, above, below)
    outs = input_grads(grads, above, below, left, right, weights)
    mine, outs = lax.optimization_barrier((mine, outs))
    return tuple(outs) + unpacked(place, mine, swapped(mine, "core", 1))


def solution(mesh):
    mesh = Mesh(mesh.devices.reshape(16, 2, 4, 2, 2), ("z", "x_lo", "y", "x_hi", "core"))
    split = P(ROWS, COLS)
    in_specs = (split,) * 4 + (P(),) * 6 + (split,)
    out_specs = (split,) * 4 + (P(),) * 6
    return jax.shard_map(on_device, mesh=mesh, in_specs=in_specs, out_specs=out_specs, check_vma=False)
```

time: 139 us -> 134 us (0.964)
  blocking collectives: 52.4 us -> 39.3 us
  starting transfers between devices: 46.8 us -> 52.6 us
  local copies, waits for them, and re-layouts: 2.02 us -> 5.37 us
  waiting for transfers between devices: 17.8 us -> 21 us
  Pallas kernels: 13.1 us -> 11 us
  other arithmetic: 4.89 us -> 2.79 us
    all_to_all x1 -> x0, blocking collectives: 15.9 us -> none  [summed_over_devices(): part = lax.all_to_all(pieces, PLANE, 0, 0).reshape(-1, width)]
    ppermute x6 -> x8, waiting for transfers between devices: 2.45 us -> 15.9 us  [moved(): return lax.ppermute(block, axis, route)]
    ppermute x6 -> x8, starting transfers between devices: 24.2 us -> 36.3 us  [moved(): return lax.ppermute(block, axis, route)]
    all_to_all x1 -> x2, waiting for transfers between devices: 11 us -> 0.38 us  [the longest x1 0.38 us: on_device(): pieces = lax.all_to_all(part.reshape(16, -1, part.shape[1]), PLANE, 0, 0)]
    ppermute x2, starting transfers between devices: 13.2 us -> 3.83 us  [swapped(): lax.ppermute(block, axis, [(i, i ^ flip) for i in range(lax.axis_size(axi...]
    slice x6 -> x8, local copies, waits for them, and re-layouts: 0.98 us -> 4.3 us  [the longest x6 2.18 us: halos(): right = moved(stacked([p[:, :RIM] for p in parts], 48), COLS, -1)]
    all_to_all x1 -> x2, starting transfers between devices: 9.39 us -> 12.5 us  [the longest x1 7.54 us: on_device(): pieces = lax.all_to_all(part.reshape(16, -1, part.shape[1]), PLANE, 0, 0)]
    all_gather x1, blocking collectives: 36.5 us -> 39.3 us  [on_device(): pieces = lax.all_gather(part, 'z')]
  transfers between devices with their start and end apart: 9 -> 12, of which waited for: 5 -> 7; matrix products, arithmetic and copies ran while one was open for 2% -> 2% of each run, Pallas kernels for 1% -> 1%
where the time goes in v4:
time: 134 us; the launch traced here: 133 us
  starting transfers between devices  52.6 us (39%)
  blocking collectives  39.3 us (29%)
  waiting for transfers between devices  21 us (16%)
  Pallas kernels  11 us (8%)
  local copies, waits for them, and re-layouts  5.37 us (4%)
  other arithmetic  2.79 us (2%)
    all_gather x1, blocking collectives, on_device(): pieces = lax.all_gather(part, 'z')  39.3 us
    ppermute x8, starting transfers between devices, moved(): return lax.ppermute(block, axis, route)  36.3 us
    ppermute x8, waiting for transfers between devices, moved(): return lax.ppermute(block, axis, route)  15.9 us
    all_to_all x1, starting transfers between devices, on_device(): pieces = lax.all_to_all(part.reshape(16, -1, part.shape[1]), PLANE, 0, 0)  7.54 us
    pallas_call x1, Pallas kernels, local_part(): call(forward_kernel, [((HALF, 256), BF), ((HALF, 256), BF), ((8, WIDE), B...  7.18 us
    all_to_all x1, starting transfers between devices, on_device(): mine = lax.all_to_all(pieces, PLANE, 0, 0).reshape(keep.shape)  4.92 us
    ppermute x2, waiting for transfers between devices, swapped(): lax.ppermute(block, axis, [(i, i ^ flip) for i in range(lax.axis_size(axi...  4.69 us
    ppermute x2, starting transfers between devices, swapped(): lax.ppermute(block, axis, [(i, i ^ flip) for i in range(lax.axis_size(axi...  3.83 us
  transfers between devices with their start and end apart: 12, of which 7 were waited for; matrix products, arithmetic and copies ran while one was open for 2% of the time, Pallas kernels for 1%

profile of v4, /device:TPU:1, one launch (start us, length us, event | category | flops | bytes accessed | tf_op | source)
XLA Modules:
  0.0 133.0 jit_solution(399180909835684016)
XLA Ops:
  0.8 1.1 fusion.10
  1.9 1.0 fusion.9
  2.9 1.0 pad_add_fusion
  3.9 1.3 collective-permute-start.1
  5.2 4.7 %collective-permute-start = (bf16[16,5120]{1,0:T(8,128)(2,1)S(1)}, bf16[16,5120]{1,0:T(8,128)(2,1)S(1)}, u32[]{:S(2)}, u32[]{:S(2)}) collective-permute-start(bf16[16,5120]{1,0:T(8,128)(2,1)S(1)} %get-tuple-element.96), channel_id=1, source_target_pairs={{0,4},{4,8},{8,12},{12,16},{16,20},{20,24},{24,28},{28,32},{32,36}... | collective-permute-start | bytes 491528 | tf_op jit(solution)/shard_map/ppermute | solution.py:32
  9.9 0.7 fusion.13
  10.6 0.7 fusion.11
  11.3 0.7 fusion.7
  12.4 6.6 %collective-permute-start.2 = (bf16[48,512]{1,0:T(8,128)(2,1)S(1)}, bf16[48,512]{1,0:T(8,128)(2,1)S(1)}, u32[]{:S(2)}, u32[]{:S(2)}) collective-permute-start(bf16[48,512]{1,0:T(8,128)(2,1)S(1)} %pad_add_fusion.5), channel_id=1, source_target_pairs={{0,1},{1,2},{2,3},{4,5},{5,6},{6,7},{8,9},{9,10},{10,11},{12,13},{... | collective-permute-start | bytes 147464 | tf_op jit(solution)/shard_map/ppermute | solution.py:32
  19.0 3.7 %collective-permute-start.3 = (bf16[48,512]{1,0:T(8,128)(2,1)S(1)}, bf16[48,512]{1,0:T(8,128)(2,1)S(1)}, u32[]{:S(2)}, u32[]{:S(2)}) collective-permute-start(bf16[48,512]{1,0:T(8,128)(2,1)S(1)} %pad_add_fusion.4), channel_id=1, source_target_pairs={{1,0},{2,1},{3,2},{5,4},{6,5},{7,6},{9,8},{10,9},{11,10},{13,12},{... | collective-permute-start | bytes 147464 | tf_op jit(solution)/shard_map/ppermute | solution.py:32
  22.8 3.1 %collective-permute-done.3.refs_8_ = bf16[48,512]{1,0:T(8,128)(2,1)S(1)} collective-permute-done((bf16[48,512]{1,0:T(8,128)(2,1)S(1)}, bf16[48,512]{1,0:T(8,128)(2,1)S(1)}, u32[]{:S(2)}, u32[]{:S(2)}) %collective-permute-start.3) | collective-permute-done | bytes 49184 | tf_op jit(solution)/shard_map/ppermute | solution.py:32
  26.0 7.2 %shard_map.186 = (bf16[1664,256]{1,0:T(8,128)(2,1)S(1)}, bf16[1664,256]{1,0:T(8,128)(2,1)S(1)}, bf16[8,5120]{1,0:T(8,128)(2,1)S(1)}, bf16[4,5120]{1,0:T(4,128)(2...) custom-call(s32[4]{0:T(128)S(1)} %pad_add_fusion.6.place_ref, ...), custom_call_target="tpu_custom_call" | custom-call | tf_op jit(solution)/shard_map/pallas_call | solution.py:497
  33.2 1.9 %collective-permute-start.4 = (bf16[1664,256]{1,0:T(8,128)(2,1)S(1)}, bf16[1664,256]{1,0:T(8,128)(2,1)S(1)}, u32[]{:S(2)}, u32[]{:S(2)}) collective-permute-start(bf16[1664,256]{1,0:T(8,128)(2,1)S(1)} %get-tuple-element.45), channel_id=1, source_target_pairs={{0,1},{1,0},{2,3},{3,2},{4,5},{5,4},{6,7},{7,6},{8,9},{9,8},{10,11... | collective-permute-start | bytes 2555912 | tf_op jit(solution)/shard_map/ppermute | solution.py:435
  35.2 2.3 %collective-permute-done.4 = bf16[1664,256]{1,0:T(8,128)(2,1)S(1)} collective-permute-done((bf16[1664,256]{1,0:T(8,128)(2,1)S(1)}, bf16[1664,256]{1,0:T(8,128)(2,1)S(1)}, u32[]{:S(2)}, u32[]{:S(2)}) %collective-permute-start.4) | collective-permute-done | bytes 852000 | tf_op jit(solution)/shard_map/ppermute | solution.py:435
  37.5 1.1 add_convert_fusion
  38.6 7.5 %all-to-all-start = ((bf16[16,104,256]{2,1,0:T(8,128)(2,1)}), bf16[16,104,256]{2,1,0:T(8,128)(2,1)S(1)}, u32[]{:S(2)}, u32[]{:S(2)}) async-start(bf16[16,104,256]{2,1,0:T(8,128)(2,1)} %bitcast.12), calls=%async_computation | async-start | bytes 1703936 | tf_op jit(solution)/shard_map/all_to_all | solution.py:558
  46.2 3.3 %collective-permute-start.5 = (bf16[8,5120]{1,0:T(8,128)(2,1)S(1)}, bf16[8,5120]{1,0:T(8,128)(2,1)S(1)}, u32[]{:S(2)}, u32[]{:S(2)}) collective-permute-start(bf16[8,5120]{1,0:T(8,128)(2,1)S(1)} %get-tuple-element.49), channel_id=1, source_target_pairs={{0,4},{4,8},{8,12},{12,16},{16,20},{20,24},{24,28},{28,32},{32,36}... | collective-permute-start | bytes 245768 | tf_op jit(solution)/shard_map/ppermute | solution.py:32
  49.5 1.3 collective-permute-start.6
  50.8 7.4 %collective-permute-done.5.above_ref = bf16[8,5120]{1,0:T(8,128)(2,1)S(1)} collective-permute-done((bf16[8,5120]{1,0:T(8,128)(2,1)S(1)}, bf16[8,5120]{1,0:T(8,128)(2,1)S(1)}, u32[]{:S(2)}, u32[]{:S(2)}) %collective-permute-start.5) | collective-permute-done | bytes 81952 | tf_op jit(solution)/shard_map/ppermute | solution.py:32
  58.1 0.9 collective-permute-done.6.below_ref
  59.1 0.4 all-to-all-done
  59.6 39.3 %all-gather = bf16[1664,256]{1,0:T(8,128)(2,1)S(1)} all-gather(bf16[104,256]{1,0:T(8,128)(2,1)S(1)} %reduce_sum.24), channel_id=2, replica_groups=mesh['z'=16,'x_lo'=2,'y'=4,'x_hi'=2,'core'=2] {'z'}, dimensions={0}, use_global_device_ids=true | all-gather | bytes 905216 | tf_op jit(solution)/shard_map/all_gather | solution.py:563
  99.0 1.0 broadcast_in_dim.10
  99.9 4.9 %all-to-all-start.1 = ((bf16[16,104,256]{2,1,0:T(8,128)(2,1)}), bf16[16,104,256]{2,1,0:T(8,128)(2,1)S(1)}, u32[]{:S(2)}, u32[]{:S(2)}) async-start(bf16[16,104,256]{2,1,0:T(8,128)(2,1)} %broadcast_in_dim.10), calls=%async_computation.1 | async-start | bytes 1703936 | tf_op jit(solution)/shard_map/all_to_all | solution.py:568
  104.9 13.5 %collective-permute-start.7 = (bf16[32,256]{1,0:T(8,128)(2,1)S(1)}, bf16[32,256]{1,0:T(8,128)(2,1)S(1)}, u32[]{:S(2)}, u32[]{:S(2)}) collective-permute-start(bf16[32,256]{1,0:T(8,128)(2,1)S(1)} %get-tuple-element.61), channel_id=1, source_target_pairs={{0,1},{1,2},{2,3},{4,5},{5,6},{6,7},{8,9},{9,10},{10,11},{12,13},{... | collective-permute-start | bytes 49160 | tf_op jit(solution)/shard_map/ppermute | solution.py:32
  118.4 1.9 %collective-permute-start.8 = (bf16[32,256]{1,0:T(8,128)(2,1)S(1)}, bf16[32,256]{1,0:T(8,128)(2,1)S(1)}, u32[]{:S(2)}, u32[]{:S(2)}) collective-permute-start(bf16[32,256]{1,0:T(8,128)(2,1)S(1)} %get-tuple-element.62), channel_id=1, source_target_pairs={{1,0},{2,1},{3,2},{5,4},{6,5},{7,6},{9,8},{10,9},{11,10},{13,12},{... | collective-permute-start | bytes 49160 | tf_op jit(solution)/shard_map/ppermute | solution.py:32
  120.4 0.1 fusion.4.t1b
  120.5 4.4 %collective-permute-done.8.right_ref = bf16[32,256]{1,0:T(8,128)(2,1)S(1)} collective-permute-done((bf16[32,256]{1,0:T(8,128)(2,1)S(1)}, bf16[32,256]{1,0:T(8,128)(2,1)S(1)}, u32[]{:S(2)}, u32[]{:S(2)}) %collective-permute-start.8) | collective-permute-done | bytes 16416 | tf_op jit(solution)/shard_map/ppermute | solution.py:32
  125.0 1.8 %shard_map.188 = (bf16[8,5120]{1,0:T(8,128)(2,1)}, bf16[4,5120]{1,0:T(4,128)(2,1)}, bf16[2,5120]{1,0:T(2,128)(2,1)}, bf16[1,5120]{1,0:T(2,128)(2,1)}) custom-call(bf16[8,5120]{1,0:T(8,128)(2,1)S(1)} %get-tuple-element.55.g1_ref, bf16[4,5120]{1,0:T(4,128)(2,1)S(1)} %get-tuple-element.56.g2_ref, bf16[2,5120]{1,0:T(2,128)(2,1)S(1)} %get-tuple-element.57.g3_ref, ...), custom_call_target="tpu_custom_call" | custom-call | tf_op jit(solution)/shard_map/pallas_call | solution.py:527
  126.8 1.9 %collective-permute-start.9 = (bf16[1664,256]{1,0:T(8,128)(2,1)S(1)}, bf16[1664,256]{1,0:T(8,128)(2,1)S(1)}, u32[]{:S(2)}, u32[]{:S(2)}) collective-permute-start(bf16[1664,256]{1,0:T(8,128)(2,1)S(1)} %bitcast.32), channel_id=1, source_target_pairs={{0,1},{1,0},{2,3},{3,2},{4,5},{5,4},{6,7},{7,6},{8,9},{9,8},{10,11... | collective-permute-start | bytes 2555912 | tf_op jit(solution)/shard_map/ppermute | solution.py:435
  128.8 2.3 %collective-permute-done.9.got = bf16[1664,256]{1,0:T(8,128)(2,1)S(1)} collective-permute-done((bf16[1664,256]{1,0:T(8,128)(2,1)S(1)}, bf16[1664,256]{1,0:T(8,128)(2,1)S(1)}, u32[]{:S(2)}, u32[]{:S(2)}) %collective-permute-start.9) | collective-permute-done | bytes 852000 | tf_op jit(solution)/shard_map/ppermute | solution.py:435
  131.1 1.9 %shard_map.189 = (bf16[576,64]{1,0:T(8,128)(2,1)}, bf16[1152,128]{1,0:T(8,128)(2,1)}, bf16[2304,256]{1,0:T(8,128)(2,1)}, bf16[64,128]{1,0:T(8,128)(2,1)}, bf16[6...) custom-call(s32[4]{0:T(128)S(1)} %pad_add_fusion.6.place_ref, bf16[1664,256]{1,0:T(8,128)(2,1)S(1)} %bitcast.33, ...), custom_call_target="tpu_custom_call" | custom-call | tf_op jit(solution)/shard_map/pallas_call | solution.py:540
  (51 shorter events, 0.7 us)
Async XLA Ops:
  0.6 25.3 %copy-start.5 = (bf16[8,5120]{1,0:T(8,128)(2,1)S(1)}, bf16[8,5120]{1,0:T(8,128)(2,1)}, u32[]{:S(2)}) copy-start(bf16[8,5120]{1,0:T(8,128)(2,1)} %refs_1_.1) | copy-start | bytes 245764
  0.7 25.3 %copy-start.2 = (bf16[4,5120]{1,0:T(4,128)(2,1)S(1)}, bf16[4,5120]{1,0:T(4,128)(2,1)}, u32[]{:S(2)}) copy-start(bf16[4,5120]{1,0:T(4,128)(2,1)} %refs_2_.1) | copy-start | bytes 122884
  0.7 25.3 %copy-start.3 = (bf16[8,5120]{1,0:T(8,128)(2,1)S(1)}, bf16[8,5120]{1,0:T(8,128)(2,1)}, u32[]{:S(2)}) copy-start(bf16[8,5120]{1,0:T(8,128)(2,1)} %refs_0_.1) | copy-start | bytes 245764
  0.7 11.4 %copy-start.7 = (bf16[1,5120]{1,0:T(2,128)(2,1)S(1)}, bf16[1,5120]{1,0:T(2,128)(2,1)}, u32[]{:S(2)}) copy-start(bf16[1,5120]{1,0:T(2,128)(2,1)} %refs_4_.1) | copy-start | bytes 30724
  0.7 25.3 %copy-start.6 = (bf16[2,5120]{1,0:T(2,128)(2,1)S(1)}, bf16[2,5120]{1,0:T(2,128)(2,1)}, u32[]{:S(2)}) copy-start(bf16[2,5120]{1,0:T(2,128)(2,1)} %refs_3_.1) | copy-start | bytes 61444
  0.7 11.3 %copy-start.16 = (bf16[3,3,64,64]{3,2,1,0:T(8,128)(2,1)S(1)}, bf16[3,3,64,64]{3,2,1,0:T(8,128)(2,1)}, u32[]{:S(2)}) copy-start(bf16[3,3,64,64]{3,2,1,0:T(8,128)(2,1)} %param.15) | copy-start | bytes 221188
  0.7 25.3 %copy-start.4 = (bf16[512,64]{0,1:T(8,128)(2,1)S(1)}, bf16[512,64]{0,1:T(8,128)(2,1)}, u32[]{:S(2)}) copy-start(bf16[512,64]{0,1:T(8,128)(2,1)} %param.20) | copy-start | bytes 196612
  0.7 25.3 %copy-start.8 = (bf16[256,64]{0,1:T(8,128)(2,1)S(1)}, bf16[256,64]{0,1:T(8,128)(2,1)}, u32[]{:S(2)}) copy-start(bf16[256,64]{0,1:T(8,128)(2,1)} %param.19) | copy-start | bytes 98308
  0.7 25.3 %copy-start.9 = (bf16[128,64]{0,1:T(8,128)(2,1)S(1)}, bf16[128,64]{0,1:T(8,128)(2,1)}, u32[]{:S(2)}) copy-start(bf16[128,64]{0,1:T(8,128)(2,1)} %param.18) | copy-start | bytes 49156
  0.7 25.3 %copy-start = (bf16[3,3,256,256]{3,2,1,0:T(8,128)(2,1)S(1)}, bf16[3,3,256,256]{3,2,1,0:T(8,128)(2,1)}, u32[]{:S(2)}) copy-start(bf16[3,3,256,256]{3,2,1,0:T(8,128)(2,1)} %param.17) | copy-start | bytes 3538948
  0.8 25.3 %copy-start.1 = (bf16[3,3,128,128]{3,2,1,0:T(8,128)(2,1)S(1)}, bf16[3,3,128,128]{3,2,1,0:T(8,128)(2,1)}, u32[]{:S(2)}) copy-start(bf16[3,3,128,128]{3,2,1,0:T(8,128)(2,1)} %param.16) | copy-start | bytes 884740
  3.9 8.4 %collective-permute-start.1 = (bf16[16,5120]{1,0:T(8,128)(2,1)S(1)}, bf16[16,5120]{1,0:T(8,128)(2,1)S(1)}, u32[]{:S(2)}, u32[]{:S(2)}) collective-permute-start(bf16[16,5120]{1,0:T(8,128)(2,1)S(1)} %get-tuple-element.95), channel_id=1, source_target_pairs={{4,0},{8,4},{12,8},{16,12},{20,16},{24,20},{28,24},{32,28},{36,32}... | collective-permute-start | bytes 491528 | tf_op jit(solution)/shard_map/ppermute | solution.py:32
  5.2 7.1 %collective-permute-start = (bf16[16,5120]{1,0:T(8,128)(2,1)S(1)}, bf16[16,5120]{1,0:T(8,128)(2,1)S(1)}, u32[]{:S(2)}, u32[]{:S(2)}) collective-permute-start(bf16[16,5120]{1,0:T(8,128)(2,1)S(1)} %get-tuple-element.96), channel_id=1, source_target_pairs={{0,4},{4,8},{8,12},{12,16},{16,20},{20,24},{24,28},{28,32},{32,36}... | collective-permute-start | bytes 491528 | tf_op jit(solution)/shard_map/ppermute | solution.py:32
  12.1 10.7 %copy-start.10 = (bf16[3,64,64]{2,1,0:T(8,128)(2,1)}, bf16[3,64,64]{2,1,0:T(8,128)(2,1)S(1)}, u32[]{:S(2)}) copy-start(bf16[3,64,64]{2,1,0:T(8,128)(2,1)S(1)} %get-tuple-element.82) | copy-start | bytes 73732
  12.1 13.9 %copy-start.12 = (bf16[3,64,64]{2,1,0:T(8,128)(2,1)}, bf16[3,64,64]{2,1,0:T(8,128)(2,1)S(1)}, u32[]{:S(2)}) copy-start(bf16[3,64,64]{2,1,0:T(8,128)(2,1)S(1)} %get-tuple-element.83) | copy-start | bytes 73732
  12.1 13.9 %copy-start.14 = (bf16[3,64,64]{2,1,0:T(8,128)(2,1)}, bf16[3,64,64]{2,1,0:T(8,128)(2,1)S(1)}, u32[]{:S(2)}) copy-start(bf16[3,64,64]{2,1,0:T(8,128)(2,1)S(1)} %get-tuple-element.84) | copy-start | bytes 73732
  12.4 10.5 %collective-permute-start.2 = (bf16[48,512]{1,0:T(8,128)(2,1)S(1)}, bf16[48,512]{1,0:T(8,128)(2,1)S(1)}, u32[]{:S(2)}, u32[]{:S(2)}) collective-permute-start(bf16[48,512]{1,0:T(8,128)(2,1)S(1)} %pad_add_fusion.5), channel_id=1, source_target_pairs={{0,1},{1,2},{2,3},{4,5},{5,6},{6,7},{8,9},{9,10},{10,11},{12,13},{... | collective-permute-start | bytes 147464 | tf_op jit(solution)/shard_map/ppermute | solution.py:32
  19.0 6.9 %collective-permute-start.3 = (bf16[48,512]{1,0:T(8,128)(2,1)S(1)}, bf16[48,512]{1,0:T(8,128)(2,1)S(1)}, u32[]{:S(2)}, u32[]{:S(2)}) collective-permute-start(bf16[48,512]{1,0:T(8,128)(2,1)S(1)} %pad_add_fusion.4), channel_id=1, source_target_pairs={{1,0},{2,1},{3,2},{5,4},{6,5},{7,6},{9,8},{10,9},{11,10},{13,12},{... | collective-permute-start | bytes 147464 | tf_op jit(solution)/shard_map/ppermute | solution.py:32
  33.2 4.3 %collective-permute-start.4 = (bf16[1664,256]{1,0:T(8,128)(2,1)S(1)}, bf16[1664,256]{1,0:T(8,128)(2,1)S(1)}, u32[]{:S(2)}, u32[]{:S(2)}) collective-permute-start(bf16[1664,256]{1,0:T(8,128)(2,1)S(1)} %get-tuple-element.45), channel_id=1, source_target_pairs={{0,1},{1,0},{2,3},{3,2},{4,5},{5,4},{6,7},{7,6},{8,9},{9,8},{10,11... | collective-permute-start | bytes 2555912 | tf_op jit(solution)/shard_map/ppermute | solution.py:435
  38.6 20.8 %all-to-all-start = ((bf16[16,104,256]{2,1,0:T(8,128)(2,1)}), bf16[16,104,256]{2,1,0:T(8,128)(2,1)S(1)}, u32[]{:S(2)}, u32[]{:S(2)}) async-start(bf16[16,104,256]{2,1,0:T(8,128)(2,1)} %bitcast.12), calls=%async_computation | async-start | bytes 1703936 | tf_op jit(solution)/shard_map/all_to_all | solution.py:558
  46.2 11.9 %collective-permute-start.5 = (bf16[8,5120]{1,0:T(8,128)(2,1)S(1)}, bf16[8,5120]{1,0:T(8,128)(2,1)S(1)}, u32[]{:S(2)}, u32[]{:S(2)}) collective-permute-start(bf16[8,5120]{1,0:T(8,128)(2,1)S(1)} %get-tuple-element.49), channel_id=1, source_target_pairs={{0,4},{4,8},{8,12},{12,16},{16,20},{20,24},{24,28},{28,32},{32,36}... | collective-permute-start | bytes 245768 | tf_op jit(solution)/shard_map/ppermute | solution.py:32
  49.5 9.6 %collective-permute-start.6 = (bf16[8,5120]{1,0:T(8,128)(2,1)S(1)}, bf16[8,5120]{1,0:T(8,128)(2,1)S(1)}, u32[]{:S(2)}, u32[]{:S(2)}) collective-permute-start(bf16[8,5120]{1,0:T(8,128)(2,1)S(1)} %get-tuple-element.50), channel_id=1, source_target_pairs={{4,0},{8,4},{12,8},{16,12},{20,16},{24,20},{28,24},{32,28},{36,32}... | collective-permute-start | bytes 245768 | tf_op jit(solution)/shard_map/ppermute | solution.py:32
  99.9 20.4 %copy-start.11 = (bf16[3,64,64]{2,1,0:T(8,128)(2,1)S(1)}, bf16[3,64,64]{2,1,0:T(8,128)(2,1)}, u32[]{:S(2)}) copy-start(bf16[3,64,64]{2,1,0:T(8,128)(2,1)} %copy-done.10) | copy-start | bytes 73732
  99.9 20.4 %copy-start.13 = (bf16[3,64,64]{2,1,0:T(8,128)(2,1)S(1)}, bf16[3,64,64]{2,1,0:T(8,128)(2,1)}, u32[]{:S(2)}) copy-start(bf16[3,64,64]{2,1,0:T(8,128)(2,1)} %copy-done.12) | copy-start | bytes 73732
  99.9 20.4 %copy-start.15 = (bf16[3,64,64]{2,1,0:T(8,128)(2,1)S(1)}, bf16[3,64,64]{2,1,0:T(8,128)(2,1)}, u32[]{:S(2)}) copy-start(bf16[3,64,64]{2,1,0:T(8,128)(2,1)} %copy-done.14) | copy-start | bytes 73732
  99.9 26.9 %all-to-all-start.1 = ((bf16[16,104,256]{2,1,0:T(8,128)(2,1)}), bf16[16,104,256]{2,1,0:T(8,128)(2,1)S(1)}, u32[]{:S(2)}, u32[]{:S(2)}) async-start(bf16[16,104,256]{2,1,0:T(8,128)(2,1)} %broadcast_in_dim.10), calls=%async_computation.1 | async-start | bytes 1703936 | tf_op jit(solution)/shard_map/all_to_all | solution.py:568
  104.9 15.6 %collective-permute-start.7 = (bf16[32,256]{1,0:T(8,128)(2,1)S(1)}, bf16[32,256]{1,0:T(8,128)(2,1)S(1)}, u32[]{:S(2)}, u32[]{:S(2)}) collective-permute-start(bf16[32,256]{1,0:T(8,128)(2,1)S(1)} %get-tuple-element.61), channel_id=1, source_target_pairs={{0,1},{1,2},{2,3},{4,5},{5,6},{6,7},{8,9},{9,10},{10,11},{12,13},{... | collective-permute-start | bytes 49160 | tf_op jit(solution)/shard_map/ppermute | solution.py:32
  118.4 6.6 %collective-permute-start.8 = (bf16[32,256]{1,0:T(8,128)(2,1)S(1)}, bf16[32,256]{1,0:T(8,128)(2,1)S(1)}, u32[]{:S(2)}, u32[]{:S(2)}) collective-permute-start(bf16[32,256]{1,0:T(8,128)(2,1)S(1)} %get-tuple-element.62), channel_id=1, source_target_pairs={{1,0},{2,1},{3,2},{5,4},{6,5},{7,6},{9,8},{10,9},{11,10},{13,12},{... | collective-permute-start | bytes 49160 | tf_op jit(solution)/shard_map/ppermute | solution.py:32
  126.8 4.3 %collective-permute-start.9 = (bf16[1664,256]{1,0:T(8,128)(2,1)S(1)}, bf16[1664,256]{1,0:T(8,128)(2,1)S(1)}, u32[]{:S(2)}, u32[]{:S(2)}) collective-permute-start(bf16[1664,256]{1,0:T(8,128)(2,1)S(1)} %bitcast.32), channel_id=1, source_target_pairs={{0,1},{1,0},{2,3},{3,2},{4,5},{5,4},{6,7},{7,6},{8,9},{9,8},{10,11... | collective-permute-start | bytes 2555912 | tf_op jit(solution)/shard_map/ppermute | solution.py:435

commit v5 on v4

--- a/solution.py
+++ b/solution.py
@@ -13,11 +13,10 @@
 FEAT_THREE = 256
 FEAT_FOUR = 512
 
-ROWS = ("z", "x_lo", "y")
+ROWS = ("z_hi", "z_lo", "x_lo", "y")
 COLS = ("x_hi", "core")
-PLANE = ("x_lo", "y", "x_hi")
+SLAB = ("z_lo", "x_lo", "y", "x_hi")
 PACK_ROWS = 3328
-HALF = PACK_ROWS // 2
 WIDE = 5120
 RIM = 512
 BF = jnp.bfloat16
@@ -41,9 +40,23 @@
     return total
 
 
+def edge_rows_kernel(x1_ref, cot_ref, x2_ref, x3_ref, x4_ref, last_ref, first_ref, last, first):
+    x1, cot, x2, x3, x4 = (ref[...].astype(F32) for ref in (x1_ref, cot_ref, x2_ref, x3_ref, x4_ref))
+    for out, ref, ones, cots, twos in (
+        (last, last_ref, x1[5:8], cot[6:8], x2[1:4]),
+        (first, first_ref, x1[0:3], cot[0:2], x2[0:3]),
+    ):
+        out[0:3, :] = ones
+        out[3:5, :] = cots
+        out[5:8, :] = twos
+        out[8:10, :] = x3
+        out[10:11, :] = x4
+        out[11:16, :] = jnp.zeros((5, WIDE), F32)
+        ref[...] = out[...].astype(BF)
+
+
 def halos(x1, x2, x3, x4, cot):
-    last = stacked((x1[5:], cot[6:], x2[1:], x3, x4), 16)
-    first = stacked((x1[:3], cot[:2], x2[:3], x3, x4), 16)
+    last, first = call(edge_rows_kernel, [((16, WIDE), BF)] * 2, [((16, WIDE), F32)] * 2, 5)(x1, cot, x2, x3, x4)
     above = moved(last, ROWS, 1)
     below = moved(first, ROWS, -1)
     parts = (x1, cot, x2, x3, x4, above[:11], below[:11])
@@ -337,8 +350,8 @@
         at, side = base + 64 * (n // 2), 128 * (n % 2)
         sums[at : at + 64, side : side + 128] = pairs[n]
     sums[3264:3328, :] = jnp.zeros((64, 256), F32)
-    keep_ref[...] = sums[pl.ds(pl.multiple_of(core * HALF, 64), HALF), :].astype(BF)
-    send_ref[...] = sums[pl.ds(pl.multiple_of((1 - core) * HALF, 64), HALF), :].astype(BF)
+    keep_ref[...] = jnp.where(core == 0, sums[:, 0:128], sums[:, 128:256]).astype(BF)
+    send_ref[...] = jnp.where(core == 0, sums[:, 128:256], sums[:, 0:128]).astype(BF)
 
 
 def rims_kernel(g1_ref, g2_ref, g3_ref, rim_ref, above_ref, below_ref, left_ref, right_ref, out):
@@ -437,8 +450,8 @@
 
 def unpack_kernel(place_ref, mine, got, k1_ref, k2_ref, k3_ref, p2_ref, p3_ref, p4_ref, whole):
     core = place_ref[3]
-    whole[pl.ds(pl.multiple_of(core * HALF, 64), HALF), :] = mine[...]
-    whole[pl.ds(pl.multiple_of((1 - core) * HALF, 64), HALF), :] = got[...]
+    whole[:, 0:128] = jnp.where(core == 0, mine[...], got[...])
+    whole[:, 128:256] = jnp.where(core == 0, got[...], mine[...])
     k3_ref[...] = whole[0:2304, :]
     k2_ref[0:576, :] = whole[2304:2880, 0:128]
     k2_ref[576:1152, :] = whole[2304:2880, 128:256]
@@ -497,7 +510,7 @@
     keep, send, g1, g2, g3, rim, up, down = call(
         forward_kernel,
         [
-            ((HALF, 256), BF), ((HALF, 256), BF),
+            ((PACK_ROWS, 128), BF), ((PACK_ROWS, 128), BF),
             ((8, WIDE), BF), ((4, WIDE), BF), ((2, WIDE), BF), ((1, 1536), F32),
             ((8, WIDE), BF), ((8, WIDE), BF),
         ],
@@ -555,17 +568,16 @@
     part = (keep.astype(F32) + swapped(send, "core", 1).astype(F32)).astype(BF)
     part, up, down = lax.optimization_barrier((part, up, down))
 
-    pieces = lax.all_to_all(part.reshape(16, -1, part.shape[1]), PLANE, 0, 0)
+    pieces = lax.all_to_all(part.reshape(32, -1, 128), SLAB, 0, 0)
     above, below = moved(down, ROWS, 1), moved(up, ROWS, -1)
-    pieces, above, below = lax.optimization_barrier((pieces, above, below))
     part = jnp.sum(pieces.astype(F32), axis=0).astype(BF)
 
-    pieces = lax.all_gather(part, "z")
+    pieces = lax.all_to_all(jnp.broadcast_to(part[None], (8,) + part.shape), "z_hi", 0, 0)
     part = jnp.sum(pieces.astype(F32), axis=0).astype(BF)
     part, above, below = lax.optimization_barrier((part, above, below))
 
-    pieces = jnp.broadcast_to(part[None], (16,) + part.shape)
-    mine = lax.all_to_all(pieces, PLANE, 0, 0).reshape(keep.shape)
+    pieces = jnp.broadcast_to(part[None], (32,) + part.shape)
+    mine = lax.all_to_all(pieces, SLAB, 0, 0).reshape(keep.shape)
     left, right = from_beside(grads, above, below)
     outs = input_grads(grads, above, below, left, right, weights)
     mine, outs = lax.optimization_barrier((mine, outs))
@@ -573,7 +585,7 @@
 
 
 def solution(mesh):
-    mesh = Mesh(mesh.devices.reshape(16, 2, 4, 2, 2), ("z", "x_lo", "y", "x_hi", "core"))
+    mesh = Mesh(mesh.devices.reshape(8, 2, 2, 4, 2, 2), ROWS + COLS)
     split = P(ROWS, COLS)
     in_specs = (split,) * 4 + (P(),) * 6 + (split,)
     out_specs = (split,) * 4 + (P(),) * 6

time: 134 us -> 130 us (0.970)
  blocking collectives: 39.3 us -> 23.5 us
  waiting for transfers between devices: 21 us -> 30 us
  local copies, waits for them, and re-layouts: 5.37 us -> 11.6 us
  other arithmetic: 2.79 us -> 0.79 us
  starting transfers between devices: 52.6 us -> 51.2 us
    all_gather x1 -> x0, blocking collectives: 39.3 us -> none  [on_device(): pieces = lax.all_gather(part, 'z')]
    all_to_all x0 -> x1, blocking collectives: none -> 23.5 us  [on_device(): pieces = lax.all_to_all(part.reshape(32, -1, 128), SLAB, 0, 0)]
    all_to_all x2, waiting for transfers between devices: 0.38 us -> 12 us  [the longest x1 12 us: on_device(): lax.all_to_all(jnp.broadcast_to(part[None], (8,) + part.shape), 'z_hi', 0...]
    unnamed x34 -> x32, local copies, waits for them, and re-layouts: 0.09 us -> 8.92 us
    ppermute x8, starting transfers between devices: 36.3 us -> 27.7 us  [moved(): return lax.ppermute(block, axis, route)]
    all_to_all x2, starting transfers between devices: 12.5 us -> 19.7 us  [the longest x1 13.3 us: on_device(): lax.all_to_all(jnp.broadcast_to(part[None], (8,) + part.shape), 'z_hi', 0...]
    ppermute x8, waiting for transfers between devices: 15.9 us -> 13.3 us  [moved(): return lax.ppermute(block, axis, route)]
    slice x6, local copies, waits for them, and re-layouts: 2.18 us -> 0.03 us  [halos(): right = moved(stacked([p[:, :RIM] for p in parts], 48), COLS, -1)]
  transfers between devices with their start and end apart: 12 -> 12, of which waited for: 7 -> 6; matrix products, arithmetic and copies ran while one was open for 2% -> 1% of each run, Pallas kernels for 1% -> 1%
where the time goes in v5:
time: 130 us; the launch traced here: 129 us
  starting transfers between devices  51.2 us (39%)
  waiting for transfers between devices  30 us (23%)
  blocking collectives  23.5 us (18%)
  local copies, waits for them, and re-layouts  11.6 us (9%)
  Pallas kernels  11.2 us (9%)
    ppermute x8, starting transfers between devices, moved(): return lax.ppermute(block, axis, route)  27.7 us
    all_to_all x1, blocking collectives, on_device(): pieces = lax.all_to_all(part.reshape(32, -1, 128), SLAB, 0, 0)  23.5 us
    all_to_all x1, starting transfers between devices, on_device(): lax.all_to_all(jnp.broadcast_to(part[None], (8,) + part.shape), 'z_hi', 0...  13.3 us
    ppermute x8, waiting for transfers between devices, moved(): return lax.ppermute(block, axis, route)  13.3 us
    all_to_all x1, waiting for transfers between devices, on_device(): lax.all_to_all(jnp.broadcast_to(part[None], (8,) + part.shape), 'z_hi', 0...  12 us
    unnamed x32, local copies, waits for them, and re-layouts  8.92 us
    pallas_call x1, Pallas kernels, local_part(): call(forward_kernel, [((PACK_ROWS, 128), BF), ((PACK_ROWS, 128), BF), ((8...  7 us
    all_to_all x1, starting transfers between devices, on_device(): mine = lax.all_to_all(pieces, SLAB, 0, 0).reshape(keep.shape)  6.34 us
  transfers between devices with their start and end apart: 12, of which 6 were waited for; matrix products, arithmetic and copies ran while one was open for 1% of the time, Pallas kernels for 1%

profile of v5, /device:TPU:1, one launch (start us, length us, event | category | flops | bytes accessed | tf_op | source)
XLA Modules:
  0.0 129.2 jit_solution(14569049217073462919)
XLA Ops:
  0.7 1.0 copy-done.2
  1.6 0.9 copy-done.4
  2.5 0.8 copy-done.8
  4.9 4.0 %collective-permute-start = (bf16[16,5120]{1,0:T(8,128)(2,1)S(1)}, bf16[16,5120]{1,0:T(8,128)(2,1)S(1)}, u32[]{:S(2)}, u32[]{:S(2)}) collective-permute-start(bf16[16,5120]{1,0:T(8,128)(2,1)S(1)} %get-tuple-element.43), channel_id=1, source_target_pairs={{0,4},{4,8},{8,12},{12,16},{16,20},{20,24},{24,28},{28,32},{32,36}... | collective-permute-start | bytes 491528 | tf_op jit(solution)/shard_map/ppermute | solution.py:31
  9.0 1.3 %collective-permute-start.1 = (bf16[16,5120]{1,0:T(8,128)(2,1)S(1)}, bf16[16,5120]{1,0:T(8,128)(2,1)S(1)}, u32[]{:S(2)}, u32[]{:S(2)}) collective-permute-start(bf16[16,5120]{1,0:T(8,128)(2,1)S(1)} %get-tuple-element.44), channel_id=1, source_target_pairs={{4,0},{8,4},{12,8},{16,12},{20,16},{24,20},{28,24},{32,28},{36,32}... | collective-permute-start | bytes 491528 | tf_op jit(solution)/shard_map/ppermute | solution.py:31
  10.3 0.9 slice_bitcast_fusion
  11.4 3.6 %collective-permute-done.1.refs_6_ = bf16[16,5120]{1,0:T(8,128)(2,1)S(1)} collective-permute-done((bf16[16,5120]{1,0:T(8,128)(2,1)S(1)}, bf16[16,5120]{1,0:T(8,128)(2,1)S(1)}, u32[]{:S(2)}, u32[]{:S(2)}) %collective-permute-start.1) | collective-permute-done | bytes 163872 | tf_op jit(solution)/shard_map/ppermute | solution.py:31
  15.1 7.0 %collective-permute-start.2 = (bf16[48,512]{1,0:T(8,128)(2,1)S(1)}, bf16[48,512]{1,0:T(8,128)(2,1)S(1)}, u32[]{:S(2)}, u32[]{:S(2)}) collective-permute-start(bf16[48,512]{1,0:T(8,128)(2,1)S(1)} %pad_add_fusion.1), channel_id=1, source_target_pairs={{0,1},{1,2},{2,3},{4,5},{5,6},{6,7},{8,9},{9,10},{10,11},{12,13},{... | collective-permute-start | bytes 147464 | tf_op jit(solution)/shard_map/ppermute | solution.py:31
  22.1 1.9 %collective-permute-start.3 = (bf16[48,512]{1,0:T(8,128)(2,1)S(1)}, bf16[48,512]{1,0:T(8,128)(2,1)S(1)}, u32[]{:S(2)}, u32[]{:S(2)}) collective-permute-start(bf16[48,512]{1,0:T(8,128)(2,1)S(1)} %pad_add_fusion), channel_id=1, source_target_pairs={{1,0},{2,1},{3,2},{5,4},{6,5},{7,6},{9,8},{10,9},{11,10},{13,12},{... | collective-permute-start | bytes 147464 | tf_op jit(solution)/shard_map/ppermute | solution.py:31
  24.1 4.9 %collective-permute-done.3.refs_8_ = bf16[48,512]{1,0:T(8,128)(2,1)S(1)} collective-permute-done((bf16[48,512]{1,0:T(8,128)(2,1)S(1)}, bf16[48,512]{1,0:T(8,128)(2,1)S(1)}, u32[]{:S(2)}, u32[]{:S(2)}) %collective-permute-start.3) | collective-permute-done | bytes 49184 | tf_op jit(solution)/shard_map/ppermute | solution.py:31
  29.0 0.9 copy-done.3
  29.9 0.9 copy-done.5
  30.8 0.8 copy-done.6
  31.7 0.7 copy-done.13
  32.4 0.8 copy-done.14
  33.9 7.0 %shard_map.187 = (bf16[3328,128]{1,0:T(8,128)(2,1)S(1)}, bf16[3328,128]{1,0:T(8,128)(2,1)S(1)}, bf16[8,5120]{1,0:T(8,128)(2,1)S(1)}, bf16[4,5120]{1,0:T(4,128)(2...) custom-call(s32[4]{0:T(128)S(1)} %pad_add_fusion.2.place_ref, ...), custom_call_target="tpu_custom_call" | custom-call | tf_op jit(solution)/shard_map/pallas_call | solution.py:510
  40.9 1.9 %collective-permute-start.4 = (bf16[3328,128]{1,0:T(8,128)(2,1)S(1)}, bf16[3328,128]{1,0:T(8,128)(2,1)S(1)}, u32[]{:S(2)}, u32[]{:S(2)}) collective-permute-start(bf16[3328,128]{1,0:T(8,128)(2,1)S(1)} %get-tuple-element.46), channel_id=1, source_target_pairs={{0,1},{1,0},{2,3},{3,2},{4,5},{5,4},{6,7},{7,6},{8,9},{9,8},{10,11... | collective-permute-start | bytes 2555912 | tf_op jit(solution)/shard_map/ppermute | solution.py:448
  42.8 2.3 %collective-permute-done.4 = bf16[3328,128]{1,0:T(8,128)(2,1)S(1)} collective-permute-done((bf16[3328,128]{1,0:T(8,128)(2,1)S(1)}, bf16[3328,128]{1,0:T(8,128)(2,1)S(1)}, u32[]{:S(2)}, u32[]{:S(2)}) %collective-permute-start.4) | collective-permute-done | bytes 852000 | tf_op jit(solution)/shard_map/ppermute | solution.py:448
  45.4 23.5 %all_to_all.15 = bf16[32,104,128]{2,1,0:T(8,128)(2,1)S(1)} all-to-all(bf16[32,104,128]{2,1,0:T(8,128)(2,1)S(1)} %bitcast.39), channel_id=1, replica_groups=mesh['z_hi'=8,'z_lo'=2,'x_lo'=2,'y'=4,'x_hi'=2,'core'=2] {'z_lo','x_lo',..., dimensions={0} | all-to-all | bytes 1703936 | tf_op jit(solution)/shard_map/all_to_all | solution.py:571
  69.7 13.3 %all-to-all-start.1 = ((bf16[8,104,128]{2,1,0:T(8,128)(2,1)}), bf16[8,104,128]{2,1,0:T(8,128)(2,1)S(1)}, u32[]{:S(2)}, u32[]{:S(2)}) async-start(bf16[8,104,128]{2,1,0:T(8,128)(2,1)} %broadcast_in_dim.7), calls=%async_computation.1 | async-start | bytes 425984 | tf_op jit(solution)/shard_map/all_to_all | solution.py:575
  83.0 2.5 %collective-permute-start.5 = (bf16[8,5120]{1,0:T(8,128)(2,1)S(1)}, bf16[8,5120]{1,0:T(8,128)(2,1)S(1)}, u32[]{:S(2)}, u32[]{:S(2)}) collective-permute-start(bf16[8,5120]{1,0:T(8,128)(2,1)S(1)} %get-tuple-element.50), channel_id=1, source_target_pairs={{0,4},{4,8},{8,12},{12,16},{16,20},{20,24},{24,28},{28,32},{32,36}... | collective-permute-start | bytes 245768 | tf_op jit(solution)/shard_map/ppermute | solution.py:31
  85.5 1.3 %collective-permute-start.6 = (bf16[8,5120]{1,0:T(8,128)(2,1)S(1)}, bf16[8,5120]{1,0:T(8,128)(2,1)S(1)}, u32[]{:S(2)}, u32[]{:S(2)}) collective-permute-start(bf16[8,5120]{1,0:T(8,128)(2,1)S(1)} %get-tuple-element.51), channel_id=1, source_target_pairs={{4,0},{8,4},{12,8},{16,12},{20,16},{24,20},{28,24},{32,28},{36,32}... | collective-permute-start | bytes 245768 | tf_op jit(solution)/shard_map/ppermute | solution.py:31
  86.8 12.0 %all-to-all-done.1 = bf16[8,104,128]{2,1,0:T(8,128)(2,1)S(1)} async-done(((bf16[8,104,128]{2,1,0:T(8,128)(2,1)}), bf16[8,104,128]{2,1,0:T(8,128)(2,1)S(1)}, u32[]{:S(2)}, u32[]{:S(2)}) %all-to-all-start.1) | async-done | bytes 213024 | tf_op jit(solution)/shard_map/all_to_all | solution.py:575
  98.9 1.0 broadcast_in_dim.8
  99.9 6.3 %all-to-all-start.2 = ((bf16[32,104,128]{2,1,0:T(8,128)(2,1)}), bf16[32,104,128]{2,1,0:T(8,128)(2,1)S(1)}, u32[]{:S(2)}, u32[]{:S(2)}) async-start(bf16[32,104,128]{2,1,0:T(8,128)(2,1)} %broadcast_in_dim.8), calls=%async_computation.2 | async-start | bytes 1703936 | tf_op jit(solution)/shard_map/all_to_all | solution.py:580
  106.2 7.8 %collective-permute-start.7 = (bf16[32,256]{1,0:T(8,128)(2,1)S(1)}, bf16[32,256]{1,0:T(8,128)(2,1)S(1)}, u32[]{:S(2)}, u32[]{:S(2)}) collective-permute-start(bf16[32,256]{1,0:T(8,128)(2,1)S(1)} %get-tuple-element.59), channel_id=1, source_target_pairs={{0,1},{1,2},{2,3},{4,5},{5,6},{6,7},{8,9},{9,10},{10,11},{12,13},{... | collective-permute-start | bytes 49160 | tf_op jit(solution)/shard_map/ppermute | solution.py:31
  114.0 1.9 %collective-permute-start.8 = (bf16[32,256]{1,0:T(8,128)(2,1)S(1)}, bf16[32,256]{1,0:T(8,128)(2,1)S(1)}, u32[]{:S(2)}, u32[]{:S(2)}) collective-permute-start(bf16[32,256]{1,0:T(8,128)(2,1)S(1)} %get-tuple-element.60), channel_id=1, source_target_pairs={{1,0},{2,1},{3,2},{5,4},{6,5},{7,6},{9,8},{10,9},{11,10},{13,12},{... | collective-permute-start | bytes 49160 | tf_op jit(solution)/shard_map/ppermute | solution.py:31
  116.1 4.8 %collective-permute-done.8.right_ref = bf16[32,256]{1,0:T(8,128)(2,1)S(1)} collective-permute-done((bf16[32,256]{1,0:T(8,128)(2,1)S(1)}, bf16[32,256]{1,0:T(8,128)(2,1)S(1)}, u32[]{:S(2)}, u32[]{:S(2)}) %collective-permute-start.8) | collective-permute-done | bytes 16416 | tf_op jit(solution)/shard_map/ppermute | solution.py:31
  120.9 1.8 %shard_map.189 = (bf16[8,5120]{1,0:T(8,128)(2,1)}, bf16[4,5120]{1,0:T(4,128)(2,1)}, bf16[2,5120]{1,0:T(2,128)(2,1)}, bf16[1,5120]{1,0:T(2,128)(2,1)}) custom-call(bf16[8,5120]{1,0:T(8,128)(2,1)S(1)} %get-tuple-element.53.g1_ref, bf16[4,5120]{1,0:T(4,128)(2,1)S(1)} %get-tuple-element.54.g2_ref, bf16[2,5120]{1,0:T(2,128)(2,1)S(1)} %get-tuple-element.55.g3_ref, ...), custom_call_target="tpu_custom_call" | custom-call | tf_op jit(solution)/shard_map/pallas_call | solution.py:540
  122.7 1.9 %collective-permute-start.9 = (bf16[3328,128]{1,0:T(8,128)(2,1)S(1)}, bf16[3328,128]{1,0:T(8,128)(2,1)S(1)}, u32[]{:S(2)}, u32[]{:S(2)}) collective-permute-start(bf16[3328,128]{1,0:T(8,128)(2,1)S(1)} %bitcast.31), channel_id=1, source_target_pairs={{0,1},{1,0},{2,3},{3,2},{4,5},{5,4},{6,7},{7,6},{8,9},{9,8},{10,11... | collective-permute-start | bytes 2555912 | tf_op jit(solution)/shard_map/ppermute | solution.py:448
  124.6 2.3 %collective-permute-done.9.got = bf16[3328,128]{1,0:T(8,128)(2,1)S(1)} collective-permute-done((bf16[3328,128]{1,0:T(8,128)(2,1)S(1)}, bf16[3328,128]{1,0:T(8,128)(2,1)S(1)}, u32[]{:S(2)}, u32[]{:S(2)}) %collective-permute-start.9) | collective-permute-done | bytes 852000 | tf_op jit(solution)/shard_map/ppermute | solution.py:448
  127.0 2.2 %shard_map.190 = (bf16[576,64]{1,0:T(8,128)(2,1)}, bf16[1152,128]{1,0:T(8,128)(2,1)}, bf16[2304,256]{1,0:T(8,128)(2,1)}, bf16[64,128]{1,0:T(8,128)(2,1)}, bf16[6...) custom-call(s32[4]{0:T(128)S(1)} %pad_add_fusion.2.place_ref, bf16[3328,128]{1,0:T(8,128)(2,1)S(1)} %bitcast.32, ...), custom_call_target="tpu_custom_call" | custom-call | tf_op jit(solution)/shard_map/pallas_call | solution.py:553
  (48 shorter events, 4.0 us)
Async XLA Ops:
  0.6 28.4 %copy-start = (bf16[3,3,256,256]{3,2,1,0:T(8,128)(2,1)S(1)}, bf16[3,3,256,256]{3,2,1,0:T(8,128)(2,1)}, u32[]{:S(2)}) copy-start(bf16[3,3,256,256]{3,2,1,0:T(8,128)(2,1)} %param.17) | copy-start | bytes 3538948
  0.7 1.0 copy-start.2
  1.6 0.9 copy-start.4
  2.5 0.8 copy-start.8
  3.3 0.7 copy-start.10
  4.0 0.7 copy-start.12
  4.8 24.3 %copy-start.1 = (bf16[3,3,128,128]{3,2,1,0:T(8,128)(2,1)S(1)}, bf16[3,3,128,128]{3,2,1,0:T(8,128)(2,1)}, u32[]{:S(2)}) copy-start(bf16[3,3,128,128]{3,2,1,0:T(8,128)(2,1)} %param.16) | copy-start | bytes 884740
  4.8 24.3 %copy-start.9 = (bf16[4,5120]{1,0:T(4,128)(2,1)S(1)}, bf16[4,5120]{1,0:T(4,128)(2,1)}, u32[]{:S(2)}) copy-start(bf16[4,5120]{1,0:T(4,128)(2,1)} %refs_2_.1) | copy-start | bytes 122884
  4.8 24.3 %copy-start.11 = (bf16[2,5120]{1,0:T(2,128)(2,1)S(1)}, bf16[2,5120]{1,0:T(2,128)(2,1)}, u32[]{:S(2)}) copy-start(bf16[2,5120]{1,0:T(2,128)(2,1)} %refs_3_.1) | copy-start | bytes 61444
  4.9 6.4 %collective-permute-start = (bf16[16,5120]{1,0:T(8,128)(2,1)S(1)}, bf16[16,5120]{1,0:T(8,128)(2,1)S(1)}, u32[]{:S(2)}, u32[]{:S(2)}) collective-permute-start(bf16[16,5120]{1,0:T(8,128)(2,1)S(1)} %get-tuple-element.43), channel_id=1, source_target_pairs={{0,4},{4,8},{8,12},{12,16},{16,20},{20,24},{24,28},{28,32},{32,36}... | collective-permute-start | bytes 491528 | tf_op jit(solution)/shard_map/ppermute | solution.py:31
  9.0 6.1 %collective-permute-start.1 = (bf16[16,5120]{1,0:T(8,128)(2,1)S(1)}, bf16[16,5120]{1,0:T(8,128)(2,1)S(1)}, u32[]{:S(2)}, u32[]{:S(2)}) collective-permute-start(bf16[16,5120]{1,0:T(8,128)(2,1)S(1)} %get-tuple-element.44), channel_id=1, source_target_pairs={{4,0},{8,4},{12,8},{16,12},{20,16},{24,20},{28,24},{32,28},{36,32}... | collective-permute-start | bytes 491528 | tf_op jit(solution)/shard_map/ppermute | solution.py:31
  15.1 9.0 %collective-permute-start.2 = (bf16[48,512]{1,0:T(8,128)(2,1)S(1)}, bf16[48,512]{1,0:T(8,128)(2,1)S(1)}, u32[]{:S(2)}, u32[]{:S(2)}) collective-permute-start(bf16[48,512]{1,0:T(8,128)(2,1)S(1)} %pad_add_fusion.1), channel_id=1, source_target_pairs={{0,1},{1,2},{2,3},{4,5},{5,6},{6,7},{8,9},{9,10},{10,11},{12,13},{... | collective-permute-start | bytes 147464 | tf_op jit(solution)/shard_map/ppermute | solution.py:31
  22.1 6.9 %collective-permute-start.3 = (bf16[48,512]{1,0:T(8,128)(2,1)S(1)}, bf16[48,512]{1,0:T(8,128)(2,1)S(1)}, u32[]{:S(2)}, u32[]{:S(2)}) collective-permute-start(bf16[48,512]{1,0:T(8,128)(2,1)S(1)} %pad_add_fusion), channel_id=1, source_target_pairs={{1,0},{2,1},{3,2},{5,4},{6,5},{7,6},{9,8},{10,9},{11,10},{13,12},{... | collective-permute-start | bytes 147464 | tf_op jit(solution)/shard_map/ppermute | solution.py:31
  29.0 0.9 copy-start.3
  29.9 0.9 copy-start.5
  30.8 0.8 copy-start.6
  31.7 0.7 copy-start.13
  32.4 0.8 copy-start.14
  33.1 0.7 copy-start.15
  40.9 4.3 %collective-permute-start.4 = (bf16[3328,128]{1,0:T(8,128)(2,1)S(1)}, bf16[3328,128]{1,0:T(8,128)(2,1)S(1)}, u32[]{:S(2)}, u32[]{:S(2)}) collective-permute-start(bf16[3328,128]{1,0:T(8,128)(2,1)S(1)} %get-tuple-element.46), channel_id=1, source_target_pairs={{0,1},{1,0},{2,3},{3,2},{4,5},{5,4},{6,7},{7,6},{8,9},{9,8},{10,11... | collective-permute-start | bytes 2555912 | tf_op jit(solution)/shard_map/ppermute | solution.py:448
  69.7 29.1 %all-to-all-start.1 = ((bf16[8,104,128]{2,1,0:T(8,128)(2,1)}), bf16[8,104,128]{2,1,0:T(8,128)(2,1)S(1)}, u32[]{:S(2)}, u32[]{:S(2)}) async-start(bf16[8,104,128]{2,1,0:T(8,128)(2,1)} %broadcast_in_dim.7), calls=%async_computation.1 | async-start | bytes 425984 | tf_op jit(solution)/shard_map/all_to_all | solution.py:575
  83.0 15.8 %collective-permute-start.5 = (bf16[8,5120]{1,0:T(8,128)(2,1)S(1)}, bf16[8,5120]{1,0:T(8,128)(2,1)S(1)}, u32[]{:S(2)}, u32[]{:S(2)}) collective-permute-start(bf16[8,5120]{1,0:T(8,128)(2,1)S(1)} %get-tuple-element.50), channel_id=1, source_target_pairs={{0,4},{4,8},{8,12},{12,16},{16,20},{20,24},{24,28},{28,32},{32,36}... | collective-permute-start | bytes 245768 | tf_op jit(solution)/shard_map/ppermute | solution.py:31
  85.5 13.3 %collective-permute-start.6 = (bf16[8,5120]{1,0:T(8,128)(2,1)S(1)}, bf16[8,5120]{1,0:T(8,128)(2,1)S(1)}, u32[]{:S(2)}, u32[]{:S(2)}) collective-permute-start(bf16[8,5120]{1,0:T(8,128)(2,1)S(1)} %get-tuple-element.51), channel_id=1, source_target_pairs={{4,0},{8,4},{12,8},{16,12},{20,16},{24,20},{28,24},{32,28},{36,32}... | collective-permute-start | bytes 245768 | tf_op jit(solution)/shard_map/ppermute | solution.py:31
  99.9 21.0 %copy-start.7 = (bf16[512,64]{0,1:T(8,128)(2,1)S(1)}, bf16[512,64]{0,1:T(8,128)(2,1)}, u32[]{:S(2)}) copy-start(bf16[512,64]{0,1:T(8,128)(2,1)} %param.20) | copy-start | bytes 196612
  99.9 22.8 %all-to-all-start.2 = ((bf16[32,104,128]{2,1,0:T(8,128)(2,1)}), bf16[32,104,128]{2,1,0:T(8,128)(2,1)S(1)}, u32[]{:S(2)}, u32[]{:S(2)}) async-start(bf16[32,104,128]{2,1,0:T(8,128)(2,1)} %broadcast_in_dim.8), calls=%async_computation.2 | async-start | bytes 1703936 | tf_op jit(solution)/shard_map/all_to_all | solution.py:580
  106.2 9.8 %collective-permute-start.7 = (bf16[32,256]{1,0:T(8,128)(2,1)S(1)}, bf16[32,256]{1,0:T(8,128)(2,1)S(1)}, u32[]{:S(2)}, u32[]{:S(2)}) collective-permute-start(bf16[32,256]{1,0:T(8,128)(2,1)S(1)} %get-tuple-element.59), channel_id=1, source_target_pairs={{0,1},{1,2},{2,3},{4,5},{5,6},{6,7},{8,9},{9,10},{10,11},{12,13},{... | collective-permute-start | bytes 49160 | tf_op jit(solution)/shard_map/ppermute | solution.py:31
  114.0 6.9 %collective-permute-start.8 = (bf16[32,256]{1,0:T(8,128)(2,1)S(1)}, bf16[32,256]{1,0:T(8,128)(2,1)S(1)}, u32[]{:S(2)}, u32[]{:S(2)}) collective-permute-start(bf16[32,256]{1,0:T(8,128)(2,1)S(1)} %get-tuple-element.60), channel_id=1, source_target_pairs={{1,0},{2,1},{3,2},{5,4},{6,5},{7,6},{9,8},{10,9},{11,10},{13,12},{... | collective-permute-start | bytes 49160 | tf_op jit(solution)/shard_map/ppermute | solution.py:31
  122.7 4.3 %collective-permute-start.9 = (bf16[3328,128]{1,0:T(8,128)(2,1)S(1)}, bf16[3328,128]{1,0:T(8,128)(2,1)S(1)}, u32[]{:S(2)}, u32[]{:S(2)}) collective-permute-start(bf16[3328,128]{1,0:T(8,128)(2,1)S(1)} %bitcast.31), channel_id=1, source_target_pairs={{0,1},{1,0},{2,3},{3,2},{4,5},{5,4},{6,7},{7,6},{8,9},{9,8},{10,11... | collective-permute-start | bytes 2555912 | tf_op jit(solution)/shard_map/ppermute | solution.py:448

commit v6 on v5

--- a/solution.py
+++ b/solution.py
@@ -40,8 +40,14 @@
     return total
 
 
-def edge_rows_kernel(x1_ref, cot_ref, x2_ref, x3_ref, x4_ref, last_ref, first_ref, last, first):
-    x1, cot, x2, x3, x4 = (ref[...].astype(F32) for ref in (x1_ref, cot_ref, x2_ref, x3_ref, x4_ref))
+def in_hbm(x):
+    return pltpu.with_memory_space_constraint(x, pltpu.HBM)
+
+
+def edge_rows_kernel(last_ref, first_ref, last, first, near, copies):
+    for copy in copies:
+        copy.wait()
+    x1, cot, x2, x3, x4 = (ref[...].astype(F32) for ref in near)
     for out, ref, ones, cots, twos in (
         (last, last_ref, x1[5:8], cot[6:8], x2[1:4]),
         (first, first_ref, x1[0:3], cot[0:2], x2[0:3]),
@@ -56,13 +62,14 @@
 
 
 def halos(x1, x2, x3, x4, cot):
-    last, first = call(edge_rows_kernel, [((16, WIDE), BF)] * 2, [((16, WIDE), F32)] * 2, 5)(x1, cot, x2, x3, x4)
+    own = tuple(in_hbm(x) for x in (x1, cot, x2, x3, x4))
+    last, first = call(edge_rows_kernel, [((16, WIDE), BF)] * 2, [((16, WIDE), F32)] * 2, *own, far=5)
     above = moved(last, ROWS, 1)
     below = moved(first, ROWS, -1)
     parts = (x1, cot, x2, x3, x4, above[:11], below[:11])
     left = moved(stacked([p[:, -RIM:] for p in parts], 48), COLS, 1)
     right = moved(stacked([p[:, :RIM] for p in parts], 48), COLS, -1)
-    return x1, cot, x2, x3, x4, above, below, left, right
+    return own + (above, below, left, right)
 
 
 def gelu_both(v):
@@ -94,16 +101,11 @@
 
 
 def forward_kernel(
-    place_ref, p2, p3, p4, *refs
+    place_ref, keep_ref, send_ref, g1_ref, g2_ref, g3_ref, rim_ref, up_ref, down_ref,
+    wx1, wc, wx2, wx3, wx4, xw1, xw2, xw3, d1, d2, d3, gm1, gm2, gm3, sums, upward, downward,
+    near, copies,
 ):
-    far, refs = refs[:12], refs[12:]
-    keep_ref, send_ref, g1_ref, g2_ref, g3_ref, rim_ref, up_ref, down_ref = refs[:8]
-    wx1, wc, wx2, wx3, wx4, xw1, xw2, xw3, d1, d2, d3, gm1, gm2, gm3, sums, upward, downward = refs[8:25]
-    near, sems = refs[25:37], refs[37]
-    copies = [pltpu.make_async_copy(far[n], near[n], sems.at[n]) for n in range(12)]
-    for copy in copies:
-        copy.start()
-    x1, cot, x2, x3, x4, above, below, left, right, t1, k2, k3 = near
+    x1, cot, x2, x3, x4, above, below, left, right, t1, k2, k3, p2, p3, p4 = near
     row_block = place_ref[0]
     at_left = place_ref[1] == 0
     at_right = place_ref[2] == 1
@@ -188,6 +190,8 @@
 
     y4 = jnp.concatenate([wx4[:, 512 * c : 512 * c + 512] for c in range(12)], axis=0).astype(BF)
 
+    for copy in copies[12:]:
+        copy.wait()
     weights = row_weights((16, 32), 1, row_block).astype(BF)
     rows_up = []
     for y, p, rim, rows, wlo in ((y2, p2, 2, 16, 0), (y3, p3, 1, 8, 16), (y4, p4, 1, 8, 24)):
@@ -374,9 +378,10 @@
 
 
 def backward_kernel(
-    g1_ref, g2_ref, g3_ref, rim_ref, above_ref, below_ref, left_ref, right_ref, t1b, k2, k3, p4,
-    gf1_ref, gf2_ref, gf3_ref, gf4_ref, wide1, wide2, wide3, xw1, xw2, xw3, out2, out3,
+    g1_ref, g2_ref, g3_ref, rim_ref, above_ref, below_ref, left_ref, right_ref,
+    gf1_ref, gf2_ref, gf3_ref, gf4_ref, wide1, wide2, wide3, xw1, xw2, xw3, out2, out3, near, copies,
 ):
+    t1b, k2, k3, p4 = near
     low = lax.broadcasted_iota(jnp.int32, (1, 128), 1) < 64
     for ref, n in ((xw1, 640), (xw2, 320), (xw3, 160)):
         ref[0:8, :] = jnp.zeros((8, ref.shape[1]), F32)
@@ -393,6 +398,8 @@
         wide[top : top + 2 + rows, 0:step] = left[start : start + 2 + rows, 0:step]
         wide[top : top + 2 + rows, end : end + step] = right[start : start + 2 + rows, 0:step]
 
+    for copy in copies:
+        copy.wait()
     for f in range(40):
         at = 8 + 16 * f
         xw1[at : at + 16, 0:128] = tile(wide1, f + 1)
@@ -466,18 +473,33 @@
             n += 1
 
 
-def call(kernel, out_shapes, scratch, count, scalars=0, far=0):
-    vmem = pl.BlockSpec(memory_space=pltpu.VMEM)
-    smem = pl.BlockSpec(memory_space=pltpu.SMEM)
+def call(kernel, out_shapes, scratch, *operands, scalars=0, far=0):
+    near = len(operands) - scalars - far
+    specs = [pl.BlockSpec(memory_space=space) for space in (pltpu.SMEM, pltpu.VMEM, pl.ANY)]
+    outs = len(out_shapes)
+
+    def body(*refs):
+        first, last = scalars + near, scalars + near + far
+        sources = refs[first:last]
+        if far:
+            buffers, sems = refs[-1 - far : -1], refs[-1]
+            copies = [pltpu.make_async_copy(sources[n], buffers[n], sems.at[n]) for n in range(far)]
+            for copy in copies:
+                copy.start()
+            kernel(*refs[:first], *refs[last : -1 - far], buffers, copies)
+        else:
+            kernel(*refs)
+
     return pl.pallas_call(
-        kernel,
+        body,
         out_shape=[jax.ShapeDtypeStruct(shape, dtype) for shape, dtype in out_shapes],
-        in_specs=[smem] * scalars + [vmem] * count + [pl.BlockSpec(memory_space=pl.ANY)] * far,
-        out_specs=[vmem] * len(out_shapes),
+        in_specs=[specs[0]] * scalars + [specs[1]] * near + [specs[2]] * far,
+        out_specs=[specs[1]] * outs,
         scratch_shapes=[pltpu.VMEM(shape, dtype) for shape, dtype in scratch]
+        + [pltpu.VMEM(operand.shape, operand.dtype) for operand in operands[len(operands) - far :]]
         + ([pltpu.SemaphoreType.DMA((far,))] if far else []),
         compiler_params=pltpu.CompilerParams(vmem_limit_bytes=48 * 1024 * 1024),
-    )
+    )(*operands)
 
 
 def pair_weights(kernel_one):
@@ -503,9 +525,9 @@
         ]
     ).astype(jnp.int32)
     ahead, back = pair_weights(kernel_one)
-    k2 = kernel_two.reshape(3, 384, 128)
-    k3 = kernel_three.reshape(3, 768, 256)
-    fars = halos(x1, x2, x3, x4, cot) + (ahead, k2, k3)
+    k2 = in_hbm(kernel_two.reshape(3, 384, 128))
+    k3 = in_hbm(kernel_three.reshape(3, 768, 256))
+    fars = halos(x1, x2, x3, x4, cot) + (ahead, k2, k3, in_hbm(p2.T), in_hbm(p3.T), in_hbm(p4.T))
     total = RIM + WIDE + RIM
     keep, send, g1, g2, g3, rim, up, down = call(
         forward_kernel,
@@ -520,19 +542,19 @@
             ((672, 128), F32), ((704, 128), F32), ((176, 256), F32),
             ((656, 128), F32), ((656, 128), F32), ((176, 256), F32),
             ((PACK_ROWS, 256), F32), ((8, WIDE), F32), ((8, WIDE), F32),
-        ]
-        + [(far.shape, BF) for far in fars],
-        3,
-        1,
-        12,
-    )(place, p2.T, p3.T, p4.T, *fars)
-    return place, keep, send, (g1, g2, g3, rim), up, down, (back, k2, k3, p4.T)
+        ],
+        place,
+        *fars,
+        scalars=1,
+        far=15,
+    )
+    return place, keep, send, (g1, g2, g3, rim), up, down, (back, k2, k3, in_hbm(p4.T))
 
 
 def from_beside(grads, above, below):
     left, right = call(
-        rims_kernel, [((32, 256), BF), ((32, 256), BF)], [((32, 256), F32)], 6
-    )(*grads, above, below)
+        rims_kernel, [((32, 256), BF), ((32, 256), BF)], [((32, 256), F32)], *grads, above, below
+    )
     return moved(right, COLS, 1), moved(left, COLS, -1)
 
 
@@ -545,8 +567,10 @@
             ((656, 256), F32), ((336, 384), F32), ((176, 768), F32),
             ((320, 128), F32), ((160, 256), F32),
         ],
-        12,
-    )(*grads, above, below, left, right, *weights)
+        *grads, above, below, left, right,
+        *weights,
+        far=4,
+    )
 
 
 def unpacked(place, mine, got):
@@ -554,9 +578,9 @@
         unpack_kernel,
         [((576, 64), BF), ((1152, 128), BF), ((2304, 256), BF), ((64, 128), BF), ((64, 256), BF), ((64, 512), BF)],
         [((PACK_ROWS, 256), BF)],
-        2,
-        1,
-    )(place, mine, got)
+        place, mine, got,
+        scalars=1,
+    )
     return (
         outs[0].reshape(3, 3, 64, 64), outs[1].reshape(3, 3, 128, 128), outs[2].reshape(3, 3, 256, 256),
         outs[3].T, outs[4].T, outs[5].T,

time: 130 us -> 123 us (0.946)
  local copies, waits for them, and re-layouts: 11.6 us -> 5.47 us
  waiting for transfers between devices: 30 us -> 27.2 us
  Pallas kernels: 11.2 us -> 13.6 us
    unnamed x32 -> x0, local copies, waits for them, and re-layouts: 8.92 us -> none
    slice x6, local copies, waits for them, and re-layouts: 0.03 us -> 2.88 us  [halos(): right = moved(stacked([p[:, :RIM] for p in parts], 48), COLS, -1)]
    ppermute x8, waiting for transfers between devices: 13.3 us -> 10.5 us  [moved(): return lax.ppermute(block, axis, route)]
    pallas_call x5, Pallas kernels: 11.2 us -> 13.6 us  [call(): pl.pallas_call(body, out_shape=[jax.ShapeDtypeStruct(shape, dtype) for sh...]
  transfers between devices with their start and end apart: 12 -> 12, of which waited for: 6 -> 6; matrix products, arithmetic and copies ran while one was open for 1% -> 3% of each run, Pallas kernels for 1% -> 3%
where the time goes in v6:
time: 123 us; the launch traced here: 122 us
  starting transfers between devices  51.1 us (42%)
  waiting for transfers between devices  27.2 us (22%)
  blocking collectives  23.5 us (19%)
  Pallas kernels  13.6 us (11%)
  local copies, waits for them, and re-layouts  5.47 us (4%)
    ppermute x8, starting transfers between devices, moved(): return lax.ppermute(block, axis, route)  27.7 us
    all_to_all x1, blocking collectives, on_device(): pieces = lax.all_to_all(part.reshape(32, -1, 128), SLAB, 0, 0)  23.5 us
    pallas_call x5, Pallas kernels, call(): pl.pallas_call(body, out_shape=[jax.ShapeDtypeStruct(shape, dtype) for sh...  13.6 us
    all_to_all x1, starting transfers between devices, on_device(): lax.all_to_all(jnp.broadcast_to(part[None], (8,) + part.shape), 'z_hi', 0...  13.3 us
    all_to_all x1, waiting for transfers between devices, on_device(): lax.all_to_all(jnp.broadcast_to(part[None], (8,) + part.shape), 'z_hi', 0...  12 us
    ppermute x8, waiting for transfers between devices, moved(): return lax.ppermute(block, axis, route)  10.5 us
    all_to_all x1, starting transfers between devices, on_device(): mine = lax.all_to_all(pieces, SLAB, 0, 0).reshape(keep.shape)  6.21 us
    ppermute x2, waiting for transfers between devices, swapped(): lax.ppermute(block, axis, [(i, i ^ flip) for i in range(lax.axis_size(axi...  4.69 us
  transfers between devices with their start and end apart: 12, of which 6 were waited for; matrix products, arithmetic and copies ran while one was open for 3% of the time, Pallas kernels for 3%

profile of v6, /device:TPU:1, one launch (start us, length us, event | category | flops | bytes accessed | tf_op | source)
XLA Modules:
  0.0 122.4 jit_solution(9760106590080302130)
XLA Ops:
  0.6 1.2 shard_map.186
  1.8 4.0 %collective-permute-start = (bf16[16,5120]{1,0:T(8,128)(2,1)S(1)}, bf16[16,5120]{1,0:T(8,128)(2,1)S(1)}, u32[]{:S(2)}, u32[]{:S(2)}) collective-permute-start(bf16[16,5120]{1,0:T(8,128)(2,1)S(1)} %get-tuple-element.43), channel_id=1, source_target_pairs={{0,4},{4,8},{8,12},{12,16},{16,20},{20,24},{24,28},{28,32},{32,36}... | collective-permute-start | bytes 491528 | tf_op jit(solution)/shard_map/ppermute | solution.py:31
  5.9 1.3 %collective-permute-start.1 = (bf16[16,5120]{1,0:T(8,128)(2,1)S(1)}, bf16[16,5120]{1,0:T(8,128)(2,1)S(1)}, u32[]{:S(2)}, u32[]{:S(2)}) collective-permute-start(bf16[16,5120]{1,0:T(8,128)(2,1)S(1)} %get-tuple-element.44), channel_id=1, source_target_pairs={{4,0},{8,4},{12,8},{16,12},{20,16},{24,20},{28,24},{32,28},{36,32}... | collective-permute-start | bytes 491528 | tf_op jit(solution)/shard_map/ppermute | solution.py:31
  7.2 0.7 fusion.10
  7.9 0.7 fusion.9
  8.6 0.7 fusion.7
  9.3 0.9 slice_bitcast_fusion
  10.2 0.7 fusion.11
  11.1 0.9 collective-permute-done.1.refs_7_
  12.0 7.0 %collective-permute-start.2 = (bf16[48,512]{1,0:T(8,128)(2,1)S(1)}, bf16[48,512]{1,0:T(8,128)(2,1)S(1)}, u32[]{:S(2)}, u32[]{:S(2)}) collective-permute-start(bf16[48,512]{1,0:T(8,128)(2,1)S(1)} %pad_add_fusion.1), channel_id=1, source_target_pairs={{0,1},{1,2},{2,3},{4,5},{5,6},{6,7},{8,9},{9,10},{10,11},{12,13},{... | collective-permute-start | bytes 147464 | tf_op jit(solution)/shard_map/ppermute | solution.py:31
  19.0 1.9 %collective-permute-start.3 = (bf16[48,512]{1,0:T(8,128)(2,1)S(1)}, bf16[48,512]{1,0:T(8,128)(2,1)S(1)}, u32[]{:S(2)}, u32[]{:S(2)}) collective-permute-start(bf16[48,512]{1,0:T(8,128)(2,1)S(1)} %pad_add_fusion), channel_id=1, source_target_pairs={{1,0},{2,1},{3,2},{5,4},{6,5},{7,6},{9,8},{10,9},{11,10},{13,12},{... | collective-permute-start | bytes 147464 | tf_op jit(solution)/shard_map/ppermute | solution.py:31
  21.0 4.9 %collective-permute-done.3.refs_9_ = bf16[48,512]{1,0:T(8,128)(2,1)S(1)} collective-permute-done((bf16[48,512]{1,0:T(8,128)(2,1)S(1)}, bf16[48,512]{1,0:T(8,128)(2,1)S(1)}, u32[]{:S(2)}, u32[]{:S(2)}) %collective-permute-start.3) | collective-permute-done | bytes 49184 | tf_op jit(solution)/shard_map/ppermute | solution.py:31
  25.9 6.8 %shard_map.187 = (bf16[3328,128]{1,0:T(8,128)(2,1)S(1)}, bf16[3328,128]{1,0:T(8,128)(2,1)S(1)}, bf16[8,5120]{1,0:T(8,128)(2,1)S(1)}, bf16[4,5120]{1,0:T(4,128)(2...) custom-call(s32[4]{0:T(128)S(1)} %pad_add_fusion.2.refs_0_, ...), custom_call_target="tpu_custom_call" | custom-call | tf_op jit(solution)/shard_map/pallas_call | solution.py:493
  32.7 1.9 %collective-permute-start.4 = (bf16[3328,128]{1,0:T(8,128)(2,1)S(1)}, bf16[3328,128]{1,0:T(8,128)(2,1)S(1)}, u32[]{:S(2)}, u32[]{:S(2)}) collective-permute-start(bf16[3328,128]{1,0:T(8,128)(2,1)S(1)} %get-tuple-element.46), channel_id=1, source_target_pairs={{0,1},{1,0},{2,3},{3,2},{4,5},{5,4},{6,7},{7,6},{8,9},{9,8},{10,11... | collective-permute-start | bytes 2555912 | tf_op jit(solution)/shard_map/ppermute | solution.py:455
  34.6 2.3 %collective-permute-done.4 = bf16[3328,128]{1,0:T(8,128)(2,1)S(1)} collective-permute-done((bf16[3328,128]{1,0:T(8,128)(2,1)S(1)}, bf16[3328,128]{1,0:T(8,128)(2,1)S(1)}, u32[]{:S(2)}, u32[]{:S(2)}) %collective-permute-start.4) | collective-permute-done | bytes 852000 | tf_op jit(solution)/shard_map/ppermute | solution.py:455
  37.0 0.2 add_convert_fusion
  37.2 23.5 %all_to_all.15 = bf16[32,104,128]{2,1,0:T(8,128)(2,1)S(1)} all-to-all(bf16[32,104,128]{2,1,0:T(8,128)(2,1)S(1)} %bitcast.33), channel_id=1, replica_groups=mesh['z_hi'=8,'z_lo'=2,'x_lo'=2,'y'=4,'x_hi'=2,'core'=2] {'z_lo','x_lo',..., dimensions={0} | all-to-all | bytes 1703936 | tf_op jit(solution)/shard_map/all_to_all | solution.py:595
  60.8 0.7 broadcast_in_dim.7
  61.5 13.3 %all-to-all-start.1 = ((bf16[8,104,128]{2,1,0:T(8,128)(2,1)}), bf16[8,104,128]{2,1,0:T(8,128)(2,1)S(1)}, u32[]{:S(2)}, u32[]{:S(2)}) async-start(bf16[8,104,128]{2,1,0:T(8,128)(2,1)} %broadcast_in_dim.7), calls=%async_computation.1 | async-start | bytes 425984 | tf_op jit(solution)/shard_map/all_to_all | solution.py:599
  74.9 2.5 %collective-permute-start.5 = (bf16[8,5120]{1,0:T(8,128)(2,1)S(1)}, bf16[8,5120]{1,0:T(8,128)(2,1)S(1)}, u32[]{:S(2)}, u32[]{:S(2)}) collective-permute-start(bf16[8,5120]{1,0:T(8,128)(2,1)S(1)} %get-tuple-element.50), channel_id=1, source_target_pairs={{0,4},{4,8},{8,12},{12,16},{16,20},{20,24},{24,28},{28,32},{32,36}... | collective-permute-start | bytes 245768 | tf_op jit(solution)/shard_map/ppermute | solution.py:31
  77.4 1.3 %collective-permute-start.6 = (bf16[8,5120]{1,0:T(8,128)(2,1)S(1)}, bf16[8,5120]{1,0:T(8,128)(2,1)S(1)}, u32[]{:S(2)}, u32[]{:S(2)}) collective-permute-start(bf16[8,5120]{1,0:T(8,128)(2,1)S(1)} %get-tuple-element.51), channel_id=1, source_target_pairs={{4,0},{8,4},{12,8},{16,12},{20,16},{24,20},{28,24},{32,28},{36,32}... | collective-permute-start | bytes 245768 | tf_op jit(solution)/shard_map/ppermute | solution.py:31
  78.7 12.0 %all-to-all-done.1 = bf16[8,104,128]{2,1,0:T(8,128)(2,1)S(1)} async-done(((bf16[8,104,128]{2,1,0:T(8,128)(2,1)}), bf16[8,104,128]{2,1,0:T(8,128)(2,1)S(1)}, u32[]{:S(2)}, u32[]{:S(2)}) %all-to-all-start.1) | async-done | bytes 213024 | tf_op jit(solution)/shard_map/all_to_all | solution.py:599
  90.7 1.0 broadcast_in_dim.8
  91.7 6.2 %all-to-all-start.2 = ((bf16[32,104,128]{2,1,0:T(8,128)(2,1)}), bf16[32,104,128]{2,1,0:T(8,128)(2,1)S(1)}, u32[]{:S(2)}, u32[]{:S(2)}) async-start(bf16[32,104,128]{2,1,0:T(8,128)(2,1)} %broadcast_in_dim.8), calls=%async_computation.2 | async-start | bytes 1703936 | tf_op jit(solution)/shard_map/all_to_all | solution.py:604
  98.0 7.8 %collective-permute-start.7 = (bf16[32,256]{1,0:T(8,128)(2,1)S(1)}, bf16[32,256]{1,0:T(8,128)(2,1)S(1)}, u32[]{:S(2)}, u32[]{:S(2)}) collective-permute-start(bf16[32,256]{1,0:T(8,128)(2,1)S(1)} %get-tuple-element.59), channel_id=1, source_target_pairs={{0,1},{1,2},{2,3},{4,5},{5,6},{6,7},{8,9},{9,10},{10,11},{12,13},{... | collective-permute-start | bytes 49160 | tf_op jit(solution)/shard_map/ppermute | solution.py:31
  105.7 1.9 %collective-permute-start.8 = (bf16[32,256]{1,0:T(8,128)(2,1)S(1)}, bf16[32,256]{1,0:T(8,128)(2,1)S(1)}, u32[]{:S(2)}, u32[]{:S(2)}) collective-permute-start(bf16[32,256]{1,0:T(8,128)(2,1)S(1)} %get-tuple-element.60), channel_id=1, source_target_pairs={{1,0},{2,1},{3,2},{5,4},{6,5},{7,6},{9,8},{10,9},{11,10},{13,12},{... | collective-permute-start | bytes 49160 | tf_op jit(solution)/shard_map/ppermute | solution.py:31
  107.7 0.1 fusion.4.refs_8_
  107.8 4.8 %collective-permute-done.8.refs_7_ = bf16[32,256]{1,0:T(8,128)(2,1)S(1)} collective-permute-done((bf16[32,256]{1,0:T(8,128)(2,1)S(1)}, bf16[32,256]{1,0:T(8,128)(2,1)S(1)}, u32[]{:S(2)}, u32[]{:S(2)}) %collective-permute-start.8) | collective-permute-done | bytes 16416 | tf_op jit(solution)/shard_map/ppermute | solution.py:31
  112.6 3.4 %shard_map.189 = (bf16[8,5120]{1,0:T(8,128)(2,1)}, bf16[4,5120]{1,0:T(4,128)(2,1)}, bf16[2,5120]{1,0:T(2,128)(2,1)}, bf16[1,5120]{1,0:T(2,128)(2,1)}) custom-call(bf16[8,5120]{1,0:T(8,128)(2,1)S(1)} %get-tuple-element.53.refs_0_, bf16[4,5120]{1,0:T(4,128)(2,1)S(1)} %get-tuple-element.54.refs_1_, bf16[2,5120]{1,0:T(2,128)(2,1)S(1)} %get-tuple-element.55.refs_2_, ...), custom_call_target="tpu_custom_call" | custom-call | tf_op jit(solution)/shard_map/pallas_call | solution.py:493
  116.0 1.9 %collective-permute-start.9 = (bf16[3328,128]{1,0:T(8,128)(2,1)S(1)}, bf16[3328,128]{1,0:T(8,128)(2,1)S(1)}, u32[]{:S(2)}, u32[]{:S(2)}) collective-permute-start(bf16[3328,128]{1,0:T(8,128)(2,1)S(1)} %bitcast.29), channel_id=1, source_target_pairs={{0,1},{1,0},{2,3},{3,2},{4,5},{5,4},{6,7},{7,6},{8,9},{9,8},{10,11... | collective-permute-start | bytes 2555912 | tf_op jit(solution)/shard_map/ppermute | solution.py:455
  117.9 2.3 %collective-permute-done.9.refs_2_ = bf16[3328,128]{1,0:T(8,128)(2,1)S(1)} collective-permute-done((bf16[3328,128]{1,0:T(8,128)(2,1)S(1)}, bf16[3328,128]{1,0:T(8,128)(2,1)S(1)}, u32[]{:S(2)}, u32[]{:S(2)}) %collective-permute-start.9) | collective-permute-done | bytes 852000 | tf_op jit(solution)/shard_map/ppermute | solution.py:455
  120.2 2.2 %shard_map.190 = (bf16[576,64]{1,0:T(8,128)(2,1)}, bf16[1152,128]{1,0:T(8,128)(2,1)}, bf16[2304,256]{1,0:T(8,128)(2,1)}, bf16[64,128]{1,0:T(8,128)(2,1)}, bf16[6...) custom-call(s32[4]{0:T(128)S(1)} %pad_add_fusion.2.refs_0_, bf16[3328,128]{1,0:T(8,128)(2,1)S(1)} %bitcast.30, ...), custom_call_target="tpu_custom_call" | custom-call | tf_op jit(solution)/shard_map/pallas_call | solution.py:493
  (16 shorter events, 0.5 us)
Async XLA Ops:
  1.8 9.2 %collective-permute-start = (bf16[16,5120]{1,0:T(8,128)(2,1)S(1)}, bf16[16,5120]{1,0:T(8,128)(2,1)S(1)}, u32[]{:S(2)}, u32[]{:S(2)}) collective-permute-start(bf16[16,5120]{1,0:T(8,128)(2,1)S(1)} %get-tuple-element.43), channel_id=1, source_target_pairs={{0,4},{4,8},{8,12},{12,16},{16,20},{20,24},{24,28},{28,32},{32,36}... | collective-permute-start | bytes 491528 | tf_op jit(solution)/shard_map/ppermute | solution.py:31
  5.9 6.1 %collective-permute-start.1 = (bf16[16,5120]{1,0:T(8,128)(2,1)S(1)}, bf16[16,5120]{1,0:T(8,128)(2,1)S(1)}, u32[]{:S(2)}, u32[]{:S(2)}) collective-permute-start(bf16[16,5120]{1,0:T(8,128)(2,1)S(1)} %get-tuple-element.44), channel_id=1, source_target_pairs={{4,0},{8,4},{12,8},{16,12},{20,16},{24,20},{28,24},{32,28},{36,32}... | collective-permute-start | bytes 491528 | tf_op jit(solution)/shard_map/ppermute | solution.py:31
  12.0 9.0 %collective-permute-start.2 = (bf16[48,512]{1,0:T(8,128)(2,1)S(1)}, bf16[48,512]{1,0:T(8,128)(2,1)S(1)}, u32[]{:S(2)}, u32[]{:S(2)}) collective-permute-start(bf16[48,512]{1,0:T(8,128)(2,1)S(1)} %pad_add_fusion.1), channel_id=1, source_target_pairs={{0,1},{1,2},{2,3},{4,5},{5,6},{6,7},{8,9},{9,10},{10,11},{12,13},{... | collective-permute-start | bytes 147464 | tf_op jit(solution)/shard_map/ppermute | solution.py:31
  19.0 6.9 %collective-permute-start.3 = (bf16[48,512]{1,0:T(8,128)(2,1)S(1)}, bf16[48,512]{1,0:T(8,128)(2,1)S(1)}, u32[]{:S(2)}, u32[]{:S(2)}) collective-permute-start(bf16[48,512]{1,0:T(8,128)(2,1)S(1)} %pad_add_fusion), channel_id=1, source_target_pairs={{1,0},{2,1},{3,2},{5,4},{6,5},{7,6},{9,8},{10,9},{11,10},{13,12},{... | collective-permute-start | bytes 147464 | tf_op jit(solution)/shard_map/ppermute | solution.py:31
  32.7 4.3 %collective-permute-start.4 = (bf16[3328,128]{1,0:T(8,128)(2,1)S(1)}, bf16[3328,128]{1,0:T(8,128)(2,1)S(1)}, u32[]{:S(2)}, u32[]{:S(2)}) collective-permute-start(bf16[3328,128]{1,0:T(8,128)(2,1)S(1)} %get-tuple-element.46), channel_id=1, source_target_pairs={{0,1},{1,0},{2,3},{3,2},{4,5},{5,4},{6,7},{7,6},{8,9},{9,8},{10,11... | collective-permute-start | bytes 2555912 | tf_op jit(solution)/shard_map/ppermute | solution.py:455
  61.5 29.1 %all-to-all-start.1 = ((bf16[8,104,128]{2,1,0:T(8,128)(2,1)}), bf16[8,104,128]{2,1,0:T(8,128)(2,1)S(1)}, u32[]{:S(2)}, u32[]{:S(2)}) async-start(bf16[8,104,128]{2,1,0:T(8,128)(2,1)} %broadcast_in_dim.7), calls=%async_computation.1 | async-start | bytes 425984 | tf_op jit(solution)/shard_map/all_to_all | solution.py:599
  74.9 15.8 %collective-permute-start.5 = (bf16[8,5120]{1,0:T(8,128)(2,1)S(1)}, bf16[8,5120]{1,0:T(8,128)(2,1)S(1)}, u32[]{:S(2)}, u32[]{:S(2)}) collective-permute-start(bf16[8,5120]{1,0:T(8,128)(2,1)S(1)} %get-tuple-element.50), channel_id=1, source_target_pairs={{0,4},{4,8},{8,12},{12,16},{16,20},{20,24},{24,28},{28,32},{32,36}... | collective-permute-start | bytes 245768 | tf_op jit(solution)/shard_map/ppermute | solution.py:31
  77.4 13.3 %collective-permute-start.6 = (bf16[8,5120]{1,0:T(8,128)(2,1)S(1)}, bf16[8,5120]{1,0:T(8,128)(2,1)S(1)}, u32[]{:S(2)}, u32[]{:S(2)}) collective-permute-start(bf16[8,5120]{1,0:T(8,128)(2,1)S(1)} %get-tuple-element.51), channel_id=1, source_target_pairs={{4,0},{8,4},{12,8},{16,12},{20,16},{24,20},{28,24},{32,28},{36,32}... | collective-permute-start | bytes 245768 | tf_op jit(solution)/shard_map/ppermute | solution.py:31
  91.7 24.2 %all-to-all-start.2 = ((bf16[32,104,128]{2,1,0:T(8,128)(2,1)}), bf16[32,104,128]{2,1,0:T(8,128)(2,1)S(1)}, u32[]{:S(2)}, u32[]{:S(2)}) async-start(bf16[32,104,128]{2,1,0:T(8,128)(2,1)} %broadcast_in_dim.8), calls=%async_computation.2 | async-start | bytes 1703936 | tf_op jit(solution)/shard_map/all_to_all | solution.py:604
  98.0 9.8 %collective-permute-start.7 = (bf16[32,256]{1,0:T(8,128)(2,1)S(1)}, bf16[32,256]{1,0:T(8,128)(2,1)S(1)}, u32[]{:S(2)}, u32[]{:S(2)}) collective-permute-start(bf16[32,256]{1,0:T(8,128)(2,1)S(1)} %get-tuple-element.59), channel_id=1, source_target_pairs={{0,1},{1,2},{2,3},{4,5},{5,6},{6,7},{8,9},{9,10},{10,11},{12,13},{... | collective-permute-start | bytes 49160 | tf_op jit(solution)/shard_map/ppermute | solution.py:31
  105.7 6.9 %collective-permute-start.8 = (bf16[32,256]{1,0:T(8,128)(2,1)S(1)}, bf16[32,256]{1,0:T(8,128)(2,1)S(1)}, u32[]{:S(2)}, u32[]{:S(2)}) collective-permute-start(bf16[32,256]{1,0:T(8,128)(2,1)S(1)} %get-tuple-element.60), channel_id=1, source_target_pairs={{1,0},{2,1},{3,2},{5,4},{6,5},{7,6},{9,8},{10,9},{11,10},{13,12},{... | collective-permute-start | bytes 49160 | tf_op jit(solution)/shard_map/ppermute | solution.py:31
  116.0 4.3 %collective-permute-start.9 = (bf16[3328,128]{1,0:T(8,128)(2,1)S(1)}, bf16[3328,128]{1,0:T(8,128)(2,1)S(1)}, u32[]{:S(2)}, u32[]{:S(2)}) collective-permute-start(bf16[3328,128]{1,0:T(8,128)(2,1)S(1)} %bitcast.29), channel_id=1, source_target_pairs={{0,1},{1,0},{2,3},{3,2},{4,5},{5,4},{6,7},{7,6},{8,9},{9,8},{10,11... | collective-permute-start | bytes 2555912 | tf_op jit(solution)/shard_map/ppermute | solution.py:455

commit v7 on v6

--- a/solution.py
+++ b/solution.py
@@ -44,7 +44,7 @@
     return pltpu.with_memory_space_constraint(x, pltpu.HBM)
 
 
-def edge_rows_kernel(last_ref, first_ref, last, first, near, copies):
+def edge_kernel(last_ref, first_ref, right_ref, left_ref, last, first, edge, near, copies):
     for copy in copies:
         copy.wait()
     x1, cot, x2, x3, x4 = (ref[...].astype(F32) for ref in near)
@@ -59,16 +59,29 @@
         out[10:11, :] = x4
         out[11:16, :] = jnp.zeros((5, WIDE), F32)
         ref[...] = out[...].astype(BF)
+    edge[...] = jnp.zeros_like(edge)
+    for ref, cols in ((right_ref, slice(WIDE - RIM, WIDE)), (left_ref, slice(0, RIM))):
+        edge[0:8, :] = x1[:, cols]
+        edge[8:16, :] = cot[:, cols]
+        edge[16:20, :] = x2[:, cols]
+        edge[20:22, :] = x3[:, cols]
+        edge[22:23, :] = x4[:, cols]
+        ref[...] = edge[...].astype(BF)
 
 
 def halos(x1, x2, x3, x4, cot):
     own = tuple(in_hbm(x) for x in (x1, cot, x2, x3, x4))
-    last, first = call(edge_rows_kernel, [((16, WIDE), BF)] * 2, [((16, WIDE), F32)] * 2, *own, far=5)
+    last, first, right_edge, left_edge = call(
+        edge_kernel,
+        [((16, WIDE), BF), ((16, WIDE), BF), ((24, RIM), BF), ((24, RIM), BF)],
+        [((16, WIDE), F32), ((16, WIDE), F32), ((24, RIM), F32)],
+        *own,
+        far=5,
+    )
     above = moved(last, ROWS, 1)
     below = moved(first, ROWS, -1)
-    parts = (x1, cot, x2, x3, x4, above[:11], below[:11])
-    left = moved(stacked([p[:, -RIM:] for p in parts], 48), COLS, 1)
-    right = moved(stacked([p[:, :RIM] for p in parts], 48), COLS, -1)
+    left = moved(stacked((right_edge, above[:11, -RIM:], below[:11, -RIM:]), 48), COLS, 1)
+    right = moved(stacked((left_edge, above[:11, :RIM], below[:11, :RIM]), 48), COLS, -1)
     return own + (above, below, left, right)
 
 
@@ -102,7 +115,7 @@
 
 def forward_kernel(
     place_ref, keep_ref, send_ref, g1_ref, g2_ref, g3_ref, rim_ref, up_ref, down_ref,
-    wx1, wc, wx2, wx3, wx4, xw1, xw2, xw3, d1, d2, d3, gm1, gm2, gm3, sums, upward, downward,
+    wx1, wc, wx2, wx3, wx4, xw1, xw2, xw3, d1, d2, d3, gm1, gm2, gm3, upward, downward,
     near, copies,
 ):
     x1, cot, x2, x3, x4, above, below, left, right, t1, k2, k3, p2, p3, p4 = near
@@ -129,7 +142,7 @@
             cols = slice(to, to + RIM)
             v = side[...].astype(F32)
             mid = [v[0:8], v[8:16], v[16:20], v[20:22], v[22:23]]
-            up, down = v[23:34], v[34:45]
+            up, down = v[24:35], v[35:46]
         wx1[1:4, cols] = up[0:3]
         wx1[4:12, cols] = mid[0]
         wx1[12:15, cols] = down[0:3]
@@ -311,23 +324,26 @@
         g3_ref[:, cols] = gm3[at : at + 2, :].astype(BF)
         upward[2:3, cols] = gm3[at : at + 1, :]
         downward[2:3, cols] = gm3[at + 1 : at + 2, :]
-    up_ref[...] = upward[...].astype(BF)
-    down_ref[...] = downward[...].astype(BF)
+    up_ref[...] = upward[0:4, :].astype(BF)
+    down_ref[...] = downward[0:4, :].astype(BF)
+
+    def put(at, first, second):
+        rows = slice(at, at + first.shape[0])
+        keep_ref[rows, :] = jnp.where(core == 0, first, second).astype(BF)
+        send_ref[rows, :] = jnp.where(core == 0, second, first).astype(BF)
 
     cells = 327680
     x = xw3[16:176, :].astype(BF)
     shifted = jnp.concatenate([gm3[9 - i : 169 - i, :] for i in range(3)], axis=1).astype(BF)
     z = lax.dot_general(x, shifted, TN, preferred_element_type=F32) * (cells // 16) ** -0.5
     for i in range(3):
-        sums[768 * i : 768 * (i + 1), :] = z[:, 256 * i : 256 * (i + 1)]
+        put(768 * i, z[:, 256 * i : 256 * i + 128], z[:, 256 * i + 128 : 256 * i + 256])
     x = xw2[40:680, :].astype(BF)
     shifted = jnp.concatenate([gm2[9 - i : 649 - i, :] for i in range(3)], axis=1).astype(BF)
     z = lax.dot_general(x, shifted, TN, preferred_element_type=F32) * (cells // 4) ** -0.5
-    base = 2304
-    sums[base : base + 384, 0:128] = z[:, 0:128]
-    sums[base + 384 : base + 576, 0:128] = z[0:192, 128:256]
-    sums[base : base + 192, 128:256] = z[192:384, 128:256]
-    sums[base + 192 : base + 576, 128:256] = z[:, 256:384]
+    put(2304, z[0:192, 0:128], z[192:384, 128:256])
+    put(2496, z[192:384, 0:128], z[0:192, 256:384])
+    put(2688, z[0:192, 128:256], z[192:384, 256:384])
     x = xw1[24:664, :].astype(BF)
     shifted = jnp.concatenate([gm1[9 - i : 649 - i, :] for i in range(3)], axis=1).astype(BF)
     z = lax.dot_general(x, shifted, TN, preferred_element_type=F32) * cells**-0.5
@@ -349,13 +365,9 @@
         masked = (flat if mask is None else jnp.where(mask, flat, 0.0)).astype(BF)
         z = lax.dot_general(masked, y, TN, preferred_element_type=F32) * (cells // 4**branch) ** -0.5
         pairs += [z[0:64, 128 * n : 128 * (n + 1)] for n in range(z.shape[1] // 128)]
-    base = 2880
-    for n in range(12):
-        at, side = base + 64 * (n // 2), 128 * (n % 2)
-        sums[at : at + 64, side : side + 128] = pairs[n]
-    sums[3264:3328, :] = jnp.zeros((64, 256), F32)
-    keep_ref[...] = jnp.where(core == 0, sums[:, 0:128], sums[:, 128:256]).astype(BF)
-    send_ref[...] = jnp.where(core == 0, sums[:, 128:256], sums[:, 0:128]).astype(BF)
+    for n in range(6):
+        put(2880 + 64 * n, pairs[2 * n], pairs[2 * n + 1])
+    put(3264, jnp.zeros((64, 128), F32), jnp.zeros((64, 128), F32))
 
 
 def rims_kernel(g1_ref, g2_ref, g3_ref, rim_ref, above_ref, below_ref, left_ref, right_ref, out):
@@ -455,21 +467,24 @@
     return lax.ppermute(block, axis, [(i, i ^ flip) for i in range(lax.axis_size(axis))])
 
 
-def unpack_kernel(place_ref, mine, got, k1_ref, k2_ref, k3_ref, p2_ref, p3_ref, p4_ref, whole):
+def unpack_kernel(place_ref, mine, got, k1_ref, k2_ref, k3_ref, p2_ref, p3_ref, p4_ref):
     core = place_ref[3]
-    whole[:, 0:128] = jnp.where(core == 0, mine[...], got[...])
-    whole[:, 128:256] = jnp.where(core == 0, got[...], mine[...])
-    k3_ref[...] = whole[0:2304, :]
-    k2_ref[0:576, :] = whole[2304:2880, 0:128]
-    k2_ref[576:1152, :] = whole[2304:2880, 128:256]
+
+    def take(side, at, count):
+        rows = slice(at, at + count)
+        return jnp.where(core == side, mine[rows, :], got[rows, :])
+
+    k3_ref[:, 0:128] = take(0, 0, 2304)
+    k3_ref[:, 128:256] = take(1, 0, 2304)
+    k2_ref[0:576, :] = take(0, 2304, 576)
+    k2_ref[576:1152, :] = take(1, 2304, 576)
+    pairs = [take(n % 2, 2880 + 64 * (n // 2), 64) for n in range(12)]
     for n in range(9):
-        at, side = 2880 + 64 * (n // 4), 64 * (n % 4)
-        k1_ref[64 * n : 64 * (n + 1), :] = whole[at : at + 64, side : side + 64]
+        k1_ref[64 * n : 64 * (n + 1), :] = pairs[n // 2][:, 64 * (n % 2) : 64 * (n % 2) + 64]
     n = 5
     for ref, count in ((p2_ref, 1), (p3_ref, 2), (p4_ref, 4)):
         for m in range(count):
-            at, side = 2880 + 64 * (n // 2), 128 * (n % 2)
-            ref[:, 128 * m : 128 * (m + 1)] = whole[at : at + 64, side : side + 128]
+            ref[:, 128 * m : 128 * (m + 1)] = pairs[n]
             n += 1
 
 
@@ -534,14 +549,14 @@
         [
             ((PACK_ROWS, 128), BF), ((PACK_ROWS, 128), BF),
             ((8, WIDE), BF), ((4, WIDE), BF), ((2, WIDE), BF), ((1, 1536), F32),
-            ((8, WIDE), BF), ((8, WIDE), BF),
+            ((4, WIDE), BF), ((4, WIDE), BF),
         ],
         [
             ((16, total), F32), ((16, total), F32), ((16, total), F32), ((8, total), F32), ((8, total), F32),
             ((688, 256), F32), ((720, 384), F32), ((192, 768), F32),
             ((672, 128), F32), ((704, 128), F32), ((176, 256), F32),
             ((656, 128), F32), ((656, 128), F32), ((176, 256), F32),
-            ((PACK_ROWS, 256), F32), ((8, WIDE), F32), ((8, WIDE), F32),
+            ((8, WIDE), F32), ((8, WIDE), F32),
         ],
         place,
         *fars,
@@ -577,7 +592,7 @@
     outs = call(
         unpack_kernel,
         [((576, 64), BF), ((1152, 128), BF), ((2304, 256), BF), ((64, 128), BF), ((64, 256), BF), ((64, 512), BF)],
-        [((PACK_ROWS, 256), BF)],
+        [],
         place, mine, got,
         scalars=1,
     )
@@ -594,15 +609,16 @@
 
     pieces = lax.all_to_all(part.reshape(32, -1, 128), SLAB, 0, 0)
     above, below = moved(down, ROWS, 1), moved(up, ROWS, -1)
+    pieces, above, below = lax.optimization_barrier((pieces, above, below))
     part = jnp.sum(pieces.astype(F32), axis=0).astype(BF)
 
     pieces = lax.all_to_all(jnp.broadcast_to(part[None], (8,) + part.shape), "z_hi", 0, 0)
+    left, right = from_beside(grads, above, below)
+    pieces, left, right = lax.optimization_barrier((pieces, left, right))
     part = jnp.sum(pieces.astype(F32), axis=0).astype(BF)
-    part, above, below = lax.optimization_barrier((part, above, below))
 
     pieces = jnp.broadcast_to(part[None], (32,) + part.shape)
     mine = lax.all_to_all(pieces, SLAB, 0, 0).reshape(keep.shape)
-    left, right = from_beside(grads, above, below)
     outs = input_grads(grads, above, below, left, right, weights)
     mine, outs = lax.optimization_barrier((mine, outs))
     return tuple(outs) + unpacked(place, mine, swapped(mine, "core", 1))

time: 123 us -> 122 us (level)
  blocking collectives: 23.5 us -> 0 us
  waiting for transfers between devices: 27.2 us -> 42.3 us
  starting transfers between devices: 51.1 us -> 60.9 us
  local copies, waits for them, and re-layouts: 5.47 us -> 2.6 us
    all_to_all x1 -> x0, blocking collectives: 23.5 us -> none  [on_device(): pieces = lax.all_to_all(part.reshape(32, -1, 128), SLAB, 0, 0)]
    ppermute x8, waiting for transfers between devices: 10.5 us -> 20.6 us  [moved(): return lax.ppermute(block, axis, route)]
    all_to_all x1, waiting for transfers between devices: 0.01 us -> 9.83 us  [on_device(): mine = lax.all_to_all(pieces, SLAB, 0, 0).reshape(keep.shape)]
    all_to_all x0 -> x1, starting transfers between devices: none -> 9.05 us  [on_device(): pieces = lax.all_to_all(part.reshape(32, -1, 128), SLAB, 0, 0)]
    all_to_all x1, waiting for transfers between devices: 12 us -> 4.42 us  [on_device(): lax.all_to_all(jnp.broadcast_to(part[None], (8,) + part.shape), 'z_hi', 0...]
    all_to_all x0 -> x1, waiting for transfers between devices: none -> 3.08 us  [on_device(): pieces = lax.all_to_all(part.reshape(32, -1, 128), SLAB, 0, 0)]
    ppermute x2, starting transfers between devices: 3.84 us -> 6.88 us  [swapped(): lax.ppermute(block, axis, [(i, i ^ flip) for i in range(lax.axis_size(axi...]
    slice x6 -> x2, local copies, waits for them, and re-layouts: 2.88 us -> 0.01 us  [the longest x1 0.01 us: halos(): above[:11, :RIM]]
  transfers between devices with their start and end apart: 12 -> 13, of which waited for: 6 -> 9; matrix products, arithmetic and copies ran while one was open for 3% -> 1% of each run, Pallas kernels for 3% -> 3%
where the time goes in v7:
time: 122 us
  starting transfers between devices  60.9 us (50%)
  waiting for transfers between devices  42.3 us (35%)
  Pallas kernels  13.4 us (11%)
  local copies, waits for them, and re-layouts  2.6 us (2%)
  other arithmetic  1.66 us (1%)
    ppermute x8, starting transfers between devices, moved(): return lax.ppermute(block, axis, route)  25.2 us
    ppermute x8, waiting for transfers between devices, moved(): return lax.ppermute(block, axis, route)  20.6 us
    all_to_all x1, starting transfers between devices, on_device(): lax.all_to_all(jnp.broadcast_to(part[None], (8,) + part.shape), 'z_hi', 0...  13.8 us
    pallas_call x5, Pallas kernels, call(): pl.pallas_call(body, out_shape=[jax.ShapeDtypeStruct(shape, dtype) for sh...  13.4 us
    all_to_all x1, waiting for transfers between devices, on_device(): mine = lax.all_to_all(pieces, SLAB, 0, 0).reshape(keep.shape)  9.83 us
    all_to_all x1, starting transfers between devices, on_device(): pieces = lax.all_to_all(part.reshape(32, -1, 128), SLAB, 0, 0)  9.05 us
    ppermute x2, starting transfers between devices, swapped(): lax.ppermute(block, axis, [(i, i ^ flip) for i in range(lax.axis_size(axi...  6.88 us
    all_to_all x1, starting transfers between devices, on_device(): mine = lax.all_to_all(pieces, SLAB, 0, 0).reshape(keep.shape)  6.03 us
  transfers between devices with their start and end apart: 13, of which 9 were waited for; matrix products, arithmetic and copies ran while one was open for 1% of the time, Pallas kernels for 3%

profile of v7, /device:TPU:1, one launch (start us, length us, event | category | flops | bytes accessed | tf_op | source)
XLA Modules:
  0.0 121.7 jit_solution(17370855553945069825)
XLA Ops:
  0.6 1.2 shard_map.186
  1.8 4.0 %collective-permute-start = (bf16[16,5120]{1,0:T(8,128)(2,1)S(1)}, bf16[16,5120]{1,0:T(8,128)(2,1)S(1)}, u32[]{:S(2)}, u32[]{:S(2)}) collective-permute-start(bf16[16,5120]{1,0:T(8,128)(2,1)S(1)} %get-tuple-element.48), channel_id=1, source_target_pairs={{0,4},{4,8},{8,12},{12,16},{16,20},{20,24},{24,28},{28,32},{32,36}... | collective-permute-start | bytes 491528 | tf_op jit(solution)/shard_map/ppermute | solution.py:31
  5.9 1.3 %collective-permute-start.1 = (bf16[16,5120]{1,0:T(8,128)(2,1)S(1)}, bf16[16,5120]{1,0:T(8,128)(2,1)S(1)}, u32[]{:S(2)}, u32[]{:S(2)}) collective-permute-start(bf16[16,5120]{1,0:T(8,128)(2,1)S(1)} %get-tuple-element.49), channel_id=1, source_target_pairs={{4,0},{8,4},{12,8},{16,12},{20,16},{24,20},{28,24},{32,28},{36,32}... | collective-permute-start | bytes 491528 | tf_op jit(solution)/shard_map/ppermute | solution.py:31
  7.2 0.9 slice_bitcast_fusion
  8.1 0.1 maximum_maximum_fusion.refs_10_
  8.2 3.7 %collective-permute-done.1.refs_7_ = bf16[16,5120]{1,0:T(8,128)(2,1)S(1)} collective-permute-done((bf16[16,5120]{1,0:T(8,128)(2,1)S(1)}, bf16[16,5120]{1,0:T(8,128)(2,1)S(1)}, u32[]{:S(2)}, u32[]{:S(2)}) %collective-permute-start.1) | collective-permute-done | bytes 163872 | tf_op jit(solution)/shard_map/ppermute | solution.py:31
  12.0 7.0 %collective-permute-start.2 = (bf16[48,512]{1,0:T(8,128)(2,1)S(1)}, bf16[48,512]{1,0:T(8,128)(2,1)S(1)}, u32[]{:S(2)}, u32[]{:S(2)}) collective-permute-start(bf16[48,512]{1,0:T(8,128)(2,1)S(1)} %pad_add_fusion.1), channel_id=1, source_target_pairs={{0,1},{1,2},{2,3},{4,5},{5,6},{6,7},{8,9},{9,10},{10,11},{12,13},{... | collective-permute-start | bytes 147464 | tf_op jit(solution)/shard_map/ppermute | solution.py:31
  19.0 1.9 %collective-permute-start.3 = (bf16[48,512]{1,0:T(8,128)(2,1)S(1)}, bf16[48,512]{1,0:T(8,128)(2,1)S(1)}, u32[]{:S(2)}, u32[]{:S(2)}) collective-permute-start(bf16[48,512]{1,0:T(8,128)(2,1)S(1)} %pad_add_fusion), channel_id=1, source_target_pairs={{1,0},{2,1},{3,2},{5,4},{6,5},{7,6},{9,8},{10,9},{11,10},{13,12},{... | collective-permute-start | bytes 147464 | tf_op jit(solution)/shard_map/ppermute | solution.py:31
  21.0 4.9 %collective-permute-done.3.refs_9_ = bf16[48,512]{1,0:T(8,128)(2,1)S(1)} collective-permute-done((bf16[48,512]{1,0:T(8,128)(2,1)S(1)}, bf16[48,512]{1,0:T(8,128)(2,1)S(1)}, u32[]{:S(2)}, u32[]{:S(2)}) %collective-permute-start.3) | collective-permute-done | bytes 49184 | tf_op jit(solution)/shard_map/ppermute | solution.py:31
  25.9 6.8 %shard_map.187 = (bf16[3328,128]{1,0:T(8,128)(2,1)S(1)}, bf16[3328,128]{1,0:T(8,128)(2,1)S(1)}, bf16[8,5120]{1,0:T(8,128)(2,1)S(1)}, bf16[4,5120]{1,0:T(4,128)(2...) custom-call(s32[4]{0:T(128)S(1)} %pad_add_fusion.2.refs_0_, ...), custom_call_target="tpu_custom_call" | custom-call | tf_op jit(solution)/shard_map/pallas_call | solution.py:508
  32.7 1.9 %collective-permute-start.4 = (bf16[3328,128]{1,0:T(8,128)(2,1)S(1)}, bf16[3328,128]{1,0:T(8,128)(2,1)S(1)}, u32[]{:S(2)}, u32[]{:S(2)}) collective-permute-start(bf16[3328,128]{1,0:T(8,128)(2,1)S(1)} %get-tuple-element.53), channel_id=1, source_target_pairs={{0,1},{1,0},{2,3},{3,2},{4,5},{5,4},{6,7},{7,6},{8,9},{9,8},{10,11... | collective-permute-start | bytes 2555912 | tf_op jit(solution)/shard_map/ppermute | solution.py:467
  34.6 2.3 %collective-permute-done.4 = bf16[3328,128]{1,0:T(8,128)(2,1)S(1)} collective-permute-done((bf16[3328,128]{1,0:T(8,128)(2,1)S(1)}, bf16[3328,128]{1,0:T(8,128)(2,1)S(1)}, u32[]{:S(2)}, u32[]{:S(2)}) %collective-permute-start.4) | collective-permute-done | bytes 852000 | tf_op jit(solution)/shard_map/ppermute | solution.py:467
  37.0 1.1 add_convert_fusion
  38.1 9.0 %all-to-all-start = ((bf16[32,104,128]{2,1,0:T(8,128)(2,1)}), bf16[32,104,128]{2,1,0:T(8,128)(2,1)S(1)}, u32[]{:S(2)}, u32[]{:S(2)}) async-start(bf16[32,104,128]{2,1,0:T(8,128)(2,1)} %bitcast.12), calls=%async_computation | async-start | bytes 1703936 | tf_op jit(solution)/shard_map/all_to_all | solution.py:610
  47.1 3.1 %collective-permute-start.5 = (bf16[4,5120]{1,0:T(4,128)(2,1)S(1)}, bf16[4,5120]{1,0:T(4,128)(2,1)S(1)}, u32[]{:S(2)}, u32[]{:S(2)}) collective-permute-start(bf16[4,5120]{1,0:T(4,128)(2,1)S(1)} %get-tuple-element.57), channel_id=1, source_target_pairs={{0,4},{4,8},{8,12},{12,16},{16,20},{20,24},{24,28},{28,32},{32,36}... | collective-permute-start | bytes 122888 | tf_op jit(solution)/shard_map/ppermute | solution.py:31
  50.3 1.3 %collective-permute-start.6 = (bf16[4,5120]{1,0:T(4,128)(2,1)S(1)}, bf16[4,5120]{1,0:T(4,128)(2,1)S(1)}, u32[]{:S(2)}, u32[]{:S(2)}) collective-permute-start(bf16[4,5120]{1,0:T(4,128)(2,1)S(1)} %get-tuple-element.58), channel_id=1, source_target_pairs={{4,0},{8,4},{12,8},{16,12},{20,16},{24,20},{28,24},{32,28},{36,32}... | collective-permute-start | bytes 122888 | tf_op jit(solution)/shard_map/ppermute | solution.py:31
  51.6 7.1 %collective-permute-done.5.refs_4_ = bf16[4,5120]{1,0:T(4,128)(2,1)S(1)} collective-permute-done((bf16[4,5120]{1,0:T(4,128)(2,1)S(1)}, bf16[4,5120]{1,0:T(4,128)(2,1)S(1)}, u32[]{:S(2)}, u32[]{:S(2)}) %collective-permute-start.5) | collective-permute-done | bytes 40992 | tf_op jit(solution)/shard_map/ppermute | solution.py:31
  58.7 3.1 %all-to-all-done = bf16[32,104,128]{2,1,0:T(8,128)(2,1)S(1)} async-done(((bf16[32,104,128]{2,1,0:T(8,128)(2,1)}), bf16[32,104,128]{2,1,0:T(8,128)(2,1)S(1)}, u32[]{:S(2)}, u32[]{:S(2)}) %all-to-all-start) | async-done | bytes 852000 | tf_op jit(solution)/shard_map/all_to_all | solution.py:610
  61.9 0.7 broadcast_in_dim.7
  62.6 13.8 %all-to-all-start.1 = ((bf16[8,104,128]{2,1,0:T(8,128)(2,1)}), bf16[8,104,128]{2,1,0:T(8,128)(2,1)S(1)}, u32[]{:S(2)}, u32[]{:S(2)}) async-start(bf16[8,104,128]{2,1,0:T(8,128)(2,1)} %broadcast_in_dim.7), calls=%async_computation.1 | async-start | bytes 425984 | tf_op jit(solution)/shard_map/all_to_all | solution.py:615
  76.4 4.6 %collective-permute-start.7 = (bf16[32,256]{1,0:T(8,128)(2,1)S(1)}, bf16[32,256]{1,0:T(8,128)(2,1)S(1)}, u32[]{:S(2)}, u32[]{:S(2)}) collective-permute-start(bf16[32,256]{1,0:T(8,128)(2,1)S(1)} %get-tuple-element.66), channel_id=1, source_target_pairs={{0,1},{1,2},{2,3},{4,5},{5,6},{6,7},{8,9},{9,10},{10,11},{12,13},{... | collective-permute-start | bytes 49160 | tf_op jit(solution)/shard_map/ppermute | solution.py:31
  81.0 1.9 %collective-permute-start.8 = (bf16[32,256]{1,0:T(8,128)(2,1)S(1)}, bf16[32,256]{1,0:T(8,128)(2,1)S(1)}, u32[]{:S(2)}, u32[]{:S(2)}) collective-permute-start(bf16[32,256]{1,0:T(8,128)(2,1)S(1)} %get-tuple-element.67), channel_id=1, source_target_pairs={{1,0},{2,1},{3,2},{5,4},{6,5},{7,6},{9,8},{10,9},{11,10},{13,12},{... | collective-permute-start | bytes 49160 | tf_op jit(solution)/shard_map/ppermute | solution.py:31
  82.9 4.9 %collective-permute-done.8.refs_7_ = bf16[32,256]{1,0:T(8,128)(2,1)S(1)} collective-permute-done((bf16[32,256]{1,0:T(8,128)(2,1)S(1)}, bf16[32,256]{1,0:T(8,128)(2,1)S(1)}, u32[]{:S(2)}, u32[]{:S(2)}) %collective-permute-start.8) | collective-permute-done | bytes 16416 | tf_op jit(solution)/shard_map/ppermute | solution.py:31
  87.9 4.4 %all-to-all-done.1 = bf16[8,104,128]{2,1,0:T(8,128)(2,1)S(1)} async-done(((bf16[8,104,128]{2,1,0:T(8,128)(2,1)}), bf16[8,104,128]{2,1,0:T(8,128)(2,1)S(1)}, u32[]{:S(2)}, u32[]{:S(2)}) %all-to-all-start.1) | async-done | bytes 213024 | tf_op jit(solution)/shard_map/all_to_all | solution.py:615
  92.3 1.0 broadcast_in_dim.8
  93.3 6.0 %all-to-all-start.2 = ((bf16[32,104,128]{2,1,0:T(8,128)(2,1)}), bf16[32,104,128]{2,1,0:T(8,128)(2,1)S(1)}, u32[]{:S(2)}, u32[]{:S(2)}) async-start(bf16[32,104,128]{2,1,0:T(8,128)(2,1)} %broadcast_in_dim.8), calls=%async_computation.2 | async-start | bytes 1703936 | tf_op jit(solution)/shard_map/all_to_all | solution.py:621
  99.4 0.1 fusion.4.refs_8_
  99.5 3.4 %shard_map.189 = (bf16[8,5120]{1,0:T(8,128)(2,1)}, bf16[4,5120]{1,0:T(4,128)(2,1)}, bf16[2,5120]{1,0:T(2,128)(2,1)}, bf16[1,5120]{1,0:T(2,128)(2,1)}) custom-call(bf16[8,5120]{1,0:T(8,128)(2,1)S(1)} %get-tuple-element.60.refs_0_, bf16[4,5120]{1,0:T(4,128)(2,1)S(1)} %get-tuple-element.61.refs_1_, bf16[2,5120]{1,0:T(2,128)(2,1)S(1)} %get-tuple-element.62.refs_2_, ...), custom_call_target="tpu_custom_call" | custom-call | tf_op jit(solution)/shard_map/pallas_call | solution.py:508
  102.9 9.8 %all-to-all-done.2 = bf16[32,104,128]{2,1,0:T(8,128)(2,1)S(1)} async-done(((bf16[32,104,128]{2,1,0:T(8,128)(2,1)}), bf16[32,104,128]{2,1,0:T(8,128)(2,1)S(1)}, u32[]{:S(2)}, u32[]{:S(2)}) %all-to-all-start.2) | async-done | bytes 852000 | tf_op jit(solution)/shard_map/all_to_all | solution.py:621
  112.7 5.0 %collective-permute-start.9 = (bf16[3328,128]{1,0:T(8,128)(2,1)S(1)}, bf16[3328,128]{1,0:T(8,128)(2,1)S(1)}, u32[]{:S(2)}, u32[]{:S(2)}) collective-permute-start(bf16[3328,128]{1,0:T(8,128)(2,1)S(1)} %bitcast.29), channel_id=1, source_target_pairs={{0,1},{1,0},{2,3},{3,2},{4,5},{5,4},{6,7},{7,6},{8,9},{9,8},{10,11... | collective-permute-start | bytes 2555912 | tf_op jit(solution)/shard_map/ppermute | solution.py:467
  117.7 2.0 %collective-permute-done.9.refs_2_ = bf16[3328,128]{1,0:T(8,128)(2,1)S(1)} collective-permute-done((bf16[3328,128]{1,0:T(8,128)(2,1)S(1)}, bf16[3328,128]{1,0:T(8,128)(2,1)S(1)}, u32[]{:S(2)}, u32[]{:S(2)}) %collective-permute-start.9) | collective-permute-done | bytes 852000 | tf_op jit(solution)/shard_map/ppermute | solution.py:467
  119.7 2.0 %shard_map.190 = (bf16[576,64]{1,0:T(8,128)(2,1)}, bf16[1152,128]{1,0:T(8,128)(2,1)}, bf16[2304,256]{1,0:T(8,128)(2,1)}, bf16[64,128]{1,0:T(8,128)(2,1)}, bf16[6...) custom-call(s32[4]{0:T(128)S(1)} %pad_add_fusion.2.refs_0_, bf16[3328,128]{1,0:T(8,128)(2,1)S(1)} %bitcast.30, ...), custom_call_target="tpu_custom_call" | custom-call | tf_op jit(solution)/shard_map/pallas_call | solution.py:508
  (13 shorter events, 0.3 us)
Async XLA Ops:
  1.8 6.4 %collective-permute-start = (bf16[16,5120]{1,0:T(8,128)(2,1)S(1)}, bf16[16,5120]{1,0:T(8,128)(2,1)S(1)}, u32[]{:S(2)}, u32[]{:S(2)}) collective-permute-start(bf16[16,5120]{1,0:T(8,128)(2,1)S(1)} %get-tuple-element.48), channel_id=1, source_target_pairs={{0,4},{4,8},{8,12},{12,16},{16,20},{20,24},{24,28},{28,32},{32,36}... | collective-permute-start | bytes 491528 | tf_op jit(solution)/shard_map/ppermute | solution.py:31
  5.9 6.1 %collective-permute-start.1 = (bf16[16,5120]{1,0:T(8,128)(2,1)S(1)}, bf16[16,5120]{1,0:T(8,128)(2,1)S(1)}, u32[]{:S(2)}, u32[]{:S(2)}) collective-permute-start(bf16[16,5120]{1,0:T(8,128)(2,1)S(1)} %get-tuple-element.49), channel_id=1, source_target_pairs={{4,0},{8,4},{12,8},{16,12},{20,16},{24,20},{28,24},{32,28},{36,32}... | collective-permute-start | bytes 491528 | tf_op jit(solution)/shard_map/ppermute | solution.py:31
  12.0 9.0 %collective-permute-start.2 = (bf16[48,512]{1,0:T(8,128)(2,1)S(1)}, bf16[48,512]{1,0:T(8,128)(2,1)S(1)}, u32[]{:S(2)}, u32[]{:S(2)}) collective-permute-start(bf16[48,512]{1,0:T(8,128)(2,1)S(1)} %pad_add_fusion.1), channel_id=1, source_target_pairs={{0,1},{1,2},{2,3},{4,5},{5,6},{6,7},{8,9},{9,10},{10,11},{12,13},{... | collective-permute-start | bytes 147464 | tf_op jit(solution)/shard_map/ppermute | solution.py:31
  19.0 6.9 %collective-permute-start.3 = (bf16[48,512]{1,0:T(8,128)(2,1)S(1)}, bf16[48,512]{1,0:T(8,128)(2,1)S(1)}, u32[]{:S(2)}, u32[]{:S(2)}) collective-permute-start(bf16[48,512]{1,0:T(8,128)(2,1)S(1)} %pad_add_fusion), channel_id=1, source_target_pairs={{1,0},{2,1},{3,2},{5,4},{6,5},{7,6},{9,8},{10,9},{11,10},{13,12},{... | collective-permute-start | bytes 147464 | tf_op jit(solution)/shard_map/ppermute | solution.py:31
  32.7 4.3 %collective-permute-start.4 = (bf16[3328,128]{1,0:T(8,128)(2,1)S(1)}, bf16[3328,128]{1,0:T(8,128)(2,1)S(1)}, u32[]{:S(2)}, u32[]{:S(2)}) collective-permute-start(bf16[3328,128]{1,0:T(8,128)(2,1)S(1)} %get-tuple-element.53), channel_id=1, source_target_pairs={{0,1},{1,0},{2,3},{3,2},{4,5},{5,4},{6,7},{7,6},{8,9},{9,8},{10,11... | collective-permute-start | bytes 2555912 | tf_op jit(solution)/shard_map/ppermute | solution.py:467
  38.1 23.7 %all-to-all-start = ((bf16[32,104,128]{2,1,0:T(8,128)(2,1)}), bf16[32,104,128]{2,1,0:T(8,128)(2,1)S(1)}, u32[]{:S(2)}, u32[]{:S(2)}) async-start(bf16[32,104,128]{2,1,0:T(8,128)(2,1)} %bitcast.12), calls=%async_computation | async-start | bytes 1703936 | tf_op jit(solution)/shard_map/all_to_all | solution.py:610
  47.1 11.5 %collective-permute-start.5 = (bf16[4,5120]{1,0:T(4,128)(2,1)S(1)}, bf16[4,5120]{1,0:T(4,128)(2,1)S(1)}, u32[]{:S(2)}, u32[]{:S(2)}) collective-permute-start(bf16[4,5120]{1,0:T(4,128)(2,1)S(1)} %get-tuple-element.57), channel_id=1, source_target_pairs={{0,4},{4,8},{8,12},{12,16},{16,20},{20,24},{24,28},{28,32},{32,36}... | collective-permute-start | bytes 122888 | tf_op jit(solution)/shard_map/ppermute | solution.py:31
  50.3 8.4 %collective-permute-start.6 = (bf16[4,5120]{1,0:T(4,128)(2,1)S(1)}, bf16[4,5120]{1,0:T(4,128)(2,1)S(1)}, u32[]{:S(2)}, u32[]{:S(2)}) collective-permute-start(bf16[4,5120]{1,0:T(4,128)(2,1)S(1)} %get-tuple-element.58), channel_id=1, source_target_pairs={{4,0},{8,4},{12,8},{16,12},{20,16},{24,20},{28,24},{32,28},{36,32}... | collective-permute-start | bytes 122888 | tf_op jit(solution)/shard_map/ppermute | solution.py:31
  62.6 29.7 %all-to-all-start.1 = ((bf16[8,104,128]{2,1,0:T(8,128)(2,1)}), bf16[8,104,128]{2,1,0:T(8,128)(2,1)S(1)}, u32[]{:S(2)}, u32[]{:S(2)}) async-start(bf16[8,104,128]{2,1,0:T(8,128)(2,1)} %broadcast_in_dim.7), calls=%async_computation.1 | async-start | bytes 425984 | tf_op jit(solution)/shard_map/all_to_all | solution.py:615
  76.4 6.5 %collective-permute-start.7 = (bf16[32,256]{1,0:T(8,128)(2,1)S(1)}, bf16[32,256]{1,0:T(8,128)(2,1)S(1)}, u32[]{:S(2)}, u32[]{:S(2)}) collective-permute-start(bf16[32,256]{1,0:T(8,128)(2,1)S(1)} %get-tuple-element.66), channel_id=1, source_target_pairs={{0,1},{1,2},{2,3},{4,5},{5,6},{6,7},{8,9},{9,10},{10,11},{12,13},{... | collective-permute-start | bytes 49160 | tf_op jit(solution)/shard_map/ppermute | solution.py:31
  81.0 6.9 %collective-permute-start.8 = (bf16[32,256]{1,0:T(8,128)(2,1)S(1)}, bf16[32,256]{1,0:T(8,128)(2,1)S(1)}, u32[]{:S(2)}, u32[]{:S(2)}) collective-permute-start(bf16[32,256]{1,0:T(8,128)(2,1)S(1)} %get-tuple-element.67), channel_id=1, source_target_pairs={{1,0},{2,1},{3,2},{5,4},{6,5},{7,6},{9,8},{10,9},{11,10},{13,12},{... | collective-permute-start | bytes 49160 | tf_op jit(solution)/shard_map/ppermute | solution.py:31
  93.3 19.4 %all-to-all-start.2 = ((bf16[32,104,128]{2,1,0:T(8,128)(2,1)}), bf16[32,104,128]{2,1,0:T(8,128)(2,1)S(1)}, u32[]{:S(2)}, u32[]{:S(2)}) async-start(bf16[32,104,128]{2,1,0:T(8,128)(2,1)} %broadcast_in_dim.8), calls=%async_computation.2 | async-start | bytes 1703936 | tf_op jit(solution)/shard_map/all_to_all | solution.py:621
  112.7 7.0 %collective-permute-start.9 = (bf16[3328,128]{1,0:T(8,128)(2,1)S(1)}, bf16[3328,128]{1,0:T(8,128)(2,1)S(1)}, u32[]{:S(2)}, u32[]{:S(2)}) collective-permute-start(bf16[3328,128]{1,0:T(8,128)(2,1)S(1)} %bitcast.29), channel_id=1, source_target_pairs={{0,1},{1,0},{2,3},{3,2},{4,5},{5,4},{6,7},{7,6},{8,9},{9,8},{10,11... | collective-permute-start | bytes 2555912 | tf_op jit(solution)/shard_map/ppermute | solution.py:467

commit v8 on v7

--- a/solution.py
+++ b/solution.py
@@ -390,10 +390,9 @@
 
 
 def backward_kernel(
-    g1_ref, g2_ref, g3_ref, rim_ref, above_ref, below_ref, left_ref, right_ref,
-    gf1_ref, gf2_ref, gf3_ref, gf4_ref, wide1, wide2, wide3, xw1, xw2, xw3, out2, out3, near, copies,
+    g1_ref, g2_ref, g3_ref, rim_ref, above_ref, below_ref, left_ref, right_ref, t1b, k2, k3, p4,
+    gf1_ref, gf2_ref, gf3_ref, gf4_ref, wide1, wide2, wide3, xw1, xw2, xw3, out2, out3,
 ):
-    t1b, k2, k3, p4 = near
     low = lax.broadcasted_iota(jnp.int32, (1, 128), 1) < 64
     for ref, n in ((xw1, 640), (xw2, 320), (xw3, 160)):
         ref[0:8, :] = jnp.zeros((8, ref.shape[1]), F32)
@@ -410,8 +409,6 @@
         wide[top : top + 2 + rows, 0:step] = left[start : start + 2 + rows, 0:step]
         wide[top : top + 2 + rows, end : end + step] = right[start : start + 2 + rows, 0:step]
 
-    for copy in copies:
-        copy.wait()
     for f in range(40):
         at = 8 + 16 * f
         xw1[at : at + 16, 0:128] = tile(wide1, f + 1)
@@ -540,9 +537,9 @@
         ]
     ).astype(jnp.int32)
     ahead, back = pair_weights(kernel_one)
-    k2 = in_hbm(kernel_two.reshape(3, 384, 128))
-    k3 = in_hbm(kernel_three.reshape(3, 768, 256))
-    fars = halos(x1, x2, x3, x4, cot) + (ahead, k2, k3, in_hbm(p2.T), in_hbm(p3.T), in_hbm(p4.T))
+    k2 = kernel_two.reshape(3, 384, 128)
+    k3 = kernel_three.reshape(3, 768, 256)
+    fars = halos(x1, x2, x3, x4, cot) + (ahead, in_hbm(k2), in_hbm(k3), in_hbm(p2.T), in_hbm(p3.T), in_hbm(p4.T))
     total = RIM + WIDE + RIM
     keep, send, g1, g2, g3, rim, up, down = call(
         forward_kernel,
@@ -563,7 +560,7 @@
         scalars=1,
         far=15,
     )
-    return place, keep, send, (g1, g2, g3, rim), up, down, (back, k2, k3, in_hbm(p4.T))
+    return place, keep, send, (g1, g2, g3, rim), up, down, (back, k2, k3, p4.T)
 
 
 def from_beside(grads, above, below):
@@ -584,7 +581,6 @@
         ],
         *grads, above, below, left, right,
         *weights,
-        far=4,
     )
 
 
@@ -614,13 +610,12 @@
 
     pieces = lax.all_to_all(jnp.broadcast_to(part[None], (8,) + part.shape), "z_hi", 0, 0)
     left, right = from_beside(grads, above, below)
-    pieces, left, right = lax.optimization_barrier((pieces, left, right))
+    outs = input_grads(grads, above, below, left, right, weights)
+    pieces, outs = lax.optimization_barrier((pieces, outs))
     part = jnp.sum(pieces.astype(F32), axis=0).astype(BF)
 
     pieces = jnp.broadcast_to(part[None], (32,) + part.shape)
     mine = lax.all_to_all(pieces, SLAB, 0, 0).reshape(keep.shape)
-    outs = input_grads(grads, above, below, left, right, weights)
-    mine, outs = lax.optimization_barrier((mine, outs))
     return tuple(outs) + unpacked(place, mine, swapped(mine, "core", 1))
 
 

time: 122 us -> 121 us (level)
  blocking collectives: 0 us -> 18.1 us
  waiting for transfers between devices: 42.3 us -> 30.6 us
  starting transfers between devices: 60.9 us -> 55.5 us
  Pallas kernels: 13.4 us -> 11.8 us
    all_to_all x0 -> x1, blocking collectives: none -> 18.1 us  [on_device(): mine = lax.all_to_all(pieces, SLAB, 0, 0).reshape(keep.shape)]
    all_to_all x1 -> x0, waiting for transfers between devices: 9.83 us -> none  [on_device(): mine = lax.all_to_all(pieces, SLAB, 0, 0).reshape(keep.shape)]
    all_to_all x1 -> x0, starting transfers between devices: 6.03 us -> none  [on_device(): mine = lax.all_to_all(pieces, SLAB, 0, 0).reshape(keep.shape)]
    pallas_call x5, Pallas kernels: 13.4 us -> 11.8 us  [call(): pl.pallas_call(body, out_shape=[jax.ShapeDtypeStruct(shape, dtype) for sh...]
    all_to_all x1, waiting for transfers between devices: 4.42 us -> 2.92 us  [on_device(): lax.all_to_all(jnp.broadcast_to(part[None], (8,) + part.shape), 'z_hi', 0...]
  transfers between devices with their start and end apart: 13 -> 12, of which waited for: 9 -> 8; matrix products, arithmetic and copies ran while one was open for 1% -> 1% of each run, Pallas kernels for 3% -> 2%
where the time goes in v8:
time: 121 us; the launch traced here: 120 us
  starting transfers between devices  55.5 us (46%)
  waiting for transfers between devices  30.6 us (25%)
  blocking collectives  18.1 us (15%)
  Pallas kernels  11.8 us (10%)
  local copies, waits for them, and re-layouts  1.72 us (1%)
  other arithmetic  1.66 us (1%)
    ppermute x8, starting transfers between devices, moved(): return lax.ppermute(block, axis, route)  25.3 us
    ppermute x8, waiting for transfers between devices, moved(): return lax.ppermute(block, axis, route)  20.3 us
    all_to_all x1, blocking collectives, on_device(): mine = lax.all_to_all(pieces, SLAB, 0, 0).reshape(keep.shape)  18.1 us
    all_to_all x1, starting transfers between devices, on_device(): lax.all_to_all(jnp.broadcast_to(part[None], (8,) + part.shape), 'z_hi', 0...  13.8 us
    pallas_call x5, Pallas kernels, call(): pl.pallas_call(body, out_shape=[jax.ShapeDtypeStruct(shape, dtype) for sh...  11.8 us
    all_to_all x1, starting transfers between devices, on_device(): pieces = lax.all_to_all(part.reshape(32, -1, 128), SLAB, 0, 0)  9.05 us
    ppermute x2, starting transfers between devices, swapped(): lax.ppermute(block, axis, [(i, i ^ flip) for i in range(lax.axis_size(axi...  7.42 us
    ppermute x2, waiting for transfers between devices, swapped(): lax.ppermute(block, axis, [(i, i ^ flip) for i in range(lax.axis_size(axi...  4.33 us
  transfers between devices with their start and end apart: 12, of which 8 were waited for; matrix products, arithmetic and copies ran while one was open for 1% of the time, Pallas kernels for 2%

profile of v8, /device:TPU:1, one launch (start us, length us, event | category | flops | bytes accessed | tf_op | source)
XLA Modules:
  0.0 120.3 jit_solution(15869474585783251839)
XLA Ops:
  0.6 1.2 shard_map.186
  1.8 4.0 %collective-permute-start = (bf16[16,5120]{1,0:T(8,128)(2,1)S(1)}, bf16[16,5120]{1,0:T(8,128)(2,1)S(1)}, u32[]{:S(2)}, u32[]{:S(2)}) collective-permute-start(bf16[16,5120]{1,0:T(8,128)(2,1)S(1)} %get-tuple-element.45), channel_id=1, source_target_pairs={{0,4},{4,8},{8,12},{12,16},{16,20},{20,24},{24,28},{28,32},{32,36}... | collective-permute-start | bytes 491528 | tf_op jit(solution)/shard_map/ppermute | solution.py:31
  5.9 1.3 %collective-permute-start.1 = (bf16[16,5120]{1,0:T(8,128)(2,1)S(1)}, bf16[16,5120]{1,0:T(8,128)(2,1)S(1)}, u32[]{:S(2)}, u32[]{:S(2)}) collective-permute-start(bf16[16,5120]{1,0:T(8,128)(2,1)S(1)} %get-tuple-element.46), channel_id=1, source_target_pairs={{4,0},{8,4},{12,8},{16,12},{20,16},{24,20},{28,24},{32,28},{36,32}... | collective-permute-start | bytes 491528 | tf_op jit(solution)/shard_map/ppermute | solution.py:31
  7.2 0.9 slice_bitcast_fusion
  8.1 0.1 maximum_maximum_fusion.refs_10_
  8.2 3.7 %collective-permute-done.1.refs_7_ = bf16[16,5120]{1,0:T(8,128)(2,1)S(1)} collective-permute-done((bf16[16,5120]{1,0:T(8,128)(2,1)S(1)}, bf16[16,5120]{1,0:T(8,128)(2,1)S(1)}, u32[]{:S(2)}, u32[]{:S(2)}) %collective-permute-start.1) | collective-permute-done | bytes 163872 | tf_op jit(solution)/shard_map/ppermute | solution.py:31
  12.0 7.0 %collective-permute-start.2 = (bf16[48,512]{1,0:T(8,128)(2,1)S(1)}, bf16[48,512]{1,0:T(8,128)(2,1)S(1)}, u32[]{:S(2)}, u32[]{:S(2)}) collective-permute-start(bf16[48,512]{1,0:T(8,128)(2,1)S(1)} %pad_add_fusion.1), channel_id=1, source_target_pairs={{0,1},{1,2},{2,3},{4,5},{5,6},{6,7},{8,9},{9,10},{10,11},{12,13},{... | collective-permute-start | bytes 147464 | tf_op jit(solution)/shard_map/ppermute | solution.py:31
  19.0 1.9 %collective-permute-start.3 = (bf16[48,512]{1,0:T(8,128)(2,1)S(1)}, bf16[48,512]{1,0:T(8,128)(2,1)S(1)}, u32[]{:S(2)}, u32[]{:S(2)}) collective-permute-start(bf16[48,512]{1,0:T(8,128)(2,1)S(1)} %pad_add_fusion), channel_id=1, source_target_pairs={{1,0},{2,1},{3,2},{5,4},{6,5},{7,6},{9,8},{10,9},{11,10},{13,12},{... | collective-permute-start | bytes 147464 | tf_op jit(solution)/shard_map/ppermute | solution.py:31
  21.0 4.9 %collective-permute-done.3.refs_9_ = bf16[48,512]{1,0:T(8,128)(2,1)S(1)} collective-permute-done((bf16[48,512]{1,0:T(8,128)(2,1)S(1)}, bf16[48,512]{1,0:T(8,128)(2,1)S(1)}, u32[]{:S(2)}, u32[]{:S(2)}) %collective-permute-start.3) | collective-permute-done | bytes 49184 | tf_op jit(solution)/shard_map/ppermute | solution.py:31
  25.9 6.8 %shard_map.187 = (bf16[3328,128]{1,0:T(8,128)(2,1)S(1)}, bf16[3328,128]{1,0:T(8,128)(2,1)S(1)}, bf16[8,5120]{1,0:T(8,128)(2,1)S(1)}, bf16[4,5120]{1,0:T(4,128)(2...) custom-call(s32[4]{0:T(128)S(1)} %pad_add_fusion.2.refs_0_, ...), custom_call_target="tpu_custom_call" | custom-call | tf_op jit(solution)/shard_map/pallas_call | solution.py:505
  32.7 1.9 %collective-permute-start.4 = (bf16[3328,128]{1,0:T(8,128)(2,1)S(1)}, bf16[3328,128]{1,0:T(8,128)(2,1)S(1)}, u32[]{:S(2)}, u32[]{:S(2)}) collective-permute-start(bf16[3328,128]{1,0:T(8,128)(2,1)S(1)} %get-tuple-element.50), channel_id=1, source_target_pairs={{0,1},{1,0},{2,3},{3,2},{4,5},{5,4},{6,7},{7,6},{8,9},{9,8},{10,11... | collective-permute-start | bytes 2555912 | tf_op jit(solution)/shard_map/ppermute | solution.py:464
  34.6 2.3 %collective-permute-done.4 = bf16[3328,128]{1,0:T(8,128)(2,1)S(1)} collective-permute-done((bf16[3328,128]{1,0:T(8,128)(2,1)S(1)}, bf16[3328,128]{1,0:T(8,128)(2,1)S(1)}, u32[]{:S(2)}, u32[]{:S(2)}) %collective-permute-start.4) | collective-permute-done | bytes 852000 | tf_op jit(solution)/shard_map/ppermute | solution.py:464
  37.0 1.1 add_convert_fusion
  38.1 9.0 %all-to-all-start = ((bf16[32,104,128]{2,1,0:T(8,128)(2,1)}), bf16[32,104,128]{2,1,0:T(8,128)(2,1)S(1)}, u32[]{:S(2)}, u32[]{:S(2)}) async-start(bf16[32,104,128]{2,1,0:T(8,128)(2,1)} %bitcast.12), calls=%async_computation | async-start | bytes 1703936 | tf_op jit(solution)/shard_map/all_to_all | solution.py:606
  47.2 3.3 %collective-permute-start.5 = (bf16[4,5120]{1,0:T(4,128)(2,1)S(1)}, bf16[4,5120]{1,0:T(4,128)(2,1)S(1)}, u32[]{:S(2)}, u32[]{:S(2)}) collective-permute-start(bf16[4,5120]{1,0:T(4,128)(2,1)S(1)} %get-tuple-element.54), channel_id=1, source_target_pairs={{0,4},{4,8},{8,12},{12,16},{16,20},{20,24},{24,28},{28,32},{32,36}... | collective-permute-start | bytes 122888 | tf_op jit(solution)/shard_map/ppermute | solution.py:31
  50.5 1.3 %collective-permute-start.6 = (bf16[4,5120]{1,0:T(4,128)(2,1)S(1)}, bf16[4,5120]{1,0:T(4,128)(2,1)S(1)}, u32[]{:S(2)}, u32[]{:S(2)}) collective-permute-start(bf16[4,5120]{1,0:T(4,128)(2,1)S(1)} %get-tuple-element.55), channel_id=1, source_target_pairs={{4,0},{8,4},{12,8},{16,12},{20,16},{24,20},{28,24},{32,28},{36,32}... | collective-permute-start | bytes 122888 | tf_op jit(solution)/shard_map/ppermute | solution.py:31
  51.8 6.9 %collective-permute-done.5.refs_4_ = bf16[4,5120]{1,0:T(4,128)(2,1)S(1)} collective-permute-done((bf16[4,5120]{1,0:T(4,128)(2,1)S(1)}, bf16[4,5120]{1,0:T(4,128)(2,1)S(1)}, u32[]{:S(2)}, u32[]{:S(2)}) %collective-permute-start.5) | collective-permute-done | bytes 40992 | tf_op jit(solution)/shard_map/ppermute | solution.py:31
  58.7 3.1 %all-to-all-done = bf16[32,104,128]{2,1,0:T(8,128)(2,1)S(1)} async-done(((bf16[32,104,128]{2,1,0:T(8,128)(2,1)}), bf16[32,104,128]{2,1,0:T(8,128)(2,1)S(1)}, u32[]{:S(2)}, u32[]{:S(2)}) %all-to-all-start) | async-done | bytes 852000 | tf_op jit(solution)/shard_map/all_to_all | solution.py:606
  61.8 0.1 reduce_sum.24
  61.9 0.7 broadcast_in_dim.7
  62.6 13.8 %all-to-all-start.1 = ((bf16[8,104,128]{2,1,0:T(8,128)(2,1)}), bf16[8,104,128]{2,1,0:T(8,128)(2,1)S(1)}, u32[]{:S(2)}, u32[]{:S(2)}) async-start(bf16[8,104,128]{2,1,0:T(8,128)(2,1)} %broadcast_in_dim.7), calls=%async_computation.1 | async-start | bytes 425984 | tf_op jit(solution)/shard_map/all_to_all | solution.py:611
  76.4 4.6 %collective-permute-start.7 = (bf16[32,256]{1,0:T(8,128)(2,1)S(1)}, bf16[32,256]{1,0:T(8,128)(2,1)S(1)}, u32[]{:S(2)}, u32[]{:S(2)}) collective-permute-start(bf16[32,256]{1,0:T(8,128)(2,1)S(1)} %get-tuple-element.63), channel_id=1, source_target_pairs={{0,1},{1,2},{2,3},{4,5},{5,6},{6,7},{8,9},{9,10},{10,11},{12,13},{... | collective-permute-start | bytes 49160 | tf_op jit(solution)/shard_map/ppermute | solution.py:31
  81.0 1.9 %collective-permute-start.8 = (bf16[32,256]{1,0:T(8,128)(2,1)S(1)}, bf16[32,256]{1,0:T(8,128)(2,1)S(1)}, u32[]{:S(2)}, u32[]{:S(2)}) collective-permute-start(bf16[32,256]{1,0:T(8,128)(2,1)S(1)} %get-tuple-element.64), channel_id=1, source_target_pairs={{1,0},{2,1},{3,2},{5,4},{6,5},{7,6},{9,8},{10,9},{11,10},{13,12},{... | collective-permute-start | bytes 49160 | tf_op jit(solution)/shard_map/ppermute | solution.py:31
  82.9 0.1 fusion.4.refs_8_
  83.1 4.8 %collective-permute-done.8.refs_7_ = bf16[32,256]{1,0:T(8,128)(2,1)S(1)} collective-permute-done((bf16[32,256]{1,0:T(8,128)(2,1)S(1)}, bf16[32,256]{1,0:T(8,128)(2,1)S(1)}, u32[]{:S(2)}, u32[]{:S(2)}) %collective-permute-start.8) | collective-permute-done | bytes 16416 | tf_op jit(solution)/shard_map/ppermute | solution.py:31
  87.9 1.8 %shard_map.189 = (bf16[8,5120]{1,0:T(8,128)(2,1)}, bf16[4,5120]{1,0:T(4,128)(2,1)}, bf16[2,5120]{1,0:T(2,128)(2,1)}, bf16[1,5120]{1,0:T(2,128)(2,1)}) custom-call(bf16[8,5120]{1,0:T(8,128)(2,1)S(1)} %get-tuple-element.57.refs_0_, bf16[4,5120]{1,0:T(4,128)(2,1)S(1)} %get-tuple-element.58.refs_1_, bf16[2,5120]{1,0:T(2,128)(2,1)S(1)} %get-tuple-element.59.refs_2_, ...), custom_call_target="tpu_custom_call" | custom-call | tf_op jit(solution)/shard_map/pallas_call | solution.py:505
  89.7 2.9 %all-to-all-done.1 = bf16[8,104,128]{2,1,0:T(8,128)(2,1)S(1)} async-done(((bf16[8,104,128]{2,1,0:T(8,128)(2,1)}), bf16[8,104,128]{2,1,0:T(8,128)(2,1)S(1)}, u32[]{:S(2)}, u32[]{:S(2)}) %all-to-all-start.1) | async-done | bytes 213024 | tf_op jit(solution)/shard_map/all_to_all | solution.py:611
  92.6 0.1 broadcast_in_dim.8
  92.8 18.1 %all_to_all.15 = bf16[32,104,128]{2,1,0:T(8,128)(2,1)S(1)} all-to-all(bf16[32,104,128]{2,1,0:T(8,128)(2,1)S(1)} %broadcast_in_dim.8), channel_id=1, replica_groups=mesh['z_hi'=8,'z_lo'=2,'x_lo'=2,'y'=4,'x_hi'=2,'core'=2] {'z_lo','x_lo',..., dimensions={0} | all-to-all | bytes 1703936 | tf_op jit(solution)/shard_map/all_to_all | solution.py:618
  110.9 5.5 %collective-permute-start.9 = (bf16[3328,128]{1,0:T(8,128)(2,1)S(1)}, bf16[3328,128]{1,0:T(8,128)(2,1)S(1)}, u32[]{:S(2)}, u32[]{:S(2)}) collective-permute-start(bf16[3328,128]{1,0:T(8,128)(2,1)S(1)} %bitcast.31), channel_id=1, source_target_pairs={{0,1},{1,0},{2,3},{3,2},{4,5},{5,4},{6,7},{7,6},{8,9},{9,8},{10,11... | collective-permute-start | bytes 2555912 | tf_op jit(solution)/shard_map/ppermute | solution.py:464
  116.4 2.0 %collective-permute-done.9.refs_2_ = bf16[3328,128]{1,0:T(8,128)(2,1)S(1)} collective-permute-done((bf16[3328,128]{1,0:T(8,128)(2,1)S(1)}, bf16[3328,128]{1,0:T(8,128)(2,1)S(1)}, u32[]{:S(2)}, u32[]{:S(2)}) %collective-permute-start.9) | collective-permute-done | bytes 852000 | tf_op jit(solution)/shard_map/ppermute | solution.py:464
  118.4 2.0 %shard_map.190 = (bf16[576,64]{1,0:T(8,128)(2,1)}, bf16[1152,128]{1,0:T(8,128)(2,1)}, bf16[2304,256]{1,0:T(8,128)(2,1)}, bf16[64,128]{1,0:T(8,128)(2,1)}, bf16[6...) custom-call(s32[4]{0:T(128)S(1)} %pad_add_fusion.2.refs_0_, bf16[3328,128]{1,0:T(8,128)(2,1)S(1)} %bitcast.32, ...), custom_call_target="tpu_custom_call" | custom-call | tf_op jit(solution)/shard_map/pallas_call | solution.py:505
  (18 shorter events, 0.2 us)
Async XLA Ops:
  1.8 6.4 %collective-permute-start = (bf16[16,5120]{1,0:T(8,128)(2,1)S(1)}, bf16[16,5120]{1,0:T(8,128)(2,1)S(1)}, u32[]{:S(2)}, u32[]{:S(2)}) collective-permute-start(bf16[16,5120]{1,0:T(8,128)(2,1)S(1)} %get-tuple-element.45), channel_id=1, source_target_pairs={{0,4},{4,8},{8,12},{12,16},{16,20},{20,24},{24,28},{28,32},{32,36}... | collective-permute-start | bytes 491528 | tf_op jit(solution)/shard_map/ppermute | solution.py:31
  5.9 6.1 %collective-permute-start.1 = (bf16[16,5120]{1,0:T(8,128)(2,1)S(1)}, bf16[16,5120]{1,0:T(8,128)(2,1)S(1)}, u32[]{:S(2)}, u32[]{:S(2)}) collective-permute-start(bf16[16,5120]{1,0:T(8,128)(2,1)S(1)} %get-tuple-element.46), channel_id=1, source_target_pairs={{4,0},{8,4},{12,8},{16,12},{20,16},{24,20},{28,24},{32,28},{36,32}... | collective-permute-start | bytes 491528 | tf_op jit(solution)/shard_map/ppermute | solution.py:31
  12.0 9.0 %collective-permute-start.2 = (bf16[48,512]{1,0:T(8,128)(2,1)S(1)}, bf16[48,512]{1,0:T(8,128)(2,1)S(1)}, u32[]{:S(2)}, u32[]{:S(2)}) collective-permute-start(bf16[48,512]{1,0:T(8,128)(2,1)S(1)} %pad_add_fusion.1), channel_id=1, source_target_pairs={{0,1},{1,2},{2,3},{4,5},{5,6},{6,7},{8,9},{9,10},{10,11},{12,13},{... | collective-permute-start | bytes 147464 | tf_op jit(solution)/shard_map/ppermute | solution.py:31
  19.0 6.9 %collective-permute-start.3 = (bf16[48,512]{1,0:T(8,128)(2,1)S(1)}, bf16[48,512]{1,0:T(8,128)(2,1)S(1)}, u32[]{:S(2)}, u32[]{:S(2)}) collective-permute-start(bf16[48,512]{1,0:T(8,128)(2,1)S(1)} %pad_add_fusion), channel_id=1, source_target_pairs={{1,0},{2,1},{3,2},{5,4},{6,5},{7,6},{9,8},{10,9},{11,10},{13,12},{... | collective-permute-start | bytes 147464 | tf_op jit(solution)/shard_map/ppermute | solution.py:31
  32.7 4.3 %collective-permute-start.4 = (bf16[3328,128]{1,0:T(8,128)(2,1)S(1)}, bf16[3328,128]{1,0:T(8,128)(2,1)S(1)}, u32[]{:S(2)}, u32[]{:S(2)}) collective-permute-start(bf16[3328,128]{1,0:T(8,128)(2,1)S(1)} %get-tuple-element.50), channel_id=1, source_target_pairs={{0,1},{1,0},{2,3},{3,2},{4,5},{5,4},{6,7},{7,6},{8,9},{9,8},{10,11... | collective-permute-start | bytes 2555912 | tf_op jit(solution)/shard_map/ppermute | solution.py:464
  38.1 23.7 %all-to-all-start = ((bf16[32,104,128]{2,1,0:T(8,128)(2,1)}), bf16[32,104,128]{2,1,0:T(8,128)(2,1)S(1)}, u32[]{:S(2)}, u32[]{:S(2)}) async-start(bf16[32,104,128]{2,1,0:T(8,128)(2,1)} %bitcast.12), calls=%async_computation | async-start | bytes 1703936 | tf_op jit(solution)/shard_map/all_to_all | solution.py:606
  47.1 40.7 %copy-start = (bf16[3,3,256,256]{3,2,1,0:T(8,128)(2,1)S(1)}, bf16[3,3,256,256]{3,2,1,0:T(8,128)(2,1)}, u32[]{:S(2)}) copy-start(bf16[3,3,256,256]{3,2,1,0:T(8,128)(2,1)} %param.17) | copy-start | bytes 3538948
  47.2 40.7 %copy-start.1 = (bf16[3,3,128,128]{3,2,1,0:T(8,128)(2,1)S(1)}, bf16[3,3,128,128]{3,2,1,0:T(8,128)(2,1)}, u32[]{:S(2)}) copy-start(bf16[3,3,128,128]{3,2,1,0:T(8,128)(2,1)} %param.16) | copy-start | bytes 884740
  47.2 40.7 %copy-start.2 = (bf16[512,64]{0,1:T(8,128)(2,1)S(1)}, bf16[512,64]{0,1:T(8,128)(2,1)}, u32[]{:S(2)}) copy-start(bf16[512,64]{0,1:T(8,128)(2,1)} %param.20) | copy-start | bytes 196612
  47.2 11.5 %collective-permute-start.5 = (bf16[4,5120]{1,0:T(4,128)(2,1)S(1)}, bf16[4,5120]{1,0:T(4,128)(2,1)S(1)}, u32[]{:S(2)}, u32[]{:S(2)}) collective-permute-start(bf16[4,5120]{1,0:T(4,128)(2,1)S(1)} %get-tuple-element.54), channel_id=1, source_target_pairs={{0,4},{4,8},{8,12},{12,16},{16,20},{20,24},{24,28},{28,32},{32,36}... | collective-permute-start | bytes 122888 | tf_op jit(solution)/shard_map/ppermute | solution.py:31
  50.5 8.2 %collective-permute-start.6 = (bf16[4,5120]{1,0:T(4,128)(2,1)S(1)}, bf16[4,5120]{1,0:T(4,128)(2,1)S(1)}, u32[]{:S(2)}, u32[]{:S(2)}) collective-permute-start(bf16[4,5120]{1,0:T(4,128)(2,1)S(1)} %get-tuple-element.55), channel_id=1, source_target_pairs={{4,0},{8,4},{12,8},{16,12},{20,16},{24,20},{28,24},{32,28},{36,32}... | collective-permute-start | bytes 122888 | tf_op jit(solution)/shard_map/ppermute | solution.py:31
  62.6 30.0 %all-to-all-start.1 = ((bf16[8,104,128]{2,1,0:T(8,128)(2,1)}), bf16[8,104,128]{2,1,0:T(8,128)(2,1)S(1)}, u32[]{:S(2)}, u32[]{:S(2)}) async-start(bf16[8,104,128]{2,1,0:T(8,128)(2,1)} %broadcast_in_dim.7), calls=%async_computation.1 | async-start | bytes 425984 | tf_op jit(solution)/shard_map/all_to_all | solution.py:611
  76.4 6.7 %collective-permute-start.7 = (bf16[32,256]{1,0:T(8,128)(2,1)S(1)}, bf16[32,256]{1,0:T(8,128)(2,1)S(1)}, u32[]{:S(2)}, u32[]{:S(2)}) collective-permute-start(bf16[32,256]{1,0:T(8,128)(2,1)S(1)} %get-tuple-element.63), channel_id=1, source_target_pairs={{0,1},{1,2},{2,3},{4,5},{5,6},{6,7},{8,9},{9,10},{10,11},{12,13},{... | collective-permute-start | bytes 49160 | tf_op jit(solution)/shard_map/ppermute | solution.py:31
  81.0 6.9 %collective-permute-start.8 = (bf16[32,256]{1,0:T(8,128)(2,1)S(1)}, bf16[32,256]{1,0:T(8,128)(2,1)S(1)}, u32[]{:S(2)}, u32[]{:S(2)}) collective-permute-start(bf16[32,256]{1,0:T(8,128)(2,1)S(1)} %get-tuple-element.64), channel_id=1, source_target_pairs={{1,0},{2,1},{3,2},{5,4},{6,5},{7,6},{9,8},{10,9},{11,10},{13,12},{... | collective-permute-start | bytes 49160 | tf_op jit(solution)/shard_map/ppermute | solution.py:31
  110.9 7.5 %collective-permute-start.9 = (bf16[3328,128]{1,0:T(8,128)(2,1)S(1)}, bf16[3328,128]{1,0:T(8,128)(2,1)S(1)}, u32[]{:S(2)}, u32[]{:S(2)}) collective-permute-start(bf16[3328,128]{1,0:T(8,128)(2,1)S(1)} %bitcast.31), channel_id=1, source_target_pairs={{0,1},{1,0},{2,3},{3,2},{4,5},{5,4},{6,7},{7,6},{8,9},{9,8},{10,11... | collective-permute-start | bytes 2555912 | tf_op jit(solution)/shard_map/ppermute | solution.py:464

commit v9 on v8

--- a/solution.py
+++ b/solution.py
@@ -31,6 +31,12 @@
     return lax.ppermute(block, axis, route)
 
 
+def traded(block, axis, start):
+    count = lax.axis_size(axis)
+    lower = [i for i in range(start, count - 1, 2)]
+    return lax.ppermute(block, axis, [(i, i + 1) for i in lower] + [(i + 1, i) for i in lower])
+
+
 def stacked(parts, rows):
     total, at = None, 0
     for part in parts:
@@ -44,45 +50,51 @@
     return pltpu.with_memory_space_constraint(x, pltpu.HBM)
 
 
-def edge_kernel(last_ref, first_ref, right_ref, left_ref, last, first, edge, near, copies):
+def edge_kernel(place_ref, odd_ref, even_ref, outer_ref, inner_ref, last, first, right, left, near, copies):
+    even = lax.rem(place_ref[0], 2) == 0
+    core = place_ref[3]
+    right[...] = jnp.zeros_like(right)
+    left[...] = jnp.zeros_like(left)
     for copy in copies:
         copy.wait()
     x1, cot, x2, x3, x4 = (ref[...].astype(F32) for ref in near)
-    for out, ref, ones, cots, twos in (
-        (last, last_ref, x1[5:8], cot[6:8], x2[1:4]),
-        (first, first_ref, x1[0:3], cot[0:2], x2[0:3]),
-    ):
+    for out, ones, cots, twos in ((last, x1[5:8], cot[6:8], x2[1:4]), (first, x1[0:3], cot[0:2], x2[0:3])):
         out[0:3, :] = ones
         out[3:5, :] = cots
         out[5:8, :] = twos
         out[8:10, :] = x3
         out[10:11, :] = x4
         out[11:16, :] = jnp.zeros((5, WIDE), F32)
-        ref[...] = out[...].astype(BF)
-    edge[...] = jnp.zeros_like(edge)
-    for ref, cols in ((right_ref, slice(WIDE - RIM, WIDE)), (left_ref, slice(0, RIM))):
-        edge[0:8, :] = x1[:, cols]
-        edge[8:16, :] = cot[:, cols]
-        edge[16:20, :] = x2[:, cols]
-        edge[20:22, :] = x3[:, cols]
-        edge[22:23, :] = x4[:, cols]
-        ref[...] = edge[...].astype(BF)
-
-
-def halos(x1, x2, x3, x4, cot):
+    odd_ref[...] = jnp.where(even, first[...], last[...]).astype(BF)
+    even_ref[...] = jnp.where(even, last[...], first[...]).astype(BF)
+    for out, cols in ((right, slice(WIDE - RIM, WIDE)), (left, slice(0, RIM))):
+        out[0:8, :] = x1[:, cols]
+        out[8:16, :] = cot[:, cols]
+        out[16:20, :] = x2[:, cols]
+        out[20:22, :] = x3[:, cols]
+        out[22:23, :] = x4[:, cols]
+    outer_ref[...] = jnp.where(core == 0, left[...], right[...]).astype(BF)
+    inner_ref[...] = jnp.where(core == 0, right[...], left[...]).astype(BF)
+
+
+def halos(place, x1, x2, x3, x4, cot):
     own = tuple(in_hbm(x) for x in (x1, cot, x2, x3, x4))
-    last, first, right_edge, left_edge = call(
+    odd, even, outer, inner = call(
         edge_kernel,
         [((16, WIDE), BF), ((16, WIDE), BF), ((24, RIM), BF), ((24, RIM), BF)],
-        [((16, WIDE), F32), ((16, WIDE), F32), ((24, RIM), F32)],
+        [((16, WIDE), F32), ((16, WIDE), F32), ((24, RIM), F32), ((24, RIM), F32)],
+        place,
         *own,
+        scalars=1,
         far=5,
     )
-    above = moved(last, ROWS, 1)
-    below = moved(first, ROWS, -1)
-    left = moved(stacked((right_edge, above[:11, -RIM:], below[:11, -RIM:]), 48), COLS, 1)
-    right = moved(stacked((left_edge, above[:11, :RIM], below[:11, :RIM]), 48), COLS, -1)
-    return own + (above, below, left, right)
+    odd = traded(odd, ROWS, 1)
+    even = traded(even, ROWS, 0)
+    core = lax.axis_index("core")
+    starts = [(v[:11, :RIM], v[:11, -RIM:]) for v in (odd, even)]
+    outer = stacked([outer] + [jnp.where(core == 0, a, b) for a, b in starts], 48)
+    inner = stacked([inner] + [jnp.where(core == 0, b, a) for a, b in starts], 48)
+    return own + (odd, even, traded(outer, COLS, 1), traded(inner, COLS, 0))
 
 
 def gelu_both(v):
@@ -118,7 +130,7 @@
     wx1, wc, wx2, wx3, wx4, xw1, xw2, xw3, d1, d2, d3, gm1, gm2, gm3, upward, downward,
     near, copies,
 ):
-    x1, cot, x2, x3, x4, above, below, left, right, t1, k2, k3, p2, p3, p4 = near
+    x1, cot, x2, x3, x4, odd, even, outer, inner, t1, k2, k3, p2, p3, p4 = near
     row_block = place_ref[0]
     at_left = place_ref[1] == 0
     at_right = place_ref[2] == 1
@@ -133,16 +145,19 @@
         ref[...] = jnp.zeros_like(ref)
     for copy in copies[:10]:
         copy.wait()
+    is_even = lax.rem(row_block, 2) == 0
+    outer, inner = outer[...].astype(F32), inner[...].astype(F32)
+    left, right = jnp.where(core == 0, outer, inner), jnp.where(core == 0, inner, outer)
     for side, to in ((None, RIM), (left, 0), (right, RIM + WIDE)):
         if side is None:
             cols = slice(to, to + WIDE)
             mid = [ref[...].astype(F32) for ref in (x1, cot, x2, x3, x4)]
-            up, down = above[...].astype(F32), below[...].astype(F32)
+            by_odd, by_even = odd[...].astype(F32), even[...].astype(F32)
         else:
             cols = slice(to, to + RIM)
-            v = side[...].astype(F32)
-            mid = [v[0:8], v[8:16], v[16:20], v[20:22], v[22:23]]
-            up, down = v[24:35], v[35:46]
+            mid = [side[0:8], side[8:16], side[16:20], side[20:22], side[22:23]]
+            by_odd, by_even = side[24:35], side[35:46]
+        up, down = jnp.where(is_even, by_odd, by_even), jnp.where(is_even, by_even, by_odd)
         wx1[1:4, cols] = up[0:3]
         wx1[4:12, cols] = mid[0]
         wx1[12:15, cols] = down[0:3]
@@ -539,7 +554,7 @@
     ahead, back = pair_weights(kernel_one)
     k2 = kernel_two.reshape(3, 384, 128)
     k3 = kernel_three.reshape(3, 768, 256)
-    fars = halos(x1, x2, x3, x4, cot) + (ahead, in_hbm(k2), in_hbm(k3), in_hbm(p2.T), in_hbm(p3.T), in_hbm(p4.T))
+    fars = halos(place, x1, x2, x3, x4, cot) + (ahead, in_hbm(k2), in_hbm(k3), in_hbm(p2.T), in_hbm(p3.T), in_hbm(p4.T))
     total = RIM + WIDE + RIM
     keep, send, g1, g2, g3, rim, up, down = call(
         forward_kernel,

time: 121 us -> 117 us (0.967)
  waiting for transfers between devices: 30.6 us -> 24.5 us
  starting transfers between devices: 55.5 us -> 56.8 us
    ppermute x0 -> x4, starting transfers between devices: none -> 16.1 us  [traded(): lax.ppermute(block, axis, [(i, i + 1) for i in lower] + [(i + 1, i) for i...]
    ppermute x8 -> x4, starting transfers between devices: 25.3 us -> 11.5 us  [moved(): return lax.ppermute(block, axis, route)]
    ppermute x8 -> x4, waiting for transfers between devices: 20.3 us -> 11.8 us  [moved(): return lax.ppermute(block, axis, route)]
    ppermute x0 -> x4, waiting for transfers between devices: none -> 2.83 us  [traded(): lax.ppermute(block, axis, [(i, i + 1) for i in lower] + [(i + 1, i) for i...]
    all_to_all x1, starting transfers between devices: 9.05 us -> 7.23 us  [on_device(): pieces = lax.all_to_all(part.reshape(32, -1, 128), SLAB, 0, 0)]
  transfers between devices with their start and end apart: 12 -> 12, of which waited for: 8 -> 9; matrix products, arithmetic and copies ran while one was open for 1% -> 1% of each run, Pallas kernels for 2% -> 2%
where the time goes in v9:
time: 117 us; the launch traced here: 116 us
  starting transfers between devices  56.8 us (49%)
  waiting for transfers between devices  24.5 us (21%)
  blocking collectives  18.2 us (16%)
  Pallas kernels  12.4 us (11%)
  local copies, waits for them, and re-layouts  1.72 us (1%)
  other arithmetic  1.67 us (1%)
    all_to_all x1, blocking collectives, on_device(): mine = lax.all_to_all(pieces, SLAB, 0, 0).reshape(keep.shape)  18.2 us
    ppermute x4, starting transfers between devices, traded(): lax.ppermute(block, axis, [(i, i + 1) for i in lower] + [(i + 1, i) for i...  16.1 us
    all_to_all x1, starting transfers between devices, on_device(): lax.all_to_all(jnp.broadcast_to(part[None], (8,) + part.shape), 'z_hi', 0...  14.1 us
    pallas_call x5, Pallas kernels, call(): pl.pallas_call(body, out_shape=[jax.ShapeDtypeStruct(shape, dtype) for sh...  12.4 us
    ppermute x4, waiting for transfers between devices, moved(): return lax.ppermute(block, axis, route)  11.8 us
    ppermute x4, starting transfers between devices, moved(): return lax.ppermute(block, axis, route)  11.5 us
    ppermute x2, starting transfers between devices, swapped(): lax.ppermute(block, axis, [(i, i ^ flip) for i in range(lax.axis_size(axi...  7.82 us
    all_to_all x1, starting transfers between devices, on_device(): pieces = lax.all_to_all(part.reshape(32, -1, 128), SLAB, 0, 0)  7.23 us
  transfers between devices with their start and end apart: 12, of which 9 were waited for; matrix products, arithmetic and copies ran while one was open for 1% of the time, Pallas kernels for 2%

profile of v9, /device:TPU:1, one launch (start us, length us, event | category | flops | bytes accessed | tf_op | source)
XLA Modules:
  0.0 116.2 jit_solution(16363105352883269461)
XLA Ops:
  0.7 1.8 %shard_map.186 = (bf16[16,5120]{1,0:T(8,128)(2,1)S(1)}, bf16[16,5120]{1,0:T(8,128)(2,1)S(1)}, bf16[24,512]{1,0:T(8,128)(2,1)S(1)}, bf16[24,512]{1,0:T(8,128)(2,1)S(1)}) custom-call(s32[4]{0:T(128)S(1)} %pad_add_fusion.2.refs_0_, bf16[8,5120]{1,0:T(8,128)(2,1)} %refs_1_.3, bf16[8,5120]{1,0:T(8,128)(2,1)} %refs_2_.3, bf16[4,5120]{1,0:T(4,128)(2,1)} %refs_3_.3, ...), custom_call_target="tpu_custom_call" | custom-call | tf_op jit(solution)/shard_map/pallas_call | solution.py:520
  2.5 0.7 collective-permute-start
  3.2 6.6 %collective-permute-start.1 = (bf16[16,5120]{1,0:T(8,128)(2,1)S(1)}, bf16[16,5120]{1,0:T(8,128)(2,1)S(1)}, u32[]{:S(2)}, u32[]{:S(2)}) collective-permute-start(bf16[16,5120]{1,0:T(8,128)(2,1)S(1)} %get-tuple-element.46), channel_id=1, source_target_pairs={{0,4},{8,12},{16,20},{24,28},{32,36},{40,44},{48,52},{56,60},{64,6... | collective-permute-start | bytes 491528 | tf_op jit(solution)/shard_map/ppermute | solution.py:37
  9.8 0.9 slice_bitcast_fusion
  10.6 1.8 %collective-permute-done.1.refs_7_ = bf16[16,5120]{1,0:T(8,128)(2,1)S(1)} collective-permute-done((bf16[16,5120]{1,0:T(8,128)(2,1)S(1)}, bf16[16,5120]{1,0:T(8,128)(2,1)S(1)}, u32[]{:S(2)}, u32[]{:S(2)}) %collective-permute-start.1) | collective-permute-done | bytes 163872 | tf_op jit(solution)/shard_map/ppermute | solution.py:37
  12.5 7.0 %collective-permute-start.2 = (bf16[48,512]{1,0:T(8,128)(2,1)S(1)}, bf16[48,512]{1,0:T(8,128)(2,1)S(1)}, u32[]{:S(2)}, u32[]{:S(2)}) collective-permute-start(bf16[48,512]{1,0:T(8,128)(2,1)S(1)} %pad_add_fusion.1), channel_id=1, source_target_pairs={{1,2},{2,1},{5,6},{6,5},{9,10},{10,9},{13,14},{14,13},{17,18},{18,... | collective-permute-start | bytes 147464 | tf_op jit(solution)/shard_map/ppermute | solution.py:37
  19.5 1.9 %collective-permute-start.3 = (bf16[48,512]{1,0:T(8,128)(2,1)S(1)}, bf16[48,512]{1,0:T(8,128)(2,1)S(1)}, u32[]{:S(2)}, u32[]{:S(2)}) collective-permute-start(bf16[48,512]{1,0:T(8,128)(2,1)S(1)} %pad_add_fusion), channel_id=1, source_target_pairs={{0,1},{2,3},{1,0},{3,2},{4,5},{6,7},{5,4},{7,6},{8,9},{10,11},{9,8... | collective-permute-start | bytes 147464 | tf_op jit(solution)/shard_map/ppermute | solution.py:37
  21.4 0.1 maximum_maximum_fusion.refs_10_
  21.6 1.0 collective-permute-done.3.refs_9_
  22.6 6.8 %shard_map.187 = (bf16[3328,128]{1,0:T(8,128)(2,1)S(1)}, bf16[3328,128]{1,0:T(8,128)(2,1)S(1)}, bf16[8,5120]{1,0:T(8,128)(2,1)S(1)}, bf16[4,5120]{1,0:T(4,128)(2...) custom-call(s32[4]{0:T(128)S(1)} %pad_add_fusion.2.refs_0_, ...), custom_call_target="tpu_custom_call" | custom-call | tf_op jit(solution)/shard_map/pallas_call | solution.py:520
  29.5 2.1 %collective-permute-start.4 = (bf16[3328,128]{1,0:T(8,128)(2,1)S(1)}, bf16[3328,128]{1,0:T(8,128)(2,1)S(1)}, u32[]{:S(2)}, u32[]{:S(2)}) collective-permute-start(bf16[3328,128]{1,0:T(8,128)(2,1)S(1)} %get-tuple-element.50), channel_id=1, source_target_pairs={{0,1},{1,0},{2,3},{3,2},{4,5},{5,4},{6,7},{7,6},{8,9},{9,8},{10,11... | collective-permute-start | bytes 2555912 | tf_op jit(solution)/shard_map/ppermute | solution.py:479
  31.5 2.2 %collective-permute-done.4 = bf16[3328,128]{1,0:T(8,128)(2,1)S(1)} collective-permute-done((bf16[3328,128]{1,0:T(8,128)(2,1)S(1)}, bf16[3328,128]{1,0:T(8,128)(2,1)S(1)}, u32[]{:S(2)}, u32[]{:S(2)}) %collective-permute-start.4) | collective-permute-done | bytes 852000 | tf_op jit(solution)/shard_map/ppermute | solution.py:479
  33.7 1.1 add_convert_fusion
  34.9 7.2 %all-to-all-start = ((bf16[32,104,128]{2,1,0:T(8,128)(2,1)}), bf16[32,104,128]{2,1,0:T(8,128)(2,1)S(1)}, u32[]{:S(2)}, u32[]{:S(2)}) async-start(bf16[32,104,128]{2,1,0:T(8,128)(2,1)} %bitcast.12), calls=%async_computation | async-start | bytes 1703936 | tf_op jit(solution)/shard_map/all_to_all | solution.py:621
  42.1 3.3 %collective-permute-start.5 = (bf16[4,5120]{1,0:T(4,128)(2,1)S(1)}, bf16[4,5120]{1,0:T(4,128)(2,1)S(1)}, u32[]{:S(2)}, u32[]{:S(2)}) collective-permute-start(bf16[4,5120]{1,0:T(4,128)(2,1)S(1)} %get-tuple-element.54), channel_id=1, source_target_pairs={{0,4},{4,8},{8,12},{12,16},{16,20},{20,24},{24,28},{28,32},{32,36}... | collective-permute-start | bytes 122888 | tf_op jit(solution)/shard_map/ppermute | solution.py:31
  45.4 1.3 %collective-permute-start.6 = (bf16[4,5120]{1,0:T(4,128)(2,1)S(1)}, bf16[4,5120]{1,0:T(4,128)(2,1)S(1)}, u32[]{:S(2)}, u32[]{:S(2)}) collective-permute-start(bf16[4,5120]{1,0:T(4,128)(2,1)S(1)} %get-tuple-element.55), channel_id=1, source_target_pairs={{4,0},{8,4},{12,8},{16,12},{20,16},{24,20},{28,24},{32,28},{36,32}... | collective-permute-start | bytes 122888 | tf_op jit(solution)/shard_map/ppermute | solution.py:31
  46.7 6.9 %collective-permute-done.5.refs_4_ = bf16[4,5120]{1,0:T(4,128)(2,1)S(1)} collective-permute-done((bf16[4,5120]{1,0:T(4,128)(2,1)S(1)}, bf16[4,5120]{1,0:T(4,128)(2,1)S(1)}, u32[]{:S(2)}, u32[]{:S(2)}) %collective-permute-start.5) | collective-permute-done | bytes 40992 | tf_op jit(solution)/shard_map/ppermute | solution.py:31
  53.6 0.2 collective-permute-done.6.refs_5_
  53.8 3.1 %all-to-all-done = bf16[32,104,128]{2,1,0:T(8,128)(2,1)S(1)} async-done(((bf16[32,104,128]{2,1,0:T(8,128)(2,1)}), bf16[32,104,128]{2,1,0:T(8,128)(2,1)S(1)}, u32[]{:S(2)}, u32[]{:S(2)}) %all-to-all-start) | async-done | bytes 852000 | tf_op jit(solution)/shard_map/all_to_all | solution.py:621
  56.9 0.1 reduce_sum.24
  57.0 0.7 broadcast_in_dim.7
  57.7 14.1 %all-to-all-start.1 = ((bf16[8,104,128]{2,1,0:T(8,128)(2,1)}), bf16[8,104,128]{2,1,0:T(8,128)(2,1)S(1)}, u32[]{:S(2)}, u32[]{:S(2)}) async-start(bf16[8,104,128]{2,1,0:T(8,128)(2,1)} %broadcast_in_dim.7), calls=%async_computation.1 | async-start | bytes 425984 | tf_op jit(solution)/shard_map/all_to_all | solution.py:626
  71.9 5.0 %collective-permute-start.7 = (bf16[32,256]{1,0:T(8,128)(2,1)S(1)}, bf16[32,256]{1,0:T(8,128)(2,1)S(1)}, u32[]{:S(2)}, u32[]{:S(2)}) collective-permute-start(bf16[32,256]{1,0:T(8,128)(2,1)S(1)} %get-tuple-element.63), channel_id=1, source_target_pairs={{0,1},{1,2},{2,3},{4,5},{5,6},{6,7},{8,9},{9,10},{10,11},{12,13},{... | collective-permute-start | bytes 49160 | tf_op jit(solution)/shard_map/ppermute | solution.py:31
  76.9 1.9 %collective-permute-start.8 = (bf16[32,256]{1,0:T(8,128)(2,1)S(1)}, bf16[32,256]{1,0:T(8,128)(2,1)S(1)}, u32[]{:S(2)}, u32[]{:S(2)}) collective-permute-start(bf16[32,256]{1,0:T(8,128)(2,1)S(1)} %get-tuple-element.64), channel_id=1, source_target_pairs={{1,0},{2,1},{3,2},{5,4},{6,5},{7,6},{9,8},{10,9},{11,10},{13,12},{... | collective-permute-start | bytes 49160 | tf_op jit(solution)/shard_map/ppermute | solution.py:31
  78.8 0.1 fusion.4.refs_8_
  79.0 4.8 %collective-permute-done.8.refs_7_ = bf16[32,256]{1,0:T(8,128)(2,1)S(1)} collective-permute-done((bf16[32,256]{1,0:T(8,128)(2,1)S(1)}, bf16[32,256]{1,0:T(8,128)(2,1)S(1)}, u32[]{:S(2)}, u32[]{:S(2)}) %collective-permute-start.8) | collective-permute-done | bytes 16416 | tf_op jit(solution)/shard_map/ppermute | solution.py:31
  83.7 1.8 %shard_map.189 = (bf16[8,5120]{1,0:T(8,128)(2,1)}, bf16[4,5120]{1,0:T(4,128)(2,1)}, bf16[2,5120]{1,0:T(2,128)(2,1)}, bf16[1,5120]{1,0:T(2,128)(2,1)}) custom-call(bf16[8,5120]{1,0:T(8,128)(2,1)S(1)} %get-tuple-element.57.refs_0_, bf16[4,5120]{1,0:T(4,128)(2,1)S(1)} %get-tuple-element.58.refs_1_, bf16[2,5120]{1,0:T(2,128)(2,1)S(1)} %get-tuple-element.59.refs_2_, ...), custom_call_target="tpu_custom_call" | custom-call | tf_op jit(solution)/shard_map/pallas_call | solution.py:520
  85.6 2.5 %all-to-all-done.1 = bf16[8,104,128]{2,1,0:T(8,128)(2,1)S(1)} async-done(((bf16[8,104,128]{2,1,0:T(8,128)(2,1)}), bf16[8,104,128]{2,1,0:T(8,128)(2,1)S(1)}, u32[]{:S(2)}, u32[]{:S(2)}) %all-to-all-start.1) | async-done | bytes 213024 | tf_op jit(solution)/shard_map/all_to_all | solution.py:626
  88.3 18.2 %all_to_all.15 = bf16[32,104,128]{2,1,0:T(8,128)(2,1)S(1)} all-to-all(bf16[32,104,128]{2,1,0:T(8,128)(2,1)S(1)} %broadcast_in_dim.8), channel_id=1, replica_groups=mesh['z_hi'=8,'z_lo'=2,'x_lo'=2,'y'=4,'x_hi'=2,'core'=2] {'z_lo','x_lo',..., dimensions={0} | all-to-all | bytes 1703936 | tf_op jit(solution)/shard_map/all_to_all | solution.py:633
  106.5 5.8 %collective-permute-start.9 = (bf16[3328,128]{1,0:T(8,128)(2,1)S(1)}, bf16[3328,128]{1,0:T(8,128)(2,1)S(1)}, u32[]{:S(2)}, u32[]{:S(2)}) collective-permute-start(bf16[3328,128]{1,0:T(8,128)(2,1)S(1)} %bitcast.31), channel_id=1, source_target_pairs={{0,1},{1,0},{2,3},{3,2},{4,5},{5,4},{6,7},{7,6},{8,9},{9,8},{10,11... | collective-permute-start | bytes 2555912 | tf_op jit(solution)/shard_map/ppermute | solution.py:479
  112.2 2.0 %collective-permute-done.9.refs_2_ = bf16[3328,128]{1,0:T(8,128)(2,1)S(1)} collective-permute-done((bf16[3328,128]{1,0:T(8,128)(2,1)S(1)}, bf16[3328,128]{1,0:T(8,128)(2,1)S(1)}, u32[]{:S(2)}, u32[]{:S(2)}) %collective-permute-start.9) | collective-permute-done | bytes 852000 | tf_op jit(solution)/shard_map/ppermute | solution.py:479
  114.2 2.0 %shard_map.190 = (bf16[576,64]{1,0:T(8,128)(2,1)}, bf16[1152,128]{1,0:T(8,128)(2,1)}, bf16[2304,256]{1,0:T(8,128)(2,1)}, bf16[64,128]{1,0:T(8,128)(2,1)}, bf16[6...) custom-call(s32[4]{0:T(128)S(1)} %pad_add_fusion.2.refs_0_, bf16[3328,128]{1,0:T(8,128)(2,1)S(1)} %bitcast.32, ...), custom_call_target="tpu_custom_call" | custom-call | tf_op jit(solution)/shard_map/pallas_call | solution.py:520
  (18 shorter events, 0.3 us)
Async XLA Ops:
  2.5 8.1 %collective-permute-start = (bf16[16,5120]{1,0:T(8,128)(2,1)S(1)}, bf16[16,5120]{1,0:T(8,128)(2,1)S(1)}, u32[]{:S(2)}, u32[]{:S(2)}) collective-permute-start(bf16[16,5120]{1,0:T(8,128)(2,1)S(1)} %get-tuple-element.45), channel_id=1, source_target_pairs={{4,8},{12,16},{20,24},{28,32},{36,40},{44,48},{52,56},{60,64},{68,... | collective-permute-start | bytes 491528 | tf_op jit(solution)/shard_map/ppermute | solution.py:37
  3.2 9.3 %collective-permute-start.1 = (bf16[16,5120]{1,0:T(8,128)(2,1)S(1)}, bf16[16,5120]{1,0:T(8,128)(2,1)S(1)}, u32[]{:S(2)}, u32[]{:S(2)}) collective-permute-start(bf16[16,5120]{1,0:T(8,128)(2,1)S(1)} %get-tuple-element.46), channel_id=1, source_target_pairs={{0,4},{8,12},{16,20},{24,28},{32,36},{40,44},{48,52},{56,60},{64,6... | collective-permute-start | bytes 491528 | tf_op jit(solution)/shard_map/ppermute | solution.py:37
  12.5 9.1 %collective-permute-start.2 = (bf16[48,512]{1,0:T(8,128)(2,1)S(1)}, bf16[48,512]{1,0:T(8,128)(2,1)S(1)}, u32[]{:S(2)}, u32[]{:S(2)}) collective-permute-start(bf16[48,512]{1,0:T(8,128)(2,1)S(1)} %pad_add_fusion.1), channel_id=1, source_target_pairs={{1,2},{2,1},{5,6},{6,5},{9,10},{10,9},{13,14},{14,13},{17,18},{18,... | collective-permute-start | bytes 147464 | tf_op jit(solution)/shard_map/ppermute | solution.py:37
  19.5 3.1 %collective-permute-start.3 = (bf16[48,512]{1,0:T(8,128)(2,1)S(1)}, bf16[48,512]{1,0:T(8,128)(2,1)S(1)}, u32[]{:S(2)}, u32[]{:S(2)}) collective-permute-start(bf16[48,512]{1,0:T(8,128)(2,1)S(1)} %pad_add_fusion), channel_id=1, source_target_pairs={{0,1},{2,3},{1,0},{3,2},{4,5},{6,7},{5,4},{7,6},{8,9},{10,11},{9,8... | collective-permute-start | bytes 147464 | tf_op jit(solution)/shard_map/ppermute | solution.py:37
  29.5 4.3 %collective-permute-start.4 = (bf16[3328,128]{1,0:T(8,128)(2,1)S(1)}, bf16[3328,128]{1,0:T(8,128)(2,1)S(1)}, u32[]{:S(2)}, u32[]{:S(2)}) collective-permute-start(bf16[3328,128]{1,0:T(8,128)(2,1)S(1)} %get-tuple-element.50), channel_id=1, source_target_pairs={{0,1},{1,0},{2,3},{3,2},{4,5},{5,4},{6,7},{7,6},{8,9},{9,8},{10,11... | collective-permute-start | bytes 2555912 | tf_op jit(solution)/shard_map/ppermute | solution.py:479
  34.9 22.0 %all-to-all-start = ((bf16[32,104,128]{2,1,0:T(8,128)(2,1)}), bf16[32,104,128]{2,1,0:T(8,128)(2,1)S(1)}, u32[]{:S(2)}, u32[]{:S(2)}) async-start(bf16[32,104,128]{2,1,0:T(8,128)(2,1)} %bitcast.12), calls=%async_computation | async-start | bytes 1703936 | tf_op jit(solution)/shard_map/all_to_all | solution.py:621
  42.1 41.6 %copy-start = (bf16[3,3,256,256]{3,2,1,0:T(8,128)(2,1)S(1)}, bf16[3,3,256,256]{3,2,1,0:T(8,128)(2,1)}, u32[]{:S(2)}) copy-start(bf16[3,3,256,256]{3,2,1,0:T(8,128)(2,1)} %param.17) | copy-start | bytes 3538948
  42.1 41.6 %copy-start.1 = (bf16[3,3,128,128]{3,2,1,0:T(8,128)(2,1)S(1)}, bf16[3,3,128,128]{3,2,1,0:T(8,128)(2,1)}, u32[]{:S(2)}) copy-start(bf16[3,3,128,128]{3,2,1,0:T(8,128)(2,1)} %param.16) | copy-start | bytes 884740
  42.1 41.6 %copy-start.2 = (bf16[512,64]{0,1:T(8,128)(2,1)S(1)}, bf16[512,64]{0,1:T(8,128)(2,1)}, u32[]{:S(2)}) copy-start(bf16[512,64]{0,1:T(8,128)(2,1)} %param.20) | copy-start | bytes 196612
  42.1 11.5 %collective-permute-start.5 = (bf16[4,5120]{1,0:T(4,128)(2,1)S(1)}, bf16[4,5120]{1,0:T(4,128)(2,1)S(1)}, u32[]{:S(2)}, u32[]{:S(2)}) collective-permute-start(bf16[4,5120]{1,0:T(4,128)(2,1)S(1)} %get-tuple-element.54), channel_id=1, source_target_pairs={{0,4},{4,8},{8,12},{12,16},{16,20},{20,24},{24,28},{28,32},{32,36}... | collective-permute-start | bytes 122888 | tf_op jit(solution)/shard_map/ppermute | solution.py:31
  45.4 8.4 %collective-permute-start.6 = (bf16[4,5120]{1,0:T(4,128)(2,1)S(1)}, bf16[4,5120]{1,0:T(4,128)(2,1)S(1)}, u32[]{:S(2)}, u32[]{:S(2)}) collective-permute-start(bf16[4,5120]{1,0:T(4,128)(2,1)S(1)} %get-tuple-element.55), channel_id=1, source_target_pairs={{4,0},{8,4},{12,8},{16,12},{20,16},{24,20},{28,24},{32,28},{36,32}... | collective-permute-start | bytes 122888 | tf_op jit(solution)/shard_map/ppermute | solution.py:31
  57.7 30.4 %all-to-all-start.1 = ((bf16[8,104,128]{2,1,0:T(8,128)(2,1)}), bf16[8,104,128]{2,1,0:T(8,128)(2,1)S(1)}, u32[]{:S(2)}, u32[]{:S(2)}) async-start(bf16[8,104,128]{2,1,0:T(8,128)(2,1)} %broadcast_in_dim.7), calls=%async_computation.1 | async-start | bytes 425984 | tf_op jit(solution)/shard_map/all_to_all | solution.py:626
  71.9 7.1 %collective-permute-start.7 = (bf16[32,256]{1,0:T(8,128)(2,1)S(1)}, bf16[32,256]{1,0:T(8,128)(2,1)S(1)}, u32[]{:S(2)}, u32[]{:S(2)}) collective-permute-start(bf16[32,256]{1,0:T(8,128)(2,1)S(1)} %get-tuple-element.63), channel_id=1, source_target_pairs={{0,1},{1,2},{2,3},{4,5},{5,6},{6,7},{8,9},{9,10},{10,11},{12,13},{... | collective-permute-start | bytes 49160 | tf_op jit(solution)/shard_map/ppermute | solution.py:31
  76.9 6.9 %collective-permute-start.8 = (bf16[32,256]{1,0:T(8,128)(2,1)S(1)}, bf16[32,256]{1,0:T(8,128)(2,1)S(1)}, u32[]{:S(2)}, u32[]{:S(2)}) collective-permute-start(bf16[32,256]{1,0:T(8,128)(2,1)S(1)} %get-tuple-element.64), channel_id=1, source_target_pairs={{1,0},{2,1},{3,2},{5,4},{6,5},{7,6},{9,8},{10,9},{11,10},{13,12},{... | collective-permute-start | bytes 49160 | tf_op jit(solution)/shard_map/ppermute | solution.py:31
  106.5 7.7 %collective-permute-start.9 = (bf16[3328,128]{1,0:T(8,128)(2,1)S(1)}, bf16[3328,128]{1,0:T(8,128)(2,1)S(1)}, u32[]{:S(2)}, u32[]{:S(2)}) collective-permute-start(bf16[3328,128]{1,0:T(8,128)(2,1)S(1)} %bitcast.31), channel_id=1, source_target_pairs={{0,1},{1,0},{2,3},{3,2},{4,5},{5,4},{6,7},{7,6},{8,9},{9,8},{10,11... | collective-permute-start | bytes 2555912 | tf_op jit(solution)/shard_map/ppermute | solution.py:479

commit v10 on v9

--- a/solution.py
+++ b/solution.py
@@ -23,12 +23,6 @@
 F32 = jnp.float32
 NT = (((1,), (1,)), ((), ()))
 TN = (((0,), (0,)), ((), ()))
-
-
-def moved(block, axis, distance):
-    count = lax.axis_size(axis)
-    route = [(i, i + distance) for i in range(count) if 0 <= i + distance < count]
-    return lax.ppermute(block, axis, route)
 
 
 def traded(block, axis, start):
@@ -126,7 +120,7 @@
 
 
 def forward_kernel(
-    place_ref, keep_ref, send_ref, g1_ref, g2_ref, g3_ref, rim_ref, up_ref, down_ref,
+    place_ref, keep_ref, send_ref, g1_ref, g2_ref, g3_ref, rim_ref, odd_ref, even_ref,
     wx1, wc, wx2, wx3, wx4, xw1, xw2, xw3, d1, d2, d3, gm1, gm2, gm3, upward, downward,
     near, copies,
 ):
@@ -339,8 +333,8 @@
         g3_ref[:, cols] = gm3[at : at + 2, :].astype(BF)
         upward[2:3, cols] = gm3[at : at + 1, :]
         downward[2:3, cols] = gm3[at + 1 : at + 2, :]
-    up_ref[...] = upward[0:4, :].astype(BF)
-    down_ref[...] = downward[0:4, :].astype(BF)
+    odd_ref[...] = jnp.where(is_even, upward[0:4, :], downward[0:4, :]).astype(BF)
+    even_ref[...] = jnp.where(is_even, downward[0:4, :], upward[0:4, :]).astype(BF)
 
     def put(at, first, second):
         rows = slice(at, at + first.shape[0])
@@ -385,10 +379,17 @@
     put(3264, jnp.zeros((64, 128), F32), jnp.zeros((64, 128), F32))
 
 
-def rims_kernel(g1_ref, g2_ref, g3_ref, rim_ref, above_ref, below_ref, left_ref, right_ref, out):
-    g1, g2, g3, above, below = (ref[...].astype(F32) for ref in (g1_ref, g2_ref, g3_ref, above_ref, below_ref))
+def by_side(flag, one_ref, other_ref):
+    one, other = one_ref[...].astype(F32), other_ref[...].astype(F32)
+    return jnp.where(flag, one, other), jnp.where(flag, other, one)
+
+
+def rims_kernel(place_ref, g1_ref, g2_ref, g3_ref, rim_ref, odd_ref, even_ref, outer_ref, inner_ref, left, right):
+    core = place_ref[3]
+    above, below = by_side(lax.rem(place_ref[0], 2) == 0, odd_ref, even_ref)
+    g1, g2, g3 = (ref[...].astype(F32) for ref in (g1_ref, g2_ref, g3_ref))
     rim = rim_ref[...] + above[3:4, 0:1536] + below[3:4, 0:1536]
-    for ref, one, three, four in ((left_ref, 0, 0, 0), (right_ref, WIDE - 128, WIDE - 256, 1408)):
+    for out, one, three, four in ((left, 0, 0, 0), (right, WIDE - 128, WIDE - 256, 1408)):
         ones, threes = slice(one, one + 128), slice(three, three + 256)
         out[...] = jnp.zeros_like(out)
         out[0:1, 0:128] = above[0:1, ones]
@@ -401,18 +402,20 @@
         out[17:19, :] = g3[:, threes]
         out[19:20, :] = below[2:3, threes]
         out[20:21, 0:128] = rim[:, four : four + 128]
-        ref[...] = out[...].astype(BF)
+    outer_ref[...] = jnp.where(core == 0, left[...], right[...]).astype(BF)
+    inner_ref[...] = jnp.where(core == 0, right[...], left[...]).astype(BF)
 
 
 def backward_kernel(
-    g1_ref, g2_ref, g3_ref, rim_ref, above_ref, below_ref, left_ref, right_ref, t1b, k2, k3, p4,
+    place_ref, g1_ref, g2_ref, g3_ref, rim_ref, odd_ref, even_ref, outer_ref, inner_ref, t1b, k2, k3, p4,
     gf1_ref, gf2_ref, gf3_ref, gf4_ref, wide1, wide2, wide3, xw1, xw2, xw3, out2, out3,
 ):
     low = lax.broadcasted_iota(jnp.int32, (1, 128), 1) < 64
     for ref, n in ((xw1, 640), (xw2, 320), (xw3, 160)):
         ref[0:8, :] = jnp.zeros((8, ref.shape[1]), F32)
         ref[8 + n : 16 + n, :] = jnp.zeros((8, ref.shape[1]), F32)
-    above, below, left, right = (ref[...].astype(F32) for ref in (above_ref, below_ref, left_ref, right_ref))
+    above, below = by_side(lax.rem(place_ref[0], 2) == 0, odd_ref, even_ref)
+    left, right = by_side(place_ref[3] == 0, outer_ref, inner_ref)
     for n, (wide, g_ref, top, rows, start, step) in enumerate(
         ((wide1, g1_ref, 3, 8, 0, 128), (wide2, g2_ref, 0, 4, 10, 128), (wide3, g3_ref, 0, 2, 16, 256))
     ):
@@ -556,7 +559,7 @@
     k3 = kernel_three.reshape(3, 768, 256)
     fars = halos(place, x1, x2, x3, x4, cot) + (ahead, in_hbm(k2), in_hbm(k3), in_hbm(p2.T), in_hbm(p3.T), in_hbm(p4.T))
     total = RIM + WIDE + RIM
-    keep, send, g1, g2, g3, rim, up, down = call(
+    keep, send, g1, g2, g3, rim, odd, even = call(
         forward_kernel,
         [
             ((PACK_ROWS, 128), BF), ((PACK_ROWS, 128), BF),
@@ -575,17 +578,21 @@
         scalars=1,
         far=15,
     )
-    return place, keep, send, (g1, g2, g3, rim), up, down, (back, k2, k3, p4.T)
-
-
-def from_beside(grads, above, below):
-    left, right = call(
-        rims_kernel, [((32, 256), BF), ((32, 256), BF)], [((32, 256), F32)], *grads, above, below
-    )
-    return moved(right, COLS, 1), moved(left, COLS, -1)
-
-
-def input_grads(grads, above, below, left, right, weights):
+    return place, keep, send, (g1, g2, g3, rim), odd, even, (back, k2, k3, p4.T)
+
+
+def from_beside(place, grads, odd, even):
+    outer, inner = call(
+        rims_kernel,
+        [((32, 256), BF), ((32, 256), BF)],
+        [((32, 256), F32), ((32, 256), F32)],
+        place, *grads, odd, even,
+        scalars=1,
+    )
+    return traded(outer, COLS, 1), traded(inner, COLS, 0)
+
+
+def input_grads(place, grads, odd, even, outer, inner, weights):
     return call(
         backward_kernel,
         [((8, WIDE), BF), ((4, WIDE), BF), ((2, WIDE), BF), ((1, WIDE), BF)],
@@ -594,8 +601,8 @@
             ((656, 256), F32), ((336, 384), F32), ((176, 768), F32),
             ((320, 128), F32), ((160, 256), F32),
         ],
-        *grads, above, below, left, right,
-        *weights,
+        place, *grads, odd, even, outer, inner, *weights,
+        scalars=1,
     )
 
 
@@ -614,23 +621,23 @@
 
 
 def on_device(*args):
-    place, keep, send, grads, up, down, weights = local_part(*args)
+    place, keep, send, grads, odd, even, weights = local_part(*args)
     part = (keep.astype(F32) + swapped(send, "core", 1).astype(F32)).astype(BF)
-    part, up, down = lax.optimization_barrier((part, up, down))
+    part, odd, even = lax.optimization_barrier((part, odd, even))
 
     pieces = lax.all_to_all(part.reshape(32, -1, 128), SLAB, 0, 0)
-    above, below = moved(down, ROWS, 1), moved(up, ROWS, -1)
-    pieces, above, below = lax.optimization_barrier((pieces, above, below))
+    odd, even = traded(odd, ROWS, 1), traded(even, ROWS, 0)
     part = jnp.sum(pieces.astype(F32), axis=0).astype(BF)
 
     pieces = lax.all_to_all(jnp.broadcast_to(part[None], (8,) + part.shape), "z_hi", 0, 0)
-    left, right = from_beside(grads, above, below)
-    outs = input_grads(grads, above, below, left, right, weights)
-    pieces, outs = lax.optimization_barrier((pieces, outs))
+    pieces, odd, even = lax.optimization_barrier((pieces, odd, even))
     part = jnp.sum(pieces.astype(F32), axis=0).astype(BF)
 
     pieces = jnp.broadcast_to(part[None], (32,) + part.shape)
     mine = lax.all_to_all(pieces, SLAB, 0, 0).reshape(keep.shape)
+    outer, inner = from_beside(place, grads, odd, even)
+    outs = input_grads(place, grads, odd, even, outer, inner, weights)
+    mine, outs = lax.optimization_barrier((mine, outs))
     return tuple(outs) + unpacked(place, mine, swapped(mine, "core", 1))
 
 

time: 117 us -> 115 us (0.983)
  blocking collectives: 18.2 us -> 21.8 us
  waiting for transfers between devices: 24.5 us -> 21.3 us
  starting transfers between devices: 56.8 us -> 53.6 us
    ppermute x4 -> x8, starting transfers between devices: 16.1 us -> 30.8 us  [traded(): lax.ppermute(block, axis, [(i, i + 1) for i in lower] + [(i + 1, i) for i...]
    ppermute x4 -> x0, waiting for transfers between devices: 11.8 us -> none  [moved(): return lax.ppermute(block, axis, route)]
    ppermute x4 -> x0, starting transfers between devices: 11.5 us -> none  [moved(): return lax.ppermute(block, axis, route)]
    all_to_all x1, waiting for transfers between devices: 2.55 us -> 11.1 us  [on_device(): lax.all_to_all(jnp.broadcast_to(part[None], (8,) + part.shape), 'z_hi', 0...]
    all_to_all x1, blocking collectives: 18.2 us -> 21.8 us  [on_device(): pieces = lax.all_to_all(part.reshape(32, -1, 128), SLAB, 0, 0)]
    ppermute x4 -> x8, waiting for transfers between devices: 2.83 us -> 6.02 us  [traded(): lax.ppermute(block, axis, [(i, i + 1) for i in lower] + [(i + 1, i) for i...]
    all_to_all x1, starting transfers between devices: 7.23 us -> 4.05 us  [on_device(): mine = lax.all_to_all(pieces, SLAB, 0, 0).reshape(keep.shape)]
    all_to_all x1, waiting for transfers between devices: 3.14 us -> 0.01 us  [on_device(): mine = lax.all_to_all(pieces, SLAB, 0, 0).reshape(keep.shape)]
  transfers between devices with their start and end apart: 12 -> 12, of which waited for: 9 -> 7; matrix products, arithmetic and copies ran while one was open for 1% -> 1% of each run, Pallas kernels for 2% -> 3%
where the time goes in v10:
time: 115 us; the launch traced here: 114 us
  starting transfers between devices  53.6 us (47%)
  blocking collectives  21.8 us (19%)
  waiting for transfers between devices  21.3 us (19%)
  Pallas kernels  13.5 us (12%)
  local copies, waits for them, and re-layouts  2.61 us (2%)
    ppermute x8, starting transfers between devices, traded(): lax.ppermute(block, axis, [(i, i + 1) for i in lower] + [(i + 1, i) for i...  30.8 us
    all_to_all x1, blocking collectives, on_device(): pieces = lax.all_to_all(part.reshape(32, -1, 128), SLAB, 0, 0)  21.8 us
    all_to_all x1, starting transfers between devices, on_device(): lax.all_to_all(jnp.broadcast_to(part[None], (8,) + part.shape), 'z_hi', 0...  14 us
    pallas_call x5, Pallas kernels, call(): pl.pallas_call(body, out_shape=[jax.ShapeDtypeStruct(shape, dtype) for sh...  13.5 us
    all_to_all x1, waiting for transfers between devices, on_device(): lax.all_to_all(jnp.broadcast_to(part[None], (8,) + part.shape), 'z_hi', 0...  11.1 us
    ppermute x8, waiting for transfers between devices, traded(): lax.ppermute(block, axis, [(i, i + 1) for i in lower] + [(i + 1, i) for i...  6.02 us
    ppermute x2, starting transfers between devices, swapped(): lax.ppermute(block, axis, [(i, i ^ flip) for i in range(lax.axis_size(axi...  4.81 us
    ppermute x2, waiting for transfers between devices, swapped(): lax.ppermute(block, axis, [(i, i ^ flip) for i in range(lax.axis_size(axi...  4.18 us
  transfers between devices with their start and end apart: 12, of which 7 were waited for; matrix products, arithmetic and copies ran while one was open for 1% of the time, Pallas kernels for 3%

profile of v10, /device:TPU:1, one launch (start us, length us, event | category | flops | bytes accessed | tf_op | source)
XLA Modules:
  0.0 114.5 jit_solution(3013211287141409432)
XLA Ops:
  0.7 1.8 %shard_map.186 = (bf16[16,5120]{1,0:T(8,128)(2,1)S(1)}, bf16[16,5120]{1,0:T(8,128)(2,1)S(1)}, bf16[24,512]{1,0:T(8,128)(2,1)S(1)}, bf16[24,512]{1,0:T(8,128)(2,1)S(1)}) custom-call(s32[4]{0:T(128)S(1)} %pad_add_fusion.2.refs_0_, bf16[8,5120]{1,0:T(8,128)(2,1)} %refs_1_.3, bf16[8,5120]{1,0:T(8,128)(2,1)} %refs_2_.3, bf16[4,5120]{1,0:T(4,128)(2,1)} %refs_3_.3, ...), custom_call_target="tpu_custom_call" | custom-call | tf_op jit(solution)/shard_map/pallas_call | solution.py:523
  2.5 0.7 collective-permute-start
  3.2 6.6 %collective-permute-start.1 = (bf16[16,5120]{1,0:T(8,128)(2,1)S(1)}, bf16[16,5120]{1,0:T(8,128)(2,1)S(1)}, u32[]{:S(2)}, u32[]{:S(2)}) collective-permute-start(bf16[16,5120]{1,0:T(8,128)(2,1)S(1)} %get-tuple-element.46), channel_id=1, source_target_pairs={{0,4},{8,12},{16,20},{24,28},{32,36},{40,44},{48,52},{56,60},{64,6... | collective-permute-start | bytes 491528 | tf_op jit(solution)/shard_map/ppermute | solution.py:31
  9.8 0.9 slice_bitcast_fusion
  10.6 1.8 %collective-permute-done.1.refs_7_ = bf16[16,5120]{1,0:T(8,128)(2,1)S(1)} collective-permute-done((bf16[16,5120]{1,0:T(8,128)(2,1)S(1)}, bf16[16,5120]{1,0:T(8,128)(2,1)S(1)}, u32[]{:S(2)}, u32[]{:S(2)}) %collective-permute-start.1) | collective-permute-done | bytes 163872 | tf_op jit(solution)/shard_map/ppermute | solution.py:31
  12.5 7.0 %collective-permute-start.2 = (bf16[48,512]{1,0:T(8,128)(2,1)S(1)}, bf16[48,512]{1,0:T(8,128)(2,1)S(1)}, u32[]{:S(2)}, u32[]{:S(2)}) collective-permute-start(bf16[48,512]{1,0:T(8,128)(2,1)S(1)} %pad_add_fusion.1), channel_id=1, source_target_pairs={{1,2},{2,1},{5,6},{6,5},{9,10},{10,9},{13,14},{14,13},{17,18},{18,... | collective-permute-start | bytes 147464 | tf_op jit(solution)/shard_map/ppermute | solution.py:31
  19.5 1.9 %collective-permute-start.3 = (bf16[48,512]{1,0:T(8,128)(2,1)S(1)}, bf16[48,512]{1,0:T(8,128)(2,1)S(1)}, u32[]{:S(2)}, u32[]{:S(2)}) collective-permute-start(bf16[48,512]{1,0:T(8,128)(2,1)S(1)} %pad_add_fusion), channel_id=1, source_target_pairs={{0,1},{2,3},{1,0},{3,2},{4,5},{6,7},{5,4},{7,6},{8,9},{10,11},{9,8... | collective-permute-start | bytes 147464 | tf_op jit(solution)/shard_map/ppermute | solution.py:31
  21.4 0.1 maximum_maximum_fusion.refs_10_
  21.6 1.0 collective-permute-done.3.refs_9_
  22.6 6.9 %shard_map.187 = (bf16[3328,128]{1,0:T(8,128)(2,1)S(1)}, bf16[3328,128]{1,0:T(8,128)(2,1)S(1)}, bf16[8,5120]{1,0:T(8,128)(2,1)S(1)}, bf16[4,5120]{1,0:T(4,128)(2...) custom-call(s32[4]{0:T(128)S(1)} %pad_add_fusion.2.refs_0_, ...), custom_call_target="tpu_custom_call" | custom-call | tf_op jit(solution)/shard_map/pallas_call | solution.py:523
  29.5 2.1 %collective-permute-start.4 = (bf16[3328,128]{1,0:T(8,128)(2,1)S(1)}, bf16[3328,128]{1,0:T(8,128)(2,1)S(1)}, u32[]{:S(2)}, u32[]{:S(2)}) collective-permute-start(bf16[3328,128]{1,0:T(8,128)(2,1)S(1)} %get-tuple-element.50), channel_id=1, source_target_pairs={{0,1},{1,0},{2,3},{3,2},{4,5},{5,4},{6,7},{7,6},{8,9},{9,8},{10,11... | collective-permute-start | bytes 2555912 | tf_op jit(solution)/shard_map/ppermute | solution.py:482
  31.5 2.2 %collective-permute-done.4 = bf16[3328,128]{1,0:T(8,128)(2,1)S(1)} collective-permute-done((bf16[3328,128]{1,0:T(8,128)(2,1)S(1)}, bf16[3328,128]{1,0:T(8,128)(2,1)S(1)}, u32[]{:S(2)}, u32[]{:S(2)}) %collective-permute-start.4) | collective-permute-done | bytes 852000 | tf_op jit(solution)/shard_map/ppermute | solution.py:482
  33.7 0.2 add_convert_fusion
  34.0 21.8 %all_to_all.15 = bf16[32,104,128]{2,1,0:T(8,128)(2,1)S(1)} all-to-all(bf16[32,104,128]{2,1,0:T(8,128)(2,1)S(1)} %bitcast.37), channel_id=1, replica_groups=mesh['z_hi'=8,'z_lo'=2,'x_lo'=2,'y'=4,'x_hi'=2,'core'=2] {'z_lo','x_lo',..., dimensions={0} | all-to-all | bytes 1703936 | tf_op jit(solution)/shard_map/all_to_all | solution.py:628
  55.8 0.1 reduce_sum.24
  55.9 0.7 broadcast_in_dim.7
  56.6 14.0 %all-to-all-start.1 = ((bf16[8,104,128]{2,1,0:T(8,128)(2,1)}), bf16[8,104,128]{2,1,0:T(8,128)(2,1)S(1)}, u32[]{:S(2)}, u32[]{:S(2)}) async-start(bf16[8,104,128]{2,1,0:T(8,128)(2,1)} %broadcast_in_dim.7), calls=%async_computation.1 | async-start | bytes 425984 | tf_op jit(solution)/shard_map/all_to_all | solution.py:632
  70.6 0.7 collective-permute-start.5
  71.3 3.4 %collective-permute-start.6 = (bf16[4,5120]{1,0:T(4,128)(2,1)S(1)}, bf16[4,5120]{1,0:T(4,128)(2,1)S(1)}, u32[]{:S(2)}, u32[]{:S(2)}) collective-permute-start(bf16[4,5120]{1,0:T(4,128)(2,1)S(1)} %get-tuple-element.55), channel_id=1, source_target_pairs={{0,4},{8,12},{16,20},{24,28},{32,36},{40,44},{48,52},{56,60},{64,6... | collective-permute-start | bytes 122888 | tf_op jit(solution)/shard_map/ppermute | solution.py:31
  74.7 1.4 %collective-permute-done.6.refs_6_ = bf16[4,5120]{1,0:T(4,128)(2,1)S(1)} collective-permute-done((bf16[4,5120]{1,0:T(4,128)(2,1)S(1)}, bf16[4,5120]{1,0:T(4,128)(2,1)S(1)}, u32[]{:S(2)}, u32[]{:S(2)}) %collective-permute-start.6) | collective-permute-done | bytes 40992 | tf_op jit(solution)/shard_map/ppermute | solution.py:31
  76.0 11.1 %all-to-all-done.1 = bf16[8,104,128]{2,1,0:T(8,128)(2,1)S(1)} async-done(((bf16[8,104,128]{2,1,0:T(8,128)(2,1)}), bf16[8,104,128]{2,1,0:T(8,128)(2,1)S(1)}, u32[]{:S(2)}, u32[]{:S(2)}) %all-to-all-start.1) | async-done | bytes 213024 | tf_op jit(solution)/shard_map/all_to_all | solution.py:632
  87.1 1.0 broadcast_in_dim.8
  88.1 4.0 %all-to-all-start.2 = ((bf16[32,104,128]{2,1,0:T(8,128)(2,1)}), bf16[32,104,128]{2,1,0:T(8,128)(2,1)S(1)}, u32[]{:S(2)}, u32[]{:S(2)}) async-start(bf16[32,104,128]{2,1,0:T(8,128)(2,1)} %broadcast_in_dim.8), calls=%async_computation.2 | async-start | bytes 1703936 | tf_op jit(solution)/shard_map/all_to_all | solution.py:637
  92.2 0.6 shard_map.188
  92.8 8.7 %collective-permute-start.7 = (bf16[32,256]{1,0:T(8,128)(2,1)S(1)}, bf16[32,256]{1,0:T(8,128)(2,1)S(1)}, u32[]{:S(2)}, u32[]{:S(2)}) collective-permute-start(bf16[32,256]{1,0:T(8,128)(2,1)S(1)} %get-tuple-element.63), channel_id=1, source_target_pairs={{1,2},{2,1},{5,6},{6,5},{9,10},{10,9},{13,14},{14,13},{17,18},{18,... | collective-permute-start | bytes 49160 | tf_op jit(solution)/shard_map/ppermute | solution.py:31
  101.5 1.9 %collective-permute-start.8 = (bf16[32,256]{1,0:T(8,128)(2,1)S(1)}, bf16[32,256]{1,0:T(8,128)(2,1)S(1)}, u32[]{:S(2)}, u32[]{:S(2)}) collective-permute-start(bf16[32,256]{1,0:T(8,128)(2,1)S(1)} %get-tuple-element.64), channel_id=1, source_target_pairs={{0,1},{2,3},{1,0},{3,2},{4,5},{6,7},{5,4},{7,6},{8,9},{10,11},{9,8... | collective-permute-start | bytes 49160 | tf_op jit(solution)/shard_map/ppermute | solution.py:31
  103.4 0.1 fusion.4.refs_9_
  103.6 1.8 %collective-permute-done.7.refs_7_ = bf16[32,256]{1,0:T(8,128)(2,1)S(1)} collective-permute-done((bf16[32,256]{1,0:T(8,128)(2,1)S(1)}, bf16[32,256]{1,0:T(8,128)(2,1)S(1)}, u32[]{:S(2)}, u32[]{:S(2)}) %collective-permute-start.7) | collective-permute-done | bytes 16416 | tf_op jit(solution)/shard_map/ppermute | solution.py:31
  105.4 2.4 %shard_map.189 = (bf16[8,5120]{1,0:T(8,128)(2,1)}, bf16[4,5120]{1,0:T(4,128)(2,1)}, bf16[2,5120]{1,0:T(2,128)(2,1)}, bf16[1,5120]{1,0:T(2,128)(2,1)}) custom-call(s32[4]{0:T(128)S(1)} %pad_add_fusion.2.refs_0_, bf16[8,5120]{1,0:T(8,128)(2,1)S(1)} %get-tuple-element.57.refs_1_, bf16[4,5120]{1,0:T(4,128)(2,1)S(1)} %get-tuple-element.58.refs_2_, ...), custom_call_target="tpu_custom_call" | custom-call | tf_op jit(solution)/shard_map/pallas_call | solution.py:523
  107.8 2.7 %collective-permute-start.9 = (bf16[3328,128]{1,0:T(8,128)(2,1)S(1)}, bf16[3328,128]{1,0:T(8,128)(2,1)S(1)}, u32[]{:S(2)}, u32[]{:S(2)}) collective-permute-start(bf16[3328,128]{1,0:T(8,128)(2,1)S(1)} %bitcast.31), channel_id=1, source_target_pairs={{0,1},{1,0},{2,3},{3,2},{4,5},{5,4},{6,7},{7,6},{8,9},{9,8},{10,11... | collective-permute-start | bytes 2555912 | tf_op jit(solution)/shard_map/ppermute | solution.py:482
  110.5 2.0 %collective-permute-done.9.refs_2_ = bf16[3328,128]{1,0:T(8,128)(2,1)S(1)} collective-permute-done((bf16[3328,128]{1,0:T(8,128)(2,1)S(1)}, bf16[3328,128]{1,0:T(8,128)(2,1)S(1)}, u32[]{:S(2)}, u32[]{:S(2)}) %collective-permute-start.9) | collective-permute-done | bytes 852000 | tf_op jit(solution)/shard_map/ppermute | solution.py:482
  112.5 2.0 %shard_map.190 = (bf16[576,64]{1,0:T(8,128)(2,1)}, bf16[1152,128]{1,0:T(8,128)(2,1)}, bf16[2304,256]{1,0:T(8,128)(2,1)}, bf16[64,128]{1,0:T(8,128)(2,1)}, bf16[6...) custom-call(s32[4]{0:T(128)S(1)} %pad_add_fusion.2.refs_0_, bf16[3328,128]{1,0:T(8,128)(2,1)S(1)} %bitcast.32, ...), custom_call_target="tpu_custom_call" | custom-call | tf_op jit(solution)/shard_map/pallas_call | solution.py:523
  (18 shorter events, 0.2 us)
Async XLA Ops:
  2.5 8.1 %collective-permute-start = (bf16[16,5120]{1,0:T(8,128)(2,1)S(1)}, bf16[16,5120]{1,0:T(8,128)(2,1)S(1)}, u32[]{:S(2)}, u32[]{:S(2)}) collective-permute-start(bf16[16,5120]{1,0:T(8,128)(2,1)S(1)} %get-tuple-element.45), channel_id=1, source_target_pairs={{4,8},{12,16},{20,24},{28,32},{36,40},{44,48},{52,56},{60,64},{68,... | collective-permute-start | bytes 491528 | tf_op jit(solution)/shard_map/ppermute | solution.py:31
  3.2 9.3 %collective-permute-start.1 = (bf16[16,5120]{1,0:T(8,128)(2,1)S(1)}, bf16[16,5120]{1,0:T(8,128)(2,1)S(1)}, u32[]{:S(2)}, u32[]{:S(2)}) collective-permute-start(bf16[16,5120]{1,0:T(8,128)(2,1)S(1)} %get-tuple-element.46), channel_id=1, source_target_pairs={{0,4},{8,12},{16,20},{24,28},{32,36},{40,44},{48,52},{56,60},{64,6... | collective-permute-start | bytes 491528 | tf_op jit(solution)/shard_map/ppermute | solution.py:31
  12.5 9.1 %collective-permute-start.2 = (bf16[48,512]{1,0:T(8,128)(2,1)S(1)}, bf16[48,512]{1,0:T(8,128)(2,1)S(1)}, u32[]{:S(2)}, u32[]{:S(2)}) collective-permute-start(bf16[48,512]{1,0:T(8,128)(2,1)S(1)} %pad_add_fusion.1), channel_id=1, source_target_pairs={{1,2},{2,1},{5,6},{6,5},{9,10},{10,9},{13,14},{14,13},{17,18},{18,... | collective-permute-start | bytes 147464 | tf_op jit(solution)/shard_map/ppermute | solution.py:31
  19.5 3.1 %collective-permute-start.3 = (bf16[48,512]{1,0:T(8,128)(2,1)S(1)}, bf16[48,512]{1,0:T(8,128)(2,1)S(1)}, u32[]{:S(2)}, u32[]{:S(2)}) collective-permute-start(bf16[48,512]{1,0:T(8,128)(2,1)S(1)} %pad_add_fusion), channel_id=1, source_target_pairs={{0,1},{2,3},{1,0},{3,2},{4,5},{6,7},{5,4},{7,6},{8,9},{10,11},{9,8... | collective-permute-start | bytes 147464 | tf_op jit(solution)/shard_map/ppermute | solution.py:31
  29.5 4.3 %collective-permute-start.4 = (bf16[3328,128]{1,0:T(8,128)(2,1)S(1)}, bf16[3328,128]{1,0:T(8,128)(2,1)S(1)}, u32[]{:S(2)}, u32[]{:S(2)}) collective-permute-start(bf16[3328,128]{1,0:T(8,128)(2,1)S(1)} %get-tuple-element.50), channel_id=1, source_target_pairs={{0,1},{1,0},{2,3},{3,2},{4,5},{5,4},{6,7},{7,6},{8,9},{9,8},{10,11... | collective-permute-start | bytes 2555912 | tf_op jit(solution)/shard_map/ppermute | solution.py:482
  56.6 30.4 %all-to-all-start.1 = ((bf16[8,104,128]{2,1,0:T(8,128)(2,1)}), bf16[8,104,128]{2,1,0:T(8,128)(2,1)S(1)}, u32[]{:S(2)}, u32[]{:S(2)}) async-start(bf16[8,104,128]{2,1,0:T(8,128)(2,1)} %broadcast_in_dim.7), calls=%async_computation.1 | async-start | bytes 425984 | tf_op jit(solution)/shard_map/all_to_all | solution.py:632
  70.6 4.0 %collective-permute-start.5 = (bf16[4,5120]{1,0:T(4,128)(2,1)S(1)}, bf16[4,5120]{1,0:T(4,128)(2,1)S(1)}, u32[]{:S(2)}, u32[]{:S(2)}) collective-permute-start(bf16[4,5120]{1,0:T(4,128)(2,1)S(1)} %get-tuple-element.54), channel_id=1, source_target_pairs={{4,8},{12,16},{20,24},{28,32},{36,40},{44,48},{52,56},{60,64},{68,... | collective-permute-start | bytes 122888 | tf_op jit(solution)/shard_map/ppermute | solution.py:31
  71.3 4.7 %collective-permute-start.6 = (bf16[4,5120]{1,0:T(4,128)(2,1)S(1)}, bf16[4,5120]{1,0:T(4,128)(2,1)S(1)}, u32[]{:S(2)}, u32[]{:S(2)}) collective-permute-start(bf16[4,5120]{1,0:T(4,128)(2,1)S(1)} %get-tuple-element.55), channel_id=1, source_target_pairs={{0,4},{8,12},{16,20},{24,28},{32,36},{40,44},{48,52},{56,60},{64,6... | collective-permute-start | bytes 122888 | tf_op jit(solution)/shard_map/ppermute | solution.py:31
  88.1 17.3 %copy-start = (bf16[3,3,256,256]{3,2,1,0:T(8,128)(2,1)S(1)}, bf16[3,3,256,256]{3,2,1,0:T(8,128)(2,1)}, u32[]{:S(2)}) copy-start(bf16[3,3,256,256]{3,2,1,0:T(8,128)(2,1)} %param.17) | copy-start | bytes 3538948
  88.1 17.3 %copy-start.1 = (bf16[3,3,128,128]{3,2,1,0:T(8,128)(2,1)S(1)}, bf16[3,3,128,128]{3,2,1,0:T(8,128)(2,1)}, u32[]{:S(2)}) copy-start(bf16[3,3,128,128]{3,2,1,0:T(8,128)(2,1)} %param.16) | copy-start | bytes 884740
  88.1 17.3 %copy-start.2 = (bf16[512,64]{0,1:T(8,128)(2,1)S(1)}, bf16[512,64]{0,1:T(8,128)(2,1)}, u32[]{:S(2)}) copy-start(bf16[512,64]{0,1:T(8,128)(2,1)} %param.20) | copy-start | bytes 196612
  88.1 19.7 %all-to-all-start.2 = ((bf16[32,104,128]{2,1,0:T(8,128)(2,1)}), bf16[32,104,128]{2,1,0:T(8,128)(2,1)S(1)}, u32[]{:S(2)}, u32[]{:S(2)}) async-start(bf16[32,104,128]{2,1,0:T(8,128)(2,1)} %broadcast_in_dim.8), calls=%async_computation.2 | async-start | bytes 1703936 | tf_op jit(solution)/shard_map/all_to_all | solution.py:637
  92.8 12.6 %collective-permute-start.7 = (bf16[32,256]{1,0:T(8,128)(2,1)S(1)}, bf16[32,256]{1,0:T(8,128)(2,1)S(1)}, u32[]{:S(2)}, u32[]{:S(2)}) collective-permute-start(bf16[32,256]{1,0:T(8,128)(2,1)S(1)} %get-tuple-element.63), channel_id=1, source_target_pairs={{1,2},{2,1},{5,6},{6,5},{9,10},{10,9},{13,14},{14,13},{17,18},{18,... | collective-permute-start | bytes 49160 | tf_op jit(solution)/shard_map/ppermute | solution.py:31
  101.5 3.9 %collective-permute-start.8 = (bf16[32,256]{1,0:T(8,128)(2,1)S(1)}, bf16[32,256]{1,0:T(8,128)(2,1)S(1)}, u32[]{:S(2)}, u32[]{:S(2)}) collective-permute-start(bf16[32,256]{1,0:T(8,128)(2,1)S(1)} %get-tuple-element.64), channel_id=1, source_target_pairs={{0,1},{2,3},{1,0},{3,2},{4,5},{6,7},{5,4},{7,6},{8,9},{10,11},{9,8... | collective-permute-start | bytes 49160 | tf_op jit(solution)/shard_map/ppermute | solution.py:31
  107.8 4.7 %collective-permute-start.9 = (bf16[3328,128]{1,0:T(8,128)(2,1)S(1)}, bf16[3328,128]{1,0:T(8,128)(2,1)S(1)}, u32[]{:S(2)}, u32[]{:S(2)}) collective-permute-start(bf16[3328,128]{1,0:T(8,128)(2,1)S(1)} %bitcast.31), channel_id=1, source_target_pairs={{0,1},{1,0},{2,3},{3,2},{4,5},{5,4},{6,7},{7,6},{8,9},{9,8},{10,11... | collective-permute-start | bytes 2555912 | tf_op jit(solution)/shard_map/ppermute | solution.py:482
